TPU v7x, 32 devices: a whole 2x2x4 slice. The times are simulated.
32 devices in a mesh: member: 4 (over y, core), space: 8 (over z, x).
Axes of the slice: x: 2, y: 2, z: 4, core: 2. Of those that a mesh axis runs over, the one named last changes fastest.
Arguments:
- states: bfloat16 [4, 73, 392, 720], P('member', None, 'space'), may hold values from -6 to 6
- observed: bfloat16 [73, 392, 720], P(None, 'space'), may hold values from -6 to 6
- band_rows: int32 [8], replicated, may hold values from 1 to 49, 361 in all
- encoder_weight: bfloat16 [73, 128], replicated, may hold values from -0.75 to 0.75
- mixing_weight: bfloat16 [128, 128], replicated, may hold values from -0.5 to 0.5
- degree_gain: float32 [368, 128], replicated, may hold values from 0.25 to 2
- decoder_weight: bfloat16 [128, 73], replicated, may hold values from -0.5 to 0.5
Outputs:
- prediction: bfloat16 [4, 73, 392, 720], P('member', None, 'space')
- state_grad: bfloat16 [4, 73, 392, 720], P('member', None, 'space')
Inputs may be any that keep to these rules, and one draw needn't show every extreme that they name: Band d holds the next band_rows[d] latitudes, from the north pole southward, in the first rows of the d-th block of 49 rows; the remaining rows of a block are padding, ignored in states and observed. The bands' rows sum to 361, and some band has exactly 49 rows.
All inputs are finite; a program needn't handle non-finite values.
Results may differ from a plain program's by a relative error of at most 0.014.
Values may be sent and summed in bfloat16 or wider, within the bound.
No kernel may reach another device: no remote copies, remote signals or barrier semaphores. Data moves between devices by JAX's collectives and lax.ppermute only.
A program may use at most 256 MiB of HBM per device.

v0:
```python
import math

import jax
import jax.numpy as jnp
from jax import lax
from jax.sharding import PartitionSpec as P

NLAT = 361
LMAX = 360


EPSILON = 1e-05


def row_geometry(band_rows, band_len, lat_count):
    band_count = band_rows.shape[0]
    row_index = jnp.arange(band_count * band_len, dtype=jnp.int32)
    row_owner = row_index // band_len
    offset = row_index - row_owner * band_len
    starts = jnp.cumsum(band_rows) - band_rows
    owner_hot = (row_owner[:, None] == jnp.arange(band_count, dtype=jnp.int32)[None, :]).astype(
        jnp.int32
    )
    first_lat = jnp.sum(owner_hot * starts[None, :], axis=1)
    length = jnp.sum(owner_hot * band_rows[None, :], axis=1)
    live_rows = offset < length
    latitude = jnp.minimum(first_lat + offset, lat_count - 1)
    colatitude = latitude.astype(jnp.float32) * (math.pi / (lat_count - 1))
    return (live_rows, jnp.cos(colatitude), jnp.sin(colatitude))


def diagonal_logs(order_count):
    kvalues = jnp.arange(order_count, dtype=jnp.float32)
    increments = jnp.where(
        kvalues >= 1.0, 0.5 * jnp.log((2.0 * kvalues + 1.0) / jnp.maximum(2.0 * kvalues, 1.0)), 0.0
    )
    return 0.5 * math.log(0.5) + jnp.cumsum(increments)


def legendre(orders, log_diag, cosines, sines, top_degree, degrees, quad_weight, live_all):
    order_count = orders.shape[0]
    row_count = cosines.shape[0]
    order_f = orders.astype(jnp.float32)[None, :]
    log_start = (
        log_diag[:, None]
        + orders.astype(jnp.float32)[:, None] * jnp.log(jnp.maximum(sines, 1e-30))[None, :]
    )
    empty_rows = jnp.zeros((order_count, row_count), jnp.float32)
    cosine_row = cosines[None, :]
    degree_int = jnp.arange(degrees, dtype=jnp.int32)
    degree_f = degree_int.astype(jnp.float32)[:, None]
    up_table = jnp.sqrt(
        (4.0 * degree_f * degree_f - 1.0)
        / jnp.maximum(degree_f * degree_f - order_f * order_f, 1.0)
    )
    back_table = jnp.sqrt(
        jnp.maximum((degree_f - 1.0) * (degree_f - 1.0) - order_f * order_f, 0.0)
        / jnp.maximum(4.0 * (degree_f - 1.0) * (degree_f - 1.0) - 1.0, 1.0)
    )
    past_table = degree_int[:, None] > orders[None, :]
    onset_table = degree_int[:, None] == orders[None, :]
    keep_table = (past_table | onset_table) & (degree_int[:, None] <= top_degree)
    block_count = degrees // 16
    quad_row = quad_weight[None, None, :]
    live_row = live_all[None, None, :]

    def blocked(table):
        return table.reshape((block_count, 16) + table.shape[1:])

    def recur_block(state_in, inputs):
        first, second, log_scale = state_in
        up_block, back_block, past_block, onset_block, keep_block = inputs
        stacked = []
        for position in range(16):
            current = jnp.where(
                past_block[position][:, None],
                up_block[position][:, None]
                * (cosine_row * first - back_block[position][:, None] * second),
                jnp.where(onset_block[position][:, None], 1.0, 0.0),
            )
            stacked.append(current)
            second = first
            first = current
        values = jnp.stack(stacked) * jnp.exp(log_scale)[None]
        values = jnp.where(keep_block[:, :, None], values, 0.0)
        forward_part = (values * quad_row).astype(jnp.bfloat16)
        inverse_part = (values * live_row).astype(jnp.bfloat16)
        magnitude = jnp.maximum(jnp.abs(first), jnp.abs(second))
        factor = jnp.where(magnitude > 1.0, magnitude, 1.0)
        return (
            (first / factor, second / factor, log_scale + jnp.log(factor)),
            (forward_part, inverse_part),
        )

    scanned = (
        blocked(up_table),
        blocked(back_table),
        blocked(past_table),
        blocked(onset_table),
        blocked(keep_table),
    )
    final_state, tables = lax.scan(recur_block, (empty_rows, empty_rows, log_start), scanned)
    forward_table = tables[0].reshape(degrees, order_count, row_count)
    inverse_table = tables[1].reshape(degrees, order_count, row_count)
    return (forward_table, inverse_table)


def transforms(lon_count, order_count, top_degree):
    lon_index = jnp.arange(lon_count, dtype=jnp.int32)
    order_index = jnp.arange(order_count, dtype=jnp.int32)
    angle_table = (order_index[:, None] * lon_index[None, :] % lon_count).astype(jnp.float32) * (
        2.0 * math.pi / lon_count
    )
    live_order = (order_index <= top_degree)[:, None]
    cosines = jnp.where(live_order, jnp.cos(angle_table), 0.0)
    sines = jnp.where(live_order, jnp.sin(angle_table), 0.0)
    weight = jnp.where((order_index == 0) | (2 * order_index == lon_count), 1.0, 2.0)[:, None]
    forward = jnp.transpose(jnp.stack([cosines, -sines]), (2, 0, 1)) / lon_count
    inverse = jnp.stack([weight * cosines, -weight * sines])
    return (forward.astype(jnp.bfloat16), inverse.astype(jnp.bfloat16))


def gelu_slope(values):
    return 0.5 * (1.0 + lax.erf(values * (1.0 / math.sqrt(2.0)))) + values * jnp.exp(
        -0.5 * values * values
    ) * (1.0 / math.sqrt(2.0 * math.pi))


def score_block(own_fields, everyone, observed, area_weight):
    own_f = own_fields.astype(jnp.float32)
    truth_gap = own_f - observed.astype(jnp.float32)[None]
    truth_dist = jnp.sqrt(jnp.sum(truth_gap * truth_gap, axis=1, keepdims=True) + EPSILON)

    def accumulate(running, other_member):
        member_gap = own_f - other_member.astype(jnp.float32)[None]
        member_dist = jnp.sqrt(jnp.sum(member_gap * member_gap, axis=1, keepdims=True) + EPSILON)
        return (running + member_gap / member_dist, None)

    pair_sum, unused = lax.scan(accumulate, jnp.zeros(own_f.shape, jnp.float32), everyone)
    result = area_weight[None, None, :, None] * (
        truth_gap / truth_dist - pair_sum / everyone.shape[0]
    )
    return result.astype(jnp.bfloat16)


def to_orders(block, finish):
    return finish(lax.all_to_all(block, "space", split_axis=1, concat_axis=2, tiled=True))


def to_bands(block, finish):
    return finish(lax.all_to_all(block, "space", split_axis=2, concat_axis=1, tiled=True))


def on_device(
    states, observed, band_rows, encoder_weight, mixing_weight, degree_gain, decoder_weight
):
    space_size = lax.axis_size("space")
    space_index = lax.axis_index("space")
    band_len = states.shape[2]
    lon_count = states.shape[3]
    order_dev = LMAX // space_size + 1
    order_count = order_dev * space_size
    degrees = degree_gain.shape[0]
    live_rows, cosines, sines = row_geometry(band_rows, band_len, NLAT)
    live_all = live_rows.astype(jnp.float32)
    first_order = space_index * order_dev
    orders = first_order + jnp.arange(order_dev, dtype=jnp.int32)
    log_diag = lax.dynamic_slice_in_dim(diagonal_logs(order_count), first_order, order_dev)
    quad_weight = live_all * sines * (math.pi / (NLAT - 1))
    legendre_forward, legendre_inverse = legendre(
        orders, log_diag, cosines, sines, LMAX, degrees, quad_weight, live_all
    )
    fwd_table, inv_table = transforms(lon_count, order_count, LMAX)
    live_own = lax.dynamic_slice_in_dim(live_all, space_index * band_len, band_len)
    sines_own = lax.dynamic_slice_in_dim(sines, space_index * band_len, band_len)
    area_weight = 8.0 * sines_own * live_own
    member = states[0]
    hidden = (
        jnp.einsum("frl,fc->rlc", member, encoder_weight, preferred_element_type=jnp.float32)
        * live_own[:, None, None]
    ).astype(jnp.bfloat16)
    longitude_modes = jnp.einsum(
        "rlc,lkm->kmrc", hidden, fwd_table, preferred_element_type=jnp.float32
    ).astype(jnp.bfloat16)

    def analyse(incoming_rows):
        return jnp.einsum(
            "ghqn,uhq->guhn", incoming_rows, legendre_forward, preferred_element_type=jnp.float32
        ).astype(jnp.bfloat16)

    harmonic_weights = to_orders(longitude_modes, analyse)
    masked_spectrum = (
        jnp.einsum(
            "klmc,cd->klmd", harmonic_weights, mixing_weight, preferred_element_type=jnp.float32
        )
        * degree_gain[None, :, None, :]
    ).astype(jnp.bfloat16)
    rebuilt_field = jnp.einsum(
        "pjcx,jco->pcox", masked_spectrum, legendre_inverse, preferred_element_type=jnp.float32
    ).astype(jnp.bfloat16)

    def longitudes(incoming_rows):
        return jnp.einsum(
            "kmrc,kml->rlc", incoming_rows, inv_table, preferred_element_type=jnp.float32
        )

    grid_field = to_bands(rebuilt_field, longitudes)
    block_out = (
        (jax.nn.gelu(grid_field, approximate=False) + hidden.astype(jnp.float32))
        * live_own[:, None, None]
    ).astype(jnp.bfloat16)
    decoded = jnp.einsum(
        "rlc,cf->frl", block_out, decoder_weight, preferred_element_type=jnp.float32
    )
    prediction = ((member.astype(jnp.float32) + decoded) * live_own[None, :, None]).astype(
        jnp.bfloat16
    )[None]
    everyone = lax.all_gather(prediction, "member", axis=0, tiled=True)
    score_grad = score_block(prediction, everyone, observed, area_weight)
    grad_pred = score_grad[0]
    grad_block = jnp.einsum(
        "frl,cf->rlc", grad_pred, decoder_weight, preferred_element_type=jnp.float32
    )
    grad_field = (grad_block * gelu_slope(grid_field)).astype(jnp.bfloat16)
    rebuilt_gradient = jnp.einsum(
        "rlc,kml->kmrc", grad_field, inv_table, preferred_element_type=jnp.float32
    ).astype(jnp.bfloat16)

    def project(incoming_rows):
        return jnp.einsum(
            "ghqn,uhq->guhn", incoming_rows, legendre_inverse, preferred_element_type=jnp.float32
        )

    masked_gradient = to_orders(rebuilt_gradient, project)
    grad_scaled = (masked_gradient * degree_gain[None, :, None, :]).astype(jnp.bfloat16)
    harmonic_gradient = jnp.einsum(
        "klmd,cd->klmc", grad_scaled, mixing_weight, preferred_element_type=jnp.float32
    ).astype(jnp.bfloat16)
    longitude_gradient = jnp.einsum(
        "sbzv,bze->szev", harmonic_gradient, legendre_forward, preferred_element_type=jnp.float32
    ).astype(jnp.bfloat16)

    def spread(incoming_rows):
        return jnp.einsum(
            "kmrc,lkm->rlc", incoming_rows, fwd_table, preferred_element_type=jnp.float32
        )

    grad_spectral = to_bands(longitude_gradient, spread)
    grad_hidden = ((grad_block + grad_spectral) * live_own[:, None, None]).astype(jnp.bfloat16)
    encoded_back = jnp.einsum(
        "rlc,fc->frl", grad_hidden, encoder_weight, preferred_element_type=jnp.float32
    )
    state_grad = ((grad_pred.astype(jnp.float32) + encoded_back) * live_own[None, :, None]).astype(
        jnp.bfloat16
    )[None]
    return (prediction, state_grad)


def solution(mesh):
    in_specs = (P("member", None, "space", None), P(None, "space", None), P(), P(), P(), P(), P())
    out_specs = (P("member", None, "space", None), P("member", None, "space", None))
    return jax.shard_map(
        on_device, mesh=mesh, in_specs=in_specs, out_specs=out_specs, check_vma=False
    )
```

profile of v0, /device:TPU:0, one launch (start us, length us, event | category | flops | bytes accessed | tf_op | source)
XLA Modules:
  0.0 1570.2 jit_solution(12066318902520710196)
XLA Ops:
  10.1 7.9 multiply_convert_fusion.2
  18.0 4.8 multiply_convert_fusion.6
  22.9 8.2 fusion.157
  31.2 29.5 %copy.77 = bf16[2,368,49,128]{3,0,2,1:T(2,128)(2,1)} copy(bf16[2,368,49,128]{3,1,2,0:T(8,128)(2,1)S(1)} %fusion.157) | data formatting | bytes 18464768 | tf_op jit(solution)/shard_map/convert_element_type | solution.py:184
  60.6 7.3 all-to-all-start
  69.5 94.2 %while.30 = (s32[]{:T(128)}, f32[46,392]{1,0:T(8,128)S(1)}, f32[46,392]{1,0:T(8,128)S(1)}, f32[46,392]{1,0:T(8,128)S(1)}, bf16[23,16,46,392]{3,2,1,0:T(8,128)(2,...) while((s32[]{:T(128)}, f32[46,392]{1,0:T(8,128)S(1)}, ...), condition=%wide.region_6.7_spmd.clone, body=%wide.region_5.6_spmd.clone.sunk | while | flops 5212001 | bytes 9275903 | solution.py:102
  72.6 1.5 fusion.279
  76.7 1.5 fusion.279
  80.8 1.5 fusion.279
  88.9 1.5 fusion.279
  93.0 1.5 fusion.279
  101.1 1.5 fusion.279
  109.3 1.5 fusion.279
  113.3 1.5 fusion.279
  117.4 1.5 fusion.279
  121.5 1.5 fusion.279
  129.6 1.6 fusion.279
  133.8 1.5 fusion.279
  137.8 1.5 fusion.279
  150.0 1.5 fusion.279
  158.1 1.5 fusion.279
  162.2 1.5 fusion.279
  163.7 23.4 %copy.103 = bf16[368,46,392,1]{0,2,3,1:T(8,128)(2,1)} copy(bf16[368,46,392,1]{2,1,0,3:T(8,128)(2,1)} %bitcast.422) | data formatting | bytes 26543104 | tf_op jit(solution)/shard_map/reshape | solution.py:103
  187.0 23.4 %copy.104 = bf16[368,46,392,1]{0,2,3,1:T(8,128)(2,1)} copy(bf16[368,46,392,1]{2,1,0,3:T(8,128)(2,1)} %bitcast.423) | data formatting | bytes 26543104 | tf_op jit(solution)/shard_map/reshape | solution.py:104
  210.4 58.7 %all-to-all-done = bf16[2,368,49,128]{3,0,2,1:T(2,128)(2,1)} async-done(((bf16[2,368,49,128]{3,0,2,1:T(2,128)(2,1)}), bf16[2,368,49,128]{3,0,2,1:T(2,128)(2,1)}, u32[]{:S(2)}, u32[]{:S(2)}) %all-to-all-start) | async-done | bytes 9232416 | tf_op jit(solution)/shard_map/all_to_all | solution.py:147
  269.1 8.7 copy.115
  277.8 16.5 %multiply_convert_fusion.4 = bf16[2,368,46,128]{3,1,0,2:T(8,128)(2,1)} fusion(f32[368,128]{1,0:T(8,128)S(1)} %copy-done.17, bf16[368,46,392,1]{0,2,3,1:T(8,128)(2,1)} %copy.103, bf16[2,46,392,128]{3,1,2,0:T(8,128)(2,1)} %bitcast.442, bf16[128,128]{1,0:T(8,128)(2,1)S(1)} %copy-done), kind=kOutput, calls=%fused_computation.235 | convolution fusion | flops 4519911424 | bytes 31392256 | tf_op jit(solution)/shard_map/klmc,cd->klmd/dot_general | solution.py:193
  294.3 10.7 convert_bitcast_fusion.2
  305.1 74.2 %copy.83 = bf16[2,46,392,128]{3,0,1,2:T(2,128)(2,1)S(1)} copy(bf16[2,46,392,128]{3,2,0,1:T(8,128)(2,1)S(1)} %convert_bitcast_fusion.2) | data formatting | bytes 18464768 | tf_op jit(solution)/shard_map/convert_element_type | solution.py:200
  379.2 205.7 %all_to_all.72 = bf16[2,46,392,128]{3,0,1,2:T(2,128)(2,1)} all-to-all(bf16[2,46,392,128]{3,0,1,2:T(2,128)(2,1)S(1)} %copy.83), channel_id=1, replica_groups=mesh['member'=4,'space'=8] {'space'}, dimensions={2} | all-to-all | bytes 18464768 | tf_op jit(solution)/shard_map/all_to_all | solution.py:151
  584.9 8.6 copy.84
  593.5 10.3 copy.116
  603.8 14.2 reshape.1321
  618.0 14.3 fusion.176
  632.2 46.6 %multiply_reduce_fusion.1 = (f32[49,720]{1,0:T(8,128)S(1)}, bf16[73,49,720]{2,0,1:T(8,128)(2,1)S(1)}) fusion(bf16[73,49,720]{2,0,1:T(8,128)(2,1)} %param.12, f32[49]{0:T(128)S(1)} %get-tuple-element.235, bf16[128,73]{0,1:T(8,128)(2,1)S(1)} %copy-done.12, f32[720,49,128,1]{2,0,3,1:T(8,128)} %fusion.176, bf16[49,720,128]{2,1,0:T(8,128)(2,1)S(1)} %bitcast.444, ...), kind=kOutput, calls=%fused_computation.248 | convolution fusion | flops 989533312 | bytes 42707684 | tf_op jit(solution)/shard_map/rlc,cf->frl/dot_general | solution.py:212
  678.8 2.6 copy-done.1
  681.4 4.7 copy.87
  686.1 11.5 convert_bitcast_fusion
  697.7 17.8 %copy.90 = f32[1,73,49,720]{3,2,1,0:T(8,128)} copy(f32[1,73,49,720]{3,1,2,0:T(8,128)} %convert_bitcast_fusion) | data formatting | bytes 20603520
  715.6 123.7 %all-gather.3.cloned.1.call-done = bf16[292,49,720]{2,1,0:T(8,128)(2,1)} async-done(((bf16[73,49,720]{2,1,0:T(8,128)(2,1)}), bf16[292,49,720]{2,1,0:T(8,128)(2,1)}) %all-gather.3.cloned.1.call-update) | async-done | bytes 20603536 | tf_op jit(solution)/shard_map/all_gather | solution.py:218
  839.2 94.0 %while.31 = (s32[]{:T(128)}, f32[1,73,49,720]{3,2,1,0:T(8,128)}, bf16[4,73,49,720]{3,2,1,0:T(8,128)(2,1)}, f32[1,73,49,720]{3,2,1,0:T(8,128)}, s32[]{:T(128)}, /*index=5*/s32[]{:T(128)}) while((s32[]{:T(128)}, f32[1,73,49,720]{3,2,1,0:T(8,128)}, bf16[4,73,49,720]{3,2,1,0:T(8,128)(2,1)}, f32[1,73,49,720]{3,2,1,0:T(8,128)}, ...), condition=%wide.region_10.11_spmd.clone, body=%wide.region_8.10_spmd.clone.sunk | while | flops 23178964 | bytes 52073364 | solution.py:139
  839.6 8.1 multiply_reduce_fusion.3
  847.8 12.6 select_add_fusion.2
  860.4 8.1 multiply_reduce_fusion.3
  868.6 16.1 %select_add_fusion.2 = f32[1,73,49,720]{3,2,1,0:T(8,128)} fusion(f32[1,73,49,720]{3,2,1,0:T(8,128)} %get-tuple-element.725, f32[1,73,49,720]{3,2,1,0:T(8,128)} %get-tuple-element.733, f32[49,720]{1,0:T(8,128)S(1)} %add_sqrt_fusion.3, pred[]{:T(512)S(6)} %compare.8, bf16[4,73,49,720]{3,2,1,0:T(8,128)(2,1)} %get-tuple-element.732, s32[]{:T(128)} %get-tuple-element.724), kind=kLoop, calls=%fused_computation.190.clone.1 | loop fusion | flops 12877200 | bytes 36197284 | tf_op jit(solution)/shard_map/while/body/eval_jaxpr/add | solution.py:137
  884.7 8.1 multiply_reduce_fusion.3
  892.9 16.1 %select_add_fusion.2 = f32[1,73,49,720]{3,2,1,0:T(8,128)} fusion(f32[1,73,49,720]{3,2,1,0:T(8,128)} %get-tuple-element.725, f32[1,73,49,720]{3,2,1,0:T(8,128)} %get-tuple-element.733, f32[49,720]{1,0:T(8,128)S(1)} %add_sqrt_fusion.3, pred[]{:T(512)S(6)} %compare.8, bf16[4,73,49,720]{3,2,1,0:T(8,128)(2,1)} %get-tuple-element.732, s32[]{:T(128)} %get-tuple-element.724), kind=kLoop, calls=%fused_computation.190.clone.1 | loop fusion | flops 12877200 | bytes 36197284 | tf_op jit(solution)/shard_map/while/body/eval_jaxpr/add | solution.py:137
  909.0 8.1 multiply_reduce_fusion.3
  917.1 16.1 %select_add_fusion.2 = f32[1,73,49,720]{3,2,1,0:T(8,128)} fusion(f32[1,73,49,720]{3,2,1,0:T(8,128)} %get-tuple-element.725, f32[1,73,49,720]{3,2,1,0:T(8,128)} %get-tuple-element.733, f32[49,720]{1,0:T(8,128)S(1)} %add_sqrt_fusion.3, pred[]{:T(512)S(6)} %compare.8, bf16[4,73,49,720]{3,2,1,0:T(8,128)(2,1)} %get-tuple-element.732, s32[]{:T(128)} %get-tuple-element.724), kind=kLoop, calls=%fused_computation.190.clone.1 | loop fusion | flops 12877200 | bytes 36197284 | tf_op jit(solution)/shard_map/while/body/eval_jaxpr/add | solution.py:137
  933.3 11.6 fusion.118
  944.8 2.6 copy-done.2
  947.4 8.9 fusion.150
  956.3 16.1 %fusion.160 = bf16[2,368,49,128]{3,1,2,0:T(8,128)(2,1)S(1)} fusion(f32[49,720,128]{2,1,0:T(8,128)} %fusion.150, f32[720,49,128,1]{2,0,3,1:T(8,128)} %fusion.176, bf16[1,368,720]{1,2,0:T(8,128)(2,1)S(1)} %copy-done.11, bf16[1,368,720]{1,2,0:T(8,128)(2,1)S(1)} %copy-done.9), kind=kOutput, calls=%fused_computation.274 | convolution fusion | flops 6699210752 | bytes 46418944 | tf_op jit(solution)/shard_map/rlc,kml->kmrc/dot_general | solution.py:225
  972.5 14.7 copy.92
  987.2 207.8 %all_to_all.73 = bf16[2,368,49,128]{3,0,2,1:T(2,128)(2,1)} all-to-all(bf16[2,368,49,128]{3,0,2,1:T(2,128)(2,1)S(1)} %copy.92), channel_id=1, replica_groups=mesh['member'=4,'space'=8] {'space'}, dimensions={1} | all-to-all | bytes 18464768 | tf_op jit(solution)/shard_map/all_to_all | solution.py:147
  1195.0 8.8 copy.123
  1203.7 16.7 %fusion.136 = bf16[2,368,46,128]{3,1,0,2:T(8,128)(2,1)} fusion(f32[368,128]{1,0:T(8,128)S(1)} %copy-done.18, bf16[368,46,392,1]{0,2,3,1:T(8,128)(2,1)} %copy.104, bf16[2,46,392,128]{3,1,2,0:T(8,128)(2,1)} %bitcast.441, bf16[128,128]{1,0:T(8,128)(2,1)S(1)} %copy-done), kind=kOutput, calls=%fused_computation.263 | convolution fusion | flops 4515577856 | bytes 31392256 | tf_op jit(solution)/shard_map/klmd,cd->klmc/dot_general | solution.py:236
  1220.5 10.8 convert_bitcast_fusion.1
  1231.2 74.2 %copy.98 = bf16[2,46,392,128]{3,0,1,2:T(2,128)(2,1)S(1)} copy(bf16[2,46,392,128]{3,2,0,1:T(8,128)(2,1)S(1)} %convert_bitcast_fusion.1) | data formatting | bytes 18464768 | tf_op jit(solution)/shard_map/convert_element_type | solution.py:241
  1305.4 205.5 %all_to_all.74 = bf16[2,46,392,128]{3,0,1,2:T(2,128)(2,1)} all-to-all(bf16[2,46,392,128]{3,0,1,2:T(2,128)(2,1)S(1)} %copy.98), channel_id=1, replica_groups=mesh['member'=4,'space'=8] {'space'}, dimensions={2} | all-to-all | bytes 18464768 | tf_op jit(solution)/shard_map/all_to_all | solution.py:151
  1510.9 8.6 copy.99
  1519.6 10.3 copy.124
  1529.9 14.3 reshape.1322
  1544.2 18.9 %fusion.149 = bf16[1,73,49,720]{3,1,2,0:T(8,128)(2,1)} fusion(bf16[1,73,49,720]{3,1,2,0:T(8,128)(2,1)} %copy-done.2, f32[49]{0:T(128)S(1)} %copy-done.15, f32[49,720,128]{2,1,0:T(8,128)} %fusion.150, bf16[2,368,49,128]{3,1,0,2:T(8,128)(2,1)} %reshape.1322, f32[1,368,720]{1,2,0:T(8,128)S(1)} %copy-done.5, f32[1,368,720]{1,2,0:T(8,128)S(1)} %copy-done.7, ...), kind=kOutput, calls=%fused_computation.269 | convolution fusion | flops 7332067840 | bytes 39736068 | tf_op jit(solution)/shard_map/rlc,fc->frl/dot_general | solution.py:250
  (575 shorter events, 70.7 us)
Async XLA Ops:
  7.2 270.6 %copy-start = (bf16[128,128]{1,0:T(8,128)(2,1)S(1)}, bf16[128,128]{1,0:T(8,128)(2,1)}, u32[]{:S(2)}) copy-start(bf16[128,128]{1,0:T(8,128)(2,1)} %param.15) | copy-start | bytes 98308
  10.1 622.1 %copy-start.14 = (f32[49]{0:T(128)}, f32[49]{0:T(128)S(1)}, u32[]{:S(2)}) copy-start(f32[49]{0:T(128)S(1)} %get-tuple-element.235) | copy-start | bytes 592
  18.0 13.1 copy-start.3
  22.8 8.3 copy-start.4
  22.8 8.3 copy-start.6
  22.9 595.1 %copy-start.8 = (bf16[1,368,720]{1,2,0:T(8,128)(2,1)}, bf16[1,368,720]{1,2,0:T(8,128)(2,1)S(1)}, u32[]{:S(2)}) copy-start(bf16[1,368,720]{1,2,0:T(8,128)(2,1)S(1)} %get-tuple-element.327) | copy-start | bytes 1589764
  22.9 595.1 %copy-start.10 = (bf16[1,368,720]{1,2,0:T(8,128)(2,1)}, bf16[1,368,720]{1,2,0:T(8,128)(2,1)S(1)}, u32[]{:S(2)}) copy-start(bf16[1,368,720]{1,2,0:T(8,128)(2,1)S(1)} %get-tuple-element.328) | copy-start | bytes 1589764
  60.6 208.5 %all-to-all-start = ((bf16[2,368,49,128]{3,0,2,1:T(2,128)(2,1)}), bf16[2,368,49,128]{3,0,2,1:T(2,128)(2,1)}, u32[]{:S(2)}, u32[]{:S(2)}) async-start(bf16[2,368,49,128]{3,0,2,1:T(2,128)(2,1)} %copy.77), calls=%async_computation | async-start | bytes 18464768 | tf_op jit(solution)/shard_map/all_to_all | solution.py:147
  67.9 771.4 %all-gather.3.cloned.1.call-start = ((), (), s32[]{:S(2)}) async-start(), calls=%async_computation.4 | async-start | bytes 31395840 | tf_op jit(solution)/shard_map/all_gather | solution.py:218
  210.4 67.4 %copy-start.17 = (f32[368,128]{1,0:T(8,128)S(1)}, f32[368,128]{1,0:T(8,128)}, u32[]{:S(2)}) copy-start(f32[368,128]{1,0:T(8,128)} %param.16) | copy-start | bytes 565252
  603.7 28.5 %slice-start = ((s8[9031680]{0:T(1024)(128)(4,1)}), s8[643072]{0:T(1024)(128)(4,1)S(1)}, s32[]{:S(2)}) async-start(s8[9031680]{0:T(1024)(128)(4,1)} %bitcast.443), calls=%async_computation.5 | async-start | bytes 1286144
  617.9 14.3 slice-start.1
  617.9 14.3 slice-start.2
  617.9 14.3 copy-start.12
  678.8 2.6 copy-start.1
  839.2 94.0 %copy-start.16 = (f32[49]{0:T(128)S(1)}, f32[49]{0:T(128)}, u32[]{:S(2)}) copy-start(f32[49]{0:T(128)} %get-tuple-element.234) | copy-start | bytes 592
  944.8 2.6 copy-start.2
  947.4 8.9 copy-start.9
  947.4 8.9 copy-start.11
  1195.0 8.8 copy-start.18
  1529.9 14.3 copy-start.5
  1529.9 14.3 copy-start.7
  1529.9 14.3 copy-start.13
  1529.9 14.3 copy-start.15
Sparse Core Ops, SparseCore 0:
  686.3 152.9 all-gather.2
where the time goes:
time: 1580 us; the launch traced here: 1570 us
  blocking collectives  619 us (39%)
  local copies, waits for them, and re-layouts  355 us (22%)
  other arithmetic  211 us (13%)
  waiting for transfers between devices  182 us (12%)
  matrix products  176 us (11%)
    all_to_all x2, blocking collectives, to_bands(): lax.all_to_all(block, 'space', split_axis=2, concat_axis=1, tiled=True)  411 us
    all_to_all x1, blocking collectives, to_orders(): lax.all_to_all(block, 'space', split_axis=1, concat_axis=2, tiled=True)  208 us
    all_gather x1, waiting for transfers between devices, on_device(): everyone = lax.all_gather(prediction, 'member', axis=0, tiled=True)  124 us
    convert_element_type x1, local copies, waits for them, and re-layouts, on_device(): longitude_gradient = jnp.einsum('sbzv,bze->szev', harmonic_gradient, lege...  74.2 us
    convert_element_type x1, local copies, waits for them, and re-layouts, on_device(): rebuilt_field = jnp.einsum('pjcx,jco->pcox', masked_spectrum, legendre_in...  74.2 us
    all_to_all x6, local copies, waits for them, and re-layouts, to_bands(): lax.all_to_all(block, 'space', split_axis=2, concat_axis=1, tiled=True)  66.3 us
    add x4, other arithmetic, accumulate(): return (running + member_gap / member_dist, None)  60.9 us
    all_to_all x1, waiting for transfers between devices, to_orders(): lax.all_to_all(block, 'space', split_axis=1, concat_axis=2, tiled=True)  58.7 us
  transfers between devices with their start and end apart: 2, of which 2 were waited for; matrix products, arithmetic and copies ran while one was open for 11% of the time, Pallas kernels for 0%

commit v1 on v0

v1 whole, which is shorter than its diff:
```python
import functools
import math

import jax
import jax.numpy as jnp
import ml_dtypes
import numpy as np
from jax import lax
from jax.experimental import pallas as pl
from jax.experimental.pallas import tpu as pltpu
from jax.sharding import PartitionSpec as P

NLAT = 361
LMAX = 360
EPSILON = 1e-05
GROUP = 192
SPLIT = 64
REST = 16
LANES = 128
VMEM = 60 * 1024 * 1024
BF = jnp.bfloat16
F32 = jnp.float32


def ceil_to(value, step):
    return -(-value // step) * step


class Plan:
    def __init__(self, space, band, fields, lon, channels, degrees):
        self.n, self.rows, self.fields, self.lon = space, band, fields, lon
        self.channels, self.degrees = channels, degrees
        self.all_rows = space * band
        self.fpad = SPLIT + REST
        self.live_t = -(-GROUP // space)
        self.tp = ceil_to(self.live_t, 8)
        self.tb = self.tp // 8
        self.rest_groups = -(-self.tb // 4)
        self.rows1 = ceil_to(self.tp + 8 * self.rest_groups, 16)
        self.rows2 = 2 * self.tp
        self.groups = -(-(LMAX + 1) // (space * self.live_t))
        self.rb = max(k for k in range(1, 9) if band % k == 0)
        blocks = band // self.rb
        parts = min(3, blocks)
        counts = [blocks // parts + (1 if p >= parts - blocks % parts else 0) for p in range(parts)]
        self.chunks = []
        start = 0
        for count in counts:
            self.chunks.append((start * self.rb, count * self.rb))
            start += count

    def orders(self, group):
        device = np.arange(self.n)[:, None]
        position = np.arange(self.tp)[None, :]
        order = group * self.n * self.live_t + device * self.live_t + position
        return np.where((position < self.live_t) & (order <= LMAX), order, 1 << 14)


def dft_rows(plan, group, inverse):
    order = plan.orders(group)
    live = (order <= LMAX)[..., None]
    turn = (np.where(order <= LMAX, order, 0)[..., None] * np.arange(plan.lon)) % plan.lon
    angle = turn * (2.0 * math.pi / plan.lon)
    if inverse:
        scale = np.where((order == 0) | (2 * order == plan.lon), 1.0, 2.0)[..., None]
    else:
        scale = 1.0 / plan.lon
    rows = np.stack([np.cos(angle) * scale, -np.sin(angle) * scale]) * live
    return rows.astype(ml_dtypes.bfloat16)


def params(**more):
    return pltpu.CompilerParams(vmem_limit_bytes=VMEM, **more)


def whole(shape):
    return pl.BlockSpec(shape, lambda *_: (0,) * len(shape))


def table_kernel(m_ref, start_ref, cos_ref, quad_ref, live_ref, fwd_ref, inv_ref, one, two, logs, stage):
    block = pl.program_id(1)
    lanes = fwd_ref.shape[2]
    order = m_ref[...]

    @pl.when(block == 0)
    def _():
        one[...] = jnp.zeros_like(one)
        two[...] = jnp.zeros_like(two)
        logs[...] = start_ref[...]

    ups, backs, pasts, onsets, keeps = [], [], [], [], []
    for p in range(16):
        degree = block * 16 + p
        deg = degree.astype(F32)
        ups.append(
            jnp.sqrt((4.0 * deg * deg - 1.0) / jnp.maximum(deg * deg - order * order, 1.0))
        )
        less = (deg - 1.0) * (deg - 1.0)
        backs.append(
            jnp.sqrt(
                jnp.maximum(less - order * order, 0.0) / jnp.maximum(4.0 * less - 1.0, 1.0)
            )
        )
        pasts.append(order < deg)
        onsets.append(jnp.where(order == deg, 1.0, 0.0))
        keeps.append((order <= deg) & (degree <= LMAX))
    for c in range(one.shape[1] // LANES):
        at = slice(c * LANES, (c + 1) * LANES)
        first, second, log_scale = one[:, at], two[:, at], logs[:, at]
        cosine = cos_ref[:, at]
        scale = jnp.exp(log_scale)
        for p in range(16):
            current = jnp.where(
                pasts[p], ups[p] * (cosine * first - backs[p] * second), onsets[p]
            )
            stage[c, pl.ds(p, 8, stride=16), :] = jnp.where(keeps[p], current * scale, 0.0)
            second = first
            first = current
        size = jnp.maximum(jnp.abs(first), jnp.abs(second))
        factor = jnp.where(size > 1.0, size, 1.0)
        one[:, at] = first / factor
        two[:, at] = second / factor
        logs[:, at] = log_scale + jnp.log(factor)
        width = min(LANES, lanes - c * LANES)
        out = slice(c * LANES, c * LANES + width)
        for i in range(8):
            values = stage[c, i * 16 : (i + 1) * 16, :]
            fwd_ref[i, :, out] = (values * quad_ref[:, at]).astype(BF)[:, :width]
            inv_ref[i, :, out] = (values * live_ref[:, at]).astype(BF)[:, :width]


def legendre_tables(plan, orders, log_start, cosines, quad, live):
    rows = cosines.shape[0]
    wide = ceil_to(rows, LANES)
    tp = orders.shape[0]

    def spread(row):
        return jnp.pad(row, (0, wide - rows))[None]

    order_f = jnp.broadcast_to(orders.astype(F32)[:, None], (tp, LANES))
    shape = jax.ShapeDtypeStruct((tp, plan.degrees, rows), BF)
    row_spec = pl.BlockSpec((1, wide), lambda i, j: (0, 0))
    out_spec = pl.BlockSpec((8, 16, rows), lambda i, j: (i, j, 0))
    return pl.pallas_call(
        table_kernel,
        grid=(tp // 8, plan.degrees // 16),
        in_specs=[
            pl.BlockSpec((8, LANES), lambda i, j: (i, 0)),
            pl.BlockSpec((8, wide), lambda i, j: (i, 0)),
            row_spec,
            row_spec,
            row_spec,
        ],
        out_specs=[out_spec, out_spec],
        out_shape=[shape, shape],
        scratch_shapes=[
            pltpu.VMEM((8, wide), F32),
            pltpu.VMEM((8, wide), F32),
            pltpu.VMEM((8, wide), F32),
            pltpu.VMEM((wide // LANES, 128, LANES), F32),
        ],
        compiler_params=params(),
        name="legendre_tables",
    )(order_f, jnp.pad(log_start, ((0, 0), (0, wide - rows))), spread(cosines), spread(quad), spread(live))


def analyse_kernel(plan, x_ref, dft_ref, *outs):
    lane = lax.broadcasted_iota(jnp.int32, (1, LANES), 1)
    part = lane // REST
    n, tp = plan.n, plan.tp
    for r in range(plan.rb):
        x = x_ref[r]
        head, tail = x[:SPLIT], x[SPLIT:]
        right = jnp.concatenate([head, head] + [tail] * (LANES // REST), axis=0)
        for g, out in enumerate(outs):
            cosine, sine = [
                lax.dot_general(
                    dft_ref[g, k], right, (((1,), (1,)), ((), ())), preferred_element_type=F32
                )
                for k in range(2)
            ]
            main = jnp.where(lane < SPLIT, cosine[:, :LANES], sine[:, :LANES])
            for o in range(n):
                pieces = [main[o * tp : (o + 1) * tp]]
                for group in range(plan.rest_groups):
                    rest = jnp.zeros((8, LANES), F32)
                    for i in range(min(4, plan.tb - group * 4)):
                        first = o * tp + (group * 4 + i) * 8
                        rest = jnp.where(part == 2 * i, cosine[first : first + 8, LANES:], rest)
                        rest = jnp.where(part == 2 * i + 1, sine[first : first + 8, LANES:], rest)
                    pieces.append(rest)
                spare = plan.rows1 - tp - 8 * plan.rest_groups
                if spare:
                    pieces.append(jnp.zeros((spare, LANES), F32))
                out[o, r] = jnp.concatenate(pieces, axis=0).astype(BF)


def analyse(plan, x, dft):
    shape = (plan.n, plan.rows, plan.rows1, LANES)
    out_spec = pl.BlockSpec((plan.n, plan.rb, plan.rows1, LANES), lambda i: (0, i, 0, 0))
    return pl.pallas_call(
        functools.partial(analyse_kernel, plan),
        grid=(plan.rows // plan.rb,),
        in_specs=[
            pl.BlockSpec((plan.rb, plan.fpad, plan.lon), lambda i: (i, 0, 0)),
            whole(dft.shape),
        ],
        out_specs=[out_spec] * plan.groups,
        out_shape=[jax.ShapeDtypeStruct(shape, BF)] * plan.groups,
        compiler_params=params(),
        name="analyse",
    )(x, dft)


def unpack(plan, refs, store, height):
    start = 0
    for ref in refs:
        count = ref.shape[1]
        for o in range(plan.n):
            base = o * plan.rows + start

            def step(r, unused, o=o, base=base, ref=ref):
                at = pl.multiple_of((base + r) * height, 8)
                store[pl.ds(at, height), :] = ref[o, r].astype(F32)
                return unused

            lax.fori_loop(0, count, step, 0)
        start += count


def repack(plan, refs, store, height):
    start = 0
    for ref in refs:
        count = ref.shape[1]
        for o in range(plan.n):
            base = o * plan.rows + start

            def step(r, unused, o=o, base=base, ref=ref):
                at = pl.multiple_of((base + r) * height, 8)
                ref[o, r] = store[pl.ds(at, height), :].astype(BF)
                return unused

            lax.fori_loop(0, count, step, 0)
        start += count


def rest_row(plan, t):
    block = t // 8
    return plan.tp + 8 * (block // 4) + t % 8


def spectrum_forward_kernel(plan, recv, fwd, inv, mix, gain, *refs):
    outs, zin, yout = refs[:-2], refs[-2], refs[-1]
    t = pl.program_id(0)

    @pl.when(t == 0)
    def _():
        unpack(plan, [recv], zin, plan.rows1)
        if plan.live_t < plan.tp:
            yout[...] = jnp.zeros_like(yout)

    z = jnp.concatenate(
        [
            zin[pl.ds(t, plan.all_rows, stride=plan.rows1), :],
            zin[pl.ds(rest_row(plan, t), plan.all_rows, stride=plan.rows1), :],
        ],
        axis=1,
    ).astype(BF)
    coeffs = jnp.dot(fwd[0], z, preferred_element_type=F32).astype(BF)
    filtered = (jnp.dot(coeffs, mix[0], preferred_element_type=F32) * gain[...]).astype(BF)
    y = lax.dot_general(
        inv[0], filtered, (((0,), (0,)), ((), ())), preferred_element_type=F32
    )
    for k in range(2):
        yout[pl.ds(k * plan.tp + t, plan.all_rows, stride=plan.rows2), :] = y[
            :, k * LANES : (k + 1) * LANES
        ]

    @pl.when(t == plan.live_t - 1)
    def _():
        repack(plan, outs, yout, plan.rows2)


def spectrum_backward_kernel(plan, count, *refs):
    recvs = refs[:count]
    fwd, inv, mix, gain = refs[count : count + 4]
    out, zin, yout = refs[count + 4 :]
    t = pl.program_id(0)

    @pl.when(t == 0)
    def _():
        unpack(plan, recvs, zin, plan.rows2)
        yout[...] = jnp.zeros_like(yout)

    z = jnp.concatenate(
        [
            zin[pl.ds(k * plan.tp + t, plan.all_rows, stride=plan.rows2), :]
            for k in range(2)
        ],
        axis=1,
    ).astype(BF)
    grad = (jnp.dot(inv[0], z, preferred_element_type=F32) * gain[...]).astype(BF)
    back = jnp.dot(grad, mix[0], preferred_element_type=F32).astype(BF)
    y = lax.dot_general(fwd[0], back, (((0,), (0,)), ((), ())), preferred_element_type=F32)
    yout[pl.ds(t, plan.all_rows, stride=plan.rows1), :] = y[:, :LANES]
    where = pl.ds(rest_row(plan, t), plan.all_rows, stride=plan.rows1)
    yout[where, :] = yout[where, :] + y[:, LANES:]

    @pl.when(t == plan.live_t - 1)
    def _():
        repack(plan, [out], yout, plan.rows1)


def spectrum_specs(plan, mix, gain):
    table = pl.BlockSpec((1, plan.degrees, plan.all_rows), lambda t: (t, 0, 0))
    return [table, table, pl.BlockSpec((1,) + mix.shape[1:], lambda t: (t // 8, 0, 0)), whole(gain.shape)]


def spectrum_forward(plan, recv, fwd, inv, mix, gain):
    shapes = [(plan.n, count, plan.rows2, LANES) for _, count in plan.chunks]
    return pl.pallas_call(
        functools.partial(spectrum_forward_kernel, plan),
        grid=(plan.live_t,),
        in_specs=[whole(recv.shape)] + spectrum_specs(plan, mix, gain),
        out_specs=[whole(s) for s in shapes],
        out_shape=[jax.ShapeDtypeStruct(s, BF) for s in shapes],
        scratch_shapes=[
            pltpu.VMEM((plan.all_rows * plan.rows1, LANES), F32),
            pltpu.VMEM((plan.all_rows * plan.rows2, LANES), F32),
        ],
        compiler_params=params(),
        name="spectrum_forward",
    )(recv, fwd, inv, mix, gain)


def spectrum_backward(plan, recvs, fwd, inv, mix, gain):
    shape = (plan.n, plan.rows, plan.rows1, LANES)
    return pl.pallas_call(
        functools.partial(spectrum_backward_kernel, plan, len(recvs)),
        grid=(plan.live_t,),
        in_specs=[whole(r.shape) for r in recvs] + spectrum_specs(plan, mix, gain),
        out_specs=whole(shape),
        out_shape=jax.ShapeDtypeStruct(shape, BF),
        scratch_shapes=[
            pltpu.VMEM((plan.all_rows * plan.rows2, LANES), F32),
            pltpu.VMEM((plan.all_rows * plan.rows1, LANES), F32),
        ],
        compiler_params=params(),
        name="spectrum_backward",
    )(*recvs, fwd, inv, mix, gain)


def predict_kernel(plan, first, live_ref, x_ref, idft_ref, enc_ref, dec_ref, *refs):
    recvs = refs[: plan.groups]
    pred_ref, slope_ref, left, field = refs[plan.groups :]
    c = plan.channels
    for r in range(plan.rb):
        for g, recv in enumerate(recvs):
            piece = recv[:, r].reshape(plan.n * plan.rows2, LANES)
            wide = plan.n * plan.rows2
            left[r * c : (r + 1) * c, g * wide : (g + 1) * wide] = piece.T
    field[...] = jnp.dot(left[...], idft_ref[...], preferred_element_type=F32)
    base = first + pl.program_id(0) * plan.rb

    def step(r, unused):
        live = live_ref[base + r]
        x = x_ref[r]
        u = field[pl.ds(pl.multiple_of(r * c, 8), c), :]
        hidden = (jnp.dot(enc_ref[...], x, preferred_element_type=F32) * live).astype(BF)
        phi = 0.5 + 0.5 * lax.erf(u * (1.0 / math.sqrt(2.0)))
        slope = phi + u * jnp.exp(-0.5 * u * u) * (1.0 / math.sqrt(2.0 * math.pi))
        slope_ref[r] = slope.astype(BF)
        block = ((u * phi + hidden.astype(F32)) * live).astype(BF)
        decoded = jnp.dot(dec_ref[...], block, preferred_element_type=F32)
        pred_ref[r] = ((x.astype(F32) + decoded) * live).astype(BF)
        return unused

    lax.fori_loop(0, plan.rb, step, 0)


def predict(plan, chunk, live, x, idft, enc_t, dec_t, recvs):
    first, count = chunk
    skip = first // plan.rb
    shape = (count, plan.fpad, plan.lon)
    slope_shape = (count, plan.channels, plan.lon)
    recv_spec = pl.BlockSpec((plan.n, plan.rb, plan.rows2, LANES), lambda i: (0, i, 0, 0))
    return pl.pallas_call(
        functools.partial(predict_kernel, plan, first),
        grid=(count // plan.rb,),
        in_specs=[
            pl.BlockSpec(memory_space=pltpu.SMEM),
            pl.BlockSpec((plan.rb,) + shape[1:], lambda i: (i + skip, 0, 0)),
            whole(idft.shape),
            whole(enc_t.shape),
            whole(dec_t.shape),
        ]
        + [recv_spec] * plan.groups,
        out_specs=[
            pl.BlockSpec((plan.rb,) + shape[1:], lambda i: (i, 0, 0)),
            pl.BlockSpec((plan.rb,) + slope_shape[1:], lambda i: (i, 0, 0)),
        ],
        out_shape=[jax.ShapeDtypeStruct(shape, BF), jax.ShapeDtypeStruct(slope_shape, BF)],
        scratch_shapes=[
            pltpu.VMEM((plan.rb * plan.channels, idft.shape[0]), BF),
            pltpu.VMEM((plan.rb * plan.channels, plan.lon), F32),
        ],
        compiler_params=params(),
        name="predict",
    )(live, x, idft, enc_t, dec_t, *recvs)


def score_kernel(plan, first, members, area_ref, own_ref, all_ref, obs_ref, slope_ref, idft_ref, dec_ref, *refs):
    grad_ref, outs, right = refs[0], refs[1 : 1 + plan.groups], refs[1 + plan.groups]
    c = plan.channels
    base = first + pl.program_id(0) * plan.rb

    def step(r, unused):
        area = area_ref[base + r]
        own = own_ref[r].astype(F32)
        gap = own - obs_ref[r].astype(F32)
        total = gap * lax.rsqrt(jnp.sum(gap * gap, axis=0, keepdims=True) + EPSILON)
        for e in range(members):
            gap = own - all_ref[e, r].astype(F32)
            near = lax.rsqrt(jnp.sum(gap * gap, axis=0, keepdims=True) + EPSILON)
            total = total - gap * (near * (1.0 / members))
        grad = (total * area).astype(BF)
        grad_ref[r] = grad
        block = jnp.dot(dec_ref[...], grad, preferred_element_type=F32)
        right[pl.ds(pl.multiple_of(r * c, 16), c), :] = (
            block * slope_ref[r].astype(F32)
        ).astype(BF)
        return unused

    lax.fori_loop(0, plan.rb, step, 0)
    wide = plan.n * plan.rows2
    for g, out in enumerate(outs):
        modes = lax.dot_general(
            idft_ref[g * wide : (g + 1) * wide, :],
            right[...],
            (((1,), (1,)), ((), ())),
            preferred_element_type=F32,
        ).astype(BF)
        for r in range(plan.rb):
            for o in range(plan.n):
                out[o, r] = modes[o * plan.rows2 : (o + 1) * plan.rows2, r * c : (r + 1) * c]


def score(plan, chunk, area, own, everyone, observed, slope, idft, dec):
    first, count = chunk
    skip = first // plan.rb
    members = everyone.shape[0]
    cell = (plan.rb, plan.fpad, plan.lon)
    out_shape = (plan.n, count, plan.rows2, LANES)
    here = pl.BlockSpec(cell, lambda i: (i, 0, 0))
    return pl.pallas_call(
        functools.partial(score_kernel, plan, first, members),
        grid=(count // plan.rb,),
        in_specs=[
            pl.BlockSpec(memory_space=pltpu.SMEM),
            here,
            pl.BlockSpec((members,) + cell, lambda i: (0, i, 0, 0)),
            pl.BlockSpec(cell, lambda i: (i + skip, 0, 0)),
            pl.BlockSpec((plan.rb, plan.channels, plan.lon), lambda i: (i, 0, 0)),
            whole(idft.shape),
            whole(dec.shape),
        ],
        out_specs=[here]
        + [pl.BlockSpec((plan.n, plan.rb, plan.rows2, LANES), lambda i: (0, i, 0, 0))] * plan.groups,
        out_shape=[jax.ShapeDtypeStruct((count,) + cell[1:], BF)]
        + [jax.ShapeDtypeStruct(out_shape, BF)] * plan.groups,
        scratch_shapes=[pltpu.VMEM((plan.rb * plan.channels, plan.lon), BF)],
        compiler_params=params(),
        name="score",
    )(area, own, everyone, observed, slope, idft, dec)


def finish_kernel(plan, live_ref, grad_ref, main_ref, rest_ref, through_ref, *refs):
    recvs, out_ref, left, small, field, field_small = refs[: plan.groups], *refs[plan.groups :]
    n, tp, tb = plan.n, plan.tp, plan.tb
    wide = n * tp
    for r in range(plan.rb):
        for g, recv in enumerate(recvs):
            piece = recv[:, r].astype(F32)
            main = piece[:, :tp].reshape(wide, LANES).T
            for k in range(2):
                at = (g * 2 + k) * wide
                left[r * SPLIT : (r + 1) * SPLIT, at : at + wide] = main[
                    k * SPLIT : (k + 1) * SPLIT
                ].astype(BF)
            for group in range(plan.rest_groups):
                first = tp + 8 * group
                rest = piece[:, first : first + 8].reshape(n * 8, LANES).T.astype(BF)
                for i in range(min(4, tb - 4 * group)):
                    for k in range(2):
                        at = ((g * tb + group * 4 + i) * 2 + k) * n * 8
                        part = 2 * i + k
                        small[r * REST : (r + 1) * REST, at : at + n * 8] = rest[
                            part * REST : (part + 1) * REST
                        ]
    field[...] = jnp.dot(left[...], main_ref[...], preferred_element_type=F32)
    field_small[...] = jnp.dot(small[...], rest_ref[...], preferred_element_type=F32)
    base = pl.program_id(0) * plan.rb

    def step(r, unused):
        live = live_ref[base + r]
        grad = grad_ref[r]
        through = jnp.dot(through_ref[...], grad, preferred_element_type=F32)
        spectral = jnp.concatenate(
            [
                field[pl.ds(pl.multiple_of(r * SPLIT, 8), SPLIT), :],
                field_small[pl.ds(pl.multiple_of(r * REST, 8), REST), :],
            ],
            axis=0,
        )
        out_ref[r] = ((grad.astype(F32) + through + spectral) * live).astype(BF)
        return unused

    lax.fori_loop(0, plan.rb, step, 0)


def finish(plan, live, grad, main, rest, through, recvs):
    cell = (plan.rb, plan.fpad, plan.lon)
    here = pl.BlockSpec(cell, lambda i: (i, 0, 0))
    recv_spec = pl.BlockSpec((plan.n, plan.rb, plan.rows1, LANES), lambda i: (0, i, 0, 0))
    return pl.pallas_call(
        functools.partial(finish_kernel, plan),
        grid=(plan.rows // plan.rb,),
        in_specs=[
            pl.BlockSpec(memory_space=pltpu.SMEM),
            here,
            whole(main.shape),
            whole(rest.shape),
            whole(through.shape),
        ]
        + [recv_spec] * plan.groups,
        out_specs=here,
        out_shape=jax.ShapeDtypeStruct((plan.rows, plan.fpad, plan.lon), BF),
        scratch_shapes=[
            pltpu.VMEM((plan.rb * SPLIT, main.shape[0]), BF),
            pltpu.VMEM((plan.rb * REST, rest.shape[0]), BF),
            pltpu.VMEM((plan.rb * SPLIT, plan.lon), F32),
            pltpu.VMEM((plan.rb * REST, plan.lon), F32),
        ],
        compiler_params=params(),
        name="finish",
    )(live, grad, main, rest, through, *recvs)


def row_geometry(band_rows, band_len, lat_count):
    band_count = band_rows.shape[0]
    row_index = jnp.arange(band_count * band_len, dtype=jnp.int32)
    row_owner = row_index // band_len
    offset = row_index - row_owner * band_len
    starts = jnp.cumsum(band_rows) - band_rows
    owner_hot = (row_owner[:, None] == jnp.arange(band_count, dtype=jnp.int32)[None, :]).astype(
        jnp.int32
    )
    first_lat = jnp.sum(owner_hot * starts[None, :], axis=1)
    length = jnp.sum(owner_hot * band_rows[None, :], axis=1)
    live_rows = offset < length
    latitude = jnp.minimum(first_lat + offset, lat_count - 1)
    colatitude = latitude.astype(F32) * (math.pi / (lat_count - 1))
    return (live_rows.astype(F32), jnp.cos(colatitude), jnp.sin(colatitude))


def log_diagonal(order):
    index = np.arange(1, LMAX + 1, dtype=np.float64)
    sums = np.concatenate([[0.0], np.cumsum(0.5 * np.log((2 * index + 1) / (2 * index)))])
    return (0.5 * math.log(0.5) + sums[np.minimum(order, LMAX)]).astype(np.float32)


def field_weights(plan, weight):
    c = plan.channels
    head, tail = weight[:SPLIT], jnp.pad(weight[SPLIT:], ((0, plan.fpad - plan.fields), (0, 0)))
    blocks = []
    for b in range(min(plan.tb, 4)):
        out = jnp.zeros((2 * LANES, 2 * c), F32)
        for k in range(2):
            out = out.at[k * SPLIT : (k + 1) * SPLIT, k * c : (k + 1) * c].set(head)
            first = LANES + (2 * b + k) * REST
            out = out.at[first : first + REST, k * c : (k + 1) * c].set(tail)
        blocks.append(out)
    return jnp.stack([blocks[b % 4] for b in range(plan.tb)]).astype(BF)


def on_device(
    states, observed, band_rows, encoder_weight, mixing_weight, degree_gain, decoder_weight
):
    space = lax.axis_size("space")
    me = lax.axis_index("space")
    fields, band, lon = observed.shape
    channels = encoder_weight.shape[1]
    plan = Plan(space, band, fields, lon, channels, degree_gain.shape[0])
    live, cosines, sines = row_geometry(band_rows, band, NLAT)
    quad = live * sines * (math.pi / (NLAT - 1))
    log_sines = jnp.log(jnp.maximum(sines, 1e-30))
    live_own = lax.dynamic_slice_in_dim(live, me * band, band)
    area = 8.0 * lax.dynamic_slice_in_dim(sines, me * band, band) * live_own

    pad = plan.fpad - fields
    rows = jnp.pad(jnp.transpose(states[0], (1, 0, 2)), ((0, 0), (0, pad), (0, 0)))
    truth = jnp.pad(jnp.transpose(observed, (1, 0, 2)), ((0, 0), (0, pad), (0, 0)))

    enc_f = encoder_weight.astype(F32)
    exact = lax.Precision.HIGHEST
    through_mix = jnp.dot(enc_f, mixing_weight.astype(F32), precision=exact)
    mix = field_weights(plan, through_mix)
    mix_back = jnp.transpose(mix, (0, 2, 1))
    gain = jnp.concatenate([degree_gain, degree_gain], axis=1)
    enc_t = jnp.pad(encoder_weight.T, ((0, 0), (0, pad)))
    dec_t = jnp.pad(decoder_weight.T, ((0, pad), (0, 0)))
    dec = jnp.pad(decoder_weight, ((0, 0), (0, pad)))
    through = jnp.pad(
        jnp.dot(enc_f, decoder_weight.astype(F32), precision=exact), ((0, pad), (0, pad))
    ).astype(BF)

    forward = [dft_rows(plan, g, False) for g in range(plan.groups)]
    inverse = [dft_rows(plan, g, True) for g in range(plan.groups)]
    n, tp, tb = plan.n, plan.tp, plan.tb
    dft = jnp.asarray(np.stack([f.reshape(2, n * tp, lon) for f in forward]))
    idft = jnp.asarray(
        np.concatenate([f.transpose(1, 0, 2, 3).reshape(n * 2 * tp, lon) for f in inverse])
    )
    dft_main = jnp.asarray(np.concatenate([f.reshape(2 * n * tp, lon) for f in forward]))
    dft_rest = jnp.asarray(
        np.concatenate(
            [
                f.reshape(2, n, tb, 8, lon).transpose(2, 0, 1, 3, 4).reshape(tb * 2 * n * 8, lon)
                for f in forward
            ]
        )
    )

    sent = analyse(plan, rows, dft)

    def exchange(block):
        return lax.all_to_all(block, "space", split_axis=0, concat_axis=0, tiled=True)

    tables = []
    for g in range(plan.groups):
        order_table = plan.orders(g)
        orders = lax.dynamic_index_in_dim(jnp.asarray(order_table, jnp.int32), me, keepdims=False)
        diagonal = lax.dynamic_index_in_dim(
            jnp.asarray(log_diagonal(order_table)), me, keepdims=False
        )
        start = diagonal[:, None] + orders.astype(F32)[:, None] * log_sines[None, :]
        tables.append(legendre_tables(plan, orders, start, cosines, quad, live))

    synth = []
    for g in range(plan.groups):
        spectrum = spectrum_forward(plan, exchange(sent[g]), *tables[g], mix, gain)
        synth.append([exchange(part) for part in spectrum])

    predictions, grads, returned = [], [], []
    for i, chunk in enumerate(plan.chunks):
        pred, slope = predict(
            plan, chunk, live_own, rows, idft, enc_t, dec_t, [synth[g][i] for g in range(plan.groups)]
        )
        everyone = lax.all_gather(pred[None], "member", axis=0, tiled=True)
        out = score(plan, chunk, area, pred, everyone, truth, slope, idft, dec)
        predictions.append(pred)
        grads.append(out[0])
        returned.append([exchange(part) for part in out[1:]])

    last = []
    for g in range(plan.groups):
        part = spectrum_backward(
            plan, [returned[i][g] for i in range(len(plan.chunks))], *tables[g], mix_back, gain
        )
        last.append(exchange(part))
    state_grad = finish(
        plan, live_own, jnp.concatenate(grads), dft_main, dft_rest, through, last
    )

    def outward(block):
        return jnp.transpose(block[:, :fields], (1, 0, 2))[None]

    return (outward(jnp.concatenate(predictions)), outward(state_grad))


def solution(mesh):
    in_specs = (P("member", None, "space", None), P(None, "space", None), P(), P(), P(), P(), P())
    out_specs = (P("member", None, "space", None), P("member", None, "space", None))
    return jax.shard_map(
        on_device, mesh=mesh, in_specs=in_specs, out_specs=out_specs, check_vma=False
    )
```

time: 1580 us -> 1010 us (0.64)
  Pallas kernels: 0 us -> 363 us
  local copies, waits for them, and re-layouts: 355 us -> 46.1 us
  blocking collectives: 619 us -> 378 us
  other arithmetic: 211 us -> 14.5 us
  matrix products: 176 us -> 0.33 us
  starting transfers between devices: 7.29 us -> 36 us
  waiting for transfers between devices: 182 us -> 155 us
    pallas_call x0 -> x14, Pallas kernels: none -> 363 us  [the longest x2 82.6 us: spectrum_backward(): pl.pallas_call(functools.partial(spectrum_backward_kernel, plan, len(recv...]
    all_to_all x3 -> x8, blocking collectives: 619 us -> 378 us  [exchange(): lax.all_to_all(block, 'space', split_axis=0, concat_axis=0, tiled=True)]
    convert_element_type x5 -> x0, local copies, waits for them, and re-layouts: 197 us -> none  [the longest x1 74.2 us: on_device(): longitude_gradient = jnp.einsum('sbzv,bze->szev', harmonic_gradient, lege...]
    dot_general x11 -> x2, matrix products: 176 us -> 0.33 us  [the longest x1 0.2 us: on_device(): through_mix = jnp.dot(enc_f, mixing_weight.astype(F32), precision=exact)]
    all_gather x1 -> x3, waiting for transfers between devices: 124 us -> 0.04 us  [on_device(): everyone = lax.all_gather(pred[None], 'member', axis=0, tiled=True)]
    all_to_all x1 -> x8, waiting for transfers between devices: 58.7 us -> 155 us  [exchange(): lax.all_to_all(block, 'space', split_axis=0, concat_axis=0, tiled=True)]
    all_to_all x8 -> x0, local copies, waits for them, and re-layouts: 83.7 us -> none  [the longest x6 66.3 us: to_bands(): lax.all_to_all(block, 'space', split_axis=2, concat_axis=1, tiled=True)]
    add x30 -> x1, other arithmetic: 64.2 us -> 0.7 us  [on_device(): start = diagonal[:, None] + orders.astype(F32)[:, None] * log_sines[None, :]]
  transfers between devices with their start and end apart: 2 -> 11, of which waited for: 2 -> 6; matrix products, arithmetic and copies ran while one was open for 11% -> 5% of each run, Pallas kernels for 0% -> 30%
where the time goes in v1:
time: 1010 us
  blocking collectives  378 us (37%)
  Pallas kernels  363 us (36%)
  waiting for transfers between devices  155 us (15%)
  local copies, waits for them, and re-layouts  46.1 us (5%)
  starting transfers between devices  36 us (4%)
  other arithmetic  14.5 us (1%)
  between operations  14.1 us (1%)
    all_to_all x8, blocking collectives, exchange(): lax.all_to_all(block, 'space', split_axis=0, concat_axis=0, tiled=True)  378 us
    all_to_all x8, waiting for transfers between devices, exchange(): lax.all_to_all(block, 'space', split_axis=0, concat_axis=0, tiled=True)  155 us
    pallas_call x2, Pallas kernels, spectrum_backward(): pl.pallas_call(functools.partial(spectrum_backward_kernel, plan, len(recv...  82.6 us
    pallas_call x2, Pallas kernels, legendre_tables(): pl.pallas_call(table_kernel, grid=(tp // 8, plan.degrees // 16), in_specs...  71 us
    pallas_call x2, Pallas kernels, spectrum_forward(): pl.pallas_call(functools.partial(spectrum_forward_kernel, plan), grid=(pl...  68.8 us
    pallas_call x3, Pallas kernels, score(): pl.pallas_call(functools.partial(score_kernel, plan, first, members), gri...  49.1 us
    pallas_call x3, Pallas kernels, predict(): pl.pallas_call(functools.partial(predict_kernel, plan, first), grid=(coun...  41.6 us
    all_to_all x8, starting transfers between devices, exchange(): lax.all_to_all(block, 'space', split_axis=0, concat_axis=0, tiled=True)  35.7 us
  transfers between devices with their start and end apart: 11, of which 6 were waited for; matrix products, arithmetic and copies ran while one was open for 5% of the time, Pallas kernels for 30%

profile of v1, /device:TPU:0, one launch (start us, length us, event | category | flops | bytes accessed | tf_op | source)
XLA Modules:
  0.0 1007.5 jit_solution(4184446682909458493)
XLA Ops:
  7.2 5.9 pad.93.x_ref
  13.1 28.5 %analyse.1 = (bf16[8,49,32,128]{3,2,1,0:T(8,128)(2,1)}, bf16[8,49,32,128]{3,2,1,0:T(8,128)(2,1)}) custom-call(bf16[49,80,720]{2,1,0:T(8,128)(2,1)} %pad.93.x_ref, bf16[2,2,192,720]{3,2,1,0:T(8,128)(2,1)} %constant.362.clone.dft_ref), custom_call_target="tpu_custom_call" | custom-call | tf_op jit(solution)/shard_map/analyse/pallas_call | solution.py:201
  41.7 80.1 %all_to_all.80.recv = bf16[8,49,32,128]{3,2,1,0:T(8,128)(2,1)} all-to-all(bf16[8,49,32,128]{3,2,1,0:T(8,128)(2,1)} %get-tuple-element.169), channel_id=1, replica_groups=mesh['member'=4,'space'=8] {'space'}, dimensions={0} | all-to-all | bytes 6422528 | tf_op jit(solution)/shard_map/all_to_all | solution.py:637
  121.8 3.8 all-to-all-start
  125.8 0.7 slice.262
  127.6 0.7 fusion.9
  128.3 0.7 fusion.7
  129.0 0.7 multiply_add_fusion
  132.0 0.8 pad_bitcast_fusion.1
  132.8 2.2 scatter.35
  135.0 0.9 scatter.40
  135.9 1.9 scatter.36
  137.9 0.9 scatter.41
  138.8 0.9 scatter.45
  139.7 0.9 scatter.46
  140.7 1.9 scatter.39
  142.6 0.9 scatter.44
  143.5 0.9 scatter.49
  144.4 1.9 fusion.13
  146.2 1.9 copy.32.mix
  148.1 0.7 broadcast_in_dim.24.m_ref
  148.8 35.5 %legendre_tables.3 = (bf16[24,368,392]{2,1,0:T(8,128)(2,1)}, bf16[24,368,392]{2,1,0:T(8,128)(2,1)}) custom-call(f32[24,128]{1,0:T(8,128)} %broadcast_in_dim.24.m_ref, f32[24,512]{1,0:T(8,128)} %pad.101.start_ref, f32[1,512]{1,0:T(1,128)} %bitcast.52, f32[1,512]{1,0:T(1,128)} %bitcast.54, f32[1,512]{1,0:T(1,128)} %bitcast.50), custom_call_target="tpu_custom_call" | custom-call | tf_op jit(solution)/shard_map/legendre_tables/pallas_call | solution.py:144
  184.3 0.9 constant_dynamic-update-slice_fusion.1
  185.2 0.9 constant_dynamic-update-slice_fusion.gain.refs_6_
  186.2 0.7 copy-done.5
  186.9 34.4 %spectrum_forward.3 = (bf16[8,14,48,128]{3,2,1,0:T(8,128)(2,1)}, bf16[8,14,48,128]{3,2,1,0:T(8,128)(2,1)}, bf16[8,21,48,128]{3,2,1,0:T(8,128)(2,1)}) custom-call(bf16[8,49,32,128]{3,2,1,0:T(8,128)(2,1)} %all_to_all.80.recv, bf16[24,368,392]{2,1,0:T(8,128)(2,1)} %get-tuple-element.170.fwd.refs_3_, bf16[24,368,392]{2,1,0:T(8,128)(2,1)} %get-tuple-element.171.inv.refs_4_, ...), custom_call_target="tpu_custom_call" | custom-call | tf_op jit(solution)/shard_map/spectrum_forward/pallas_call | solution.py:321
  221.4 5.9 all-to-all-start.3
  227.9 0.7 broadcast_in_dim.20.m_ref
  228.6 35.5 %legendre_tables.2 = (bf16[24,368,392]{2,1,0:T(8,128)(2,1)}, bf16[24,368,392]{2,1,0:T(8,128)(2,1)}) custom-call(f32[24,128]{1,0:T(8,128)} %broadcast_in_dim.20.m_ref, f32[24,512]{1,0:T(8,128)} %pad.96.start_ref, f32[1,512]{1,0:T(1,128)} %bitcast.53, f32[1,512]{1,0:T(1,128)} %bitcast.55, f32[1,512]{1,0:T(1,128)} %bitcast.51), custom_call_target="tpu_custom_call" | custom-call | tf_op jit(solution)/shard_map/legendre_tables/pallas_call | solution.py:144
  264.1 34.4 %spectrum_forward.2 = (bf16[8,14,48,128]{3,2,1,0:T(8,128)(2,1)}, bf16[8,14,48,128]{3,2,1,0:T(8,128)(2,1)}, bf16[8,21,48,128]{3,2,1,0:T(8,128)(2,1)}) custom-call(bf16[8,49,32,128]{3,2,1,0:T(8,128)(2,1)} %copy-done.3, bf16[24,368,392]{2,1,0:T(8,128)(2,1)} %get-tuple-element.166.fwd.refs_3_, bf16[24,368,392]{2,1,0:T(8,128)(2,1)} %get-tuple-element.167.inv.refs_4_, ...), custom_call_target="tpu_custom_call" | custom-call | tf_op jit(solution)/shard_map/spectrum_forward/pallas_call | solution.py:321
  298.5 6.1 all-to-all-start.1
  306.8 28.9 %all-to-all-done.1.refs_0_ = bf16[8,14,48,128]{3,2,1,0:T(8,128)(2,1)S(1)} async-done(((bf16[8,14,48,128]{3,2,1,0:T(8,128)(2,1)}), bf16[8,14,48,128]{3,2,1,0:T(8,128)(2,1)S(1)}, u32[]{:S(2)}, u32[]{:S(2)}) %all-to-all-start.1) | async-done | bytes 1376288 | tf_op jit(solution)/shard_map/all_to_all | solution.py:637
  335.7 1.1 copy-done.8
  336.7 12.4 %predict.3 = (bf16[14,80,720]{2,1,0:T(8,128)(2,1)}, bf16[14,128,720]{2,1,0:T(8,128)(2,1)}) custom-call(f32[49]{0:T(128)} %get-tuple-element.195.live_ref, bf16[49,80,720]{2,1,0:T(8,128)(2,1)} %pad.93.x_ref, bf16[768,720]{1,0:T(8,128)(2,1)} %constant.363.clone.idft_ref, bf16[128,80]{1,0:T(8,128)(2,1)} %pad.94.enc_ref, bf16[80,128]{1,0:T(8,128)(2,1)} %pad.95.dec_ref, ...), custom_call_target="tpu_custom_call" | custom-call | tf_op jit(solution)/shard_map/predict/pallas_call | solution.py:387
  349.2 37.0 %all_to_all.81.refs_1_ = bf16[8,14,48,128]{3,2,1,0:T(8,128)(2,1)} all-to-all(bf16[8,14,48,128]{3,2,1,0:T(8,128)(2,1)S(1)} %copy-done.14), channel_id=1, replica_groups=mesh['member'=4,'space'=8] {'space'}, dimensions={0} | all-to-all | bytes 2752512 | tf_op jit(solution)/shard_map/all_to_all | solution.py:637
  386.3 36.2 %all_to_all.82.refs_0_ = bf16[8,14,48,128]{3,2,1,0:T(8,128)(2,1)} all-to-all(bf16[8,14,48,128]{3,2,1,0:T(8,128)(2,1)S(1)} %copy-done.15), channel_id=1, replica_groups=mesh['member'=4,'space'=8] {'space'}, dimensions={0} | all-to-all | bytes 2752512 | tf_op jit(solution)/shard_map/all_to_all | solution.py:637
  422.5 12.4 %predict.4 = (bf16[14,80,720]{2,1,0:T(8,128)(2,1)}, bf16[14,128,720]{2,1,0:T(8,128)(2,1)}) custom-call(f32[49]{0:T(128)} %get-tuple-element.195.live_ref, bf16[49,80,720]{2,1,0:T(8,128)(2,1)} %pad.93.x_ref, bf16[768,720]{1,0:T(8,128)(2,1)} %constant.363.clone.idft_ref, bf16[128,80]{1,0:T(8,128)(2,1)} %pad.94.enc_ref, bf16[80,128]{1,0:T(8,128)(2,1)} %pad.95.dec_ref, ...), custom_call_target="tpu_custom_call" | custom-call | tf_op jit(solution)/shard_map/predict/pallas_call | solution.py:387
  434.9 50.1 %all_to_all.83.refs_1_ = bf16[8,21,48,128]{3,2,1,0:T(8,128)(2,1)} all-to-all(bf16[8,21,48,128]{3,2,1,0:T(8,128)(2,1)S(1)} %copy-done.10), channel_id=1, replica_groups=mesh['member'=4,'space'=8] {'space'}, dimensions={0} | all-to-all | bytes 4128768 | tf_op jit(solution)/shard_map/all_to_all | solution.py:637
  485.1 50.5 %all_to_all.84.refs_0_ = bf16[8,21,48,128]{3,2,1,0:T(8,128)(2,1)} all-to-all(bf16[8,21,48,128]{3,2,1,0:T(8,128)(2,1)S(1)} %copy-done.11), channel_id=1, replica_groups=mesh['member'=4,'space'=8] {'space'}, dimensions={0} | all-to-all | bytes 4128768 | tf_op jit(solution)/shard_map/all_to_all | solution.py:637
  535.6 16.8 %predict.5 = (bf16[21,80,720]{2,1,0:T(8,128)(2,1)}, bf16[21,128,720]{2,1,0:T(8,128)(2,1)}) custom-call(f32[49]{0:T(128)} %get-tuple-element.195.live_ref, bf16[49,80,720]{2,1,0:T(8,128)(2,1)} %pad.93.x_ref, bf16[768,720]{1,0:T(8,128)(2,1)} %constant.363.clone.idft_ref, bf16[128,80]{1,0:T(8,128)(2,1)} %pad.94.enc_ref, bf16[80,128]{1,0:T(8,128)(2,1)} %pad.95.dec_ref, ...), custom_call_target="tpu_custom_call" | custom-call | tf_op jit(solution)/shard_map/predict/pallas_call | solution.py:387
  552.5 6.0 pad.102.obs_ref
  559.2 15.5 %score.3 = (bf16[14,80,720]{2,1,0:T(8,128)(2,1)}, bf16[8,14,48,128]{3,2,1,0:T(8,128)(2,1)}, bf16[8,14,48,128]{3,2,1,0:T(8,128)(2,1)}) custom-call(f32[49]{0:T(128)} %get-tuple-element.194.area_ref, bf16[14,80,720]{2,1,0:T(8,128)(2,1)} %get-tuple-element.173.own_ref, bf16[4,14,80,720]{3,2,1,0:T(8,128)(2,1)} %bitcast.44, bf16[49,80,720]{2,1,0:T(8,128)(2,1)} %pad.102.obs_ref, ...), custom_call_target="tpu_custom_call" | custom-call | tf_op jit(solution)/shard_map/score/pallas_call | solution.py:455
  574.6 3.6 all-to-all-start.12
  578.2 14.4 %score.4 = (bf16[14,80,720]{2,1,0:T(8,128)(2,1)}, bf16[8,14,48,128]{3,2,1,0:T(8,128)(2,1)}, bf16[8,14,48,128]{3,2,1,0:T(8,128)(2,1)}) custom-call(f32[49]{0:T(128)} %get-tuple-element.194.area_ref, bf16[14,80,720]{2,1,0:T(8,128)(2,1)} %get-tuple-element.176.own_ref, bf16[4,14,80,720]{3,2,1,0:T(8,128)(2,1)} %bitcast.45, bf16[49,80,720]{2,1,0:T(8,128)(2,1)} %pad.102.obs_ref, ...), custom_call_target="tpu_custom_call" | custom-call | tf_op jit(solution)/shard_map/score/pallas_call | solution.py:455
  592.6 17.6 %all-to-all-done.12.refs_0_ = bf16[8,14,48,128]{3,2,1,0:T(8,128)(2,1)S(1)} async-done(((bf16[8,14,48,128]{3,2,1,0:T(8,128)(2,1)}), bf16[8,14,48,128]{3,2,1,0:T(8,128)(2,1)S(1)}, u32[]{:S(2)}, u32[]{:S(2)}) %all-to-all-start.12) | async-done | bytes 1376288 | tf_op jit(solution)/shard_map/all_to_all | solution.py:637
  610.3 37.1 %all_to_all.85.refs_1_ = bf16[8,14,48,128]{3,2,1,0:T(8,128)(2,1)} all-to-all(bf16[8,14,48,128]{3,2,1,0:T(8,128)(2,1)} %get-tuple-element.190), channel_id=1, replica_groups=mesh['member'=4,'space'=8] {'space'}, dimensions={0} | all-to-all | bytes 2752512 | tf_op jit(solution)/shard_map/all_to_all | solution.py:637
  647.4 35.7 %all_to_all.86.refs_0_ = bf16[8,14,48,128]{3,2,1,0:T(8,128)(2,1)} all-to-all(bf16[8,14,48,128]{3,2,1,0:T(8,128)(2,1)S(1)} %copy-done.16), channel_id=1, replica_groups=mesh['member'=4,'space'=8] {'space'}, dimensions={0} | all-to-all | bytes 2752512 | tf_op jit(solution)/shard_map/all_to_all | solution.py:637
  683.1 3.6 all-to-all-start.9
  686.7 19.3 %score.5 = (bf16[21,80,720]{2,1,0:T(8,128)(2,1)}, bf16[8,21,48,128]{3,2,1,0:T(8,128)(2,1)}, bf16[8,21,48,128]{3,2,1,0:T(8,128)(2,1)}) custom-call(f32[49]{0:T(128)} %get-tuple-element.194.area_ref, bf16[21,80,720]{2,1,0:T(8,128)(2,1)} %get-tuple-element.179.own_ref, bf16[4,21,80,720]{3,2,1,0:T(8,128)(2,1)} %bitcast.43, bf16[49,80,720]{2,1,0:T(8,128)(2,1)} %pad.102.obs_ref, ...), custom_call_target="tpu_custom_call" | custom-call | tf_op jit(solution)/shard_map/score/pallas_call | solution.py:455
  706.0 12.6 %all-to-all-done.9.refs_1_ = bf16[8,14,48,128]{3,2,1,0:T(8,128)(2,1)S(1)} async-done(((bf16[8,14,48,128]{3,2,1,0:T(8,128)(2,1)}), bf16[8,14,48,128]{3,2,1,0:T(8,128)(2,1)S(1)}, u32[]{:S(2)}, u32[]{:S(2)}) %all-to-all-start.9) | async-done | bytes 1376288 | tf_op jit(solution)/shard_map/all_to_all | solution.py:637
  718.6 51.3 %all_to_all.87.refs_2_ = bf16[8,21,48,128]{3,2,1,0:T(8,128)(2,1)} all-to-all(bf16[8,21,48,128]{3,2,1,0:T(8,128)(2,1)} %get-tuple-element.191), channel_id=1, replica_groups=mesh['member'=4,'space'=8] {'space'}, dimensions={0} | all-to-all | bytes 4128768 | tf_op jit(solution)/shard_map/all_to_all | solution.py:637
  769.9 3.8 all-to-all-start.10
  773.7 41.3 %spectrum_backward.3 = bf16[8,49,32,128]{3,2,1,0:T(8,128)(2,1)} custom-call(bf16[8,14,48,128]{3,2,1,0:T(8,128)(2,1)} %copy-done.6, bf16[8,14,48,128]{3,2,1,0:T(8,128)(2,1)} %all_to_all.85.refs_1_, bf16[8,21,48,128]{3,2,1,0:T(8,128)(2,1)} %all_to_all.87.refs_2_, bf16[24,368,392]{2,1,0:T(8,128)(2,1)} %get-tuple-element.170.fwd.refs_3_, ...), custom_call_target="tpu_custom_call" | custom-call | tf_op jit(solution)/shard_map/spectrum_backward/pallas_call | solution.py:338
  815.1 5.5 all-to-all-done.10.refs_2_
  820.6 1.3 copy-done.4
  821.9 4.5 all-to-all-start.15
  826.3 41.3 %spectrum_backward.2 = bf16[8,49,32,128]{3,2,1,0:T(8,128)(2,1)} custom-call(bf16[8,14,48,128]{3,2,1,0:T(8,128)(2,1)} %all_to_all.86.refs_0_, bf16[8,14,48,128]{3,2,1,0:T(8,128)(2,1)} %copy-done.7, bf16[8,21,48,128]{3,2,1,0:T(8,128)(2,1)} %copy-done.4, bf16[24,368,392]{2,1,0:T(8,128)(2,1)} %get-tuple-element.166.fwd.refs_3_, ...), custom_call_target="tpu_custom_call" | custom-call | tf_op jit(solution)/shard_map/spectrum_backward/pallas_call | solution.py:338
  867.6 30.2 %all-to-all-done.15.refs_1_ = bf16[8,49,32,128]{3,2,1,0:T(8,128)(2,1)} async-done(((bf16[8,49,32,128]{3,2,1,0:T(8,128)(2,1)}), bf16[8,49,32,128]{3,2,1,0:T(8,128)(2,1)}, u32[]{:S(2)}, u32[]{:S(2)}) %all-to-all-start.15) | async-done | bytes 3211296 | tf_op jit(solution)/shard_map/all_to_all | solution.py:637
  897.8 4.5 all-to-all-start.11
  903.0 6.8 fusion
  909.9 3.5 pad_maximum_fusion.2.grad_ref
  913.3 60.5 %all-to-all-done.11.refs_0_ = bf16[8,49,32,128]{3,2,1,0:T(8,128)(2,1)} async-done(((bf16[8,49,32,128]{3,2,1,0:T(8,128)(2,1)}), bf16[8,49,32,128]{3,2,1,0:T(8,128)(2,1)}, u32[]{:S(2)}, u32[]{:S(2)}) %all-to-all-start.11) | async-done | bytes 3211296 | tf_op jit(solution)/shard_map/all_to_all | solution.py:637
  973.8 21.4 %finish.1 = bf16[49,80,720]{2,1,0:T(8,128)(2,1)} custom-call(f32[49]{0:T(128)} %get-tuple-element.195.live_ref, bf16[49,80,720]{2,1,0:T(8,128)(2,1)} %pad_maximum_fusion.2.grad_ref, bf16[768,720]{1,0:T(8,128)(2,1)} %constant.364.clone.main_ref, bf16[768,720]{1,0:T(8,128)(2,1)} %constant.365.clone.rest_ref, bf16[80,80]{1,0:T(8,128)(2,1)} %pad.104.through_ref, ...), custom_call_target="tpu_custom_call" | custom-call | tf_op jit(solution)/shard_map/finish/pallas_call | solution.py:525
  995.2 5.7 slice_bitcast_fusion
  (76 shorter events, 8.1 us)
Async XLA Ops:
  7.2 118.4 %copy-start = (bf16[128,128]{1,0:T(8,128)(2,1)S(1)}, bf16[128,128]{1,0:T(8,128)(2,1)}, u32[]{:S(2)}) copy-start(bf16[128,128]{1,0:T(8,128)(2,1)} %param.43) | copy-start | bytes 98308
  121.8 3.8 copy-start.19
  121.8 5.4 copy-start.21
  121.8 99.6 %all-to-all-start = ((bf16[8,49,32,128]{3,2,1,0:T(8,128)(2,1)}), bf16[8,49,32,128]{3,2,1,0:T(8,128)(2,1)S(1)}, u32[]{:S(2)}, u32[]{:S(2)}) async-start(bf16[8,49,32,128]{3,2,1,0:T(8,128)(2,1)} %get-tuple-element.165), calls=%async_computation | async-start | bytes 6422528 | tf_op jit(solution)/shard_map/all_to_all | solution.py:637
  186.2 0.8 copy-start.5
  221.3 6.0 copy-start.17
  221.4 42.7 %copy-start.3 = (bf16[8,49,32,128]{3,2,1,0:T(8,128)(2,1)}, bf16[8,49,32,128]{3,2,1,0:T(8,128)(2,1)S(1)}, u32[]{:S(2)}) copy-start(bf16[8,49,32,128]{3,2,1,0:T(8,128)(2,1)S(1)} %all-to-all-done.recv) | copy-start | bytes 9633796
  221.4 77.1 %all-to-all-start.3 = ((bf16[8,14,48,128]{3,2,1,0:T(8,128)(2,1)}), bf16[8,14,48,128]{3,2,1,0:T(8,128)(2,1)}, u32[]{:S(2)}, u32[]{:S(2)}) async-start(bf16[8,14,48,128]{3,2,1,0:T(8,128)(2,1)} %get-tuple-element.172), calls=%async_computation.3 | async-start | bytes 2752512 | tf_op jit(solution)/shard_map/all_to_all | solution.py:637
  298.4 6.4 copy-start.20
  298.4 7.1 copy-start.18
  298.5 37.2 %all-to-all-start.1 = ((bf16[8,14,48,128]{3,2,1,0:T(8,128)(2,1)}), bf16[8,14,48,128]{3,2,1,0:T(8,128)(2,1)S(1)}, u32[]{:S(2)}, u32[]{:S(2)}) async-start(bf16[8,14,48,128]{3,2,1,0:T(8,128)(2,1)} %get-tuple-element.168), calls=%async_computation.1 | async-start | bytes 2752512 | tf_op jit(solution)/shard_map/all_to_all | solution.py:637
  304.6 254.6 %all-gather.7.cloned.1.call-start = ((), (), s32[]{:S(2)}) async-start(), calls=%async_computation.16 | async-start | bytes 8601600 | tf_op jit(solution)/shard_map/all_gather | solution.py:659
  335.7 1.1 copy-start.8
  336.7 12.5 %copy-start.14 = (bf16[8,14,48,128]{3,2,1,0:T(8,128)(2,1)S(1)}, bf16[8,14,48,128]{3,2,1,0:T(8,128)(2,1)}, u32[]{:S(2)}) copy-start(bf16[8,14,48,128]{3,2,1,0:T(8,128)(2,1)} %get-tuple-element.175) | copy-start | bytes 4128772
  349.1 37.1 %copy-start.15 = (bf16[8,14,48,128]{3,2,1,0:T(8,128)(2,1)S(1)}, bf16[8,14,48,128]{3,2,1,0:T(8,128)(2,1)}, u32[]{:S(2)}) copy-start(bf16[8,14,48,128]{3,2,1,0:T(8,128)(2,1)} %get-tuple-element.174) | copy-start | bytes 4128772
  349.2 229.1 %all-gather.9.cloned.1.call-start = ((), (), s32[]{:S(2)}) async-start(), calls=%async_computation.17 | async-start | bytes 8601600 | tf_op jit(solution)/shard_map/all_gather | solution.py:659
  422.4 12.5 %copy-start.10 = (bf16[8,21,48,128]{3,2,1,0:T(8,128)(2,1)S(1)}, bf16[8,21,48,128]{3,2,1,0:T(8,128)(2,1)}, u32[]{:S(2)}) copy-start(bf16[8,21,48,128]{3,2,1,0:T(8,128)(2,1)} %get-tuple-element.178) | copy-start | bytes 6193156
  434.9 251.9 %all-gather.11.cloned.1.call-start = ((), (), s32[]{:S(2)}) async-start(), calls=%async_computation.18 | async-start | bytes 12902400 | tf_op jit(solution)/shard_map/all_gather | solution.py:659
  434.9 50.2 %copy-start.11 = (bf16[8,21,48,128]{3,2,1,0:T(8,128)(2,1)S(1)}, bf16[8,21,48,128]{3,2,1,0:T(8,128)(2,1)}, u32[]{:S(2)}) copy-start(bf16[8,21,48,128]{3,2,1,0:T(8,128)(2,1)} %get-tuple-element.177) | copy-start | bytes 6193156
  574.6 35.6 %all-to-all-start.12 = ((bf16[8,14,48,128]{3,2,1,0:T(8,128)(2,1)}), bf16[8,14,48,128]{3,2,1,0:T(8,128)(2,1)S(1)}, u32[]{:S(2)}, u32[]{:S(2)}) async-start(bf16[8,14,48,128]{3,2,1,0:T(8,128)(2,1)} %get-tuple-element.189), calls=%async_computation.12 | async-start | bytes 2752512 | tf_op jit(solution)/shard_map/all_to_all | solution.py:637
  592.6 54.8 %copy-start.16 = (bf16[8,14,48,128]{3,2,1,0:T(8,128)(2,1)S(1)}, bf16[8,14,48,128]{3,2,1,0:T(8,128)(2,1)}, u32[]{:S(2)}) copy-start(bf16[8,14,48,128]{3,2,1,0:T(8,128)(2,1)} %get-tuple-element.186) | copy-start | bytes 4128772
  610.3 72.9 %copy-start.6 = (bf16[8,14,48,128]{3,2,1,0:T(8,128)(2,1)}, bf16[8,14,48,128]{3,2,1,0:T(8,128)(2,1)S(1)}, u32[]{:S(2)}) copy-start(bf16[8,14,48,128]{3,2,1,0:T(8,128)(2,1)S(1)} %all-to-all-done.12.refs_0_) | copy-start | bytes 4128772
  683.1 35.5 %all-to-all-start.9 = ((bf16[8,14,48,128]{3,2,1,0:T(8,128)(2,1)}), bf16[8,14,48,128]{3,2,1,0:T(8,128)(2,1)S(1)}, u32[]{:S(2)}, u32[]{:S(2)}) async-start(bf16[8,14,48,128]{3,2,1,0:T(8,128)(2,1)} %get-tuple-element.187), calls=%async_computation.9 | async-start | bytes 2752512 | tf_op jit(solution)/shard_map/all_to_all | solution.py:637
  718.6 51.3 %copy-start.7 = (bf16[8,14,48,128]{3,2,1,0:T(8,128)(2,1)}, bf16[8,14,48,128]{3,2,1,0:T(8,128)(2,1)S(1)}, u32[]{:S(2)}) copy-start(bf16[8,14,48,128]{3,2,1,0:T(8,128)(2,1)S(1)} %all-to-all-done.9.refs_1_) | copy-start | bytes 4128772
  769.9 50.7 %all-to-all-start.10 = ((bf16[8,21,48,128]{3,2,1,0:T(8,128)(2,1)}), bf16[8,21,48,128]{3,2,1,0:T(8,128)(2,1)S(1)}, u32[]{:S(2)}, u32[]{:S(2)}) async-start(bf16[8,21,48,128]{3,2,1,0:T(8,128)(2,1)} %get-tuple-element.188), calls=%async_computation.10 | async-start | bytes 4128768 | tf_op jit(solution)/shard_map/all_to_all | solution.py:637
  820.6 1.3 copy-start.4
  821.9 75.9 %all-to-all-start.15 = ((bf16[8,49,32,128]{3,2,1,0:T(8,128)(2,1)}), bf16[8,49,32,128]{3,2,1,0:T(8,128)(2,1)}, u32[]{:S(2)}, u32[]{:S(2)}) async-start(bf16[8,49,32,128]{3,2,1,0:T(8,128)(2,1)} %spectrum_backward.3), calls=%async_computation.15 | async-start | bytes 6422528 | tf_op jit(solution)/shard_map/all_to_all | solution.py:637
  867.6 35.4 %copy-start.2 = (bf16[21,80,720]{2,1,0:T(8,128)(2,1)S(1)}, bf16[21,80,720]{2,1,0:T(8,128)(2,1)}, u32[]{:S(2)}) copy-start(bf16[21,80,720]{2,1,0:T(8,128)(2,1)} %get-tuple-element.179.own_ref) | copy-start | bytes 7257604
  897.8 76.0 %all-to-all-start.11 = ((bf16[8,49,32,128]{3,2,1,0:T(8,128)(2,1)}), bf16[8,49,32,128]{3,2,1,0:T(8,128)(2,1)}, u32[]{:S(2)}, u32[]{:S(2)}) async-start(bf16[8,49,32,128]{3,2,1,0:T(8,128)(2,1)} %spectrum_backward.2), calls=%async_computation.11 | async-start | bytes 6422528 | tf_op jit(solution)/shard_map/all_to_all | solution.py:637
  903.0 6.8 copy-start.9
  903.0 6.8 copy-start.12
  903.0 6.8 copy-start.13
  995.2 5.7 copy-start.1
Sparse Core Ops, SparseCore 0:
  349.3 48.5 all-gather.6
  435.0 48.1 all-gather.8
  552.5 68.2 all-gather.10

commit v2 on v1

--- a/solution.py
+++ b/solution.py
@@ -17,6 +17,7 @@
 SPLIT = 64
 REST = 16
 LANES = 128
+NONE = 1 << 14
 VMEM = 60 * 1024 * 1024
 BF = jnp.bfloat16
 F32 = jnp.float32
@@ -38,7 +39,14 @@
         self.rest_groups = -(-self.tb // 4)
         self.rows1 = ceil_to(self.tp + 8 * self.rest_groups, 16)
         self.rows2 = 2 * self.tp
-        self.groups = -(-(LMAX + 1) // (space * self.live_t))
+        self.low = space * self.live_t
+        self.high = LMAX + 1 - self.low
+        self.pairs = ceil_to(-(-self.high // 2), 8)
+        self.quads = self.pairs // 4
+        self.quad_pad = ceil_to(self.quads, 8)
+        self.span = ceil_to(self.high + 1, 16)
+        self.half = ceil_to(band, 16)
+        self.half_lanes = LANES // 2
         self.rb = max(k for k in range(1, 9) if band % k == 0)
         blocks = band // self.rb
         parts = min(3, blocks)
@@ -49,15 +57,19 @@
             self.chunks.append((start * self.rb, count * self.rb))
             start += count
 
-    def orders(self, group):
+    def low_orders(self):
         device = np.arange(self.n)[:, None]
         position = np.arange(self.tp)[None, :]
-        order = group * self.n * self.live_t + device * self.live_t + position
-        return np.where((position < self.live_t) & (order <= LMAX), order, 1 << 14)
-
-
-def dft_rows(plan, group, inverse):
-    order = plan.orders(group)
+        return np.where(position < self.live_t, device * self.live_t + position, NONE)
+
+    def high_orders(self):
+        pair = np.arange(self.pairs)
+        first = np.where(2 * pair < self.high, self.low + pair, NONE)
+        second = np.where(2 * pair < self.high - 1, LMAX - pair, NONE)
+        return np.stack([first, second])
+
+
+def dft_rows(plan, order, inverse):
     live = (order <= LMAX)[..., None]
     turn = (np.where(order <= LMAX, order, 0)[..., None] * np.arange(plan.lon)) % plan.lon
     angle = turn * (2.0 * math.pi / plan.lon)
@@ -77,10 +89,10 @@
     return pl.BlockSpec(shape, lambda *_: (0,) * len(shape))
 
 
-def table_kernel(m_ref, start_ref, cos_ref, quad_ref, live_ref, fwd_ref, inv_ref, one, two, logs, stage):
+def table_kernel(m_ref, shift_ref, start_ref, cos_ref, quad_ref, live_ref, fwd_ref, inv_ref, one, two, logs, stage):
     block = pl.program_id(1)
     lanes = fwd_ref.shape[2]
-    order = m_ref[...]
+    order, shift = m_ref[...], shift_ref[...]
 
     @pl.when(block == 0)
     def _():
@@ -90,8 +102,7 @@
 
     ups, backs, pasts, onsets, keeps = [], [], [], [], []
     for p in range(16):
-        degree = block * 16 + p
-        deg = degree.astype(F32)
+        deg = shift + (block * 16 + p).astype(F32)
         ups.append(
             jnp.sqrt((4.0 * deg * deg - 1.0) / jnp.maximum(deg * deg - order * order, 1.0))
         )
@@ -103,7 +114,7 @@
         )
         pasts.append(order < deg)
         onsets.append(jnp.where(order == deg, 1.0, 0.0))
-        keeps.append((order <= deg) & (degree <= LMAX))
+        keeps.append((order <= deg) & (deg <= LMAX))
     for c in range(one.shape[1] // LANES):
         at = slice(c * LANES, (c + 1) * LANES)
         first, second, log_scale = one[:, at], two[:, at], logs[:, at]
@@ -129,7 +140,7 @@
             inv_ref[i, :, out] = (values * live_ref[:, at]).astype(BF)[:, :width]
 
 
-def legendre_tables(plan, orders, log_start, cosines, quad, live):
+def legendre_tables(orders, shift, log_start, cosines, quad, live, degrees):
     rows = cosines.shape[0]
     wide = ceil_to(rows, LANES)
     tp = orders.shape[0]
@@ -137,15 +148,16 @@
     def spread(row):
         return jnp.pad(row, (0, wide - rows))[None]
 
-    order_f = jnp.broadcast_to(orders.astype(F32)[:, None], (tp, LANES))
-    shape = jax.ShapeDtypeStruct((tp, plan.degrees, rows), BF)
+    shape = jax.ShapeDtypeStruct((tp, degrees, rows), BF)
     row_spec = pl.BlockSpec((1, wide), lambda i, j: (0, 0))
+    lane_spec = pl.BlockSpec((8, LANES), lambda i, j: (i, 0))
     out_spec = pl.BlockSpec((8, 16, rows), lambda i, j: (i, j, 0))
     return pl.pallas_call(
         table_kernel,
-        grid=(tp // 8, plan.degrees // 16),
+        grid=(tp // 8, degrees // 16),
         in_specs=[
-            pl.BlockSpec((8, LANES), lambda i, j: (i, 0)),
+            lane_spec,
+            lane_spec,
             pl.BlockSpec((8, wide), lambda i, j: (i, 0)),
             row_spec,
             row_spec,
@@ -161,10 +173,17 @@
         ],
         compiler_params=params(),
         name="legendre_tables",
-    )(order_f, jnp.pad(log_start, ((0, 0), (0, wide - rows))), spread(cosines), spread(quad), spread(live))
-
-
-def analyse_kernel(plan, x_ref, dft_ref, *outs):
+    )(
+        orders.astype(F32),
+        shift.astype(F32),
+        jnp.pad(log_start, ((0, 0), (0, wide - rows))),
+        spread(cosines),
+        spread(quad),
+        spread(live),
+    )
+
+
+def analyse_kernel(plan, x_ref, low_ref, high_ref, out, out_high):
     lane = lax.broadcasted_iota(jnp.int32, (1, LANES), 1)
     part = lane // REST
     n, tp = plan.n, plan.tp
@@ -172,44 +191,55 @@
         x = x_ref[r]
         head, tail = x[:SPLIT], x[SPLIT:]
         right = jnp.concatenate([head, head] + [tail] * (LANES // REST), axis=0)
-        for g, out in enumerate(outs):
-            cosine, sine = [
+
+        def modes(dft_ref):
+            return [
                 lax.dot_general(
-                    dft_ref[g, k], right, (((1,), (1,)), ((), ())), preferred_element_type=F32
+                    dft_ref[k], right, (((1,), (1,)), ((), ())), preferred_element_type=F32
                 )
                 for k in range(2)
             ]
-            main = jnp.where(lane < SPLIT, cosine[:, :LANES], sine[:, :LANES])
-            for o in range(n):
-                pieces = [main[o * tp : (o + 1) * tp]]
-                for group in range(plan.rest_groups):
-                    rest = jnp.zeros((8, LANES), F32)
-                    for i in range(min(4, plan.tb - group * 4)):
-                        first = o * tp + (group * 4 + i) * 8
-                        rest = jnp.where(part == 2 * i, cosine[first : first + 8, LANES:], rest)
-                        rest = jnp.where(part == 2 * i + 1, sine[first : first + 8, LANES:], rest)
-                    pieces.append(rest)
-                spare = plan.rows1 - tp - 8 * plan.rest_groups
-                if spare:
-                    pieces.append(jnp.zeros((spare, LANES), F32))
-                out[o, r] = jnp.concatenate(pieces, axis=0).astype(BF)
-
-
-def analyse(plan, x, dft):
+
+        cosine, sine = modes(low_ref)
+        main = jnp.where(lane < SPLIT, cosine[:, :LANES], sine[:, :LANES])
+        for o in range(n):
+            pieces = [main[o * tp : (o + 1) * tp]]
+            for group in range(plan.rest_groups):
+                rest = jnp.zeros((8, LANES), F32)
+                for i in range(min(4, plan.tb - group * 4)):
+                    first = o * tp + (group * 4 + i) * 8
+                    rest = jnp.where(part == 2 * i, cosine[first : first + 8, LANES:], rest)
+                    rest = jnp.where(part == 2 * i + 1, sine[first : first + 8, LANES:], rest)
+                pieces.append(rest)
+            spare = plan.rows1 - tp - 8 * plan.rest_groups
+            if spare:
+                pieces.append(jnp.zeros((spare, LANES), F32))
+            out[o, r] = jnp.concatenate(pieces, axis=0).astype(BF)
+        cosine, sine = modes(high_ref)
+        main = jnp.where(lane < SPLIT, cosine[:, :LANES], sine[:, :LANES])
+        rest = jnp.where(part % 2 == 0, cosine[:, LANES:], sine[:, LANES:])
+        out_high[r] = jnp.concatenate([main, rest], axis=1).astype(BF)
+
+
+def analyse(plan, x, low, high):
     shape = (plan.n, plan.rows, plan.rows1, LANES)
-    out_spec = pl.BlockSpec((plan.n, plan.rb, plan.rows1, LANES), lambda i: (0, i, 0, 0))
+    high_shape = (plan.rows, 2 * plan.pairs, 2 * LANES)
     return pl.pallas_call(
         functools.partial(analyse_kernel, plan),
         grid=(plan.rows // plan.rb,),
         in_specs=[
             pl.BlockSpec((plan.rb, plan.fpad, plan.lon), lambda i: (i, 0, 0)),
-            whole(dft.shape),
-        ],
-        out_specs=[out_spec] * plan.groups,
-        out_shape=[jax.ShapeDtypeStruct(shape, BF)] * plan.groups,
+            whole(low.shape),
+            whole(high.shape),
+        ],
+        out_specs=[
+            pl.BlockSpec((plan.n, plan.rb, plan.rows1, LANES), lambda i: (0, i, 0, 0)),
+            pl.BlockSpec((plan.rb,) + high_shape[1:], lambda i: (i, 0, 0)),
+        ],
+        out_shape=[jax.ShapeDtypeStruct(shape, BF), jax.ShapeDtypeStruct(high_shape, BF)],
         compiler_params=params(),
         name="analyse",
-    )(x, dft)
+    )(x, low, high)
 
 
 def unpack(plan, refs, store, height):
@@ -313,7 +343,7 @@
 
 def spectrum_specs(plan, mix, gain):
     table = pl.BlockSpec((1, plan.degrees, plan.all_rows), lambda t: (t, 0, 0))
-    return [table, table, pl.BlockSpec((1,) + mix.shape[1:], lambda t: (t // 8, 0, 0)), whole(gain.shape)]
+    return [table, table, pl.BlockSpec((1,) + mix.shape[1:], lambda t: ((t // 8) % 4, 0, 0)), whole(gain.shape)]
 
 
 def spectrum_forward(plan, recv, fwd, inv, mix, gain):
@@ -350,15 +380,223 @@
     )(*recvs, fwd, inv, mix, gain)
 
 
+def pair_gain(plan, pair, gain):
+    row = lax.broadcasted_iota(jnp.int32, (plan.span, 1), 0)
+    first, second = plan.low + pair, plan.low - 1
+    first_at = pl.multiple_of(first // 8 * 8, 8)
+    one = jnp.where(
+        row < plan.high - pair,
+        gain[first % 8, pl.ds(first_at, plan.span), :],
+        gain[second % 8, pl.ds(second // 8 * 8, plan.span), :],
+    )
+    return jnp.concatenate([one, one], axis=1)
+
+
+def load_rows(plan, refs, store, height, wide):
+    start = 0
+    for ref in refs:
+
+        def step(r, unused, start=start, ref=ref):
+            at = pl.multiple_of((start + r) * height, 8)
+            for w in range(wide):
+                store[w, pl.ds(at, height), :] = ref[r, :, w * LANES : (w + 1) * LANES].astype(F32)
+            return unused
+
+        lax.fori_loop(0, ref.shape[0], step, 0)
+        start += ref.shape[0]
+
+    def clear(r, unused):
+        at = pl.multiple_of(r * height, 8)
+        for w in range(wide):
+            store[w, pl.ds(at, height), :] = jnp.zeros((height, LANES), F32)
+        return unused
+
+    lax.fori_loop(start, plan.half_lanes, clear, 0)
+
+
+def high_partial_kernel(plan, zonal, fwd, out, zin):
+    quad = pl.program_id(0)
+    block = lax.broadcasted_iota(jnp.int32, (1, LANES), 1) // (2 * REST)
+
+    @pl.when(quad == 0)
+    def _():
+        load_rows(plan, [zonal], zin, 2 * plan.pairs, 2)
+
+    rest = jnp.zeros((plan.span, LANES), F32)
+    for i in range(4):
+        pair = quad * 4 + i
+        z = jnp.concatenate(
+            [
+                jnp.concatenate(
+                    [
+                        zin[w, pl.ds(s * plan.pairs + pair, plan.half_lanes, stride=2 * plan.pairs), :]
+                        for s in range(2)
+                    ],
+                    axis=0,
+                )
+                for w in range(2)
+            ],
+            axis=1,
+        ).astype(BF)
+        coeffs = jnp.dot(fwd[i], z, preferred_element_type=F32)
+        out[0, i] = coeffs[:, :LANES].astype(BF)
+        rest = rest + jnp.where(block == i, coeffs[:, LANES:], 0.0)
+    out[0, 4] = rest.astype(BF)
+
+
+def high_synthesis_kernel(plan, coeffs, inv, mix, gain, out, yout):
+    quad = pl.program_id(0)
+    height = 4 * plan.pairs
+    for i in range(4):
+        pair = quad * 4 + i
+        both = jnp.concatenate([coeffs[0, i], coeffs[0, 4]], axis=1)
+        filtered = jnp.dot(both, mix[i], preferred_element_type=F32) * pair_gain(plan, pair, gain)
+        y = lax.dot_general(
+            inv[i], filtered.astype(BF), (((0,), (0,)), ((), ())), preferred_element_type=F32
+        )
+        for k in range(2):
+            for s in range(2):
+                yout[pl.ds((2 * k + s) * plan.pairs + pair, plan.half_lanes, stride=height), :] = y[
+                    s * plan.half_lanes : (s + 1) * plan.half_lanes, k * LANES : (k + 1) * LANES
+                ]
+
+    @pl.when(quad == plan.quads - 1)
+    def _():
+        def step(r, unused):
+            out[r] = yout[pl.ds(pl.multiple_of(r * height, 8), height), :].astype(BF)
+            return unused
+
+        lax.fori_loop(0, plan.rows, step, 0)
+
+
+def high_adjoint_kernel(plan, count, *refs):
+    grads, (inv, mix, gain, out, zin) = refs[:count], refs[count:]
+    quad = pl.program_id(0)
+    height = 4 * plan.pairs
+
+    @pl.when(quad == 0)
+    def _():
+        load_rows(plan, grads, zin, height, 1)
+
+    rest = jnp.zeros((plan.span, LANES), F32)
+    for i in range(4):
+        pair = quad * 4 + i
+        z = jnp.concatenate(
+            [
+                jnp.concatenate(
+                    [
+                        zin[0, pl.ds((2 * k + s) * plan.pairs + pair, plan.half_lanes, stride=height), :]
+                        for s in range(2)
+                    ],
+                    axis=0,
+                )
+                for k in range(2)
+            ],
+            axis=1,
+        ).astype(BF)
+        grad = jnp.dot(inv[i], z, preferred_element_type=F32) * pair_gain(plan, pair, gain)
+        back = jnp.dot(grad.astype(BF), mix[i], preferred_element_type=F32)
+        out[0, i] = back[:, :LANES].astype(BF)
+        rest = rest + back[:, LANES:]
+    out[0, 4] = rest.astype(BF)
+
+
+def high_zonal_kernel(plan, grads, fwd, out, yout):
+    quad = pl.program_id(0)
+    height = 2 * plan.pairs + 2 * plan.quad_pad
+    block = lax.broadcasted_iota(jnp.int32, (1, LANES), 1) // (2 * REST)
+
+    if plan.quad_pad > plan.quads:
+
+        @pl.when(quad == 0)
+        def _():
+            yout[...] = jnp.zeros_like(yout)
+
+    rest = jnp.zeros((LANES, LANES), F32)
+    for i in range(4):
+        pair = quad * 4 + i
+        both = jnp.concatenate([grads[0, i], grads[0, 4]], axis=1)
+        y = lax.dot_general(
+            fwd[i], both, (((0,), (0,)), ((), ())), preferred_element_type=F32
+        )
+        for s in range(2):
+            yout[pl.ds(s * plan.pairs + pair, plan.half_lanes, stride=height), :] = y[
+                s * plan.half_lanes : (s + 1) * plan.half_lanes, :LANES
+            ]
+        rest = rest + jnp.where(block == i, y[:, LANES:], 0.0)
+    for s in range(2):
+        row = 2 * plan.pairs + s * plan.quad_pad + quad
+        yout[pl.ds(row, plan.half_lanes, stride=height), :] = rest[
+            s * plan.half_lanes : (s + 1) * plan.half_lanes
+        ]
+
+    @pl.when(quad == plan.quads - 1)
+    def _():
+        def step(r, unused):
+            out[r] = yout[pl.ds(pl.multiple_of(r * height, 8), height), :].astype(BF)
+            return unused
+
+        lax.fori_loop(0, plan.rows, step, 0)
+
+
+def high_call(plan, kernel, name, whole_in, blocked, fixed, out_shape, out_whole, scratch):
+    def quad_spec(array):
+        size = array.shape[0] // plan.quads
+        rest = array.shape[1:]
+        return pl.BlockSpec((size,) + rest, lambda q: (q,) + (0,) * len(rest))
+
+    return pl.pallas_call(
+        kernel,
+        grid=(plan.quads,),
+        in_specs=[whole(a.shape) for a in whole_in]
+        + [quad_spec(a) for a in blocked]
+        + [whole(a.shape) for a in fixed],
+        out_specs=whole(out_shape) if out_whole else quad_spec(jax.ShapeDtypeStruct(out_shape, BF)),
+        out_shape=jax.ShapeDtypeStruct(out_shape, BF),
+        scratch_shapes=[pltpu.VMEM(scratch, F32)],
+        compiler_params=params(),
+        name=name,
+    )(*whole_in, *blocked, *fixed)
+
+
+def high_partial(plan, zonal, fwd):
+    return high_call(
+        plan, functools.partial(high_partial_kernel, plan), "high_partial", [zonal], [fwd], [],
+        (plan.quads, 5, plan.span, LANES), False, (2, plan.half_lanes * 2 * plan.pairs, LANES),
+    )
+
+
+def high_synthesis(plan, coeffs, inv, mix, gain):
+    return high_call(
+        plan, functools.partial(high_synthesis_kernel, plan), "high_synthesis", [], [coeffs, inv],
+        [mix, gain], (plan.rows, 4 * plan.pairs, LANES), True,
+        (plan.half_lanes * 4 * plan.pairs, LANES),
+    )
+
+
+def high_adjoint(plan, grads, inv, mix, gain):
+    return high_call(
+        plan, functools.partial(high_adjoint_kernel, plan, len(grads)), "high_adjoint", grads, [inv],
+        [mix, gain], (plan.quads, 5, plan.span, LANES), False,
+        (1, plan.half_lanes * 4 * plan.pairs, LANES),
+    )
+
+
+def high_zonal(plan, grads, fwd):
+    height = 2 * plan.pairs + 2 * plan.quad_pad
+    return high_call(
+        plan, functools.partial(high_zonal_kernel, plan), "high_zonal", [], [grads, fwd], [],
+        (plan.rows, height, LANES), True, (plan.half_lanes * height, LANES),
+    )
+
+
 def predict_kernel(plan, first, live_ref, x_ref, idft_ref, enc_ref, dec_ref, *refs):
-    recvs = refs[: plan.groups]
-    pred_ref, slope_ref, left, field = refs[plan.groups :]
+    recv, high, pred_ref, slope_ref, left, field = refs
     c = plan.channels
+    wide = plan.n * plan.rows2
     for r in range(plan.rb):
-        for g, recv in enumerate(recvs):
-            piece = recv[:, r].reshape(plan.n * plan.rows2, LANES)
-            wide = plan.n * plan.rows2
-            left[r * c : (r + 1) * c, g * wide : (g + 1) * wide] = piece.T
+        left[r * c : (r + 1) * c, :wide] = recv[:, r].reshape(wide, LANES).T
+        left[r * c : (r + 1) * c, wide:] = high[r].T
     field[...] = jnp.dot(left[...], idft_ref[...], preferred_element_type=F32)
     base = first + pl.program_id(0) * plan.rb
 
@@ -378,12 +616,11 @@
     lax.fori_loop(0, plan.rb, step, 0)
 
 
-def predict(plan, chunk, live, x, idft, enc_t, dec_t, recvs):
+def predict(plan, chunk, live, x, idft, enc_t, dec_t, recv, high):
     first, count = chunk
     skip = first // plan.rb
     shape = (count, plan.fpad, plan.lon)
     slope_shape = (count, plan.channels, plan.lon)
-    recv_spec = pl.BlockSpec((plan.n, plan.rb, plan.rows2, LANES), lambda i: (0, i, 0, 0))
     return pl.pallas_call(
         functools.partial(predict_kernel, plan, first),
         grid=(count // plan.rb,),
@@ -393,8 +630,9 @@
             whole(idft.shape),
             whole(enc_t.shape),
             whole(dec_t.shape),
-        ]
-        + [recv_spec] * plan.groups,
+            pl.BlockSpec((plan.n, plan.rb, plan.rows2, LANES), lambda i: (0, i, 0, 0)),
+            pl.BlockSpec((plan.rb,) + high.shape[1:], lambda i: (i + skip, 0, 0)),
+        ],
         out_specs=[
             pl.BlockSpec((plan.rb,) + shape[1:], lambda i: (i, 0, 0)),
             pl.BlockSpec((plan.rb,) + slope_shape[1:], lambda i: (i, 0, 0)),
@@ -406,11 +644,11 @@
         ],
         compiler_params=params(),
         name="predict",
-    )(live, x, idft, enc_t, dec_t, *recvs)
+    )(live, x, idft, enc_t, dec_t, recv, high)
 
 
 def score_kernel(plan, first, members, area_ref, own_ref, all_ref, obs_ref, slope_ref, idft_ref, dec_ref, *refs):
-    grad_ref, outs, right = refs[0], refs[1 : 1 + plan.groups], refs[1 + plan.groups]
+    grad_ref, out, out_high, right = refs
     c = plan.channels
     base = first + pl.program_id(0) * plan.rb
 
@@ -433,16 +671,20 @@
 
     lax.fori_loop(0, plan.rb, step, 0)
     wide = plan.n * plan.rows2
-    for g, out in enumerate(outs):
-        modes = lax.dot_general(
-            idft_ref[g * wide : (g + 1) * wide, :],
+
+    def modes(first, last):
+        return lax.dot_general(
+            idft_ref[first:last, :],
             right[...],
             (((1,), (1,)), ((), ())),
             preferred_element_type=F32,
         ).astype(BF)
-        for r in range(plan.rb):
-            for o in range(plan.n):
-                out[o, r] = modes[o * plan.rows2 : (o + 1) * plan.rows2, r * c : (r + 1) * c]
+
+    low, high = modes(0, wide), modes(wide, idft_ref.shape[0])
+    for r in range(plan.rb):
+        for o in range(plan.n):
+            out[o, r] = low[o * plan.rows2 : (o + 1) * plan.rows2, r * c : (r + 1) * c]
+        out_high[r] = high[:, r * c : (r + 1) * c]
 
 
 def score(plan, chunk, area, own, everyone, observed, slope, idft, dec):
@@ -451,6 +693,7 @@
     members = everyone.shape[0]
     cell = (plan.rb, plan.fpad, plan.lon)
     out_shape = (plan.n, count, plan.rows2, LANES)
+    high = 4 * plan.pairs
     here = pl.BlockSpec(cell, lambda i: (i, 0, 0))
     return pl.pallas_call(
         functools.partial(score_kernel, plan, first, members),
@@ -464,39 +707,50 @@
             whole(idft.shape),
             whole(dec.shape),
         ],
-        out_specs=[here]
-        + [pl.BlockSpec((plan.n, plan.rb, plan.rows2, LANES), lambda i: (0, i, 0, 0))] * plan.groups,
-        out_shape=[jax.ShapeDtypeStruct((count,) + cell[1:], BF)]
-        + [jax.ShapeDtypeStruct(out_shape, BF)] * plan.groups,
+        out_specs=[
+            here,
+            pl.BlockSpec((plan.n, plan.rb, plan.rows2, LANES), lambda i: (0, i, 0, 0)),
+            pl.BlockSpec((plan.rb, high, LANES), lambda i: (i, 0, 0)),
+        ],
+        out_shape=[
+            jax.ShapeDtypeStruct((count,) + cell[1:], BF),
+            jax.ShapeDtypeStruct(out_shape, BF),
+            jax.ShapeDtypeStruct((count, high, LANES), BF),
+        ],
         scratch_shapes=[pltpu.VMEM((plan.rb * plan.channels, plan.lon), BF)],
         compiler_params=params(),
         name="score",
     )(area, own, everyone, observed, slope, idft, dec)
 
 
-def finish_kernel(plan, live_ref, grad_ref, main_ref, rest_ref, through_ref, *refs):
-    recvs, out_ref, left, small, field, field_small = refs[: plan.groups], *refs[plan.groups :]
+def finish_kernel(
+    plan, live_ref, grad_ref, main_ref, rest_ref, through_ref, recv, high_ref, out_ref, left, small, field, field_small
+):
     n, tp, tb = plan.n, plan.tp, plan.tb
-    wide = n * tp
+    wide, tall, quads = n * tp, 2 * plan.pairs, 2 * plan.quad_pad
     for r in range(plan.rb):
-        for g, recv in enumerate(recvs):
-            piece = recv[:, r].astype(F32)
-            main = piece[:, :tp].reshape(wide, LANES).T
+        piece = recv[:, r].astype(F32)
+        high = high_ref[r].astype(F32)
+        mains = [(0, piece[:, :tp].reshape(wide, LANES).T), (2 * wide, high[:tall].T)]
+        for first, main in mains:
+            size = main.shape[1]
             for k in range(2):
-                at = (g * 2 + k) * wide
-                left[r * SPLIT : (r + 1) * SPLIT, at : at + wide] = main[
+                at = first + k * size
+                left[r * SPLIT : (r + 1) * SPLIT, at : at + size] = main[
                     k * SPLIT : (k + 1) * SPLIT
                 ].astype(BF)
-            for group in range(plan.rest_groups):
-                first = tp + 8 * group
-                rest = piece[:, first : first + 8].reshape(n * 8, LANES).T.astype(BF)
-                for i in range(min(4, tb - 4 * group)):
-                    for k in range(2):
-                        at = ((g * tb + group * 4 + i) * 2 + k) * n * 8
-                        part = 2 * i + k
-                        small[r * REST : (r + 1) * REST, at : at + n * 8] = rest[
-                            part * REST : (part + 1) * REST
-                        ]
+        at = 0
+        rests = [
+            (piece[:, tp + 8 * group : tp + 8 * (group + 1)].reshape(n * 8, LANES), min(4, tb - 4 * group))
+            for group in range(plan.rest_groups)
+        ] + [(high[tall:], 4)]
+        for rest, blocks in rests:
+            turned = rest.T.astype(BF)
+            for part in range(2 * blocks):
+                small[r * REST : (r + 1) * REST, at : at + turned.shape[1]] = turned[
+                    part * REST : (part + 1) * REST
+                ]
+                at += turned.shape[1]
     field[...] = jnp.dot(left[...], main_ref[...], preferred_element_type=F32)
     field_small[...] = jnp.dot(small[...], rest_ref[...], preferred_element_type=F32)
     base = pl.program_id(0) * plan.rb
@@ -518,10 +772,9 @@
     lax.fori_loop(0, plan.rb, step, 0)
 
 
-def finish(plan, live, grad, main, rest, through, recvs):
+def finish(plan, live, grad, main, rest, through, recv, high):
     cell = (plan.rb, plan.fpad, plan.lon)
     here = pl.BlockSpec(cell, lambda i: (i, 0, 0))
-    recv_spec = pl.BlockSpec((plan.n, plan.rb, plan.rows1, LANES), lambda i: (0, i, 0, 0))
     return pl.pallas_call(
         functools.partial(finish_kernel, plan),
         grid=(plan.rows // plan.rb,),
@@ -531,8 +784,9 @@
             whole(main.shape),
             whole(rest.shape),
             whole(through.shape),
-        ]
-        + [recv_spec] * plan.groups,
+            pl.BlockSpec((plan.n, plan.rb, plan.rows1, LANES), lambda i: (0, i, 0, 0)),
+            pl.BlockSpec((plan.rb,) + high.shape[1:], lambda i: (i, 0, 0)),
+        ],
         out_specs=here,
         out_shape=jax.ShapeDtypeStruct((plan.rows, plan.fpad, plan.lon), BF),
         scratch_shapes=[
@@ -543,7 +797,7 @@
         ],
         compiler_params=params(),
         name="finish",
-    )(live, grad, main, rest, through, *recvs)
+    )(live, grad, main, rest, through, recv, high)
 
 
 def row_geometry(band_rows, band_len, lat_count):
@@ -573,14 +827,14 @@
     c = plan.channels
     head, tail = weight[:SPLIT], jnp.pad(weight[SPLIT:], ((0, plan.fpad - plan.fields), (0, 0)))
     blocks = []
-    for b in range(min(plan.tb, 4)):
+    for b in range(4):
         out = jnp.zeros((2 * LANES, 2 * c), F32)
         for k in range(2):
             out = out.at[k * SPLIT : (k + 1) * SPLIT, k * c : (k + 1) * c].set(head)
             first = LANES + (2 * b + k) * REST
             out = out.at[first : first + REST, k * c : (k + 1) * c].set(tail)
         blocks.append(out)
-    return jnp.stack([blocks[b % 4] for b in range(plan.tb)]).astype(BF)
+    return jnp.stack(blocks).astype(BF)
 
 
 def on_device(
@@ -614,62 +868,91 @@
         jnp.dot(enc_f, decoder_weight.astype(F32), precision=exact), ((0, pad), (0, pad))
     ).astype(BF)
 
-    forward = [dft_rows(plan, g, False) for g in range(plan.groups)]
-    inverse = [dft_rows(plan, g, True) for g in range(plan.groups)]
     n, tp, tb = plan.n, plan.tp, plan.tb
-    dft = jnp.asarray(np.stack([f.reshape(2, n * tp, lon) for f in forward]))
+    low, high = plan.low_orders(), plan.high_orders()
+    low_f, high_f = dft_rows(plan, low, False), dft_rows(plan, high, False)
+    low_i, high_i = dft_rows(plan, low, True), dft_rows(plan, high, True)
+    dft_low = jnp.asarray(low_f.reshape(2, n * tp, lon))
+    dft_high = jnp.asarray(high_f.reshape(2, 2 * plan.pairs, lon))
     idft = jnp.asarray(
-        np.concatenate([f.transpose(1, 0, 2, 3).reshape(n * 2 * tp, lon) for f in inverse])
-    )
-    dft_main = jnp.asarray(np.concatenate([f.reshape(2 * n * tp, lon) for f in forward]))
+        np.concatenate(
+            [
+                low_i.transpose(1, 0, 2, 3).reshape(n * 2 * tp, lon),
+                high_i.reshape(4 * plan.pairs, lon),
+            ]
+        )
+    )
+    dft_main = jnp.asarray(
+        np.concatenate([low_f.reshape(2 * n * tp, lon), high_f.reshape(4 * plan.pairs, lon)])
+    )
+    low_rest = low_f.reshape(2, n, tb, 8, lon).transpose(2, 0, 1, 3, 4)
+    quads = np.zeros((2, 2, plan.quad_pad, 4, lon), low_f.dtype)
+    quads[:, :, : plan.quads] = high_f.reshape(2, 2, plan.quads, 4, lon)
     dft_rest = jnp.asarray(
         np.concatenate(
-            [
-                f.reshape(2, n, tb, 8, lon).transpose(2, 0, 1, 3, 4).reshape(tb * 2 * n * 8, lon)
-                for f in forward
-            ]
+            [low_rest.reshape(-1, lon), quads.transpose(3, 0, 1, 2, 4).reshape(-1, lon)]
         )
     )
-
-    sent = analyse(plan, rows, dft)
 
     def exchange(block):
         return lax.all_to_all(block, "space", split_axis=0, concat_axis=0, tiled=True)
 
-    tables = []
-    for g in range(plan.groups):
-        order_table = plan.orders(g)
-        orders = lax.dynamic_index_in_dim(jnp.asarray(order_table, jnp.int32), me, keepdims=False)
-        diagonal = lax.dynamic_index_in_dim(
-            jnp.asarray(log_diagonal(order_table)), me, keepdims=False
-        )
-        start = diagonal[:, None] + orders.astype(F32)[:, None] * log_sines[None, :]
-        tables.append(legendre_tables(plan, orders, start, cosines, quad, live))
-
-    synth = []
-    for g in range(plan.groups):
-        spectrum = spectrum_forward(plan, exchange(sent[g]), *tables[g], mix, gain)
-        synth.append([exchange(part) for part in spectrum])
-
-    predictions, grads, returned = [], [], []
+    sent, zonal_high = analyse(plan, rows, dft_low, dft_high)
+    recv = exchange(sent)
+
+    half = plan.half_lanes
+
+    def side(value):
+        value = jnp.pad(value, (0, half - band))
+        return jnp.concatenate([value, value])
+
+    def sides(pair_values):
+        return jnp.asarray(np.repeat(pair_values.T, half, axis=1))
+
+    own = [
+        side(lax.dynamic_slice_in_dim(v, me * band, band)) for v in (cosines, quad, live, log_sines)
+    ]
+    shift = np.stack([plan.low + np.arange(plan.pairs), np.full(plan.pairs, plan.low - 1)])
+    start = sides(log_diagonal(high)) + sides(high.astype(np.float32)) * own[3][None, :]
+    high_fwd, high_inv = legendre_tables(
+        sides(high), sides(shift), start, own[0], own[1], own[2], plan.span
+    )
+    high_coeffs = lax.psum(high_partial(plan, zonal_high, high_fwd), "space")
+
+    orders = lax.dynamic_index_in_dim(jnp.asarray(low, jnp.int32), me, keepdims=False)
+    diagonal = lax.dynamic_index_in_dim(jnp.asarray(log_diagonal(low)), me, keepdims=False)
+    orders_wide = jnp.broadcast_to(orders[:, None], (tp, LANES))
+    start = diagonal[:, None] + orders.astype(F32)[:, None] * log_sines[None, :]
+    low_fwd, low_inv = legendre_tables(
+        orders_wide, jnp.zeros_like(orders_wide), start, cosines, quad, live, plan.degrees
+    )
+
+    spectrum = spectrum_forward(plan, recv, low_fwd, low_inv, mix, gain)
+    synth = [exchange(part) for part in spectrum]
+    reach = ceil_to(plan.low + plan.pairs + plan.span, 8)
+    longer = jnp.pad(degree_gain, ((0, reach + 8 - degree_gain.shape[0]), (0, 0)))
+    gain_long = jnp.stack([longer[s : s + reach] for s in range(8)])
+    synth_high = high_synthesis(plan, high_coeffs, high_inv, mix, gain_long)
+
+    predictions, grads, returned, returned_high = [], [], [], []
     for i, chunk in enumerate(plan.chunks):
         pred, slope = predict(
-            plan, chunk, live_own, rows, idft, enc_t, dec_t, [synth[g][i] for g in range(plan.groups)]
+            plan, chunk, live_own, rows, idft, enc_t, dec_t, synth[i], synth_high
         )
         everyone = lax.all_gather(pred[None], "member", axis=0, tiled=True)
-        out = score(plan, chunk, area, pred, everyone, truth, slope, idft, dec)
+        grad, out, out_high = score(plan, chunk, area, pred, everyone, truth, slope, idft, dec)
         predictions.append(pred)
-        grads.append(out[0])
-        returned.append([exchange(part) for part in out[1:]])
-
-    last = []
-    for g in range(plan.groups):
-        part = spectrum_backward(
-            plan, [returned[i][g] for i in range(len(plan.chunks))], *tables[g], mix_back, gain
-        )
-        last.append(exchange(part))
+        grads.append(grad)
+        returned.append(exchange(out))
+        returned_high.append(out_high)
+
+    high_grads = lax.psum(
+        high_adjoint(plan, returned_high, high_inv, mix_back, gain_long), "space"
+    )
+    last = exchange(spectrum_backward(plan, returned, low_fwd, low_inv, mix_back, gain))
+    zonal_grad = high_zonal(plan, high_grads, high_fwd)
     state_grad = finish(
-        plan, live_own, jnp.concatenate(grads), dft_main, dft_rest, through, last
+        plan, live_own, jnp.concatenate(grads), dft_main, dft_rest, through, last, zonal_grad
     )
 
     def outward(block):

time: 1010 us -> 970 us (0.960)
  blocking collectives: 378 us -> 139 us
  waiting for transfers between devices: 155 us -> 319 us
  Pallas kernels: 363 us -> 390 us
  local copies, waits for them, and re-layouts: 46.1 us -> 60.2 us
  starting transfers between devices: 36 us -> 25.5 us
    psum x0 -> x2, waiting for transfers between devices: none -> 288 us  [the longest x1 203 us: on_device(): lax.psum(high_adjoint(plan, returned_high, high_inv, mix_back, gain_long)...]
    all_to_all x8 -> x3, blocking collectives: 378 us -> 139 us  [exchange(): lax.all_to_all(block, 'space', split_axis=0, concat_axis=0, tiled=True)]
    all_to_all x8 -> x5, waiting for transfers between devices: 155 us -> 24.6 us  [exchange(): lax.all_to_all(block, 'space', split_axis=0, concat_axis=0, tiled=True)]
    pallas_call x2 -> x6, Pallas kernels: 71 us -> 173 us  [the longest x4 87.4 us: high_call(): pl.pallas_call(kernel, grid=(plan.quads,), in_specs=[whole(a.shape) for a...]
    pallas_call x2 -> x1, Pallas kernels: 82.6 us -> 41.5 us  [spectrum_backward(): pl.pallas_call(functools.partial(spectrum_backward_kernel, plan, len(recv...]
    pallas_call x2 -> x1, Pallas kernels: 68.8 us -> 34.6 us  [spectrum_forward(): pl.pallas_call(functools.partial(spectrum_forward_kernel, plan), grid=(pl...]
    all_to_all x8 -> x5, starting transfers between devices: 35.7 us -> 25 us  [exchange(): lax.all_to_all(block, 'space', split_axis=0, concat_axis=0, tiled=True)]
  transfers between devices with their start and end apart: 11 -> 10, of which waited for: 6 -> 5; matrix products, arithmetic and copies ran while one was open for 5% -> 6% of each run, Pallas kernels for 30% -> 30%
where the time goes in v2:
time: 970 us; the launch traced here: 965 us
  Pallas kernels  390 us (40%)
  waiting for transfers between devices  319 us (33%)
  blocking collectives  139 us (14%)
  local copies, waits for them, and re-layouts  60.2 us (6%)
  starting transfers between devices  25.5 us (3%)
  other arithmetic  16.7 us (2%)
  between operations  14.1 us (1%)
    psum x1, waiting for transfers between devices, on_device(): lax.psum(high_adjoint(plan, returned_high, high_inv, mix_back, gain_long)...  203 us
    all_to_all x3, blocking collectives, exchange(): lax.all_to_all(block, 'space', split_axis=0, concat_axis=0, tiled=True)  139 us
    pallas_call x4, Pallas kernels, high_call(): pl.pallas_call(kernel, grid=(plan.quads,), in_specs=[whole(a.shape) for a...  87.4 us
    pallas_call x2, Pallas kernels, legendre_tables(): pl.pallas_call(table_kernel, grid=(tp // 8, degrees // 16), in_specs=[lan...  85.6 us
    psum x1, waiting for transfers between devices, on_device(): high_coeffs = lax.psum(high_partial(plan, zonal_high, high_fwd), 'space')  84.3 us
    pallas_call x3, Pallas kernels, score(): pl.pallas_call(functools.partial(score_kernel, plan, first, members), gri...  48.6 us
    pallas_call x3, Pallas kernels, predict(): pl.pallas_call(functools.partial(predict_kernel, plan, first), grid=(coun...  41.6 us
    pallas_call x1, Pallas kernels, spectrum_backward(): pl.pallas_call(functools.partial(spectrum_backward_kernel, plan, len(recv...  41.5 us
  transfers between devices with their start and end apart: 10, of which 5 were waited for; matrix products, arithmetic and copies ran while one was open for 6% of the time, Pallas kernels for 30%

profile of v2, /device:TPU:0, one launch (start us, length us, event | category | flops | bytes accessed | tf_op | source)
XLA Modules:
  0.0 964.9 jit_solution(11190388652263079997)
XLA Ops:
  7.2 5.9 pad.118.x_ref
  13.1 28.6 %analyse.1 = (bf16[8,49,32,128]{3,2,1,0:T(8,128)(2,1)}, bf16[49,176,256]{2,1,0:T(8,128)(2,1)}) custom-call(bf16[49,80,720]{2,1,0:T(8,128)(2,1)} %pad.118.x_ref, bf16[2,192,720]{2,1,0:T(8,128)(2,1)} %constant.455.clone.low_ref, bf16[2,176,720]{2,1,0:T(8,128)(2,1)} %constant.456.clone.high_ref), custom_call_target="tpu_custom_call" | custom-call | tf_op jit(solution)/shard_map/analyse/pallas_call | solution.py:227
  41.7 7.4 all-to-all-start
  49.7 0.7 multiply_multiply_fusion
  51.1 0.7 maximum_bitcast_fusion
  51.8 0.6 multiply_add_fusion.1.start_ref
  52.4 50.3 %legendre_tables.3 = (bf16[88,176,128]{2,1,0:T(8,128)(2,1)}, bf16[88,176,128]{2,1,0:T(8,128)(2,1)}) custom-call(f32[88,128]{1,0:T(8,128)} %constant.461.clone.m_ref, f32[88,128]{1,0:T(8,128)} %constant.503.shift_ref, f32[88,128]{1,0:T(8,128)} %multiply_add_fusion.1.start_ref, f32[1,128]{1,0:T(1,128)} %get-tuple-element.245.cos_ref, ...), custom_call_target="tpu_custom_call" | custom-call | tf_op jit(solution)/shard_map/legendre_tables/pallas_call | solution.py:155
  102.7 18.6 %high_partial.1 = bf16[22,5,176,128]{3,2,1,0:T(8,128)(2,1)} custom-call(bf16[49,176,256]{2,1,0:T(8,128)(2,1)} %get-tuple-element.210.zonal, bf16[88,176,128]{2,1,0:T(8,128)(2,1)} %get-tuple-element.211.fwd), custom_call_target="tpu_custom_call" | custom-call | tf_op jit(solution)/shard_map/high_partial/pallas_call | solution.py:548
  121.4 0.7 copy-done.15
  122.4 0.7 copy.48
  123.1 0.6 copy.45
  123.7 0.7 copy.42
  126.2 2.3 scatter.45
  128.4 2.5 scatter.50
  130.9 1.9 scatter.46
  132.8 1.9 scatter.51
  134.7 2.5 scatter.55
  137.2 1.9 scatter.56
  139.1 2.5 scatter.60
  141.6 1.9 scatter.61
  143.5 1.9 scatter.49
  145.4 1.9 scatter.54
  147.3 1.9 scatter.59
  149.2 1.9 scatter.64
  151.1 2.2 fusion.23
  153.3 2.0 copy.35.mix
  155.3 0.7 convert_bitcast_fusion
  156.0 0.7 dynamic-slice_bitcast_fusion
  157.4 0.7 broadcast_in_dim.47.m_ref
  158.7 35.3 %legendre_tables.2 = (bf16[24,368,392]{2,1,0:T(8,128)(2,1)}, bf16[24,368,392]{2,1,0:T(8,128)(2,1)}) custom-call(f32[24,128]{1,0:T(8,128)} %broadcast_in_dim.47.m_ref, f32[24,128]{1,0:T(8,128)} %convert_element_type.63.shift_ref, f32[24,512]{1,0:T(8,128)} %pad.121.start_ref, f32[1,512]{1,0:T(1,128)} %bitcast.85, f32[1,512]{1,0:T(1,128)} %bitcast.86, ...), custom_call_target="tpu_custom_call" | custom-call | tf_op jit(solution)/shard_map/legendre_tables/pallas_call | solution.py:155
  194.0 0.7 constant_dynamic-update-slice_fusion.1
  194.7 0.7 constant_dynamic-update-slice_fusion.gain.refs_6_
  195.4 1.7 copy-done.4
  197.1 34.6 %spectrum_forward.1 = (bf16[8,14,48,128]{3,2,1,0:T(8,128)(2,1)}, bf16[8,14,48,128]{3,2,1,0:T(8,128)(2,1)}, bf16[8,21,48,128]{3,2,1,0:T(8,128)(2,1)}) custom-call(bf16[8,49,32,128]{3,2,1,0:T(8,128)(2,1)} %copy-done.4, bf16[24,368,392]{2,1,0:T(8,128)(2,1)} %get-tuple-element.207.fwd.refs_3_, bf16[24,368,392]{2,1,0:T(8,128)(2,1)} %get-tuple-element.208.inv.refs_4_, ...), custom_call_target="tpu_custom_call" | custom-call | tf_op jit(solution)/shard_map/spectrum_forward/pallas_call | solution.py:351
  231.7 6.0 all-to-all-start.1
  239.3 84.3 %all-reduce.20.cloned.1.call-done.coeffs = bf16[22,5,176,128]{3,2,1,0:T(8,128)(2,1)} async-done(((bf16[22,5,176,128]{3,2,1,0:T(8,128)(2,1)}), bf16[22,5,176,128]{3,2,1,0:T(8,128)(2,1)}) %all-reduce.20.cloned.1.call-update) | async-done | bytes 4956176 | tf_op jit(solution)/shard_map/psum | solution.py:920
  323.7 26.7 %high_synthesis.1.refs_1_ = bf16[49,352,128]{2,1,0:T(8,128)(2,1)} custom-call(bf16[22,5,176,128]{3,2,1,0:T(8,128)(2,1)} %all-reduce.20.cloned.1.call-done.coeffs, bf16[88,176,128]{2,1,0:T(8,128)(2,1)} %get-tuple-element.212.inv.refs_3_, bf16[4,256,256]{2,1,0:T(8,128)(2,1)} %copy.35.mix, f32[8,456,128]{2,1,0:T(8,128)} %copy-done.5), custom_call_target="tpu_custom_call" | custom-call | tf_op jit(solution)/shard_map/high_synthesis/pallas_call | solution.py:548
  350.4 12.3 %predict.3 = (bf16[14,80,720]{2,1,0:T(8,128)(2,1)}, bf16[14,128,720]{2,1,0:T(8,128)(2,1)}) custom-call(f32[49]{0:T(128)} %copy-done.18, bf16[49,80,720]{2,1,0:T(8,128)(2,1)} %pad.118.x_ref, bf16[736,720]{1,0:T(8,128)(2,1)} %constant.457.clone.idft_ref, bf16[128,80]{1,0:T(8,128)(2,1)} %pad.119.enc_ref, bf16[80,128]{1,0:T(8,128)(2,1)} %pad.120.dec_ref, ...), custom_call_target="tpu_custom_call" | custom-call | tf_op jit(solution)/shard_map/predict/pallas_call | solution.py:624
  362.7 1.3 copy-done.13
  364.0 37.0 %all_to_all.40.refs_0_ = bf16[8,14,48,128]{3,2,1,0:T(8,128)(2,1)} all-to-all(bf16[8,14,48,128]{3,2,1,0:T(8,128)(2,1)S(1)} %copy-done.13), channel_id=1, replica_groups=mesh['member'=4,'space'=8] {'space'}, dimensions={0} | all-to-all | bytes 2752512 | tf_op jit(solution)/shard_map/all_to_all | solution.py:898
  401.0 12.5 %predict.4 = (bf16[14,80,720]{2,1,0:T(8,128)(2,1)}, bf16[14,128,720]{2,1,0:T(8,128)(2,1)}) custom-call(f32[49]{0:T(128)} %copy-done.18, bf16[49,80,720]{2,1,0:T(8,128)(2,1)} %pad.118.x_ref, bf16[736,720]{1,0:T(8,128)(2,1)} %constant.457.clone.idft_ref, bf16[128,80]{1,0:T(8,128)(2,1)} %pad.119.enc_ref, bf16[80,128]{1,0:T(8,128)(2,1)} %pad.120.dec_ref, ...), custom_call_target="tpu_custom_call" | custom-call | tf_op jit(solution)/shard_map/predict/pallas_call | solution.py:624
  413.5 50.3 %all_to_all.41.refs_0_ = bf16[8,21,48,128]{3,2,1,0:T(8,128)(2,1)} all-to-all(bf16[8,21,48,128]{3,2,1,0:T(8,128)(2,1)S(1)} %copy-done.10), channel_id=1, replica_groups=mesh['member'=4,'space'=8] {'space'}, dimensions={0} | all-to-all | bytes 4128768 | tf_op jit(solution)/shard_map/all_to_all | solution.py:898
  463.9 16.8 %predict.5 = (bf16[21,80,720]{2,1,0:T(8,128)(2,1)}, bf16[21,128,720]{2,1,0:T(8,128)(2,1)}) custom-call(f32[49]{0:T(128)} %copy-done.18, bf16[49,80,720]{2,1,0:T(8,128)(2,1)} %pad.118.x_ref, bf16[736,720]{1,0:T(8,128)(2,1)} %constant.457.clone.idft_ref, bf16[128,80]{1,0:T(8,128)(2,1)} %pad.119.enc_ref, bf16[80,128]{1,0:T(8,128)(2,1)} %pad.120.dec_ref, ...), custom_call_target="tpu_custom_call" | custom-call | tf_op jit(solution)/shard_map/predict/pallas_call | solution.py:624
  480.8 6.0 pad.131.obs_ref
  487.5 15.3 %score.3 = (bf16[14,80,720]{2,1,0:T(8,128)(2,1)}, bf16[8,14,48,128]{3,2,1,0:T(8,128)(2,1)}, bf16[14,352,128]{2,1,0:T(8,128)(2,1)}) custom-call(f32[49]{0:T(128)} %get-tuple-element.232.area_ref, bf16[14,80,720]{2,1,0:T(8,128)(2,1)} %get-tuple-element.213.own_ref, bf16[4,14,80,720]{3,2,1,0:T(8,128)(2,1)} %bitcast.78, bf16[49,80,720]{2,1,0:T(8,128)(2,1)} %pad.131.obs_ref, ...), custom_call_target="tpu_custom_call" | custom-call | tf_op jit(solution)/shard_map/score/pallas_call | solution.py:698
  502.8 3.6 all-to-all-start.4
  506.4 14.2 %score.4 = (bf16[14,80,720]{2,1,0:T(8,128)(2,1)}, bf16[8,14,48,128]{3,2,1,0:T(8,128)(2,1)}, bf16[14,352,128]{2,1,0:T(8,128)(2,1)}) custom-call(f32[49]{0:T(128)} %get-tuple-element.232.area_ref, bf16[14,80,720]{2,1,0:T(8,128)(2,1)} %get-tuple-element.215.own_ref, bf16[4,14,80,720]{3,2,1,0:T(8,128)(2,1)} %bitcast.79, bf16[49,80,720]{2,1,0:T(8,128)(2,1)} %pad.131.obs_ref, ...), custom_call_target="tpu_custom_call" | custom-call | tf_op jit(solution)/shard_map/score/pallas_call | solution.py:698
  520.7 17.9 %all-to-all-done.4.refs_0_ = bf16[8,14,48,128]{3,2,1,0:T(8,128)(2,1)S(1)} async-done(((bf16[8,14,48,128]{3,2,1,0:T(8,128)(2,1)}), bf16[8,14,48,128]{3,2,1,0:T(8,128)(2,1)S(1)}, u32[]{:S(2)}, u32[]{:S(2)}) %all-to-all-start.4) | async-done | bytes 1376288 | tf_op jit(solution)/shard_map/all_to_all | solution.py:898
  538.5 3.6 all-to-all-start.5
  542.1 7.0 all-gather.11.cloned.1.call-done
  549.1 19.1 %score.5 = (bf16[21,80,720]{2,1,0:T(8,128)(2,1)}, bf16[8,21,48,128]{3,2,1,0:T(8,128)(2,1)}, bf16[21,352,128]{2,1,0:T(8,128)(2,1)}) custom-call(f32[49]{0:T(128)} %get-tuple-element.232.area_ref, bf16[21,80,720]{2,1,0:T(8,128)(2,1)} %get-tuple-element.217.own_ref, bf16[4,21,80,720]{3,2,1,0:T(8,128)(2,1)} %bitcast.77, bf16[49,80,720]{2,1,0:T(8,128)(2,1)} %pad.131.obs_ref, ...), custom_call_target="tpu_custom_call" | custom-call | tf_op jit(solution)/shard_map/score/pallas_call | solution.py:698
  568.2 6.7 all-to-all-done.5.refs_1_
  574.9 51.5 %all_to_all.42.refs_2_ = bf16[8,21,48,128]{3,2,1,0:T(8,128)(2,1)} all-to-all(bf16[8,21,48,128]{3,2,1,0:T(8,128)(2,1)} %get-tuple-element.226), channel_id=1, replica_groups=mesh['member'=4,'space'=8] {'space'}, dimensions={0} | all-to-all | bytes 4128768 | tf_op jit(solution)/shard_map/all_to_all | solution.py:898
  626.4 41.5 %spectrum_backward.1 = bf16[8,49,32,128]{3,2,1,0:T(8,128)(2,1)} custom-call(bf16[8,14,48,128]{3,2,1,0:T(8,128)(2,1)} %copy-done.6, bf16[8,14,48,128]{3,2,1,0:T(8,128)(2,1)} %copy-done.7, bf16[8,21,48,128]{3,2,1,0:T(8,128)(2,1)} %all_to_all.42.refs_2_, bf16[24,368,392]{2,1,0:T(8,128)(2,1)} %get-tuple-element.207.fwd.refs_3_, ...), custom_call_target="tpu_custom_call" | custom-call | tf_op jit(solution)/shard_map/spectrum_backward/pallas_call | solution.py:368
  667.9 4.5 all-to-all-start.7
  672.7 22.4 %high_adjoint.1 = bf16[22,5,176,128]{3,2,1,0:T(8,128)(2,1)} custom-call(bf16[14,352,128]{2,1,0:T(8,128)(2,1)} %get-tuple-element.227.refs_0_, bf16[14,352,128]{2,1,0:T(8,128)(2,1)} %get-tuple-element.228.refs_1_, bf16[21,352,128]{2,1,0:T(8,128)(2,1)} %get-tuple-element.229.refs_2_, bf16[88,176,128]{2,1,0:T(8,128)(2,1)} %get-tuple-element.212.inv.refs_3_, ...), custom_call_target="tpu_custom_call" | custom-call | tf_op jit(solution)/shard_map/high_adjoint/pallas_call | solution.py:548
  695.2 0.6 pad.133.through_ref
  695.8 0.9 copy-done.2
  696.8 7.3 fusion
  704.1 3.5 pad_maximum_fusion.2.grad_ref
  707.6 203.4 %all-reduce.22.cloned.1.call-done.grads = bf16[22,5,176,128]{3,2,1,0:T(8,128)(2,1)} async-done(((bf16[22,5,176,128]{3,2,1,0:T(8,128)(2,1)}), bf16[22,5,176,128]{3,2,1,0:T(8,128)(2,1)}) %all-reduce.22.cloned.1.call-update) | async-done | bytes 4956176 | tf_op jit(solution)/shard_map/psum | solution.py:949
  910.9 19.6 %high_zonal.1.high_ref = bf16[49,224,128]{2,1,0:T(8,128)(2,1)} custom-call(bf16[22,5,176,128]{3,2,1,0:T(8,128)(2,1)} %all-reduce.22.cloned.1.call-done.grads, bf16[88,176,128]{2,1,0:T(8,128)(2,1)} %get-tuple-element.211.fwd), custom_call_target="tpu_custom_call" | custom-call | tf_op jit(solution)/shard_map/high_zonal/pallas_call | solution.py:548
  930.6 22.1 %finish.1 = bf16[49,80,720]{2,1,0:T(8,128)(2,1)} custom-call(f32[49]{0:T(128)} %copy-done.18, bf16[49,80,720]{2,1,0:T(8,128)(2,1)} %pad_maximum_fusion.2.grad_ref, bf16[736,720]{1,0:T(8,128)(2,1)} %constant.458.clone.main_ref, bf16[768,720]{1,0:T(8,128)(2,1)} %constant.459.clone.rest_ref, bf16[80,80]{1,0:T(8,128)(2,1)} %pad.133.through_ref, ...), custom_call_target="tpu_custom_call" | custom-call | tf_op jit(solution)/shard_map/finish/pallas_call | solution.py:778
  952.7 5.7 slice_bitcast_fusion
  (91 shorter events, 7.6 us)
Async XLA Ops:
  7.2 114.2 %copy-start = (bf16[128,128]{1,0:T(8,128)(2,1)S(1)}, bf16[128,128]{1,0:T(8,128)(2,1)}, u32[]{:S(2)}) copy-start(bf16[128,128]{1,0:T(8,128)(2,1)} %param.54) | copy-start | bytes 98308
  41.7 7.5 copy-start.19
  41.7 10.1 %copy-start.16 = (f32[88,128]{1,0:T(8,128)S(1)}, f32[88,128]{1,0:T(8,128)}, u32[]{:S(2)}) copy-start(f32[88,128]{1,0:T(8,128)} %constant.461.clone.m_ref) | copy-start | bytes 135172
  41.7 10.1 %copy-start.17 = (f32[88,128]{1,0:T(8,128)S(1)}, f32[88,128]{1,0:T(8,128)}, u32[]{:S(2)}) copy-start(f32[88,128]{1,0:T(8,128)} %constant.460.clone) | copy-start | bytes 135172
  41.7 153.7 %all-to-all-start = ((bf16[8,49,32,128]{3,2,1,0:T(8,128)(2,1)}), bf16[8,49,32,128]{3,2,1,0:T(8,128)(2,1)S(1)}, u32[]{:S(2)}, u32[]{:S(2)}) async-start(bf16[8,49,32,128]{3,2,1,0:T(8,128)(2,1)} %get-tuple-element.206), calls=%async_computation | async-start | bytes 6422528 | tf_op jit(solution)/shard_map/all_to_all | solution.py:898
  49.1 274.6 %all-reduce.20.cloned.1.call-start = ((), (), s32[]{:S(2)}) async-start(), calls=%async_computation.8 | async-start | bytes 9912320 | tf_op jit(solution)/shard_map/psum | solution.py:920
  50.3 71.0 %copy-start.18 = (f32[49]{0:T(128)}, f32[49]{0:T(128)S(1)}, u32[]{:S(2)}) copy-start(f32[49]{0:T(128)S(1)} %get-tuple-element.233.live_ref) | copy-start | bytes 592
  121.3 0.7 copy-start.15
  122.4 1.3 copy-start.8
  123.7 70.2 %copy-start.3 = (f32[368,128]{1,0:T(8,128)S(1)}, f32[368,128]{1,0:T(8,128)}, u32[]{:S(2)}) copy-start(f32[368,128]{1,0:T(8,128)} %param.55) | copy-start | bytes 565252
  195.4 1.7 copy-start.4
  231.7 6.8 copy-start.14
  231.7 118.7 %all-to-all-start.1 = ((bf16[8,14,48,128]{3,2,1,0:T(8,128)(2,1)}), bf16[8,14,48,128]{3,2,1,0:T(8,128)(2,1)}, u32[]{:S(2)}, u32[]{:S(2)}) async-start(bf16[8,14,48,128]{3,2,1,0:T(8,128)(2,1)} %get-tuple-element.209), calls=%async_computation.1 | async-start | bytes 2752512 | tf_op jit(solution)/shard_map/all_to_all | solution.py:898
  237.7 249.8 %all-gather.7.cloned.1.call-start = ((), (), s32[]{:S(2)}) async-start(), calls=%async_computation.10 | async-start | bytes 8601600 | tf_op jit(solution)/shard_map/all_gather | solution.py:942
  239.3 84.3 %copy-start.5 = (f32[8,456,128]{2,1,0:T(8,128)}, f32[8,456,128]{2,1,0:T(8,128)S(1)}, u32[]{:S(2)}) copy-start(f32[8,456,128]{2,1,0:T(8,128)S(1)} %fusion.16.gain.refs_5_) | copy-start | bytes 5603332
  362.6 1.3 copy-start.13
  362.7 143.8 %all-gather.9.cloned.1.call-start = ((), (), s32[]{:S(2)}) async-start(), calls=%async_computation.11 | async-start | bytes 8601600 | tf_op jit(solution)/shard_map/all_gather | solution.py:942
  401.0 12.6 %copy-start.10 = (bf16[8,21,48,128]{3,2,1,0:T(8,128)(2,1)S(1)}, bf16[8,21,48,128]{3,2,1,0:T(8,128)(2,1)}, u32[]{:S(2)}) copy-start(bf16[8,21,48,128]{3,2,1,0:T(8,128)(2,1)} %get-tuple-element.216) | copy-start | bytes 6193156
  413.5 135.6 %all-gather.11.cloned.1.call-start = ((), (), s32[]{:S(2)}) async-start(), calls=%async_computation.12 | async-start | bytes 12902400 | tf_op jit(solution)/shard_map/all_gather | solution.py:942
  502.8 35.7 %all-to-all-start.4 = ((bf16[8,14,48,128]{3,2,1,0:T(8,128)(2,1)}), bf16[8,14,48,128]{3,2,1,0:T(8,128)(2,1)S(1)}, u32[]{:S(2)}, u32[]{:S(2)}) async-start(bf16[8,14,48,128]{3,2,1,0:T(8,128)(2,1)} %get-tuple-element.224), calls=%async_computation.4 | async-start | bytes 2752512 | tf_op jit(solution)/shard_map/all_to_all | solution.py:898
  538.5 29.7 %copy-start.6 = (bf16[8,14,48,128]{3,2,1,0:T(8,128)(2,1)}, bf16[8,14,48,128]{3,2,1,0:T(8,128)(2,1)S(1)}, u32[]{:S(2)}) copy-start(bf16[8,14,48,128]{3,2,1,0:T(8,128)(2,1)S(1)} %all-to-all-done.4.refs_0_) | copy-start | bytes 4128772
  538.5 36.4 %all-to-all-start.5 = ((bf16[8,14,48,128]{3,2,1,0:T(8,128)(2,1)}), bf16[8,14,48,128]{3,2,1,0:T(8,128)(2,1)S(1)}, u32[]{:S(2)}, u32[]{:S(2)}) async-start(bf16[8,14,48,128]{3,2,1,0:T(8,128)(2,1)} %get-tuple-element.225), calls=%async_computation.5 | async-start | bytes 2752512 | tf_op jit(solution)/shard_map/all_to_all | solution.py:898
  574.9 51.6 %copy-start.7 = (bf16[8,14,48,128]{3,2,1,0:T(8,128)(2,1)}, bf16[8,14,48,128]{3,2,1,0:T(8,128)(2,1)S(1)}, u32[]{:S(2)}) copy-start(bf16[8,14,48,128]{3,2,1,0:T(8,128)(2,1)S(1)} %all-to-all-done.5.refs_1_) | copy-start | bytes 4128772
  667.9 262.7 %all-to-all-start.7 = ((bf16[8,49,32,128]{3,2,1,0:T(8,128)(2,1)}), bf16[8,49,32,128]{3,2,1,0:T(8,128)(2,1)}, u32[]{:S(2)}, u32[]{:S(2)}) async-start(bf16[8,49,32,128]{3,2,1,0:T(8,128)(2,1)} %spectrum_backward.1), calls=%async_computation.7 | async-start | bytes 6422528 | tf_op jit(solution)/shard_map/all_to_all | solution.py:898
  672.4 238.6 %all-reduce.22.cloned.1.call-start = ((), (), s32[]{:S(2)}) async-start(), calls=%async_computation.9 | async-start | bytes 9912320 | tf_op jit(solution)/shard_map/psum | solution.py:949
  695.1 1.7 copy-start.2
  696.8 7.3 copy-start.9
  696.8 7.3 copy-start.11
  696.8 7.3 copy-start.12
  952.7 5.7 copy-start.1
Sparse Core Ops, SparseCore 0:
  121.5 202.1 all-reduce.19
  362.8 48.6 all-gather.6
  413.6 49.1 all-gather.8
  480.8 68.2 all-gather.10
  695.2 215.6 all-reduce.21

commit v3 on v2

--- a/solution.py
+++ b/solution.py
@@ -13,7 +13,7 @@
 NLAT = 361
 LMAX = 360
 EPSILON = 1e-05
-GROUP = 192
+GROUP = 256
 SPLIT = 64
 REST = 16
 LANES = 128
@@ -37,7 +37,7 @@
         self.tp = ceil_to(self.live_t, 8)
         self.tb = self.tp // 8
         self.rest_groups = -(-self.tb // 4)
-        self.rows1 = ceil_to(self.tp + 8 * self.rest_groups, 16)
+        self.rows1 = self.tp + 8 * self.rest_groups
         self.rows2 = 2 * self.tp
         self.low = space * self.live_t
         self.high = LMAX + 1 - self.low
@@ -49,8 +49,8 @@
         self.half_lanes = LANES // 2
         self.rb = max(k for k in range(1, 9) if band % k == 0)
         blocks = band // self.rb
-        parts = min(3, blocks)
-        counts = [blocks // parts + (1 if p >= parts - blocks % parts else 0) for p in range(parts)]
+        half = blocks // 2
+        counts = [count for count in (half, blocks - 1 - half, 1) if count > 0]
         self.chunks = []
         start = 0
         for count in counts:
@@ -183,24 +183,23 @@
     )
 
 
-def analyse_kernel(plan, x_ref, low_ref, high_ref, out, out_high):
+def analyse_modes(x, dft_ref):
+    head, tail = x[:SPLIT], x[SPLIT:]
+    right = jnp.concatenate([head, head] + [tail] * (LANES // REST), axis=0)
+    return [
+        lax.dot_general(
+            dft_ref[k], right, (((1,), (1,)), ((), ())), preferred_element_type=F32
+        )
+        for k in range(2)
+    ]
+
+
+def analyse_low_kernel(plan, x_ref, dft_ref, out):
     lane = lax.broadcasted_iota(jnp.int32, (1, LANES), 1)
     part = lane // REST
     n, tp = plan.n, plan.tp
     for r in range(plan.rb):
-        x = x_ref[r]
-        head, tail = x[:SPLIT], x[SPLIT:]
-        right = jnp.concatenate([head, head] + [tail] * (LANES // REST), axis=0)
-
-        def modes(dft_ref):
-            return [
-                lax.dot_general(
-                    dft_ref[k], right, (((1,), (1,)), ((), ())), preferred_element_type=F32
-                )
-                for k in range(2)
-            ]
-
-        cosine, sine = modes(low_ref)
+        cosine, sine = analyse_modes(x_ref[r], dft_ref)
         main = jnp.where(lane < SPLIT, cosine[:, :LANES], sine[:, :LANES])
         for o in range(n):
             pieces = [main[o * tp : (o + 1) * tp]]
@@ -211,35 +210,43 @@
                     rest = jnp.where(part == 2 * i, cosine[first : first + 8, LANES:], rest)
                     rest = jnp.where(part == 2 * i + 1, sine[first : first + 8, LANES:], rest)
                 pieces.append(rest)
-            spare = plan.rows1 - tp - 8 * plan.rest_groups
-            if spare:
-                pieces.append(jnp.zeros((spare, LANES), F32))
             out[o, r] = jnp.concatenate(pieces, axis=0).astype(BF)
-        cosine, sine = modes(high_ref)
+
+
+def analyse_high_kernel(plan, x_ref, dft_ref, out):
+    lane = lax.broadcasted_iota(jnp.int32, (1, LANES), 1)
+    even = lane // REST % 2 == 0
+    for r in range(plan.rb):
+        cosine, sine = analyse_modes(x_ref[r], dft_ref)
         main = jnp.where(lane < SPLIT, cosine[:, :LANES], sine[:, :LANES])
-        rest = jnp.where(part % 2 == 0, cosine[:, LANES:], sine[:, LANES:])
-        out_high[r] = jnp.concatenate([main, rest], axis=1).astype(BF)
-
-
-def analyse(plan, x, low, high):
-    shape = (plan.n, plan.rows, plan.rows1, LANES)
-    high_shape = (plan.rows, 2 * plan.pairs, 2 * LANES)
+        rest = jnp.where(even, cosine[:, LANES:], sine[:, LANES:])
+        out[r] = jnp.concatenate([main, rest], axis=1).astype(BF)
+
+
+def analyse(plan, kernel, name, x, dft, shape, axis):
+    block = shape[:axis] + (plan.rb,) + shape[axis + 1 :]
     return pl.pallas_call(
-        functools.partial(analyse_kernel, plan),
+        functools.partial(kernel, plan),
         grid=(plan.rows // plan.rb,),
         in_specs=[
             pl.BlockSpec((plan.rb, plan.fpad, plan.lon), lambda i: (i, 0, 0)),
-            whole(low.shape),
-            whole(high.shape),
-        ],
-        out_specs=[
-            pl.BlockSpec((plan.n, plan.rb, plan.rows1, LANES), lambda i: (0, i, 0, 0)),
-            pl.BlockSpec((plan.rb,) + high_shape[1:], lambda i: (i, 0, 0)),
-        ],
-        out_shape=[jax.ShapeDtypeStruct(shape, BF), jax.ShapeDtypeStruct(high_shape, BF)],
+            whole(dft.shape),
+        ],
+        out_specs=pl.BlockSpec(block, lambda i: tuple(i if a == axis else 0 for a in range(len(shape)))),
+        out_shape=jax.ShapeDtypeStruct(shape, BF),
         compiler_params=params(),
-        name="analyse",
-    )(x, low, high)
+        name=name,
+    )(x, dft)
+
+
+def analyse_low(plan, x, dft):
+    shape = (plan.n, plan.rows, plan.rows1, LANES)
+    return analyse(plan, analyse_low_kernel, "analyse_low", x, dft, shape, 1)
+
+
+def analyse_high(plan, x, dft):
+    shape = (plan.rows, 2 * plan.pairs, 2 * LANES)
+    return analyse(plan, analyse_high_kernel, "analyse_high", x, dft, shape, 0)
 
 
 def unpack(plan, refs, store, height):
@@ -824,17 +831,17 @@
 
 
 def field_weights(plan, weight):
-    c = plan.channels
-    head, tail = weight[:SPLIT], jnp.pad(weight[SPLIT:], ((0, plan.fpad - plan.fields), (0, 0)))
-    blocks = []
+    select = np.zeros((4, 2 * LANES, plan.fields), np.float32)
+    side = np.zeros((4, 2 * LANES, 2), np.float32)
     for b in range(4):
-        out = jnp.zeros((2 * LANES, 2 * c), F32)
         for k in range(2):
-            out = out.at[k * SPLIT : (k + 1) * SPLIT, k * c : (k + 1) * c].set(head)
-            first = LANES + (2 * b + k) * REST
-            out = out.at[first : first + REST, k * c : (k + 1) * c].set(tail)
-        blocks.append(out)
-    return jnp.stack(blocks).astype(BF)
+            for f in range(plan.fields):
+                first = k * SPLIT + f if f < SPLIT else LANES + (2 * b + k) * REST + f - SPLIT
+                select[b, first, f] = 1.0
+                side[b, first, k] = 1.0
+    spread = jnp.einsum("blf,fc->blc", select, weight, precision=lax.Precision.HIGHEST)
+    both = jnp.concatenate([spread, spread], axis=2)
+    return (both * np.repeat(side, plan.channels, axis=2)).astype(BF)
 
 
 def on_device(
@@ -897,8 +904,8 @@
     def exchange(block):
         return lax.all_to_all(block, "space", split_axis=0, concat_axis=0, tiled=True)
 
-    sent, zonal_high = analyse(plan, rows, dft_low, dft_high)
-    recv = exchange(sent)
+    recv = exchange(analyse_low(plan, rows, dft_low))
+    zonal_high = analyse_high(plan, rows, dft_high)
 
     half = plan.half_lanes
 
@@ -943,12 +950,13 @@
         grad, out, out_high = score(plan, chunk, area, pred, everyone, truth, slope, idft, dec)
         predictions.append(pred)
         grads.append(grad)
+        returned_high.append(out_high)
+        if i == len(plan.chunks) - 1:
+            high_grads = high_adjoint(plan, returned_high, high_inv, mix_back, gain_long)
+            out, high_grads = lax.optimization_barrier((out, high_grads))
+            high_grads = lax.psum(high_grads, "space")
         returned.append(exchange(out))
-        returned_high.append(out_high)
-
-    high_grads = lax.psum(
-        high_adjoint(plan, returned_high, high_inv, mix_back, gain_long), "space"
-    )
+
     last = exchange(spectrum_backward(plan, returned, low_fwd, low_inv, mix_back, gain))
     zonal_grad = high_zonal(plan, high_grads, high_fwd)
     state_grad = finish(

time: 970 us -> 931 us (0.960)
  blocking collectives: 139 us -> 296 us
  waiting for transfers between devices: 319 us -> 200 us
  local copies, waits for them, and re-layouts: 60.2 us -> 27.5 us
  Pallas kernels: 390 us -> 359 us
    all_to_all x3 -> x5, blocking collectives: 139 us -> 296 us  [exchange(): lax.all_to_all(block, 'space', split_axis=0, concat_axis=0, tiled=True)]
    psum x1, waiting for transfers between devices: 84.3 us -> 5.76 us  [on_device(): high_coeffs = lax.psum(high_partial(plan, zonal_high, high_fwd), 'space')]
    psum x1, waiting for transfers between devices: 203 us -> 154 us  [on_device(): high_grads = lax.psum(high_grads, 'space')]
    pallas_call x4, Pallas kernels: 87.4 us -> 53.6 us  [high_call(): pl.pallas_call(kernel, grid=(plan.quads,), in_specs=[whole(a.shape) for a...]
    scatter x12 -> x0, local copies, waits for them, and re-layouts: 24.9 us -> none  [the longest x8 17.2 us: field_weights(): out = out.at[first:first + REST, k * c:(k + 1) * c].set(tail)]
    all_gather x3, waiting for transfers between devices: 7.04 us -> 31.2 us  [on_device(): everyone = lax.all_gather(pred[None], 'member', axis=0, tiled=True)]
    pallas_call x2, Pallas kernels: 85.6 us -> 68.3 us  [legendre_tables(): pl.pallas_call(table_kernel, grid=(tp // 8, degrees // 16), in_specs=[lan...]
    all_to_all x5 -> x3, waiting for transfers between devices: 24.6 us -> 8.9 us  [exchange(): lax.all_to_all(block, 'space', split_axis=0, concat_axis=0, tiled=True)]
  transfers between devices with their start and end apart: 10 -> 8, of which waited for: 5 -> 5; matrix products, arithmetic and copies ran while one was open for 6% -> 3% of each run, Pallas kernels for 30% -> 25%
where the time goes in v3:
time: 931 us; the launch traced here: 928 us
  Pallas kernels  359 us (39%)
  blocking collectives  296 us (32%)
  waiting for transfers between devices  200 us (21%)
  local copies, waits for them, and re-layouts  27.5 us (3%)
  starting transfers between devices  16.2 us (2%)
  other arithmetic  14.7 us (2%)
  between operations  14 us (2%)
    all_to_all x5, blocking collectives, exchange(): lax.all_to_all(block, 'space', split_axis=0, concat_axis=0, tiled=True)  296 us
    psum x1, waiting for transfers between devices, on_device(): high_grads = lax.psum(high_grads, 'space')  154 us
    pallas_call x2, Pallas kernels, legendre_tables(): pl.pallas_call(table_kernel, grid=(tp // 8, degrees // 16), in_specs=[lan...  68.3 us
    pallas_call x4, Pallas kernels, high_call(): pl.pallas_call(kernel, grid=(plan.quads,), in_specs=[whole(a.shape) for a...  53.6 us
    pallas_call x3, Pallas kernels, score(): pl.pallas_call(functools.partial(score_kernel, plan, first, members), gri...  49 us
    pallas_call x1, Pallas kernels, spectrum_backward(): pl.pallas_call(functools.partial(spectrum_backward_kernel, plan, len(recv...  48.9 us
    pallas_call x1, Pallas kernels, spectrum_forward(): pl.pallas_call(functools.partial(spectrum_forward_kernel, plan), grid=(pl...  48.3 us
    pallas_call x3, Pallas kernels, predict(): pl.pallas_call(functools.partial(predict_kernel, plan, first), grid=(coun...  41.1 us
  transfers between devices with their start and end apart: 8, of which 5 were waited for; matrix products, arithmetic and copies ran while one was open for 3% of the time, Pallas kernels for 25%

profile of v3, /device:TPU:0, one launch (start us, length us, event | category | flops | bytes accessed | tf_op | source)
XLA Modules:
  0.0 928.1 jit_solution(7490316233584806017)
XLA Ops:
  7.2 5.9 pad.54.x_ref
  13.1 13.7 %analyse_low.1 = bf16[8,49,40,128]{3,2,1,0:T(8,128)(2,1)} custom-call(bf16[49,80,720]{2,1,0:T(8,128)(2,1)} %pad.54.x_ref, bf16[2,256,720]{2,1,0:T(8,128)(2,1)} %constant.76.clone.dft_ref), custom_call_target="tpu_custom_call" | custom-call | tf_op jit(solution)/shard_map/analyse_low/pallas_call | solution.py:228
  26.8 7.4 all-to-all-start
  34.3 0.2 reduce-window.9
  34.5 0.1 select_reduce_fusion
  34.6 0.1 dynamic_slice.28
  34.9 0.7 multiply_multiply_fusion
  35.5 15.0 %analyse_high.1.zonal = bf16[49,112,256]{2,1,0:T(8,128)(2,1)} custom-call(bf16[49,80,720]{2,1,0:T(8,128)(2,1)} %pad.54.x_ref, bf16[2,112,720]{2,1,0:T(8,128)(2,1)} %constant.77.clone.dft_ref), custom_call_target="tpu_custom_call" | custom-call | tf_op jit(solution)/shard_map/analyse_high/pallas_call | solution.py:228
  50.6 0.6 maximum_bitcast_fusion.2.live_ref
  51.2 0.7 maximum_bitcast_fusion
  51.9 0.6 multiply_add_fusion.1.start_ref
  52.5 21.6 %legendre_tables.3 = (bf16[56,112,128]{2,1,0:T(8,128)(2,1)}, bf16[56,112,128]{2,1,0:T(8,128)(2,1)}) custom-call(f32[56,128]{1,0:T(8,128)} %constant.82.clone.m_ref, f32[56,128]{1,0:T(8,128)} %constant.120.shift_ref, f32[56,128]{1,0:T(8,128)} %multiply_add_fusion.1.start_ref, f32[1,128]{1,0:T(1,128)} %get-tuple-element.63.cos_ref, ...), custom_call_target="tpu_custom_call" | custom-call | tf_op jit(solution)/shard_map/legendre_tables/pallas_call | solution.py:155
  74.1 11.9 %high_partial.1 = bf16[14,5,112,128]{3,2,1,0:T(8,128)(2,1)} custom-call(bf16[49,112,256]{2,1,0:T(8,128)(2,1)} %analyse_high.1.zonal, bf16[56,112,128]{2,1,0:T(8,128)(2,1)} %get-tuple-element.29.fwd), custom_call_target="tpu_custom_call" | custom-call | tf_op jit(solution)/shard_map/high_partial/pallas_call | solution.py:555
  86.0 0.6 pad.58
  86.6 0.6 pad.59
  87.2 0.5 pad.60
  87.7 0.7 convert_bitcast_fusion
  88.4 0.7 dynamic-slice_bitcast_fusion
  89.2 0.6 pad.57.start_ref
  89.8 0.1 convolution_bitcast_fusion
  90.0 0.6 fusion.26
  90.6 1.0 fusion.24
  91.6 1.0 copy.31.mix
  92.6 0.7 broadcast_in_dim.47.m_ref
  93.3 0.6 convert_element_type.63.shift_ref
  93.9 46.7 %legendre_tables.2 = (bf16[32,368,392]{2,1,0:T(8,128)(2,1)}, bf16[32,368,392]{2,1,0:T(8,128)(2,1)}) custom-call(f32[32,128]{1,0:T(8,128)} %broadcast_in_dim.47.m_ref, f32[32,128]{1,0:T(8,128)} %convert_element_type.63.shift_ref, f32[32,512]{1,0:T(8,128)} %pad.57.start_ref, f32[1,512]{1,0:T(1,128)} %bitcast.82, f32[1,512]{1,0:T(1,128)} %bitcast.83, ...), custom_call_target="tpu_custom_call" | custom-call | tf_op jit(solution)/shard_map/legendre_tables/pallas_call | solution.py:155
  140.6 6.8 all-to-all-done.recv
  147.4 48.3 %spectrum_forward.1 = (bf16[8,21,64,128]{3,2,1,0:T(8,128)(2,1)}, bf16[8,21,64,128]{3,2,1,0:T(8,128)(2,1)}, bf16[8,7,64,128]{3,2,1,0:T(8,128)(2,1)}) custom-call(bf16[8,49,40,128]{3,2,1,0:T(8,128)(2,1)} %all-to-all-done.recv, bf16[32,368,392]{2,1,0:T(8,128)(2,1)} %get-tuple-element.26.fwd.refs_3_, bf16[32,368,392]{2,1,0:T(8,128)(2,1)} %get-tuple-element.27.inv.refs_4_, ...), custom_call_target="tpu_custom_call" | custom-call | tf_op jit(solution)/shard_map/spectrum_forward/pallas_call | solution.py:358
  195.7 3.6 all-to-all-start.3
  199.3 0.1 copy.30
  199.4 0.6 pad.56.dec_ref
  200.1 0.6 pad.55.enc_ref
  200.9 5.8 all-reduce.18.cloned.1.call-done.coeffs
  206.6 16.1 %high_synthesis.1.refs_1_ = bf16[49,224,128]{2,1,0:T(8,128)(2,1)} custom-call(bf16[14,5,112,128]{3,2,1,0:T(8,128)(2,1)} %all-reduce.18.cloned.1.call-done.coeffs, bf16[56,112,128]{2,1,0:T(8,128)(2,1)} %get-tuple-element.30.inv.refs_3_, bf16[4,256,256]{2,1,0:T(8,128)(2,1)} %copy.31.mix, f32[8,424,128]{2,1,0:T(8,128)} %copy-done.4), custom_call_target="tpu_custom_call" | custom-call | tf_op jit(solution)/shard_map/high_synthesis/pallas_call | solution.py:555
  222.7 2.1 all-to-all-done.3.refs_0_
  224.8 1.0 copy-done.6
  225.8 7.5 predict.5
  233.4 69.6 %all_to_all.40.refs_0_ = bf16[8,21,64,128]{3,2,1,0:T(8,128)(2,1)} all-to-all(bf16[8,21,64,128]{3,2,1,0:T(8,128)(2,1)} %get-tuple-element.32), channel_id=1, replica_groups=mesh['member'=4,'space'=8] {'space'}, dimensions={0} | all-to-all | bytes 5505024 | tf_op jit(solution)/shard_map/all_to_all | solution.py:905
  303.1 16.8 %predict.4 = (bf16[21,80,720]{2,1,0:T(8,128)(2,1)}, bf16[21,128,720]{2,1,0:T(8,128)(2,1)}) custom-call(f32[49]{0:T(128)} %copy-done.20, bf16[49,80,720]{2,1,0:T(8,128)(2,1)} %pad.54.x_ref, bf16[736,720]{1,0:T(8,128)(2,1)} %constant.78.clone.idft_ref, bf16[128,80]{1,0:T(8,128)(2,1)} %pad.55.enc_ref, bf16[80,128]{1,0:T(8,128)(2,1)} %pad.56.dec_ref, ...), custom_call_target="tpu_custom_call" | custom-call | tf_op jit(solution)/shard_map/predict/pallas_call | solution.py:631
  320.0 65.6 %all_to_all.41.refs_0_ = bf16[8,21,64,128]{3,2,1,0:T(8,128)(2,1)} all-to-all(bf16[8,21,64,128]{3,2,1,0:T(8,128)(2,1)S(1)} %copy-done.7), channel_id=1, replica_groups=mesh['member'=4,'space'=8] {'space'}, dimensions={0} | all-to-all | bytes 5505024 | tf_op jit(solution)/shard_map/all_to_all | solution.py:905
  385.6 16.7 %predict.3 = (bf16[21,80,720]{2,1,0:T(8,128)(2,1)}, bf16[21,128,720]{2,1,0:T(8,128)(2,1)}) custom-call(f32[49]{0:T(128)} %copy-done.20, bf16[49,80,720]{2,1,0:T(8,128)(2,1)} %pad.54.x_ref, bf16[736,720]{1,0:T(8,128)(2,1)} %constant.78.clone.idft_ref, bf16[128,80]{1,0:T(8,128)(2,1)} %pad.55.enc_ref, bf16[80,128]{1,0:T(8,128)(2,1)} %pad.56.dec_ref, ...), custom_call_target="tpu_custom_call" | custom-call | tf_op jit(solution)/shard_map/predict/pallas_call | solution.py:631
  402.3 0.1 copy.33
  402.5 0.6 pad.67.dec_ref
  403.1 6.3 pad.66.obs_ref
  409.4 10.3 %score.5 = (bf16[7,80,720]{2,1,0:T(8,128)(2,1)}, bf16[8,7,64,128]{3,2,1,0:T(8,128)(2,1)}, bf16[7,224,128]{2,1,0:T(8,128)(2,1)}) custom-call(f32[49]{0:T(128)} %get-tuple-element.52.area_ref, bf16[7,80,720]{2,1,0:T(8,128)(2,1)} %get-tuple-element.35.own_ref, bf16[4,7,80,720]{3,2,1,0:T(8,128)(2,1)} %bitcast.79, bf16[49,80,720]{2,1,0:T(8,128)(2,1)} %pad.66.obs_ref, ...), custom_call_target="tpu_custom_call" | custom-call | tf_op jit(solution)/shard_map/score/pallas_call | solution.py:705
  419.7 19.4 %score.4 = (bf16[21,80,720]{2,1,0:T(8,128)(2,1)}, bf16[8,21,64,128]{3,2,1,0:T(8,128)(2,1)}, bf16[21,224,128]{2,1,0:T(8,128)(2,1)}) custom-call(f32[49]{0:T(128)} %get-tuple-element.52.area_ref, bf16[21,80,720]{2,1,0:T(8,128)(2,1)} %get-tuple-element.33.own_ref, bf16[4,21,80,720]{3,2,1,0:T(8,128)(2,1)} %bitcast.75, bf16[49,80,720]{2,1,0:T(8,128)(2,1)} %pad.66.obs_ref, ...), custom_call_target="tpu_custom_call" | custom-call | tf_op jit(solution)/shard_map/score/pallas_call | solution.py:705
  439.1 31.2 %all-gather.7.cloned.1.call-done = bf16[84,80,720]{2,1,0:T(8,128)(2,1)} async-done(((bf16[21,80,720]{2,1,0:T(8,128)(2,1)}), bf16[84,80,720]{2,1,0:T(8,128)(2,1)}) %all-gather.7.cloned.1.call-update) | async-done | bytes 9676816 | tf_op jit(solution)/shard_map/all_gather | solution.py:949
  470.3 19.3 %score.3 = (bf16[21,80,720]{2,1,0:T(8,128)(2,1)}, bf16[8,21,64,128]{3,2,1,0:T(8,128)(2,1)}, bf16[21,224,128]{2,1,0:T(8,128)(2,1)}) custom-call(f32[49]{0:T(128)} %get-tuple-element.52.area_ref, bf16[21,80,720]{2,1,0:T(8,128)(2,1)} %get-tuple-element.31.own_ref, bf16[4,21,80,720]{3,2,1,0:T(8,128)(2,1)} %bitcast.76, bf16[49,80,720]{2,1,0:T(8,128)(2,1)} %pad.66.obs_ref, ...), custom_call_target="tpu_custom_call" | custom-call | tf_op jit(solution)/shard_map/score/pallas_call | solution.py:705
  489.6 14.4 %high_adjoint.1 = bf16[14,5,112,128]{3,2,1,0:T(8,128)(2,1)} custom-call(bf16[21,224,128]{2,1,0:T(8,128)(2,1)} %get-tuple-element.45.refs_0_, bf16[21,224,128]{2,1,0:T(8,128)(2,1)} %get-tuple-element.46.refs_1_, bf16[7,224,128]{2,1,0:T(8,128)(2,1)} %get-tuple-element.47.refs_2_, bf16[56,112,128]{2,1,0:T(8,128)(2,1)} %get-tuple-element.30.inv.refs_3_, ...), custom_call_target="tpu_custom_call" | custom-call | tf_op jit(solution)/shard_map/high_adjoint/pallas_call | solution.py:555
  504.0 29.3 %all_to_all.42.refs_2_ = bf16[8,7,64,128]{3,2,1,0:T(8,128)(2,1)} all-to-all(bf16[8,7,64,128]{3,2,1,0:T(8,128)(2,1)} %get-tuple-element.48), channel_id=1, replica_groups=mesh['member'=4,'space'=8] {'space'}, dimensions={0} | all-to-all | bytes 1835008 | tf_op jit(solution)/shard_map/all_to_all | solution.py:905
  533.3 65.9 %all_to_all.43.refs_0_ = bf16[8,21,64,128]{3,2,1,0:T(8,128)(2,1)} all-to-all(bf16[8,21,64,128]{3,2,1,0:T(8,128)(2,1)S(1)} %copy-done.9), channel_id=1, replica_groups=mesh['member'=4,'space'=8] {'space'}, dimensions={0} | all-to-all | bytes 5505024 | tf_op jit(solution)/shard_map/all_to_all | solution.py:905
  599.2 65.5 %all_to_all.44.refs_1_ = bf16[8,21,64,128]{3,2,1,0:T(8,128)(2,1)} all-to-all(bf16[8,21,64,128]{3,2,1,0:T(8,128)(2,1)S(1)} %copy-done.8), channel_id=1, replica_groups=mesh['member'=4,'space'=8] {'space'}, dimensions={0} | all-to-all | bytes 5505024 | tf_op jit(solution)/shard_map/all_to_all | solution.py:905
  664.7 48.9 %spectrum_backward.1 = bf16[8,49,40,128]{3,2,1,0:T(8,128)(2,1)} custom-call(bf16[8,21,64,128]{3,2,1,0:T(8,128)(2,1)} %all_to_all.43.refs_0_, bf16[8,21,64,128]{3,2,1,0:T(8,128)(2,1)} %all_to_all.44.refs_1_, bf16[8,7,64,128]{3,2,1,0:T(8,128)(2,1)} %all_to_all.42.refs_2_, bf16[32,368,392]{2,1,0:T(8,128)(2,1)} %get-tuple-element.26.fwd.refs_3_, ...), custom_call_target="tpu_custom_call" | custom-call | tf_op jit(solution)/shard_map/spectrum_backward/pallas_call | solution.py:375
  713.6 4.8 all-to-all-start.7
  718.4 0.3 all-reduce.20.cloned.1.call-start
  718.7 0.3 all-reduce.20.cloned.1.call-update
  719.0 0.1 convolution_convert_fusion
  719.1 0.6 pad.68.through_ref
  719.8 6.6 fusion
  726.4 3.5 pad_maximum_fusion.2.grad_ref
  729.9 153.8 %all-reduce.20.cloned.1.call-done.grads = bf16[14,5,112,128]{3,2,1,0:T(8,128)(2,1)} async-done(((bf16[14,5,112,128]{3,2,1,0:T(8,128)(2,1)}), bf16[14,5,112,128]{3,2,1,0:T(8,128)(2,1)}) %all-reduce.20.cloned.1.call-update) | async-done | bytes 2007056 | tf_op jit(solution)/shard_map/psum | solution.py:957
  883.7 11.3 %high_zonal.1.high_ref = bf16[49,144,128]{2,1,0:T(8,128)(2,1)} custom-call(bf16[14,5,112,128]{3,2,1,0:T(8,128)(2,1)} %all-reduce.20.cloned.1.call-done.grads, bf16[56,112,128]{2,1,0:T(8,128)(2,1)} %get-tuple-element.29.fwd), custom_call_target="tpu_custom_call" | custom-call | tf_op jit(solution)/shard_map/high_zonal/pallas_call | solution.py:555
  894.9 20.9 %finish.1 = bf16[49,80,720]{2,1,0:T(8,128)(2,1)} custom-call(f32[49]{0:T(128)} %copy-done.20, bf16[49,80,720]{2,1,0:T(8,128)(2,1)} %pad_maximum_fusion.2.grad_ref, bf16[736,720]{1,0:T(8,128)(2,1)} %constant.79.clone.main_ref, bf16[768,720]{1,0:T(8,128)(2,1)} %constant.80.clone.rest_ref, bf16[80,80]{1,0:T(8,128)(2,1)} %pad.68.through_ref, ...), custom_call_target="tpu_custom_call" | custom-call | tf_op jit(solution)/shard_map/finish/pallas_call | solution.py:785
  915.9 5.7 slice_bitcast_fusion
  (76 shorter events, 0.9 us)
Async XLA Ops:
  7.2 82.7 %copy-start = (bf16[128,128]{1,0:T(8,128)(2,1)S(1)}, bf16[128,128]{1,0:T(8,128)(2,1)}, u32[]{:S(2)}) copy-start(bf16[128,128]{1,0:T(8,128)(2,1)} %param.24) | copy-start | bytes 98308
  26.8 7.4 copy-start.21
  26.8 120.6 %all-to-all-start = ((bf16[8,49,40,128]{3,2,1,0:T(8,128)(2,1)}), bf16[8,49,40,128]{3,2,1,0:T(8,128)(2,1)}, u32[]{:S(2)}, u32[]{:S(2)}) async-start(bf16[8,49,40,128]{3,2,1,0:T(8,128)(2,1)} %analyse_low.1), calls=%async_computation | async-start | bytes 8028160 | tf_op jit(solution)/shard_map/all_to_all | solution.py:905
  34.2 172.4 %all-reduce.18.cloned.1.call-start = ((), (), s32[]{:S(2)}) async-start(), calls=%async_computation.8 | async-start | bytes 4014080 | tf_op jit(solution)/shard_map/psum | solution.py:927
  35.5 15.0 %copy-start.20 = (f32[49]{0:T(128)}, f32[49]{0:T(128)S(1)}, u32[]{:S(2)}) copy-start(f32[49]{0:T(128)S(1)} %get-tuple-element.53.live_ref) | copy-start | bytes 592
  35.5 16.3 %copy-start.18 = (f32[56,128]{1,0:T(8,128)S(1)}, f32[56,128]{1,0:T(8,128)}, u32[]{:S(2)}) copy-start(f32[56,128]{1,0:T(8,128)} %constant.82.clone.m_ref) | copy-start | bytes 86020
  35.5 16.3 %copy-start.19 = (f32[56,128]{1,0:T(8,128)S(1)}, f32[56,128]{1,0:T(8,128)}, u32[]{:S(2)}) copy-start(f32[56,128]{1,0:T(8,128)} %constant.81.clone) | copy-start | bytes 86020
  74.1 15.8 %copy-start.17 = (bf16[73,128]{1,0:T(8,128)(2,1)S(1)}, bf16[73,128]{1,0:T(8,128)(2,1)}, u32[]{:S(2)}) copy-start(bf16[73,128]{1,0:T(8,128)(2,1)} %param.23) | copy-start | bytes 56068
  74.1 15.9 %copy-start.15 = (f32[4,256,73]{1,2,0:T(8,128)S(1)}, f32[4,256,73]{1,2,0:T(8,128)}, u32[]{:S(2)}) copy-start(f32[4,256,73]{1,2,0:T(8,128)} %constant.74.clone) | copy-start | bytes 897028
  86.0 4.6 copy-start.13
  86.0 54.6 %copy-start.3 = (f32[368,128]{1,0:T(8,128)S(1)}, f32[368,128]{1,0:T(8,128)}, u32[]{:S(2)}) copy-start(f32[368,128]{1,0:T(8,128)} %param.25) | copy-start | bytes 565252
  140.6 6.8 copy-start.12
  147.4 52.1 %copy-start.16 = (bf16[128,73]{0,1:T(8,128)(2,1)S(1)}, bf16[128,73]{0,1:T(8,128)(2,1)}, u32[]{:S(2)}) copy-start(bf16[128,73]{0,1:T(8,128)(2,1)} %param.26) | copy-start | bytes 56068
  195.7 29.1 %all-to-all-start.3 = ((bf16[8,7,64,128]{3,2,1,0:T(8,128)(2,1)}), bf16[8,7,64,128]{3,2,1,0:T(8,128)(2,1)S(1)}, u32[]{:S(2)}, u32[]{:S(2)}) async-start(bf16[8,7,64,128]{3,2,1,0:T(8,128)(2,1)} %get-tuple-element.34), calls=%async_computation.3 | async-start | bytes 1835008 | tf_op jit(solution)/shard_map/all_to_all | solution.py:905
  199.3 210.1 %all-gather.11.cloned.1.call-start = ((), (), s32[]{:S(2)}) async-start(), calls=%async_computation.12 | async-start | bytes 4300800 | tf_op jit(solution)/shard_map/all_gather | solution.py:949
  200.9 5.8 copy-start.4
  224.8 1.0 copy-start.6
  233.4 186.3 %all-gather.9.cloned.1.call-start = ((), (), s32[]{:S(2)}) async-start(), calls=%async_computation.11 | async-start | bytes 12902400 | tf_op jit(solution)/shard_map/all_gather | solution.py:949
  303.1 16.9 %copy-start.7 = (bf16[8,21,64,128]{3,2,1,0:T(8,128)(2,1)S(1)}, bf16[8,21,64,128]{3,2,1,0:T(8,128)(2,1)}, u32[]{:S(2)}) copy-start(bf16[8,21,64,128]{3,2,1,0:T(8,128)(2,1)} %get-tuple-element.28) | copy-start | bytes 8257540
  319.9 150.4 %all-gather.7.cloned.1.call-start = ((), (), s32[]{:S(2)}) async-start(), calls=%async_computation.10 | async-start | bytes 12902400 | tf_op jit(solution)/shard_map/all_gather | solution.py:949
  489.6 43.7 %copy-start.9 = (bf16[8,21,64,128]{3,2,1,0:T(8,128)(2,1)S(1)}, bf16[8,21,64,128]{3,2,1,0:T(8,128)(2,1)}, u32[]{:S(2)}) copy-start(bf16[8,21,64,128]{3,2,1,0:T(8,128)(2,1)} %get-tuple-element.42) | copy-start | bytes 8257540
  533.3 65.9 %copy-start.8 = (bf16[8,21,64,128]{3,2,1,0:T(8,128)(2,1)S(1)}, bf16[8,21,64,128]{3,2,1,0:T(8,128)(2,1)}, u32[]{:S(2)}) copy-start(bf16[8,21,64,128]{3,2,1,0:T(8,128)(2,1)} %get-tuple-element.43) | copy-start | bytes 8257540
  713.6 6.2 copy-start.2
  713.6 6.2 copy-start.5
  713.6 181.3 %all-to-all-start.7 = ((bf16[8,49,40,128]{3,2,1,0:T(8,128)(2,1)}), bf16[8,49,40,128]{3,2,1,0:T(8,128)(2,1)}, u32[]{:S(2)}, u32[]{:S(2)}) async-start(bf16[8,49,40,128]{3,2,1,0:T(8,128)(2,1)} %spectrum_backward.1), calls=%async_computation.7 | async-start | bytes 8028160 | tf_op jit(solution)/shard_map/all_to_all | solution.py:905
  718.4 165.2 %all-reduce.20.cloned.1.call-start = ((), (), s32[]{:S(2)}) async-start(), calls=%async_computation.9 | async-start | bytes 4014080 | tf_op jit(solution)/shard_map/psum | solution.py:957
  719.8 6.6 copy-start.10
  719.8 6.6 copy-start.11
  719.8 6.6 copy-start.14
  915.9 5.7 copy-start.1
Sparse Core Ops, SparseCore 0:
  86.1 120.4 all-reduce.17
  233.5 32.2 all-gather.10
  320.0 67.8 all-gather.8
  402.5 67.7 all-gather.6
  723.0 160.6 all-reduce.19

commit v4 on v3

--- a/solution.py
+++ b/solution.py
@@ -50,7 +50,7 @@
         self.rb = max(k for k in range(1, 9) if band % k == 0)
         blocks = band // self.rb
         half = blocks // 2
-        counts = [count for count in (half, blocks - 1 - half, 1) if count > 0]
+        counts = [count for count in (1, blocks - 1 - half, half) if count > 0]
         self.chunks = []
         start = 0
         for count in counts:
@@ -83,6 +83,22 @@
 
 def params(**more):
     return pltpu.CompilerParams(vmem_limit_bytes=VMEM, **more)
+
+
+def call(kernel, name, operands, in_specs, out_specs, out_shape, grid, scratch=()):
+    results = out_shape if isinstance(out_shape, (list, tuple)) else [out_shape]
+    moved = sum(math.prod(a.shape) * a.dtype.itemsize for a in list(operands) + list(results))
+    return pl.pallas_call(
+        kernel,
+        grid=grid,
+        in_specs=in_specs,
+        out_specs=out_specs,
+        out_shape=out_shape,
+        scratch_shapes=list(scratch),
+        compiler_params=params(),
+        cost_estimate=pl.CostEstimate(flops=0, transcendentals=0, bytes_accessed=4 * moved),
+        name=name,
+    )(*operands)
 
 
 def whole(shape):
@@ -152,10 +168,18 @@
     row_spec = pl.BlockSpec((1, wide), lambda i, j: (0, 0))
     lane_spec = pl.BlockSpec((8, LANES), lambda i, j: (i, 0))
     out_spec = pl.BlockSpec((8, 16, rows), lambda i, j: (i, j, 0))
-    return pl.pallas_call(
+    return call(
         table_kernel,
-        grid=(tp // 8, degrees // 16),
-        in_specs=[
+        "legendre_tables",
+        [
+            orders.astype(F32),
+            shift.astype(F32),
+            jnp.pad(log_start, ((0, 0), (0, wide - rows))),
+            spread(cosines),
+            spread(quad),
+            spread(live),
+        ],
+        [
             lane_spec,
             lane_spec,
             pl.BlockSpec((8, wide), lambda i, j: (i, 0)),
@@ -163,23 +187,15 @@
             row_spec,
             row_spec,
         ],
-        out_specs=[out_spec, out_spec],
-        out_shape=[shape, shape],
-        scratch_shapes=[
+        [out_spec, out_spec],
+        [shape, shape],
+        (tp // 8, degrees // 16),
+        [
             pltpu.VMEM((8, wide), F32),
             pltpu.VMEM((8, wide), F32),
             pltpu.VMEM((8, wide), F32),
             pltpu.VMEM((wide // LANES, 128, LANES), F32),
         ],
-        compiler_params=params(),
-        name="legendre_tables",
-    )(
-        orders.astype(F32),
-        shift.astype(F32),
-        jnp.pad(log_start, ((0, 0), (0, wide - rows))),
-        spread(cosines),
-        spread(quad),
-        spread(live),
     )
 
 
@@ -194,7 +210,7 @@
     ]
 
 
-def analyse_low_kernel(plan, x_ref, dft_ref, out):
+def analyse_low_kernel(plan, x_ref, dft_ref, *outs):
     lane = lax.broadcasted_iota(jnp.int32, (1, LANES), 1)
     part = lane // REST
     n, tp = plan.n, plan.tp
@@ -210,7 +226,7 @@
                     rest = jnp.where(part == 2 * i, cosine[first : first + 8, LANES:], rest)
                     rest = jnp.where(part == 2 * i + 1, sine[first : first + 8, LANES:], rest)
                 pieces.append(rest)
-            out[o, r] = jnp.concatenate(pieces, axis=0).astype(BF)
+            outs[o][r] = jnp.concatenate(pieces, axis=0).astype(BF)
 
 
 def analyse_high_kernel(plan, x_ref, dft_ref, out):
@@ -223,62 +239,59 @@
         out[r] = jnp.concatenate([main, rest], axis=1).astype(BF)
 
 
-def analyse(plan, kernel, name, x, dft, shape, axis):
-    block = shape[:axis] + (plan.rb,) + shape[axis + 1 :]
-    return pl.pallas_call(
+def analyse(plan, kernel, name, x, dft, height, lanes, count):
+    shape = jax.ShapeDtypeStruct((plan.rows, height, lanes), BF)
+    return call(
         functools.partial(kernel, plan),
-        grid=(plan.rows // plan.rb,),
-        in_specs=[
-            pl.BlockSpec((plan.rb, plan.fpad, plan.lon), lambda i: (i, 0, 0)),
-            whole(dft.shape),
-        ],
-        out_specs=pl.BlockSpec(block, lambda i: tuple(i if a == axis else 0 for a in range(len(shape)))),
-        out_shape=jax.ShapeDtypeStruct(shape, BF),
-        compiler_params=params(),
-        name=name,
-    )(x, dft)
+        name,
+        [x, dft],
+        [pl.BlockSpec((plan.rb, plan.fpad, plan.lon), lambda i: (i, 0, 0)), whole(dft.shape)],
+        [pl.BlockSpec((plan.rb, height, lanes), lambda i: (i, 0, 0))] * count,
+        [shape] * count,
+        (plan.rows // plan.rb,),
+    )
 
 
 def analyse_low(plan, x, dft):
-    shape = (plan.n, plan.rows, plan.rows1, LANES)
-    return analyse(plan, analyse_low_kernel, "analyse_low", x, dft, shape, 1)
+    return analyse(plan, analyse_low_kernel, "analyse_low", x, dft, plan.rows1, LANES, plan.n)
 
 
 def analyse_high(plan, x, dft):
-    shape = (plan.rows, 2 * plan.pairs, 2 * LANES)
-    return analyse(plan, analyse_high_kernel, "analyse_high", x, dft, shape, 0)
+    return analyse(
+        plan, analyse_high_kernel, "analyse_high", x, dft, 2 * plan.pairs, 2 * LANES, 1
+    )[0]
 
 
 def unpack(plan, refs, store, height):
     start = 0
-    for ref in refs:
-        count = ref.shape[1]
-        for o in range(plan.n):
-            base = o * plan.rows + start
-
-            def step(r, unused, o=o, base=base, ref=ref):
+    for parts in refs:
+        for o, ref in enumerate(parts):
+
+            def step(r, unused, base=o * plan.rows + start, ref=ref):
                 at = pl.multiple_of((base + r) * height, 8)
-                store[pl.ds(at, height), :] = ref[o, r].astype(F32)
+                store[pl.ds(at, height), :] = ref[r].astype(F32)
                 return unused
 
-            lax.fori_loop(0, count, step, 0)
-        start += count
+            lax.fori_loop(0, ref.shape[0], step, 0)
+        start += parts[0].shape[0]
 
 
 def repack(plan, refs, store, height):
     start = 0
-    for ref in refs:
-        count = ref.shape[1]
-        for o in range(plan.n):
-            base = o * plan.rows + start
-
-            def step(r, unused, o=o, base=base, ref=ref):
+    for parts in refs:
+        for o, ref in enumerate(parts):
+
+            def step(r, unused, base=o * plan.rows + start, ref=ref):
                 at = pl.multiple_of((base + r) * height, 8)
-                ref[o, r] = store[pl.ds(at, height), :].astype(BF)
+                ref[r] = store[pl.ds(at, height), :].astype(BF)
                 return unused
 
-            lax.fori_loop(0, count, step, 0)
-        start += count
+            lax.fori_loop(0, ref.shape[0], step, 0)
+        start += parts[0].shape[0]
+
+
+def by_device(plan, refs):
+    return [refs[i : i + plan.n] for i in range(0, len(refs), plan.n)]
 
 
 def rest_row(plan, t):
@@ -286,8 +299,9 @@
     return plan.tp + 8 * (block // 4) + t % 8
 
 
-def spectrum_forward_kernel(plan, recv, fwd, inv, mix, gain, *refs):
-    outs, zin, yout = refs[:-2], refs[-2], refs[-1]
+def spectrum_forward_kernel(plan, *refs):
+    recv, (fwd, inv, mix, gain) = refs[: plan.n], refs[plan.n : plan.n + 4]
+    outs, zin, yout = refs[plan.n + 4 : -2], refs[-2], refs[-1]
     t = pl.program_id(0)
 
     @pl.when(t == 0)
@@ -315,18 +329,18 @@
 
     @pl.when(t == plan.live_t - 1)
     def _():
-        repack(plan, outs, yout, plan.rows2)
+        repack(plan, by_device(plan, outs), yout, plan.rows2)
 
 
 def spectrum_backward_kernel(plan, count, *refs):
     recvs = refs[:count]
     fwd, inv, mix, gain = refs[count : count + 4]
-    out, zin, yout = refs[count + 4 :]
+    outs, zin, yout = refs[count + 4 : -2], refs[-2], refs[-1]
     t = pl.program_id(0)
 
     @pl.when(t == 0)
     def _():
-        unpack(plan, recvs, zin, plan.rows2)
+        unpack(plan, by_device(plan, recvs), zin, plan.rows2)
         yout[...] = jnp.zeros_like(yout)
 
     z = jnp.concatenate(
@@ -345,7 +359,7 @@
 
     @pl.when(t == plan.live_t - 1)
     def _():
-        repack(plan, [out], yout, plan.rows1)
+        repack(plan, [outs], yout, plan.rows1)
 
 
 def spectrum_specs(plan, mix, gain):
@@ -354,37 +368,39 @@
 
 
 def spectrum_forward(plan, recv, fwd, inv, mix, gain):
-    shapes = [(plan.n, count, plan.rows2, LANES) for _, count in plan.chunks]
-    return pl.pallas_call(
+    shapes = [(count, plan.rows2, LANES) for _, count in plan.chunks for _ in range(plan.n)]
+    parts = call(
         functools.partial(spectrum_forward_kernel, plan),
-        grid=(plan.live_t,),
-        in_specs=[whole(recv.shape)] + spectrum_specs(plan, mix, gain),
-        out_specs=[whole(s) for s in shapes],
-        out_shape=[jax.ShapeDtypeStruct(s, BF) for s in shapes],
-        scratch_shapes=[
+        "spectrum_forward",
+        [*recv, fwd, inv, mix, gain],
+        [whole(r.shape) for r in recv] + spectrum_specs(plan, mix, gain),
+        [whole(s) for s in shapes],
+        [jax.ShapeDtypeStruct(s, BF) for s in shapes],
+        (plan.live_t,),
+        [
             pltpu.VMEM((plan.all_rows * plan.rows1, LANES), F32),
             pltpu.VMEM((plan.all_rows * plan.rows2, LANES), F32),
         ],
-        compiler_params=params(),
-        name="spectrum_forward",
-    )(recv, fwd, inv, mix, gain)
+    )
+    return by_device(plan, parts)
 
 
 def spectrum_backward(plan, recvs, fwd, inv, mix, gain):
-    shape = (plan.n, plan.rows, plan.rows1, LANES)
-    return pl.pallas_call(
-        functools.partial(spectrum_backward_kernel, plan, len(recvs)),
-        grid=(plan.live_t,),
-        in_specs=[whole(r.shape) for r in recvs] + spectrum_specs(plan, mix, gain),
-        out_specs=whole(shape),
-        out_shape=jax.ShapeDtypeStruct(shape, BF),
-        scratch_shapes=[
+    shape = (plan.rows, plan.rows1, LANES)
+    flat = [part for parts in recvs for part in parts]
+    return call(
+        functools.partial(spectrum_backward_kernel, plan, len(flat)),
+        "spectrum_backward",
+        [*flat, fwd, inv, mix, gain],
+        [whole(r.shape) for r in flat] + spectrum_specs(plan, mix, gain),
+        [whole(shape)] * plan.n,
+        [jax.ShapeDtypeStruct(shape, BF)] * plan.n,
+        (plan.live_t,),
+        [
             pltpu.VMEM((plan.all_rows * plan.rows2, LANES), F32),
             pltpu.VMEM((plan.all_rows * plan.rows1, LANES), F32),
         ],
-        compiler_params=params(),
-        name="spectrum_backward",
-    )(*recvs, fwd, inv, mix, gain)
+    )
 
 
 def pair_gain(plan, pair, gain):
@@ -552,18 +568,18 @@
         rest = array.shape[1:]
         return pl.BlockSpec((size,) + rest, lambda q: (q,) + (0,) * len(rest))
 
-    return pl.pallas_call(
+    return call(
         kernel,
-        grid=(plan.quads,),
-        in_specs=[whole(a.shape) for a in whole_in]
+        name,
+        [*whole_in, *blocked, *fixed],
+        [whole(a.shape) for a in whole_in]
         + [quad_spec(a) for a in blocked]
         + [whole(a.shape) for a in fixed],
-        out_specs=whole(out_shape) if out_whole else quad_spec(jax.ShapeDtypeStruct(out_shape, BF)),
-        out_shape=jax.ShapeDtypeStruct(out_shape, BF),
-        scratch_shapes=[pltpu.VMEM(scratch, F32)],
-        compiler_params=params(),
-        name=name,
-    )(*whole_in, *blocked, *fixed)
+        whole(out_shape) if out_whole else quad_spec(jax.ShapeDtypeStruct(out_shape, BF)),
+        jax.ShapeDtypeStruct(out_shape, BF),
+        (plan.quads,),
+        [pltpu.VMEM(scratch, F32)],
+    )
 
 
 def high_partial(plan, zonal, fwd):
@@ -598,11 +614,11 @@
 
 
 def predict_kernel(plan, first, live_ref, x_ref, idft_ref, enc_ref, dec_ref, *refs):
-    recv, high, pred_ref, slope_ref, left, field = refs
+    recv, (high, pred_ref, slope_ref, left, field) = refs[: plan.n], refs[plan.n :]
     c = plan.channels
     wide = plan.n * plan.rows2
     for r in range(plan.rb):
-        left[r * c : (r + 1) * c, :wide] = recv[:, r].reshape(wide, LANES).T
+        left[r * c : (r + 1) * c, :wide] = jnp.concatenate([ref[r] for ref in recv], axis=0).T
         left[r * c : (r + 1) * c, wide:] = high[r].T
     field[...] = jnp.dot(left[...], idft_ref[...], preferred_element_type=F32)
     base = first + pl.program_id(0) * plan.rb
@@ -628,34 +644,34 @@
     skip = first // plan.rb
     shape = (count, plan.fpad, plan.lon)
     slope_shape = (count, plan.channels, plan.lon)
-    return pl.pallas_call(
+    return call(
         functools.partial(predict_kernel, plan, first),
-        grid=(count // plan.rb,),
-        in_specs=[
+        "predict",
+        [live, x, idft, enc_t, dec_t, *recv, high],
+        [
             pl.BlockSpec(memory_space=pltpu.SMEM),
             pl.BlockSpec((plan.rb,) + shape[1:], lambda i: (i + skip, 0, 0)),
             whole(idft.shape),
             whole(enc_t.shape),
             whole(dec_t.shape),
-            pl.BlockSpec((plan.n, plan.rb, plan.rows2, LANES), lambda i: (0, i, 0, 0)),
-            pl.BlockSpec((plan.rb,) + high.shape[1:], lambda i: (i + skip, 0, 0)),
-        ],
-        out_specs=[
+        ]
+        + [pl.BlockSpec((plan.rb, plan.rows2, LANES), lambda i: (i, 0, 0))] * plan.n
+        + [pl.BlockSpec((plan.rb,) + high.shape[1:], lambda i: (i + skip, 0, 0))],
+        [
             pl.BlockSpec((plan.rb,) + shape[1:], lambda i: (i, 0, 0)),
             pl.BlockSpec((plan.rb,) + slope_shape[1:], lambda i: (i, 0, 0)),
         ],
-        out_shape=[jax.ShapeDtypeStruct(shape, BF), jax.ShapeDtypeStruct(slope_shape, BF)],
-        scratch_shapes=[
+        [jax.ShapeDtypeStruct(shape, BF), jax.ShapeDtypeStruct(slope_shape, BF)],
+        (count // plan.rb,),
+        [
             pltpu.VMEM((plan.rb * plan.channels, idft.shape[0]), BF),
             pltpu.VMEM((plan.rb * plan.channels, plan.lon), F32),
         ],
-        compiler_params=params(),
-        name="predict",
-    )(live, x, idft, enc_t, dec_t, recv, high)
+    )
 
 
 def score_kernel(plan, first, members, area_ref, own_ref, all_ref, obs_ref, slope_ref, idft_ref, dec_ref, *refs):
-    grad_ref, out, out_high, right = refs
+    grad_ref, outs, (out_high, right) = refs[0], refs[1 : 1 + plan.n], refs[1 + plan.n :]
     c = plan.channels
     base = first + pl.program_id(0) * plan.rb
 
@@ -690,7 +706,7 @@
     low, high = modes(0, wide), modes(wide, idft_ref.shape[0])
     for r in range(plan.rb):
         for o in range(plan.n):
-            out[o, r] = low[o * plan.rows2 : (o + 1) * plan.rows2, r * c : (r + 1) * c]
+            outs[o][r] = low[o * plan.rows2 : (o + 1) * plan.rows2, r * c : (r + 1) * c]
         out_high[r] = high[:, r * c : (r + 1) * c]
 
 
@@ -699,13 +715,14 @@
     skip = first // plan.rb
     members = everyone.shape[0]
     cell = (plan.rb, plan.fpad, plan.lon)
-    out_shape = (plan.n, count, plan.rows2, LANES)
+    out_shape = (count, plan.rows2, LANES)
     high = 4 * plan.pairs
     here = pl.BlockSpec(cell, lambda i: (i, 0, 0))
-    return pl.pallas_call(
+    grad, *outs = call(
         functools.partial(score_kernel, plan, first, members),
-        grid=(count // plan.rb,),
-        in_specs=[
+        "score",
+        [area, own, everyone, observed, slope, idft, dec],
+        [
             pl.BlockSpec(memory_space=pltpu.SMEM),
             here,
             pl.BlockSpec((members,) + cell, lambda i: (0, i, 0, 0)),
@@ -714,31 +731,31 @@
             whole(idft.shape),
             whole(dec.shape),
         ],
-        out_specs=[
-            here,
-            pl.BlockSpec((plan.n, plan.rb, plan.rows2, LANES), lambda i: (0, i, 0, 0)),
-            pl.BlockSpec((plan.rb, high, LANES), lambda i: (i, 0, 0)),
-        ],
-        out_shape=[
-            jax.ShapeDtypeStruct((count,) + cell[1:], BF),
-            jax.ShapeDtypeStruct(out_shape, BF),
-            jax.ShapeDtypeStruct((count, high, LANES), BF),
-        ],
-        scratch_shapes=[pltpu.VMEM((plan.rb * plan.channels, plan.lon), BF)],
-        compiler_params=params(),
-        name="score",
-    )(area, own, everyone, observed, slope, idft, dec)
+        [here]
+        + [pl.BlockSpec((plan.rb, plan.rows2, LANES), lambda i: (i, 0, 0))] * plan.n
+        + [pl.BlockSpec((plan.rb, high, LANES), lambda i: (i, 0, 0))],
+        [jax.ShapeDtypeStruct((count,) + cell[1:], BF)]
+        + [jax.ShapeDtypeStruct(out_shape, BF)] * plan.n
+        + [jax.ShapeDtypeStruct((count, high, LANES), BF)],
+        (count // plan.rb,),
+        [pltpu.VMEM((plan.rb * plan.channels, plan.lon), BF)],
+    )
+    return grad, outs[:-1], outs[-1]
 
 
 def finish_kernel(
-    plan, live_ref, grad_ref, main_ref, rest_ref, through_ref, recv, high_ref, out_ref, left, small, field, field_small
+    plan, live_ref, grad_ref, main_ref, rest_ref, through_ref, *refs
 ):
     n, tp, tb = plan.n, plan.tp, plan.tb
+    recv, (high_ref, out_ref, left, small, field, field_small) = refs[:n], refs[n:]
     wide, tall, quads = n * tp, 2 * plan.pairs, 2 * plan.quad_pad
     for r in range(plan.rb):
-        piece = recv[:, r].astype(F32)
+        piece = [ref[r].astype(F32) for ref in recv]
         high = high_ref[r].astype(F32)
-        mains = [(0, piece[:, :tp].reshape(wide, LANES).T), (2 * wide, high[:tall].T)]
+        mains = [
+            (0, jnp.concatenate([p[:tp] for p in piece], axis=0).T),
+            (2 * wide, high[:tall].T),
+        ]
         for first, main in mains:
             size = main.shape[1]
             for k in range(2):
@@ -748,7 +765,10 @@
                 ].astype(BF)
         at = 0
         rests = [
-            (piece[:, tp + 8 * group : tp + 8 * (group + 1)].reshape(n * 8, LANES), min(4, tb - 4 * group))
+            (
+                jnp.concatenate([p[tp + 8 * group : tp + 8 * (group + 1)] for p in piece], axis=0),
+                min(4, tb - 4 * group),
+            )
             for group in range(plan.rest_groups)
         ] + [(high[tall:], 4)]
         for rest, blocks in rests:
@@ -782,29 +802,29 @@
 def finish(plan, live, grad, main, rest, through, recv, high):
     cell = (plan.rb, plan.fpad, plan.lon)
     here = pl.BlockSpec(cell, lambda i: (i, 0, 0))
-    return pl.pallas_call(
+    return call(
         functools.partial(finish_kernel, plan),
-        grid=(plan.rows // plan.rb,),
-        in_specs=[
+        "finish",
+        [live, grad, main, rest, through, *recv, high],
+        [
             pl.BlockSpec(memory_space=pltpu.SMEM),
             here,
             whole(main.shape),
             whole(rest.shape),
             whole(through.shape),
-            pl.BlockSpec((plan.n, plan.rb, plan.rows1, LANES), lambda i: (0, i, 0, 0)),
-            pl.BlockSpec((plan.rb,) + high.shape[1:], lambda i: (i, 0, 0)),
-        ],
-        out_specs=here,
-        out_shape=jax.ShapeDtypeStruct((plan.rows, plan.fpad, plan.lon), BF),
-        scratch_shapes=[
+        ]
+        + [pl.BlockSpec((plan.rb, plan.rows1, LANES), lambda i: (i, 0, 0))] * plan.n
+        + [pl.BlockSpec((plan.rb,) + high.shape[1:], lambda i: (i, 0, 0))],
+        here,
+        jax.ShapeDtypeStruct((plan.rows, plan.fpad, plan.lon), BF),
+        (plan.rows // plan.rb,),
+        [
             pltpu.VMEM((plan.rb * SPLIT, main.shape[0]), BF),
             pltpu.VMEM((plan.rb * REST, rest.shape[0]), BF),
             pltpu.VMEM((plan.rb * SPLIT, plan.lon), F32),
             pltpu.VMEM((plan.rb * REST, plan.lon), F32),
         ],
-        compiler_params=params(),
-        name="finish",
-    )(live, grad, main, rest, through, recv, high)
+    )
 
 
 def row_geometry(band_rows, band_len, lat_count):
@@ -879,30 +899,36 @@
     low, high = plan.low_orders(), plan.high_orders()
     low_f, high_f = dft_rows(plan, low, False), dft_rows(plan, high, False)
     low_i, high_i = dft_rows(plan, low, True), dft_rows(plan, high, True)
-    dft_low = jnp.asarray(low_f.reshape(2, n * tp, lon))
+
+    def from_here(table):
+        table = jnp.asarray(table)
+        return lax.dynamic_slice_in_dim(jnp.concatenate([table, table]), me, n)
+
+    low_sums = from_here(low_f.transpose(1, 2, 0, 3))
+    low_sums = jnp.transpose(low_sums, (2, 0, 1, 3))
+    dft_low = low_sums.reshape(2, n * tp, lon)
     dft_high = jnp.asarray(high_f.reshape(2, 2 * plan.pairs, lon))
-    idft = jnp.asarray(
-        np.concatenate(
-            [
-                low_i.transpose(1, 0, 2, 3).reshape(n * 2 * tp, lon),
-                high_i.reshape(4 * plan.pairs, lon),
-            ]
-        )
-    )
-    dft_main = jnp.asarray(
-        np.concatenate([low_f.reshape(2 * n * tp, lon), high_f.reshape(4 * plan.pairs, lon)])
-    )
-    low_rest = low_f.reshape(2, n, tb, 8, lon).transpose(2, 0, 1, 3, 4)
+    idft = jnp.concatenate(
+        [
+            from_here(low_i.transpose(1, 0, 2, 3)).reshape(n * 2 * tp, lon),
+            jnp.asarray(high_i.reshape(4 * plan.pairs, lon)),
+        ]
+    )
+    dft_main = jnp.concatenate(
+        [low_sums.reshape(2 * n * tp, lon), jnp.asarray(high_f.reshape(4 * plan.pairs, lon))]
+    )
+    low_rest = jnp.transpose(low_sums.reshape(2, n, tb, 8, lon), (2, 0, 1, 3, 4))
     quads = np.zeros((2, 2, plan.quad_pad, 4, lon), low_f.dtype)
     quads[:, :, : plan.quads] = high_f.reshape(2, 2, plan.quads, 4, lon)
-    dft_rest = jnp.asarray(
-        np.concatenate(
-            [low_rest.reshape(-1, lon), quads.transpose(3, 0, 1, 2, 4).reshape(-1, lon)]
-        )
-    )
-
-    def exchange(block):
-        return lax.all_to_all(block, "space", split_axis=0, concat_axis=0, tiled=True)
+    dft_rest = jnp.concatenate(
+        [low_rest.reshape(-1, lon), jnp.asarray(quads.transpose(3, 0, 1, 2, 4).reshape(-1, lon))]
+    )
+
+    def exchange(parts):
+        got = [parts[0]] + [None] * (n - 1)
+        for s in range(1, n):
+            got[n - s] = lax.ppermute(parts[s], "space", [(i, (i + s) % n) for i in range(n)])
+        return got
 
     recv = exchange(analyse_low(plan, rows, dft_low))
     zonal_high = analyse_high(plan, rows, dft_high)
@@ -929,9 +955,10 @@
     orders = lax.dynamic_index_in_dim(jnp.asarray(low, jnp.int32), me, keepdims=False)
     diagonal = lax.dynamic_index_in_dim(jnp.asarray(log_diagonal(low)), me, keepdims=False)
     orders_wide = jnp.broadcast_to(orders[:, None], (tp, LANES))
-    start = diagonal[:, None] + orders.astype(F32)[:, None] * log_sines[None, :]
+    ordered = [from_here(v.reshape(n, band)).reshape(-1) for v in (cosines, quad, live, log_sines)]
+    start = diagonal[:, None] + orders.astype(F32)[:, None] * ordered[3][None, :]
     low_fwd, low_inv = legendre_tables(
-        orders_wide, jnp.zeros_like(orders_wide), start, cosines, quad, live, plan.degrees
+        orders_wide, jnp.zeros_like(orders_wide), start, *ordered[:3], plan.degrees
     )
 
     spectrum = spectrum_forward(plan, recv, low_fwd, low_inv, mix, gain)
@@ -941,24 +968,34 @@
     gain_long = jnp.stack([longer[s : s + reach] for s in range(8)])
     synth_high = high_synthesis(plan, high_coeffs, high_inv, mix, gain_long)
 
+    def after(value, other):
+        return lax.optimization_barrier((value, other))
+
     predictions, grads, returned, returned_high = [], [], [], []
+    gathered = []
     for i, chunk in enumerate(plan.chunks):
         pred, slope = predict(
             plan, chunk, live_own, rows, idft, enc_t, dec_t, synth[i], synth_high
         )
-        everyone = lax.all_gather(pred[None], "member", axis=0, tiled=True)
+        predictions.append(pred)
+        gathered.append((lax.all_gather(pred[None], "member", axis=0, tiled=True), slope))
+    for i, chunk in enumerate(plan.chunks):
+        pred, (everyone, slope) = predictions[i], gathered[i]
+        if i:
+            pred, returned[i - 1] = after(pred, returned[i - 1])
         grad, out, out_high = score(plan, chunk, area, pred, everyone, truth, slope, idft, dec)
-        predictions.append(pred)
         grads.append(grad)
         returned_high.append(out_high)
         if i == len(plan.chunks) - 1:
             high_grads = high_adjoint(plan, returned_high, high_inv, mix_back, gain_long)
-            out, high_grads = lax.optimization_barrier((out, high_grads))
+            out, high_grads = after(out, high_grads)
             high_grads = lax.psum(high_grads, "space")
         returned.append(exchange(out))
 
-    last = exchange(spectrum_backward(plan, returned, low_fwd, low_inv, mix_back, gain))
+    parts = spectrum_backward(plan, returned, low_fwd, low_inv, mix_back, gain)
+    parts, high_grads = after(parts, high_grads)
     zonal_grad = high_zonal(plan, high_grads, high_fwd)
+    last = exchange(parts)
     state_grad = finish(
         plan, live_own, jnp.concatenate(grads), dft_main, dft_rest, through, last, zonal_grad
     )

time: 931 us -> 857 us (0.921)
  blocking collectives: 296 us -> 0 us
  waiting for transfers between devices: 200 us -> 362 us
  starting transfers between devices: 16.2 us -> 57 us
  local copies, waits for them, and re-layouts: 27.5 us -> 38.3 us
    ppermute x0 -> x56, waiting for transfers between devices: none -> 360 us  [exchange(): lax.ppermute(parts[s], 'space', [(i, (i + s) % n) for i in range(n)])]
    all_to_all x5 -> x0, blocking collectives: 296 us -> none  [exchange(): lax.all_to_all(block, 'space', split_axis=0, concat_axis=0, tiled=True)]
    psum x1, waiting for transfers between devices: 154 us -> 1.94 us  [on_device(): high_grads = lax.psum(high_grads, 'space')]
    ppermute x0 -> x56, starting transfers between devices: none -> 56.8 us  [exchange(): lax.ppermute(parts[s], 'space', [(i, (i + s) % n) for i in range(n)])]
    all_gather x3, waiting for transfers between devices: 31.2 us -> 0.03 us  [on_device(): lax.all_gather(pred[None], 'member', axis=0, tiled=True)]
    all_to_all x3 -> x0, starting transfers between devices: 15.7 us -> none  [exchange(): lax.all_to_all(block, 'space', split_axis=0, concat_axis=0, tiled=True)]
  transfers between devices with their start and end apart: 8 -> 61, of which waited for: 5 -> 33; matrix products, arithmetic and copies ran while one was open for 3% -> 4% of each run, Pallas kernels for 25% -> 34%
where the time goes in v4:
time: 857 us; the launch traced here: 855 us
  Pallas kernels  363 us (42%)
  waiting for transfers between devices  362 us (42%)
  starting transfers between devices  57 us (7%)
  local copies, waits for them, and re-layouts  38.3 us (4%)
  other arithmetic  18.8 us (2%)
  between operations  14.5 us (2%)
    pallas_call x17, Pallas kernels, call(): pl.pallas_call(kernel, grid=grid, in_specs=in_specs, out_specs=out_specs,...  363 us
    ppermute x56, waiting for transfers between devices, exchange(): lax.ppermute(parts[s], 'space', [(i, (i + s) % n) for i in range(n)])  360 us
    ppermute x56, starting transfers between devices, exchange(): lax.ppermute(parts[s], 'space', [(i, (i + s) % n) for i in range(n)])  56.8 us
  transfers between devices with their start and end apart: 61, of which 33 were waited for; matrix products, arithmetic and copies ran while one was open for 4% of the time, Pallas kernels for 34%

profile of v4, /device:TPU:0, one launch (start us, length us, event | category | flops | bytes accessed | tf_op | source)
XLA Modules:
  0.0 854.5 jit_solution(4635247440322418933)
XLA Ops:
  7.2 2.2 dynamic-slice_bitcast_fusion
  9.4 5.9 pad.54.x_ref
  15.4 13.8 %analyse_low.1 = (bf16[49,40,128]{2,1,0:T(8,128)(2,1)}, bf16[49,40,128]{2,1,0:T(8,128)(2,1)}, bf16[49,40,128]{2,1,0:T(8,128)(2,1)}, bf16[49,40,128]{2,1,0:T(8,12...) custom-call(bf16[49,80,720]{2,1,0:T(8,128)(2,1)} %pad.54.x_ref, ...), custom_call_target="tpu_custom_call" | custom-call | bytes 41584640 | tf_op jit(solution)/shard_map/analyse_low/pallas_call | solution.py:91
  29.2 6.0 collective-permute-start
  35.6 3.0 collective-permute-start.3
  40.6 15.0 %analyse_high.1.zonal = bf16[49,112,256]{2,1,0:T(8,128)(2,1)} custom-call(bf16[49,80,720]{2,1,0:T(8,128)(2,1)} %pad.54.x_ref, bf16[2,112,720]{2,1,0:T(8,128)(2,1)} %constant.97.clone.dft_ref), custom_call_target="tpu_custom_call" | custom-call | bytes 35108864 | tf_op jit(solution)/shard_map/analyse_high/pallas_call | solution.py:91
  56.9 21.7 %legendre_tables.3 = (bf16[56,112,128]{2,1,0:T(8,128)(2,1)}, bf16[56,112,128]{2,1,0:T(8,128)(2,1)}) custom-call(f32[56,128]{1,0:T(8,128)} %constant.103.clone.m_ref, f32[56,128]{1,0:T(8,128)} %constant.143.shift_ref, f32[56,128]{1,0:T(8,128)} %multiply_add_fusion.1.start_ref, f32[1,128]{1,0:T(1,128)} %get-tuple-element.255.cos_ref, ...), custom_call_target="tpu_custom_call" | custom-call | bytes 13195264 | tf_op jit(solution)/shard_map/legendre_tables/pallas_call | solution.py:91
  78.6 11.9 %high_partial.1 = bf16[14,5,112,128]{3,2,1,0:T(8,128)(2,1)} custom-call(bf16[49,112,256]{2,1,0:T(8,128)(2,1)} %analyse_high.1.zonal, bf16[56,112,128]{2,1,0:T(8,128)(2,1)} %get-tuple-element.136.fwd), custom_call_target="tpu_custom_call" | custom-call | bytes 25690112 | tf_op jit(solution)/shard_map/high_partial/pallas_call | solution.py:91
  94.3 2.4 fusion.38
  99.5 2.0 copy.38.refs_10_.mix
  104.6 46.7 %legendre_tables.2 = (bf16[32,368,392]{2,1,0:T(8,128)(2,1)}, bf16[32,368,392]{2,1,0:T(8,128)(2,1)}) custom-call(f32[32,128]{1,0:T(8,128)} %broadcast_in_dim.46.m_ref, f32[32,128]{1,0:T(8,128)} %convert_element_type.65.shift_ref, f32[32,512]{1,0:T(8,128)} %pad.57.start_ref, f32[1,512]{1,0:T(1,128)} %bitcast.98, f32[1,512]{1,0:T(1,128)} %bitcast.99, ...), custom_call_target="tpu_custom_call" | custom-call | bytes 74276864 | tf_op jit(solution)/shard_map/legendre_tables/pallas_call | solution.py:91
  155.8 16.3 %collective-permute-done.5.refs_6_ = bf16[49,40,128]{2,1,0:T(8,128)(2,1)S(1)} collective-permute-done((bf16[49,40,128]{2,1,0:T(8,128)(2,1)}, bf16[49,40,128]{2,1,0:T(8,128)(2,1)S(1)}, u32[]{:S(2)}, u32[]{:S(2)}) %collective-permute-start.5) | collective-permute-done | bytes 501792 | tf_op jit(solution)/shard_map/ppermute | solution.py:930
  172.0 10.9 %collective-permute-done.6.refs_7_ = bf16[49,40,128]{2,1,0:T(8,128)(2,1)} collective-permute-done((bf16[49,40,128]{2,1,0:T(8,128)(2,1)}, bf16[49,40,128]{2,1,0:T(8,128)(2,1)}, u32[]{:S(2)}, u32[]{:S(2)}) %collective-permute-start.6) | collective-permute-done | bytes 501792 | tf_op jit(solution)/shard_map/ppermute | solution.py:930
  183.0 50.1 %spectrum_forward.1 = (bf16[7,64,128]{2,1,0:T(8,128)(2,1)}, bf16[7,64,128]{2,1,0:T(8,128)(2,1)}, bf16[7,64,128]{2,1,0:T(8,128)(2,1)}, bf16[7,64,128]{2,1,0:T(8,1...) custom-call(bf16[49,40,128]{2,1,0:T(8,128)(2,1)} %get-tuple-element., ...), custom_call_target="tpu_custom_call" | custom-call | bytes 119209984 | tf_op jit(solution)/shard_map/spectrum_forward/pallas_call | solution.py:91
  234.1 3.6 collective-permute-start.13
  237.7 3.2 collective-permute-start.7
  240.9 2.8 collective-permute-done.10.refs_4_
  243.7 4.2 collective-permute-done.11.refs_5_
  249.2 16.0 %high_synthesis.1.refs_8_ = bf16[49,224,128]{2,1,0:T(8,128)(2,1)} custom-call(bf16[14,5,112,128]{3,2,1,0:T(8,128)(2,1)} %all-reduce.18.cloned.1.call-done.coeffs, bf16[56,112,128]{2,1,0:T(8,128)(2,1)} %get-tuple-element.137.inv.refs_3_, bf16[4,256,256]{2,1,0:T(8,128)(2,1)} %copy.38.refs_10_.mix, f32[8,424,128]{2,1,0:T(8,128)} %copy-done.5), custom_call_target="tpu_custom_call" | custom-call | bytes 34734080 | tf_op jit(solution)/shard_map/high_synthesis/pallas_call | solution.py:91
  266.0 7.7 predict.3
  275.4 2.9 collective-permute-start.16
  278.3 2.9 collective-permute-start.18
  281.1 2.8 collective-permute-done.14.refs_1_
  285.3 4.6 collective-permute-done.15.refs_2_
  289.8 7.5 collective-permute-done.16.refs_3_
  297.4 38.9 %collective-permute-done.17.refs_4_ = bf16[21,64,128]{2,1,0:T(8,128)(2,1)S(1)} collective-permute-done((bf16[21,64,128]{2,1,0:T(8,128)(2,1)}, bf16[21,64,128]{2,1,0:T(8,128)(2,1)S(1)}, u32[]{:S(2)}, u32[]{:S(2)}) %collective-permute-start.17) | collective-permute-done | bytes 344096 | tf_op jit(solution)/shard_map/ppermute | solution.py:930
  337.3 17.0 %predict.4 = (bf16[21,80,720]{2,1,0:T(8,128)(2,1)}, bf16[21,128,720]{2,1,0:T(8,128)(2,1)}) custom-call(f32[49]{0:T(128)} %copy-done.52, bf16[49,80,720]{2,1,0:T(8,128)(2,1)} %pad.54.x_ref, bf16[736,720]{1,0:T(8,128)(2,1)} %pad_maximum_fusion.4.idft_ref, bf16[128,80]{1,0:T(8,128)(2,1)} %pad.55.enc_ref, bf16[80,128]{1,0:T(8,128)(2,1)} %pad.56.dec_ref, ...), custom_call_target="tpu_custom_call" | custom-call | bytes 74392336 | tf_op jit(solution)/shard_map/predict/pallas_call | solution.py:91
  356.8 2.9 collective-permute-start.24
  359.7 5.7 collective-permute-done.21.refs_1_
  365.4 5.9 collective-permute-done.22.refs_2_
  371.3 7.5 collective-permute-done.23.refs_3_
  378.7 36.4 %collective-permute-done.24.refs_4_ = bf16[21,64,128]{2,1,0:T(8,128)(2,1)S(1)} collective-permute-done((bf16[21,64,128]{2,1,0:T(8,128)(2,1)}, bf16[21,64,128]{2,1,0:T(8,128)(2,1)S(1)}, u32[]{:S(2)}, u32[]{:S(2)}) %collective-permute-start.24) | collective-permute-done | bytes 344096 | tf_op jit(solution)/shard_map/ppermute | solution.py:930
  417.3 17.0 %predict.5 = (bf16[21,80,720]{2,1,0:T(8,128)(2,1)}, bf16[21,128,720]{2,1,0:T(8,128)(2,1)}) custom-call(f32[49]{0:T(128)} %copy-done.52, bf16[49,80,720]{2,1,0:T(8,128)(2,1)} %pad.54.x_ref, bf16[736,720]{1,0:T(8,128)(2,1)} %pad_maximum_fusion.4.idft_ref, bf16[128,80]{1,0:T(8,128)(2,1)} %pad.55.enc_ref, bf16[80,128]{1,0:T(8,128)(2,1)} %pad.56.dec_ref, ...), custom_call_target="tpu_custom_call" | custom-call | bytes 74392336 | tf_op jit(solution)/shard_map/predict/pallas_call | solution.py:91
  434.5 6.4 pad.66.obs_ref
  441.5 10.6 %score.3 = (bf16[7,80,720]{2,1,0:T(8,128)(2,1)}, bf16[7,64,128]{2,1,0:T(8,128)(2,1)}, bf16[7,64,128]{2,1,0:T(8,128)(2,1)}, bf16[7,64,128]{2,1,0:T(8,128)(2,1)}, ...) custom-call(f32[49]{0:T(128)} %get-tuple-element.236.area_ref, ...), custom_call_target="tpu_custom_call" | custom-call | bytes 56691472 | tf_op jit(solution)/shard_map/score/pallas_call | solution.py:91
  453.0 3.5 collective-permute-start.31
  458.6 2.1 collective-permute-start.34
  461.7 10.7 %collective-permute-done.31.refs_4_ = bf16[7,64,128]{2,1,0:T(8,128)(2,1)} collective-permute-done((bf16[7,64,128]{2,1,0:T(8,128)(2,1)}, bf16[7,64,128]{2,1,0:T(8,128)(2,1)}, u32[]{:S(2)}, u32[]{:S(2)}) %collective-permute-start.31) | collective-permute-done | bytes 114720 | tf_op jit(solution)/shard_map/ppermute | solution.py:930
  473.6 19.1 %score.4 = (bf16[21,80,720]{2,1,0:T(8,128)(2,1)}, bf16[21,64,128]{2,1,0:T(8,128)(2,1)}, bf16[21,64,128]{2,1,0:T(8,128)(2,1)}, bf16[21,64,128]{2,1,0:T(8,128)(2,1...) custom-call(f32[49]{0:T(128)} %get-tuple-element.236.area_ref, ...), custom_call_target="tpu_custom_call" | custom-call | bytes 116271888 | tf_op jit(solution)/shard_map/score/pallas_call | solution.py:91
  494.2 2.3 collective-permute-start.37
  498.5 4.6 collective-permute-done.35.refs_9_
  503.1 5.9 collective-permute-done.36.refs_10_
  509.0 7.4 collective-permute-done.37.refs_11_
  516.4 38.8 %collective-permute-done.38.refs_12_ = bf16[21,64,128]{2,1,0:T(8,128)(2,1)} collective-permute-done((bf16[21,64,128]{2,1,0:T(8,128)(2,1)}, bf16[21,64,128]{2,1,0:T(8,128)(2,1)}, u32[]{:S(2)}, u32[]{:S(2)}) %collective-permute-start.38) | collective-permute-done | bytes 344096 | tf_op jit(solution)/shard_map/ppermute | solution.py:930
  556.4 19.0 %score.5 = (bf16[21,80,720]{2,1,0:T(8,128)(2,1)}, bf16[21,64,128]{2,1,0:T(8,128)(2,1)}, bf16[21,64,128]{2,1,0:T(8,128)(2,1)}, bf16[21,64,128]{2,1,0:T(8,128)(2,1...) custom-call(f32[49]{0:T(128)} %get-tuple-element.236.area_ref, ...), custom_call_target="tpu_custom_call" | custom-call | bytes 116271888 | tf_op jit(solution)/shard_map/score/pallas_call | solution.py:91
  575.5 14.4 %high_adjoint.1 = bf16[14,5,112,128]{3,2,1,0:T(8,128)(2,1)} custom-call(bf16[7,224,128]{2,1,0:T(8,128)(2,1)} %get-tuple-element.205.refs_0_, bf16[21,224,128]{2,1,0:T(8,128)(2,1)} %get-tuple-element.206.refs_1_, bf16[21,224,128]{2,1,0:T(8,128)(2,1)} %get-tuple-element.207.refs_2_, bf16[56,112,128]{2,1,0:T(8,128)(2,1)} %get-tuple-element.137.inv.refs_3_, ...), custom_call_target="tpu_custom_call" | custom-call | bytes 34734080 | tf_op jit(solution)/shard_map/high_adjoint/pallas_call | solution.py:91
  591.0 3.5 collective-permute-start.45
  594.4 11.6 %collective-permute-done.42.refs_17_ = bf16[21,64,128]{2,1,0:T(8,128)(2,1)S(1)} collective-permute-done((bf16[21,64,128]{2,1,0:T(8,128)(2,1)S(1)}, bf16[21,64,128]{2,1,0:T(8,128)(2,1)S(1)}, u32[]{:S(2)}, u32[]{:S(2)}) %collective-permute-start.42) | collective-permute-done | bytes 344096 | tf_op jit(solution)/shard_map/ppermute | solution.py:930
  606.0 13.4 %collective-permute-done.43.refs_18_ = bf16[21,64,128]{2,1,0:T(8,128)(2,1)} collective-permute-done((bf16[21,64,128]{2,1,0:T(8,128)(2,1)S(1)}, bf16[21,64,128]{2,1,0:T(8,128)(2,1)}, u32[]{:S(2)}, u32[]{:S(2)}) %collective-permute-start.43) | collective-permute-done | bytes 344096 | tf_op jit(solution)/shard_map/ppermute | solution.py:930
  620.4 13.8 %collective-permute-done.44.refs_19_ = bf16[21,64,128]{2,1,0:T(8,128)(2,1)S(1)} collective-permute-done((bf16[21,64,128]{2,1,0:T(8,128)(2,1)S(1)}, bf16[21,64,128]{2,1,0:T(8,128)(2,1)S(1)}, u32[]{:S(2)}, u32[]{:S(2)}) %collective-permute-start.44) | collective-permute-done | bytes 344096 | tf_op jit(solution)/shard_map/ppermute | solution.py:930
  634.2 39.2 %collective-permute-done.45.refs_20_ = bf16[21,64,128]{2,1,0:T(8,128)(2,1)S(1)} collective-permute-done((bf16[21,64,128]{2,1,0:T(8,128)(2,1)S(1)}, bf16[21,64,128]{2,1,0:T(8,128)(2,1)S(1)}, u32[]{:S(2)}, u32[]{:S(2)}) %collective-permute-start.45) | collective-permute-done | bytes 344096 | tf_op jit(solution)/shard_map/ppermute | solution.py:930
  673.3 3.7 collective-permute-done.46.refs_21_
  678.5 50.8 %spectrum_backward.1 = (bf16[49,40,128]{2,1,0:T(8,128)(2,1)}, bf16[49,40,128]{2,1,0:T(8,128)(2,1)}, bf16[49,40,128]{2,1,0:T(8,128)(2,1)}, bf16[49,40,128]{2,1,0:...) custom-call(bf16[7,64,128]{2,1,0:T(8,128)(2,1)} %get-tuple-element.1, ...), custom_call_target="tpu_custom_call" | custom-call | bytes 119209984 | tf_op jit(solution)/shard_map/spectrum_backward/pallas_call | solution.py:91
  731.3 2.2 collective-permute-start.49
  735.8 2.3 pad_maximum_fusion.5.main_ref
  739.2 2.1 collective-permute-start.52
  742.1 3.6 collective-permute-done.49.refs_1_
  745.7 10.7 %collective-permute-done.50.refs_2_ = bf16[49,40,128]{2,1,0:T(8,128)(2,1)} collective-permute-done((bf16[49,40,128]{2,1,0:T(8,128)(2,1)}, bf16[49,40,128]{2,1,0:T(8,128)(2,1)}, u32[]{:S(2)}, u32[]{:S(2)}) %collective-permute-start.50) | collective-permute-done | bytes 501792 | tf_op jit(solution)/shard_map/ppermute | solution.py:930
  756.4 3.4 fusion
  759.8 3.5 pad_maximum_fusion.2.grad_ref
  763.3 11.3 %high_zonal.1.refs_8_ = bf16[49,144,128]{2,1,0:T(8,128)(2,1)} custom-call(bf16[14,5,112,128]{3,2,1,0:T(8,128)(2,1)} %all-reduce.20.cloned.1.call-done.grads, bf16[56,112,128]{2,1,0:T(8,128)(2,1)} %get-tuple-element.136.fwd), custom_call_target="tpu_custom_call" | custom-call | bytes 21676032 | tf_op jit(solution)/shard_map/high_zonal/pallas_call | solution.py:91
  774.6 46.3 %collective-permute-done.52.refs_4_ = bf16[49,40,128]{2,1,0:T(8,128)(2,1)} collective-permute-done((bf16[49,40,128]{2,1,0:T(8,128)(2,1)}, bf16[49,40,128]{2,1,0:T(8,128)(2,1)}, u32[]{:S(2)}, u32[]{:S(2)}) %collective-permute-start.52) | collective-permute-done | bytes 501792 | tf_op jit(solution)/shard_map/ppermute | solution.py:930
  821.1 21.1 %finish.1 = bf16[49,80,720]{2,1,0:T(8,128)(2,1)} custom-call(f32[49]{0:T(128)} %copy-done.52, bf16[49,80,720]{2,1,0:T(8,128)(2,1)} %pad_maximum_fusion.2.grad_ref, bf16[736,720]{1,0:T(8,128)(2,1)} %pad_maximum_fusion.5.main_ref, bf16[768,720]{1,0:T(8,128)(2,1)} %pad_maximum_fusion.3.rest_ref, bf16[80,80]{1,0:T(8,128)(2,1)} %pad.68.through_ref, ...), custom_call_target="tpu_custom_call" | custom-call | bytes 77155088 | tf_op jit(solution)/shard_map/finish/pallas_call | solution.py:91
  842.3 5.7 slice_bitcast_fusion
  (287 shorter events, 50.0 us)
Async XLA Ops:
  7.2 85.6 %copy-start = (bf16[128,128]{1,0:T(8,128)(2,1)S(1)}, bf16[128,128]{1,0:T(8,128)(2,1)}, u32[]{:S(2)}) copy-start(bf16[128,128]{1,0:T(8,128)(2,1)} %param.25) | copy-start | bytes 98308
  7.2 240.8 %all-reduce.18.cloned.1.call-start = ((), (), s32[]{:S(2)}) async-start(), calls=%async_computation | async-start | bytes 4014080 | tf_op jit(solution)/shard_map/psum | solution.py:953
  29.2 122.3 %collective-permute-start = (bf16[49,40,128]{2,1,0:T(8,128)(2,1)}, bf16[49,40,128]{2,1,0:T(8,128)(2,1)}, u32[]{:S(2)}, u32[]{:S(2)}) collective-permute-start(bf16[49,40,128]{2,1,0:T(8,128)(2,1)} %get-tuple-element.119), channel_id=1, source_target_pairs={{0,7},{1,0},{2,1},{3,2},{4,3},{5,4},{6,5},{7,6},{8,15},{9,8},{10,9... | collective-permute-start | bytes 1505288 | tf_op jit(solution)/shard_map/ppermute | solution.py:930
  35.2 118.2 %collective-permute-start.1 = (bf16[49,40,128]{2,1,0:T(8,128)(2,1)}, bf16[49,40,128]{2,1,0:T(8,128)(2,1)}, u32[]{:S(2)}, u32[]{:S(2)}) collective-permute-start(bf16[49,40,128]{2,1,0:T(8,128)(2,1)} %get-tuple-element.120), channel_id=1, source_target_pairs={{0,6},{1,7},{2,0},{3,1},{4,2},{5,3},{6,4},{7,5},{8,14},{9,15},{10,... | collective-permute-start | bytes 1505288 | tf_op jit(solution)/shard_map/ppermute | solution.py:930
  35.6 120.2 %collective-permute-start.2 = (bf16[49,40,128]{2,1,0:T(8,128)(2,1)}, bf16[49,40,128]{2,1,0:T(8,128)(2,1)}, u32[]{:S(2)}, u32[]{:S(2)}) collective-permute-start(bf16[49,40,128]{2,1,0:T(8,128)(2,1)} %get-tuple-element.121), channel_id=1, source_target_pairs={{0,5},{1,6},{2,7},{3,0},{4,1},{5,2},{6,3},{7,4},{8,13},{9,14},{10,... | collective-permute-start | bytes 1505288 | tf_op jit(solution)/shard_map/ppermute | solution.py:930
  35.6 120.2 %collective-permute-start.3 = (bf16[49,40,128]{2,1,0:T(8,128)(2,1)}, bf16[49,40,128]{2,1,0:T(8,128)(2,1)}, u32[]{:S(2)}, u32[]{:S(2)}) collective-permute-start(bf16[49,40,128]{2,1,0:T(8,128)(2,1)} %get-tuple-element.122), channel_id=1, source_target_pairs={{0,4},{1,5},{2,6},{3,7},{4,0},{5,1},{6,2},{7,3},{8,12},{9,13},{10,... | collective-permute-start | bytes 1505288 | tf_op jit(solution)/shard_map/ppermute | solution.py:930
  38.6 117.2 %collective-permute-start.4 = (bf16[49,40,128]{2,1,0:T(8,128)(2,1)}, bf16[49,40,128]{2,1,0:T(8,128)(2,1)}, u32[]{:S(2)}, u32[]{:S(2)}) collective-permute-start(bf16[49,40,128]{2,1,0:T(8,128)(2,1)} %get-tuple-element.123), channel_id=1, source_target_pairs={{0,3},{1,4},{2,5},{3,6},{4,7},{5,0},{6,1},{7,2},{8,11},{9,12},{10,... | collective-permute-start | bytes 1505288 | tf_op jit(solution)/shard_map/ppermute | solution.py:930
  90.4 351.0 %all-gather.7.cloned.1.call-start = ((), (), s32[]{:S(2)}) async-start(), calls=%async_computation.2 | async-start | bytes 4300800 | tf_op jit(solution)/shard_map/all_gather | solution.py:981
  151.5 20.6 %collective-permute-start.5 = (bf16[49,40,128]{2,1,0:T(8,128)(2,1)}, bf16[49,40,128]{2,1,0:T(8,128)(2,1)S(1)}, u32[]{:S(2)}, u32[]{:S(2)}) collective-permute-start(bf16[49,40,128]{2,1,0:T(8,128)(2,1)} %get-tuple-element.124), channel_id=1, source_target_pairs={{0,2},{1,3},{2,4},{3,5},{4,6},{5,7},{6,0},{7,1},{8,10},{9,11},{10,... | collective-permute-start | bytes 1505288 | tf_op jit(solution)/shard_map/ppermute | solution.py:930
  153.4 29.6 %collective-permute-start.6 = (bf16[49,40,128]{2,1,0:T(8,128)(2,1)}, bf16[49,40,128]{2,1,0:T(8,128)(2,1)}, u32[]{:S(2)}, u32[]{:S(2)}) collective-permute-start(bf16[49,40,128]{2,1,0:T(8,128)(2,1)} %get-tuple-element.125), channel_id=1, source_target_pairs={{0,1},{1,2},{2,3},{3,4},{4,5},{5,6},{6,7},{7,0},{8,9},{9,10},{10,1... | collective-permute-start | bytes 1505288 | tf_op jit(solution)/shard_map/ppermute | solution.py:930
  233.1 10.6 %collective-permute-start.10 = (bf16[7,64,128]{2,1,0:T(8,128)(2,1)}, bf16[7,64,128]{2,1,0:T(8,128)(2,1)S(1)}, u32[]{:S(2)}, u32[]{:S(2)}) collective-permute-start(bf16[7,64,128]{2,1,0:T(8,128)(2,1)} %get-tuple-element.132), channel_id=1, source_target_pairs={{0,4},{1,5},{2,6},{3,7},{4,0},{5,1},{6,2},{7,3},{8,12},{9,13},{10,... | collective-permute-start | bytes 344072 | tf_op jit(solution)/shard_map/ppermute | solution.py:930
  233.7 14.2 %collective-permute-start.11 = (bf16[7,64,128]{2,1,0:T(8,128)(2,1)}, bf16[7,64,128]{2,1,0:T(8,128)(2,1)S(1)}, u32[]{:S(2)}, u32[]{:S(2)}) collective-permute-start(bf16[7,64,128]{2,1,0:T(8,128)(2,1)} %get-tuple-element.133), channel_id=1, source_target_pairs={{0,3},{1,4},{2,5},{3,6},{4,7},{5,0},{6,1},{7,2},{8,11},{9,12},{10,... | collective-permute-start | bytes 344072 | tf_op jit(solution)/shard_map/ppermute | solution.py:930
  233.7 31.5 %collective-permute-start.12 = (bf16[7,64,128]{2,1,0:T(8,128)(2,1)}, bf16[7,64,128]{2,1,0:T(8,128)(2,1)S(1)}, u32[]{:S(2)}, u32[]{:S(2)}) collective-permute-start(bf16[7,64,128]{2,1,0:T(8,128)(2,1)} %get-tuple-element.134), channel_id=1, source_target_pairs={{0,2},{1,3},{2,4},{3,5},{4,6},{5,7},{6,0},{7,1},{8,10},{9,11},{10,... | collective-permute-start | bytes 344072 | tf_op jit(solution)/shard_map/ppermute | solution.py:930
  234.1 31.2 %collective-permute-start.13 = (bf16[7,64,128]{2,1,0:T(8,128)(2,1)}, bf16[7,64,128]{2,1,0:T(8,128)(2,1)S(1)}, u32[]{:S(2)}, u32[]{:S(2)}) collective-permute-start(bf16[7,64,128]{2,1,0:T(8,128)(2,1)} %get-tuple-element.135), channel_id=1, source_target_pairs={{0,1},{1,2},{2,3},{3,4},{4,5},{5,6},{6,7},{7,0},{8,9},{9,10},{10,1... | collective-permute-start | bytes 344072 | tf_op jit(solution)/shard_map/ppermute | solution.py:930
  237.7 27.6 %collective-permute-start.7 = (bf16[7,64,128]{2,1,0:T(8,128)(2,1)}, bf16[7,64,128]{2,1,0:T(8,128)(2,1)S(1)}, u32[]{:S(2)}, u32[]{:S(2)}) collective-permute-start(bf16[7,64,128]{2,1,0:T(8,128)(2,1)} %get-tuple-element.129), channel_id=1, source_target_pairs={{0,7},{1,0},{2,1},{3,2},{4,3},{5,4},{6,5},{7,6},{8,15},{9,8},{10,9... | collective-permute-start | bytes 344072 | tf_op jit(solution)/shard_map/ppermute | solution.py:930
  243.7 21.6 %collective-permute-start.8 = (bf16[7,64,128]{2,1,0:T(8,128)(2,1)}, bf16[7,64,128]{2,1,0:T(8,128)(2,1)S(1)}, u32[]{:S(2)}, u32[]{:S(2)}) collective-permute-start(bf16[7,64,128]{2,1,0:T(8,128)(2,1)} %get-tuple-element.130), channel_id=1, source_target_pairs={{0,6},{1,7},{2,0},{3,1},{4,2},{5,3},{6,4},{7,5},{8,14},{9,15},{10,... | collective-permute-start | bytes 344072 | tf_op jit(solution)/shard_map/ppermute | solution.py:930
  248.0 17.4 %collective-permute-start.9 = (bf16[7,64,128]{2,1,0:T(8,128)(2,1)}, bf16[7,64,128]{2,1,0:T(8,128)(2,1)}, u32[]{:S(2)}, u32[]{:S(2)}) collective-permute-start(bf16[7,64,128]{2,1,0:T(8,128)(2,1)} %get-tuple-element.131), channel_id=1, source_target_pairs={{0,5},{1,6},{2,7},{3,0},{4,1},{5,2},{6,3},{7,4},{8,13},{9,14},{10,... | collective-permute-start | bytes 344072 | tf_op jit(solution)/shard_map/ppermute | solution.py:930
  273.7 199.8 %all-gather.9.cloned.1.call-start = ((), (), s32[]{:S(2)}) async-start(), calls=%async_computation.3 | async-start | bytes 12902400 | tf_op jit(solution)/shard_map/all_gather | solution.py:981
  273.8 10.1 %collective-permute-start.14 = (bf16[21,64,128]{2,1,0:T(8,128)(2,1)S(1)}, bf16[21,64,128]{2,1,0:T(8,128)(2,1)S(1)}, u32[]{:S(2)}, u32[]{:S(2)}) collective-permute-start(bf16[21,64,128]{2,1,0:T(8,128)(2,1)S(1)} %copy-done.61), channel_id=1, source_target_pairs={{0,7},{1,0},{2,1},{3,2},{4,3},{5,4},{6,5},{7,6},{8,15},{9,8},{10,9... | collective-permute-start | bytes 1032200 | tf_op jit(solution)/shard_map/ppermute | solution.py:930
  273.9 16.0 %collective-permute-start.15 = (bf16[21,64,128]{2,1,0:T(8,128)(2,1)S(1)}, bf16[21,64,128]{2,1,0:T(8,128)(2,1)S(1)}, u32[]{:S(2)}, u32[]{:S(2)}) collective-permute-start(bf16[21,64,128]{2,1,0:T(8,128)(2,1)S(1)} %copy-done.60), channel_id=1, source_target_pairs={{0,6},{1,7},{2,0},{3,1},{4,2},{5,3},{6,4},{7,5},{8,14},{9,15},{10,... | collective-permute-start | bytes 1032200 | tf_op jit(solution)/shard_map/ppermute | solution.py:930
  275.4 22.0 %collective-permute-start.16 = (bf16[21,64,128]{2,1,0:T(8,128)(2,1)}, bf16[21,64,128]{2,1,0:T(8,128)(2,1)S(1)}, u32[]{:S(2)}, u32[]{:S(2)}) collective-permute-start(bf16[21,64,128]{2,1,0:T(8,128)(2,1)} %get-tuple-element.142), channel_id=1, source_target_pairs={{0,5},{1,6},{2,7},{3,0},{4,1},{5,2},{6,3},{7,4},{8,13},{9,14},{10,... | collective-permute-start | bytes 1032200 | tf_op jit(solution)/shard_map/ppermute | solution.py:930
  278.3 58.0 %collective-permute-start.17 = (bf16[21,64,128]{2,1,0:T(8,128)(2,1)}, bf16[21,64,128]{2,1,0:T(8,128)(2,1)S(1)}, u32[]{:S(2)}, u32[]{:S(2)}) collective-permute-start(bf16[21,64,128]{2,1,0:T(8,128)(2,1)} %get-tuple-element.143), channel_id=1, source_target_pairs={{0,4},{1,5},{2,6},{3,7},{4,0},{5,1},{6,2},{7,3},{8,12},{9,13},{10,... | collective-permute-start | bytes 1032200 | tf_op jit(solution)/shard_map/ppermute | solution.py:930
  278.3 58.0 %collective-permute-start.18 = (bf16[21,64,128]{2,1,0:T(8,128)(2,1)}, bf16[21,64,128]{2,1,0:T(8,128)(2,1)S(1)}, u32[]{:S(2)}, u32[]{:S(2)}) collective-permute-start(bf16[21,64,128]{2,1,0:T(8,128)(2,1)} %get-tuple-element.144), channel_id=1, source_target_pairs={{0,3},{1,4},{2,5},{3,6},{4,7},{5,0},{6,1},{7,2},{8,11},{9,12},{10,... | collective-permute-start | bytes 1032200 | tf_op jit(solution)/shard_map/ppermute | solution.py:930
  283.9 52.4 %collective-permute-start.19 = (bf16[21,64,128]{2,1,0:T(8,128)(2,1)}, bf16[21,64,128]{2,1,0:T(8,128)(2,1)S(1)}, u32[]{:S(2)}, u32[]{:S(2)}) collective-permute-start(bf16[21,64,128]{2,1,0:T(8,128)(2,1)} %get-tuple-element.145), channel_id=1, source_target_pairs={{0,2},{1,3},{2,4},{3,5},{4,6},{5,7},{6,0},{7,1},{8,10},{9,11},{10,... | collective-permute-start | bytes 1032200 | tf_op jit(solution)/shard_map/ppermute | solution.py:930
  289.8 46.5 %collective-permute-start.20 = (bf16[21,64,128]{2,1,0:T(8,128)(2,1)}, bf16[21,64,128]{2,1,0:T(8,128)(2,1)S(1)}, u32[]{:S(2)}, u32[]{:S(2)}) collective-permute-start(bf16[21,64,128]{2,1,0:T(8,128)(2,1)} %get-tuple-element.146), channel_id=1, source_target_pairs={{0,1},{1,2},{2,3},{3,4},{4,5},{5,6},{6,7},{7,0},{8,9},{9,10},{10,1... | collective-permute-start | bytes 1032200 | tf_op jit(solution)/shard_map/ppermute | solution.py:930
  354.4 202.0 %all-gather.11.cloned.1.call-start = ((), (), s32[]{:S(2)}) async-start(), calls=%async_computation.4 | async-start | bytes 12902400 | tf_op jit(solution)/shard_map/all_gather | solution.py:981
  355.3 10.1 %collective-permute-start.21 = (bf16[21,64,128]{2,1,0:T(8,128)(2,1)S(1)}, bf16[21,64,128]{2,1,0:T(8,128)(2,1)S(1)}, u32[]{:S(2)}, u32[]{:S(2)}) collective-permute-start(bf16[21,64,128]{2,1,0:T(8,128)(2,1)S(1)} %copy-done.59), channel_id=1, source_target_pairs={{0,7},{1,0},{2,1},{3,2},{4,3},{5,4},{6,5},{7,6},{8,15},{9,8},{10,9... | collective-permute-start | bytes 1032200 | tf_op jit(solution)/shard_map/ppermute | solution.py:930
  355.4 15.9 %collective-permute-start.22 = (bf16[21,64,128]{2,1,0:T(8,128)(2,1)S(1)}, bf16[21,64,128]{2,1,0:T(8,128)(2,1)S(1)}, u32[]{:S(2)}, u32[]{:S(2)}) collective-permute-start(bf16[21,64,128]{2,1,0:T(8,128)(2,1)S(1)} %copy-done.58), channel_id=1, source_target_pairs={{0,6},{1,7},{2,0},{3,1},{4,2},{5,3},{6,4},{7,5},{8,14},{9,15},{10,... | collective-permute-start | bytes 1032200 | tf_op jit(solution)/shard_map/ppermute | solution.py:930
  356.4 22.4 %collective-permute-start.23 = (bf16[21,64,128]{2,1,0:T(8,128)(2,1)}, bf16[21,64,128]{2,1,0:T(8,128)(2,1)S(1)}, u32[]{:S(2)}, u32[]{:S(2)}) collective-permute-start(bf16[21,64,128]{2,1,0:T(8,128)(2,1)} %get-tuple-element.151), channel_id=1, source_target_pairs={{0,5},{1,6},{2,7},{3,0},{4,1},{5,2},{6,3},{7,4},{8,13},{9,14},{10,... | collective-permute-start | bytes 1032200 | tf_op jit(solution)/shard_map/ppermute | solution.py:930
  356.8 58.4 %collective-permute-start.24 = (bf16[21,64,128]{2,1,0:T(8,128)(2,1)}, bf16[21,64,128]{2,1,0:T(8,128)(2,1)S(1)}, u32[]{:S(2)}, u32[]{:S(2)}) collective-permute-start(bf16[21,64,128]{2,1,0:T(8,128)(2,1)} %get-tuple-element.152), channel_id=1, source_target_pairs={{0,4},{1,5},{2,6},{3,7},{4,0},{5,1},{6,2},{7,3},{8,12},{9,13},{10,... | collective-permute-start | bytes 1032200 | tf_op jit(solution)/shard_map/ppermute | solution.py:930
  359.7 56.7 %collective-permute-start.25 = (bf16[21,64,128]{2,1,0:T(8,128)(2,1)}, bf16[21,64,128]{2,1,0:T(8,128)(2,1)S(1)}, u32[]{:S(2)}, u32[]{:S(2)}) collective-permute-start(bf16[21,64,128]{2,1,0:T(8,128)(2,1)} %get-tuple-element.153), channel_id=1, source_target_pairs={{0,3},{1,4},{2,5},{3,6},{4,7},{5,0},{6,1},{7,2},{8,11},{9,12},{10,... | collective-permute-start | bytes 1032200 | tf_op jit(solution)/shard_map/ppermute | solution.py:930
  365.4 51.0 %collective-permute-start.26 = (bf16[21,64,128]{2,1,0:T(8,128)(2,1)S(1)}, bf16[21,64,128]{2,1,0:T(8,128)(2,1)S(1)}, u32[]{:S(2)}, u32[]{:S(2)}) collective-permute-start(bf16[21,64,128]{2,1,0:T(8,128)(2,1)S(1)} %copy-done.57), channel_id=1, source_target_pairs={{0,2},{1,3},{2,4},{3,5},{4,6},{5,7},{6,0},{7,1},{8,10},{9,11},{10,... | collective-permute-start | bytes 1032200 | tf_op jit(solution)/shard_map/ppermute | solution.py:930
  371.3 45.1 %collective-permute-start.27 = (bf16[21,64,128]{2,1,0:T(8,128)(2,1)S(1)}, bf16[21,64,128]{2,1,0:T(8,128)(2,1)S(1)}, u32[]{:S(2)}, u32[]{:S(2)}) collective-permute-start(bf16[21,64,128]{2,1,0:T(8,128)(2,1)S(1)} %copy-done.56), channel_id=1, source_target_pairs={{0,1},{1,2},{2,3},{3,4},{4,5},{5,6},{6,7},{7,0},{8,9},{9,10},{10,1... | collective-permute-start | bytes 1032200 | tf_op jit(solution)/shard_map/ppermute | solution.py:930
  434.3 297.0 %all-reduce.20.cloned.1.call-start = ((), (), s32[]{:S(2)}) async-start(), calls=%async_computation.1 | async-start | bytes 4014080 | tf_op jit(solution)/shard_map/psum | solution.py:992
  452.1 6.2 collective-permute-start.28
  452.1 6.5 collective-permute-start.29
  452.5 9.1 %collective-permute-start.30 = (bf16[7,64,128]{2,1,0:T(8,128)(2,1)}, bf16[7,64,128]{2,1,0:T(8,128)(2,1)}, u32[]{:S(2)}, u32[]{:S(2)}) collective-permute-start(bf16[7,64,128]{2,1,0:T(8,128)(2,1)} %get-tuple-element.162), channel_id=1, source_target_pairs={{0,5},{1,6},{2,7},{3,0},{4,1},{5,2},{6,3},{7,4},{8,13},{9,14},{10,... | collective-permute-start | bytes 344072 | tf_op jit(solution)/shard_map/ppermute | solution.py:930
  453.0 19.4 %collective-permute-start.31 = (bf16[7,64,128]{2,1,0:T(8,128)(2,1)}, bf16[7,64,128]{2,1,0:T(8,128)(2,1)}, u32[]{:S(2)}, u32[]{:S(2)}) collective-permute-start(bf16[7,64,128]{2,1,0:T(8,128)(2,1)} %get-tuple-element.163), channel_id=1, source_target_pairs={{0,4},{1,5},{2,6},{3,7},{4,0},{5,1},{6,2},{7,3},{8,12},{9,13},{10,... | collective-permute-start | bytes 344072 | tf_op jit(solution)/shard_map/ppermute | solution.py:930
  456.5 17.0 %collective-permute-start.32 = (bf16[7,64,128]{2,1,0:T(8,128)(2,1)}, bf16[7,64,128]{2,1,0:T(8,128)(2,1)}, u32[]{:S(2)}, u32[]{:S(2)}) collective-permute-start(bf16[7,64,128]{2,1,0:T(8,128)(2,1)} %get-tuple-element.164), channel_id=1, source_target_pairs={{0,3},{1,4},{2,5},{3,6},{4,7},{5,0},{6,1},{7,2},{8,11},{9,12},{10,... | collective-permute-start | bytes 344072 | tf_op jit(solution)/shard_map/ppermute | solution.py:930
  458.3 15.2 %collective-permute-start.33 = (bf16[7,64,128]{2,1,0:T(8,128)(2,1)}, bf16[7,64,128]{2,1,0:T(8,128)(2,1)}, u32[]{:S(2)}, u32[]{:S(2)}) collective-permute-start(bf16[7,64,128]{2,1,0:T(8,128)(2,1)} %get-tuple-element.165), channel_id=1, source_target_pairs={{0,2},{1,3},{2,4},{3,5},{4,6},{5,7},{6,0},{7,1},{8,10},{9,11},{10,... | collective-permute-start | bytes 344072 | tf_op jit(solution)/shard_map/ppermute | solution.py:930
  458.6 14.9 %collective-permute-start.34 = (bf16[7,64,128]{2,1,0:T(8,128)(2,1)}, bf16[7,64,128]{2,1,0:T(8,128)(2,1)}, u32[]{:S(2)}, u32[]{:S(2)}) collective-permute-start(bf16[7,64,128]{2,1,0:T(8,128)(2,1)} %get-tuple-element.166), channel_id=1, source_target_pairs={{0,1},{1,2},{2,3},{3,4},{4,5},{5,6},{6,7},{7,0},{8,9},{9,10},{10,1... | collective-permute-start | bytes 344072 | tf_op jit(solution)/shard_map/ppermute | solution.py:930
  492.7 10.5 %collective-permute-start.35 = (bf16[21,64,128]{2,1,0:T(8,128)(2,1)}, bf16[21,64,128]{2,1,0:T(8,128)(2,1)}, u32[]{:S(2)}, u32[]{:S(2)}) collective-permute-start(bf16[21,64,128]{2,1,0:T(8,128)(2,1)} %get-tuple-element.171), channel_id=1, source_target_pairs={{0,7},{1,0},{2,1},{3,2},{4,3},{5,4},{6,5},{7,6},{8,15},{9,8},{10,9... | collective-permute-start | bytes 1032200 | tf_op jit(solution)/shard_map/ppermute | solution.py:930
  492.7 16.3 %collective-permute-start.36 = (bf16[21,64,128]{2,1,0:T(8,128)(2,1)}, bf16[21,64,128]{2,1,0:T(8,128)(2,1)}, u32[]{:S(2)}, u32[]{:S(2)}) collective-permute-start(bf16[21,64,128]{2,1,0:T(8,128)(2,1)} %get-tuple-element.172), channel_id=1, source_target_pairs={{0,6},{1,7},{2,0},{3,1},{4,2},{5,3},{6,4},{7,5},{8,14},{9,15},{10,... | collective-permute-start | bytes 1032200 | tf_op jit(solution)/shard_map/ppermute | solution.py:930
  494.2 22.2 %collective-permute-start.37 = (bf16[21,64,128]{2,1,0:T(8,128)(2,1)}, bf16[21,64,128]{2,1,0:T(8,128)(2,1)}, u32[]{:S(2)}, u32[]{:S(2)}) collective-permute-start(bf16[21,64,128]{2,1,0:T(8,128)(2,1)} %get-tuple-element.173), channel_id=1, source_target_pairs={{0,5},{1,6},{2,7},{3,0},{4,1},{5,2},{6,3},{7,4},{8,13},{9,14},{10,... | collective-permute-start | bytes 1032200 | tf_op jit(solution)/shard_map/ppermute | solution.py:930
  496.5 58.7 %collective-permute-start.38 = (bf16[21,64,128]{2,1,0:T(8,128)(2,1)}, bf16[21,64,128]{2,1,0:T(8,128)(2,1)}, u32[]{:S(2)}, u32[]{:S(2)}) collective-permute-start(bf16[21,64,128]{2,1,0:T(8,128)(2,1)} %get-tuple-element.174), channel_id=1, source_target_pairs={{0,4},{1,5},{2,6},{3,7},{4,0},{5,1},{6,2},{7,3},{8,12},{9,13},{10,... | collective-permute-start | bytes 1032200 | tf_op jit(solution)/shard_map/ppermute | solution.py:930
  497.1 59.3 %collective-permute-start.39 = (bf16[21,64,128]{2,1,0:T(8,128)(2,1)}, bf16[21,64,128]{2,1,0:T(8,128)(2,1)}, u32[]{:S(2)}, u32[]{:S(2)}) collective-permute-start(bf16[21,64,128]{2,1,0:T(8,128)(2,1)} %get-tuple-element.175), channel_id=1, source_target_pairs={{0,3},{1,4},{2,5},{3,6},{4,7},{5,0},{6,1},{7,2},{8,11},{9,12},{10,... | collective-permute-start | bytes 1032200 | tf_op jit(solution)/shard_map/ppermute | solution.py:930
  503.1 53.2 %collective-permute-start.40 = (bf16[21,64,128]{2,1,0:T(8,128)(2,1)}, bf16[21,64,128]{2,1,0:T(8,128)(2,1)}, u32[]{:S(2)}, u32[]{:S(2)}) collective-permute-start(bf16[21,64,128]{2,1,0:T(8,128)(2,1)} %get-tuple-element.176), channel_id=1, source_target_pairs={{0,2},{1,3},{2,4},{3,5},{4,6},{5,7},{6,0},{7,1},{8,10},{9,11},{10,... | collective-permute-start | bytes 1032200 | tf_op jit(solution)/shard_map/ppermute | solution.py:930
  509.0 47.4 %collective-permute-start.41 = (bf16[21,64,128]{2,1,0:T(8,128)(2,1)}, bf16[21,64,128]{2,1,0:T(8,128)(2,1)}, u32[]{:S(2)}, u32[]{:S(2)}) collective-permute-start(bf16[21,64,128]{2,1,0:T(8,128)(2,1)} %get-tuple-element.177), channel_id=1, source_target_pairs={{0,1},{1,2},{2,3},{3,4},{4,5},{5,6},{6,7},{7,0},{8,9},{9,10},{10,1... | collective-permute-start | bytes 1032200 | tf_op jit(solution)/shard_map/ppermute | solution.py:930
  589.9 16.1 %collective-permute-start.42 = (bf16[21,64,128]{2,1,0:T(8,128)(2,1)S(1)}, bf16[21,64,128]{2,1,0:T(8,128)(2,1)S(1)}, u32[]{:S(2)}, u32[]{:S(2)}) collective-permute-start(bf16[21,64,128]{2,1,0:T(8,128)(2,1)S(1)} %copy-done.68), channel_id=1, source_target_pairs={{0,7},{1,0},{2,1},{3,2},{4,3},{5,4},{6,5},{7,6},{8,15},{9,8},{10,9... | collective-permute-start | bytes 1032200 | tf_op jit(solution)/shard_map/ppermute | solution.py:930
  590.0 29.4 %collective-permute-start.43 = (bf16[21,64,128]{2,1,0:T(8,128)(2,1)S(1)}, bf16[21,64,128]{2,1,0:T(8,128)(2,1)}, u32[]{:S(2)}, u32[]{:S(2)}) collective-permute-start(bf16[21,64,128]{2,1,0:T(8,128)(2,1)S(1)} %copy-done.67), channel_id=1, source_target_pairs={{0,6},{1,7},{2,0},{3,1},{4,2},{5,3},{6,4},{7,5},{8,14},{9,15},{10,... | collective-permute-start | bytes 1032200 | tf_op jit(solution)/shard_map/ppermute | solution.py:930
  590.9 43.2 %collective-permute-start.44 = (bf16[21,64,128]{2,1,0:T(8,128)(2,1)S(1)}, bf16[21,64,128]{2,1,0:T(8,128)(2,1)S(1)}, u32[]{:S(2)}, u32[]{:S(2)}) collective-permute-start(bf16[21,64,128]{2,1,0:T(8,128)(2,1)S(1)} %copy-done.66), channel_id=1, source_target_pairs={{0,5},{1,6},{2,7},{3,0},{4,1},{5,2},{6,3},{7,4},{8,13},{9,14},{10,... | collective-permute-start | bytes 1032200 | tf_op jit(solution)/shard_map/ppermute | solution.py:930
  591.0 82.4 %collective-permute-start.45 = (bf16[21,64,128]{2,1,0:T(8,128)(2,1)S(1)}, bf16[21,64,128]{2,1,0:T(8,128)(2,1)S(1)}, u32[]{:S(2)}, u32[]{:S(2)}) collective-permute-start(bf16[21,64,128]{2,1,0:T(8,128)(2,1)S(1)} %copy-done.65), channel_id=1, source_target_pairs={{0,4},{1,5},{2,6},{3,7},{4,0},{5,1},{6,2},{7,3},{8,12},{9,13},{10,... | collective-permute-start | bytes 1032200 | tf_op jit(solution)/shard_map/ppermute | solution.py:930
  594.4 82.6 %collective-permute-start.46 = (bf16[21,64,128]{2,1,0:T(8,128)(2,1)S(1)}, bf16[21,64,128]{2,1,0:T(8,128)(2,1)S(1)}, u32[]{:S(2)}, u32[]{:S(2)}) collective-permute-start(bf16[21,64,128]{2,1,0:T(8,128)(2,1)S(1)} %copy-done.64), channel_id=1, source_target_pairs={{0,3},{1,4},{2,5},{3,6},{4,7},{5,0},{6,1},{7,2},{8,11},{9,12},{10,... | collective-permute-start | bytes 1032200 | tf_op jit(solution)/shard_map/ppermute | solution.py:930
  606.0 71.0 %collective-permute-start.47 = (bf16[21,64,128]{2,1,0:T(8,128)(2,1)S(1)}, bf16[21,64,128]{2,1,0:T(8,128)(2,1)S(1)}, u32[]{:S(2)}, u32[]{:S(2)}) collective-permute-start(bf16[21,64,128]{2,1,0:T(8,128)(2,1)S(1)} %copy-done.63), channel_id=1, source_target_pairs={{0,2},{1,3},{2,4},{3,5},{4,6},{5,7},{6,0},{7,1},{8,10},{9,11},{10,... | collective-permute-start | bytes 1032200 | tf_op jit(solution)/shard_map/ppermute | solution.py:930
  619.4 59.1 %collective-permute-start.48 = (bf16[21,64,128]{2,1,0:T(8,128)(2,1)S(1)}, bf16[21,64,128]{2,1,0:T(8,128)(2,1)}, u32[]{:S(2)}, u32[]{:S(2)}) collective-permute-start(bf16[21,64,128]{2,1,0:T(8,128)(2,1)S(1)} %copy-done.62), channel_id=1, source_target_pairs={{0,1},{1,2},{2,3},{3,4},{4,5},{5,6},{6,7},{7,0},{8,9},{9,10},{10,1... | collective-permute-start | bytes 1032200 | tf_op jit(solution)/shard_map/ppermute | solution.py:930
  620.4 115.4 %copy-start.7 = (bf16[8,32,2,720]{3,1,0,2:T(8,128)(2,1)S(1)}, bf16[8,32,2,720]{3,1,0,2:T(8,128)(2,1)}, u32[]{:S(2)}) copy-start(bf16[8,32,2,720]{3,1,0,2:T(8,128)(2,1)} %get-tuple-element.245) | copy-start | bytes 2211844
  678.5 77.9 %copy-start.3 = (bf16[21,80,720]{2,1,0:T(8,128)(2,1)S(1)}, bf16[21,80,720]{2,1,0:T(8,128)(2,1)}, u32[]{:S(2)}) copy-start(bf16[21,80,720]{2,1,0:T(8,128)(2,1)} %get-tuple-element.178.own_ref) | copy-start | bytes 7257604
  731.3 14.4 %collective-permute-start.49 = (bf16[49,40,128]{2,1,0:T(8,128)(2,1)}, bf16[49,40,128]{2,1,0:T(8,128)(2,1)S(1)}, u32[]{:S(2)}, u32[]{:S(2)}) collective-permute-start(bf16[49,40,128]{2,1,0:T(8,128)(2,1)} %get-tuple-element.226), channel_id=1, source_target_pairs={{0,7},{1,0},{2,1},{3,2},{4,3},{5,4},{6,5},{7,6},{8,15},{9,8},{10,9... | collective-permute-start | bytes 1505288 | tf_op jit(solution)/shard_map/ppermute | solution.py:930
  733.5 23.0 %collective-permute-start.50 = (bf16[49,40,128]{2,1,0:T(8,128)(2,1)}, bf16[49,40,128]{2,1,0:T(8,128)(2,1)}, u32[]{:S(2)}, u32[]{:S(2)}) collective-permute-start(bf16[49,40,128]{2,1,0:T(8,128)(2,1)} %get-tuple-element.227), channel_id=1, source_target_pairs={{0,6},{1,7},{2,0},{3,1},{4,2},{5,3},{6,4},{7,5},{8,14},{9,15},{10,... | collective-permute-start | bytes 1505288 | tf_op jit(solution)/shard_map/ppermute | solution.py:930
  739.2 35.4 %collective-permute-start.51 = (bf16[49,40,128]{2,1,0:T(8,128)(2,1)}, bf16[49,40,128]{2,1,0:T(8,128)(2,1)S(1)}, u32[]{:S(2)}, u32[]{:S(2)}) collective-permute-start(bf16[49,40,128]{2,1,0:T(8,128)(2,1)} %get-tuple-element.228), channel_id=1, source_target_pairs={{0,5},{1,6},{2,7},{3,0},{4,1},{5,2},{6,3},{7,4},{8,13},{9,14},{10,... | collective-permute-start | bytes 1505288 | tf_op jit(solution)/shard_map/ppermute | solution.py:930
  739.2 81.6 %collective-permute-start.52 = (bf16[49,40,128]{2,1,0:T(8,128)(2,1)}, bf16[49,40,128]{2,1,0:T(8,128)(2,1)}, u32[]{:S(2)}, u32[]{:S(2)}) collective-permute-start(bf16[49,40,128]{2,1,0:T(8,128)(2,1)} %get-tuple-element.229), channel_id=1, source_target_pairs={{0,4},{1,5},{2,6},{3,7},{4,0},{5,1},{6,2},{7,3},{8,12},{9,13},{10,... | collective-permute-start | bytes 1505288 | tf_op jit(solution)/shard_map/ppermute | solution.py:930
  741.3 79.8 %collective-permute-start.53 = (bf16[49,40,128]{2,1,0:T(8,128)(2,1)}, bf16[49,40,128]{2,1,0:T(8,128)(2,1)}, u32[]{:S(2)}, u32[]{:S(2)}) collective-permute-start(bf16[49,40,128]{2,1,0:T(8,128)(2,1)} %get-tuple-element.230), channel_id=1, source_target_pairs={{0,3},{1,4},{2,5},{3,6},{4,7},{5,0},{6,1},{7,2},{8,11},{9,12},{10,... | collective-permute-start | bytes 1505288 | tf_op jit(solution)/shard_map/ppermute | solution.py:930
  745.7 75.4 %collective-permute-start.54 = (bf16[49,40,128]{2,1,0:T(8,128)(2,1)}, bf16[49,40,128]{2,1,0:T(8,128)(2,1)}, u32[]{:S(2)}, u32[]{:S(2)}) collective-permute-start(bf16[49,40,128]{2,1,0:T(8,128)(2,1)} %get-tuple-element.231), channel_id=1, source_target_pairs={{0,2},{1,3},{2,4},{3,5},{4,6},{5,7},{6,0},{7,1},{8,10},{9,11},{10,... | collective-permute-start | bytes 1505288 | tf_op jit(solution)/shard_map/ppermute | solution.py:930
  756.4 64.7 %collective-permute-start.55 = (bf16[49,40,128]{2,1,0:T(8,128)(2,1)}, bf16[49,40,128]{2,1,0:T(8,128)(2,1)}, u32[]{:S(2)}, u32[]{:S(2)}) collective-permute-start(bf16[49,40,128]{2,1,0:T(8,128)(2,1)} %get-tuple-element.232), channel_id=1, source_target_pairs={{0,1},{1,2},{2,3},{3,4},{4,5},{5,6},{6,7},{7,0},{8,9},{9,10},{10,1... | collective-permute-start | bytes 1505288 | tf_op jit(solution)/shard_map/ppermute | solution.py:930
  (66 other events, 1052.2 us)
Sparse Core Ops, SparseCore 0:
  90.6 121.3 all-reduce.17
  273.9 29.7 all-gather.6
  354.5 66.5 all-gather.8
  434.4 66.6 all-gather.10
  590.0 141.2 all-reduce.19

commit v5 on v4

--- a/solution.py
+++ b/solution.py
@@ -40,6 +40,7 @@
         self.rows1 = self.tp + 8 * self.rest_groups
         self.rows2 = 2 * self.tp
         self.low = space * self.live_t
+        self.step = max(k for k in (1, 2, 4) if self.live_t % k == 0)
         self.high = LMAX + 1 - self.low
         self.pairs = ceil_to(-(-self.high // 2), 8)
         self.quads = self.pairs // 4
@@ -105,55 +106,55 @@
     return pl.BlockSpec(shape, lambda *_: (0,) * len(shape))
 
 
-def table_kernel(m_ref, shift_ref, start_ref, cos_ref, quad_ref, live_ref, fwd_ref, inv_ref, one, two, logs, stage):
-    block = pl.program_id(1)
+def table_kernel(m_ref, shift_ref, start_ref, cos_ref, quad_ref, live_ref, fwd_ref, inv_ref, stage):
     lanes = fwd_ref.shape[2]
     order, shift = m_ref[...], shift_ref[...]
-
-    @pl.when(block == 0)
-    def _():
-        one[...] = jnp.zeros_like(one)
-        two[...] = jnp.zeros_like(two)
-        logs[...] = start_ref[...]
-
-    ups, backs, pasts, onsets, keeps = [], [], [], [], []
-    for p in range(16):
-        deg = shift + (block * 16 + p).astype(F32)
-        ups.append(
-            jnp.sqrt((4.0 * deg * deg - 1.0) / jnp.maximum(deg * deg - order * order, 1.0))
-        )
-        less = (deg - 1.0) * (deg - 1.0)
-        backs.append(
-            jnp.sqrt(
-                jnp.maximum(less - order * order, 0.0) / jnp.maximum(4.0 * less - 1.0, 1.0)
-            )
-        )
-        pasts.append(order < deg)
-        onsets.append(jnp.where(order == deg, 1.0, 0.0))
-        keeps.append((order <= deg) & (deg <= LMAX))
-    for c in range(one.shape[1] // LANES):
-        at = slice(c * LANES, (c + 1) * LANES)
-        first, second, log_scale = one[:, at], two[:, at], logs[:, at]
-        cosine = cos_ref[:, at]
-        scale = jnp.exp(log_scale)
+    square = order * order
+    parts = [slice(c, c + LANES) for c in range(0, start_ref.shape[1], LANES)]
+
+    def block(index, state):
+        before = state[0]
+        at_row = pl.multiple_of(index * 16, 16)
+        ups, backs, pasts, onsets, keeps = [], [], [], [], []
         for p in range(16):
-            current = jnp.where(
-                pasts[p], ups[p] * (cosine * first - backs[p] * second), onsets[p]
-            )
-            stage[c, pl.ds(p, 8, stride=16), :] = jnp.where(keeps[p], current * scale, 0.0)
-            second = first
-            first = current
-        size = jnp.maximum(jnp.abs(first), jnp.abs(second))
-        factor = jnp.where(size > 1.0, size, 1.0)
-        one[:, at] = first / factor
-        two[:, at] = second / factor
-        logs[:, at] = log_scale + jnp.log(factor)
-        width = min(LANES, lanes - c * LANES)
-        out = slice(c * LANES, c * LANES + width)
-        for i in range(8):
-            values = stage[c, i * 16 : (i + 1) * 16, :]
-            fwd_ref[i, :, out] = (values * quad_ref[:, at]).astype(BF)[:, :width]
-            inv_ref[i, :, out] = (values * live_ref[:, at]).astype(BF)[:, :width]
+            deg = shift + (index * 16 + p).astype(F32)
+            ratio = jnp.maximum((deg * deg - square) / (4.0 * deg * deg - 1.0), 0.0)
+            root = lax.rsqrt(jnp.maximum(ratio, 1e-20))
+            ups.append(root)
+            backs.append(before)
+            before = ratio * root
+            pasts.append(order < deg)
+            onsets.append(jnp.where(order == deg, 1.0, 0.0))
+            keeps.append(deg <= LMAX)
+        after = [before]
+        for c, at in enumerate(parts):
+            first, second, log_scale = state[1 + 3 * c : 4 + 3 * c]
+            cosine = cos_ref[:, at]
+            scale = jnp.exp(log_scale)
+            for p in range(16):
+                current = jnp.where(
+                    pasts[p], ups[p] * (cosine * first - backs[p] * second), onsets[p]
+                )
+                stage[c, pl.ds(p, 8, stride=16), :] = jnp.where(keeps[p], current * scale, 0.0)
+                second = first
+                first = current
+            size = jnp.maximum(jnp.abs(first), jnp.abs(second))
+            factor = jnp.where(size > 1.0, size, 1.0)
+            after += [first / factor, second / factor, log_scale + jnp.log(factor)]
+        for c, at in enumerate(parts):
+            width = min(LANES, lanes - c * LANES)
+            out = slice(c * LANES, c * LANES + width)
+            for i in range(8):
+                values = stage[c, i * 16 : (i + 1) * 16, :]
+                fwd_ref[i, pl.ds(at_row, 16), out] = (values * quad_ref[:, at]).astype(BF)[:, :width]
+                inv_ref[i, pl.ds(at_row, 16), out] = (values * live_ref[:, at]).astype(BF)[:, :width]
+        return tuple(after)
+
+    zero = jnp.zeros((8, LANES), F32)
+    state = [zero]
+    for at in parts:
+        state += [zero, zero, start_ref[:, at]]
+    lax.fori_loop(0, fwd_ref.shape[1] // 16, block, tuple(state))
 
 
 def legendre_tables(orders, shift, log_start, cosines, quad, live, degrees):
@@ -165,9 +166,9 @@
         return jnp.pad(row, (0, wide - rows))[None]
 
     shape = jax.ShapeDtypeStruct((tp, degrees, rows), BF)
-    row_spec = pl.BlockSpec((1, wide), lambda i, j: (0, 0))
-    lane_spec = pl.BlockSpec((8, LANES), lambda i, j: (i, 0))
-    out_spec = pl.BlockSpec((8, 16, rows), lambda i, j: (i, j, 0))
+    row_spec = whole((1, wide))
+    lane_spec = pl.BlockSpec((8, LANES), lambda i: (i, 0))
+    out_spec = pl.BlockSpec((8, degrees, rows), lambda i: (i, 0, 0))
     return call(
         table_kernel,
         "legendre_tables",
@@ -182,20 +183,15 @@
         [
             lane_spec,
             lane_spec,
-            pl.BlockSpec((8, wide), lambda i, j: (i, 0)),
+            pl.BlockSpec((8, wide), lambda i: (i, 0)),
             row_spec,
             row_spec,
             row_spec,
         ],
         [out_spec, out_spec],
         [shape, shape],
-        (tp // 8, degrees // 16),
-        [
-            pltpu.VMEM((8, wide), F32),
-            pltpu.VMEM((8, wide), F32),
-            pltpu.VMEM((8, wide), F32),
-            pltpu.VMEM((wide // LANES, 128, LANES), F32),
-        ],
+        (tp // 8,),
+        [pltpu.VMEM((wide // LANES, 128, LANES), F32)],
     )
 
 
@@ -302,32 +298,34 @@
 def spectrum_forward_kernel(plan, *refs):
     recv, (fwd, inv, mix, gain) = refs[: plan.n], refs[plan.n : plan.n + 4]
     outs, zin, yout = refs[plan.n + 4 : -2], refs[-2], refs[-1]
-    t = pl.program_id(0)
-
-    @pl.when(t == 0)
+    step = pl.program_id(0)
+
+    @pl.when(step == 0)
     def _():
         unpack(plan, [recv], zin, plan.rows1)
         if plan.live_t < plan.tp:
             yout[...] = jnp.zeros_like(yout)
 
-    z = jnp.concatenate(
-        [
-            zin[pl.ds(t, plan.all_rows, stride=plan.rows1), :],
-            zin[pl.ds(rest_row(plan, t), plan.all_rows, stride=plan.rows1), :],
-        ],
-        axis=1,
-    ).astype(BF)
-    coeffs = jnp.dot(fwd[0], z, preferred_element_type=F32).astype(BF)
-    filtered = (jnp.dot(coeffs, mix[0], preferred_element_type=F32) * gain[...]).astype(BF)
-    y = lax.dot_general(
-        inv[0], filtered, (((0,), (0,)), ((), ())), preferred_element_type=F32
-    )
-    for k in range(2):
-        yout[pl.ds(k * plan.tp + t, plan.all_rows, stride=plan.rows2), :] = y[
-            :, k * LANES : (k + 1) * LANES
-        ]
-
-    @pl.when(t == plan.live_t - 1)
+    for i in range(plan.step):
+        t = step * plan.step + i
+        z = jnp.concatenate(
+            [
+                zin[pl.ds(t, plan.all_rows, stride=plan.rows1), :],
+                zin[pl.ds(rest_row(plan, t), plan.all_rows, stride=plan.rows1), :],
+            ],
+            axis=1,
+        ).astype(BF)
+        coeffs = jnp.dot(fwd[i], z, preferred_element_type=F32).astype(BF)
+        filtered = (jnp.dot(coeffs, mix[0], preferred_element_type=F32) * gain[...]).astype(BF)
+        y = lax.dot_general(
+            inv[i], filtered, (((0,), (0,)), ((), ())), preferred_element_type=F32
+        )
+        for k in range(2):
+            yout[pl.ds(k * plan.tp + t, plan.all_rows, stride=plan.rows2), :] = y[
+                :, k * LANES : (k + 1) * LANES
+            ]
+
+    @pl.when(step == plan.live_t // plan.step - 1)
     def _():
         repack(plan, by_device(plan, outs), yout, plan.rows2)
 
@@ -336,35 +334,37 @@
     recvs = refs[:count]
     fwd, inv, mix, gain = refs[count : count + 4]
     outs, zin, yout = refs[count + 4 : -2], refs[-2], refs[-1]
-    t = pl.program_id(0)
-
-    @pl.when(t == 0)
+    step = pl.program_id(0)
+
+    @pl.when(step == 0)
     def _():
         unpack(plan, by_device(plan, recvs), zin, plan.rows2)
         yout[...] = jnp.zeros_like(yout)
 
-    z = jnp.concatenate(
-        [
-            zin[pl.ds(k * plan.tp + t, plan.all_rows, stride=plan.rows2), :]
-            for k in range(2)
-        ],
-        axis=1,
-    ).astype(BF)
-    grad = (jnp.dot(inv[0], z, preferred_element_type=F32) * gain[...]).astype(BF)
-    back = jnp.dot(grad, mix[0], preferred_element_type=F32).astype(BF)
-    y = lax.dot_general(fwd[0], back, (((0,), (0,)), ((), ())), preferred_element_type=F32)
-    yout[pl.ds(t, plan.all_rows, stride=plan.rows1), :] = y[:, :LANES]
-    where = pl.ds(rest_row(plan, t), plan.all_rows, stride=plan.rows1)
-    yout[where, :] = yout[where, :] + y[:, LANES:]
-
-    @pl.when(t == plan.live_t - 1)
+    for i in range(plan.step):
+        t = step * plan.step + i
+        z = jnp.concatenate(
+            [
+                zin[pl.ds(k * plan.tp + t, plan.all_rows, stride=plan.rows2), :]
+                for k in range(2)
+            ],
+            axis=1,
+        ).astype(BF)
+        grad = (jnp.dot(inv[i], z, preferred_element_type=F32) * gain[...]).astype(BF)
+        back = jnp.dot(grad, mix[0], preferred_element_type=F32).astype(BF)
+        y = lax.dot_general(fwd[i], back, (((0,), (0,)), ((), ())), preferred_element_type=F32)
+        yout[pl.ds(t, plan.all_rows, stride=plan.rows1), :] = y[:, :LANES]
+        where = pl.ds(rest_row(plan, t), plan.all_rows, stride=plan.rows1)
+        yout[where, :] = yout[where, :] + y[:, LANES:]
+
+    @pl.when(step == plan.live_t // plan.step - 1)
     def _():
         repack(plan, [outs], yout, plan.rows1)
 
 
 def spectrum_specs(plan, mix, gain):
-    table = pl.BlockSpec((1, plan.degrees, plan.all_rows), lambda t: (t, 0, 0))
-    return [table, table, pl.BlockSpec((1,) + mix.shape[1:], lambda t: ((t // 8) % 4, 0, 0)), whole(gain.shape)]
+    table = pl.BlockSpec((plan.step, plan.degrees, plan.all_rows), lambda t: (t, 0, 0))
+    return [table, table, pl.BlockSpec((1,) + mix.shape[1:], lambda t: ((t * plan.step // 8) % 4, 0, 0)), whole(gain.shape)]
 
 
 def spectrum_forward(plan, recv, fwd, inv, mix, gain):
@@ -376,7 +376,7 @@
         [whole(r.shape) for r in recv] + spectrum_specs(plan, mix, gain),
         [whole(s) for s in shapes],
         [jax.ShapeDtypeStruct(s, BF) for s in shapes],
-        (plan.live_t,),
+        (plan.live_t // plan.step,),
         [
             pltpu.VMEM((plan.all_rows * plan.rows1, LANES), F32),
             pltpu.VMEM((plan.all_rows * plan.rows2, LANES), F32),
@@ -395,7 +395,7 @@
         [whole(r.shape) for r in flat] + spectrum_specs(plan, mix, gain),
         [whole(shape)] * plan.n,
         [jax.ShapeDtypeStruct(shape, BF)] * plan.n,
-        (plan.live_t,),
+        (plan.live_t // plan.step,),
         [
             pltpu.VMEM((plan.all_rows * plan.rows2, LANES), F32),
             pltpu.VMEM((plan.all_rows * plan.rows1, LANES), F32),
@@ -926,7 +926,7 @@
 
     def exchange(parts):
         got = [parts[0]] + [None] * (n - 1)
-        for s in range(1, n):
+        for s in sorted(range(1, n), key=lambda s: abs(2 * s - n)):
             got[n - s] = lax.ppermute(parts[s], "space", [(i, (i + s) % n) for i in range(n)])
         return got
 
@@ -974,8 +974,11 @@
     predictions, grads, returned, returned_high = [], [], [], []
     gathered = []
     for i, chunk in enumerate(plan.chunks):
+        live_now = live_own
+        if i == 1:
+            live_now, truth = after(live_own, truth)
         pred, slope = predict(
-            plan, chunk, live_own, rows, idft, enc_t, dec_t, synth[i], synth_high
+            plan, chunk, live_now, rows, idft, enc_t, dec_t, synth[i], synth_high
         )
         predictions.append(pred)
         gathered.append((lax.all_gather(pred[None], "member", axis=0, tiled=True), slope))
@@ -993,7 +996,8 @@
         returned.append(exchange(out))
 
     parts = spectrum_backward(plan, returned, low_fwd, low_inv, mix_back, gain)
-    parts, high_grads = after(parts, high_grads)
+    ends, high_grads = after([parts[1], parts[n - 1]], high_grads)
+    parts = [parts[0], ends[0], *parts[2 : n - 1], ends[1]]
     zonal_grad = high_zonal(plan, high_grads, high_fwd)
     last = exchange(parts)
     state_grad = finish(

time: 857 us -> 828 us (0.966)
  Pallas kernels: 363 us -> 295 us
  starting transfers between devices: 57 us -> 119 us
  waiting for transfers between devices: 362 us -> 338 us
    pallas_call x17, Pallas kernels: 363 us -> 295 us  [call(): pl.pallas_call(kernel, grid=grid, in_specs=in_specs, out_specs=out_specs,...]
    ppermute x56, starting transfers between devices: 56.8 us -> 119 us  [exchange(): lax.ppermute(parts[s], 'space', [(i, (i + s) % n) for i in range(n)])]
    ppermute x56, waiting for transfers between devices: 360 us -> 311 us  [exchange(): lax.ppermute(parts[s], 'space', [(i, (i + s) % n) for i in range(n)])]
    psum x1, waiting for transfers between devices: 0.02 us -> 17 us  [on_device(): high_coeffs = lax.psum(high_partial(plan, zonal_high, high_fwd), 'space')]
  transfers between devices with their start and end apart: 61 -> 61, of which waited for: 33 -> 33; matrix products, arithmetic and copies ran while one was open for 4% -> 5% of each run, Pallas kernels for 34% -> 26%
where the time goes in v5:
time: 828 us; the launch traced here: 826 us
  waiting for transfers between devices  338 us (41%)
  Pallas kernels  295 us (36%)
  starting transfers between devices  119 us (14%)
  local copies, waits for them, and re-layouts  38.9 us (5%)
  other arithmetic  19.3 us (2%)
  between operations  14.6 us (2%)
    ppermute x56, waiting for transfers between devices, exchange(): lax.ppermute(parts[s], 'space', [(i, (i + s) % n) for i in range(n)])  311 us
    pallas_call x17, Pallas kernels, call(): pl.pallas_call(kernel, grid=grid, in_specs=in_specs, out_specs=out_specs,...  295 us
    ppermute x56, starting transfers between devices, exchange(): lax.ppermute(parts[s], 'space', [(i, (i + s) % n) for i in range(n)])  119 us
    psum x1, waiting for transfers between devices, on_device(): high_coeffs = lax.psum(high_partial(plan, zonal_high, high_fwd), 'space')  17 us
  transfers between devices with their start and end apart: 61, of which 33 were waited for; matrix products, arithmetic and copies ran while one was open for 5% of the time, Pallas kernels for 26%

profile of v5, /device:TPU:0, one launch (start us, length us, event | category | flops | bytes accessed | tf_op | source)
XLA Modules:
  0.0 826.0 jit_solution(1943681965659244605)
XLA Ops:
  7.2 2.1 dynamic-slice_bitcast_fusion
  9.4 5.9 pad.54.x_ref
  15.3 13.8 %analyse_low.1 = (bf16[49,40,128]{2,1,0:T(8,128)(2,1)}, bf16[49,40,128]{2,1,0:T(8,128)(2,1)}, bf16[49,40,128]{2,1,0:T(8,128)(2,1)}, bf16[49,40,128]{2,1,0:T(8,12...) custom-call(bf16[49,80,720]{2,1,0:T(8,128)(2,1)} %pad.54.x_ref, ...), custom_call_target="tpu_custom_call" | custom-call | bytes 41584640 | tf_op jit(solution)/shard_map/analyse_low/pallas_call | solution.py:92
  29.1 6.0 collective-permute-start
  35.5 3.0 collective-permute-start.3
  40.5 15.0 %analyse_high.1.zonal = bf16[49,112,256]{2,1,0:T(8,128)(2,1)} custom-call(bf16[49,80,720]{2,1,0:T(8,128)(2,1)} %pad.54.x_ref, bf16[2,112,720]{2,1,0:T(8,128)(2,1)} %constant.97.clone.dft_ref), custom_call_target="tpu_custom_call" | custom-call | bytes 35108864 | tf_op jit(solution)/shard_map/analyse_high/pallas_call | solution.py:92
  56.8 6.6 legendre_tables.3
  63.4 11.9 %high_partial.1 = bf16[14,5,112,128]{3,2,1,0:T(8,128)(2,1)} custom-call(bf16[49,112,256]{2,1,0:T(8,128)(2,1)} %analyse_high.1.zonal, bf16[56,112,128]{2,1,0:T(8,128)(2,1)} %get-tuple-element.132.fwd), custom_call_target="tpu_custom_call" | custom-call | bytes 25690112 | tf_op jit(solution)/shard_map/high_partial/pallas_call | solution.py:92
  78.0 2.4 fusion.38
  83.8 2.0 copy.38.refs_10_.mix
  89.1 19.4 %legendre_tables.2 = (bf16[32,368,392]{2,1,0:T(8,128)(2,1)}, bf16[32,368,392]{2,1,0:T(8,128)(2,1)}) custom-call(f32[32,128]{1,0:T(8,128)} %broadcast_in_dim.46.m_ref, f32[32,128]{1,0:T(8,128)} %convert_element_type.65.shift_ref, f32[32,512]{1,0:T(8,128)} %pad.57.start_ref, f32[1,512]{1,0:T(1,128)} %bitcast.98, f32[1,512]{1,0:T(1,128)} %bitcast.99, ...), custom_call_target="tpu_custom_call" | custom-call | bytes 74276864 | tf_op jit(solution)/shard_map/legendre_tables/pallas_call | solution.py:92
  112.8 30.1 %collective-permute-done.3.refs_4_ = bf16[49,40,128]{2,1,0:T(8,128)(2,1)} collective-permute-done((bf16[49,40,128]{2,1,0:T(8,128)(2,1)}, bf16[49,40,128]{2,1,0:T(8,128)(2,1)}, u32[]{:S(2)}, u32[]{:S(2)}) %collective-permute-start.3) | collective-permute-done | bytes 501792 | tf_op jit(solution)/shard_map/ppermute | solution.py:930
  143.9 38.2 %spectrum_forward.1 = (bf16[7,64,128]{2,1,0:T(8,128)(2,1)}, bf16[7,64,128]{2,1,0:T(8,128)(2,1)}, bf16[7,64,128]{2,1,0:T(8,128)(2,1)}, bf16[7,64,128]{2,1,0:T(8,1...) custom-call(bf16[49,40,128]{2,1,0:T(8,128)(2,1)} %get-tuple-element., ...), custom_call_target="tpu_custom_call" | custom-call | bytes 119209984 | tf_op jit(solution)/shard_map/spectrum_forward/pallas_call | solution.py:92
  182.1 3.2 collective-permute-start.10
  188.0 3.1 collective-permute-start.7
  191.1 12.0 %collective-permute-done.10.refs_4_ = bf16[7,64,128]{2,1,0:T(8,128)(2,1)S(1)} collective-permute-done((bf16[7,64,128]{2,1,0:T(8,128)(2,1)}, bf16[7,64,128]{2,1,0:T(8,128)(2,1)S(1)}, u32[]{:S(2)}, u32[]{:S(2)}) %collective-permute-start.10) | collective-permute-done | bytes 114720 | tf_op jit(solution)/shard_map/ppermute | solution.py:930
  203.1 8.0 collective-permute-done.11.refs_5_
  211.1 17.0 %all-reduce.18.cloned.1.call-done.coeffs = bf16[14,5,112,128]{3,2,1,0:T(8,128)(2,1)} async-done(((bf16[14,5,112,128]{3,2,1,0:T(8,128)(2,1)}), bf16[14,5,112,128]{3,2,1,0:T(8,128)(2,1)}) %all-reduce.18.cloned.1.call-update) | async-done | bytes 2007056 | tf_op jit(solution)/shard_map/psum | solution.py:953
  228.2 16.0 %high_synthesis.1.refs_8_ = bf16[49,224,128]{2,1,0:T(8,128)(2,1)} custom-call(bf16[14,5,112,128]{3,2,1,0:T(8,128)(2,1)} %all-reduce.18.cloned.1.call-done.coeffs, bf16[56,112,128]{2,1,0:T(8,128)(2,1)} %get-tuple-element.133.inv.refs_3_, bf16[4,256,256]{2,1,0:T(8,128)(2,1)} %copy.38.refs_10_.mix, f32[8,424,128]{2,1,0:T(8,128)} %copy-done.4), custom_call_target="tpu_custom_call" | custom-call | bytes 34734080 | tf_op jit(solution)/shard_map/high_synthesis/pallas_call | solution.py:92
  244.9 7.7 predict.3
  254.2 4.3 collective-permute-start.17
  258.5 4.5 collective-permute-done.14.refs_1_
  263.0 8.0 collective-permute-done.15.refs_2_
  271.0 6.1 pad.66.obs_ref
  277.1 34.9 %collective-permute-done.17.refs_4_ = bf16[21,64,128]{2,1,0:T(8,128)(2,1)S(1)} collective-permute-done((bf16[21,64,128]{2,1,0:T(8,128)(2,1)}, bf16[21,64,128]{2,1,0:T(8,128)(2,1)S(1)}, u32[]{:S(2)}, u32[]{:S(2)}) %collective-permute-start.17) | collective-permute-done | bytes 344096 | tf_op jit(solution)/shard_map/ppermute | solution.py:930
  314.2 17.0 %predict.4 = (bf16[21,80,720]{2,1,0:T(8,128)(2,1)}, bf16[21,128,720]{2,1,0:T(8,128)(2,1)}) custom-call(f32[49]{0:T(128)} %copy-done.62, bf16[49,80,720]{2,1,0:T(8,128)(2,1)} %pad.54.x_ref, bf16[736,720]{1,0:T(8,128)(2,1)} %pad_maximum_fusion.4.idft_ref, bf16[128,80]{1,0:T(8,128)(2,1)} %pad.55.enc_ref, bf16[80,128]{1,0:T(8,128)(2,1)} %pad.56.dec_ref, ...), custom_call_target="tpu_custom_call" | custom-call | bytes 74392336 | tf_op jit(solution)/shard_map/predict/pallas_call | solution.py:92
  333.3 4.8 collective-permute-start.23
  338.1 2.0 collective-permute-start.25
  341.1 2.5 collective-permute-start.26
  343.6 4.9 collective-permute-done.22.refs_2_
  348.4 7.2 collective-permute-done.23.refs_3_
  355.6 40.8 %collective-permute-done.24.refs_4_ = bf16[21,64,128]{2,1,0:T(8,128)(2,1)S(1)} collective-permute-done((bf16[21,64,128]{2,1,0:T(8,128)(2,1)}, bf16[21,64,128]{2,1,0:T(8,128)(2,1)S(1)}, u32[]{:S(2)}, u32[]{:S(2)}) %collective-permute-start.24) | collective-permute-done | bytes 344096 | tf_op jit(solution)/shard_map/ppermute | solution.py:930
  398.6 17.0 %predict.5 = (bf16[21,80,720]{2,1,0:T(8,128)(2,1)}, bf16[21,128,720]{2,1,0:T(8,128)(2,1)}) custom-call(f32[49]{0:T(128)} %copy-done.62, bf16[49,80,720]{2,1,0:T(8,128)(2,1)} %pad.54.x_ref, bf16[736,720]{1,0:T(8,128)(2,1)} %pad_maximum_fusion.4.idft_ref, bf16[128,80]{1,0:T(8,128)(2,1)} %pad.55.enc_ref, bf16[80,128]{1,0:T(8,128)(2,1)} %pad.56.dec_ref, ...), custom_call_target="tpu_custom_call" | custom-call | bytes 74392336 | tf_op jit(solution)/shard_map/predict/pallas_call | solution.py:92
  416.4 9.2 %score.3 = (bf16[7,80,720]{2,1,0:T(8,128)(2,1)}, bf16[7,64,128]{2,1,0:T(8,128)(2,1)}, bf16[7,64,128]{2,1,0:T(8,128)(2,1)}, bf16[7,64,128]{2,1,0:T(8,128)(2,1)}, ...) custom-call(f32[49]{0:T(128)} %get-tuple-element.228.area_ref, ...), custom_call_target="tpu_custom_call" | custom-call | bytes 56691472 | tf_op jit(solution)/shard_map/score/pallas_call | solution.py:92
  426.4 3.5 collective-permute-start.31
  434.6 9.6 %collective-permute-done.31.refs_4_ = bf16[7,64,128]{2,1,0:T(8,128)(2,1)S(1)} collective-permute-done((bf16[7,64,128]{2,1,0:T(8,128)(2,1)}, bf16[7,64,128]{2,1,0:T(8,128)(2,1)S(1)}, u32[]{:S(2)}, u32[]{:S(2)}) %collective-permute-start.31) | collective-permute-done | bytes 114720 | tf_op jit(solution)/shard_map/ppermute | solution.py:930
  444.1 2.5 collective-permute-done.32.refs_5_
  446.7 19.1 %score.4 = (bf16[21,80,720]{2,1,0:T(8,128)(2,1)}, bf16[21,64,128]{2,1,0:T(8,128)(2,1)}, bf16[21,64,128]{2,1,0:T(8,128)(2,1)}, bf16[21,64,128]{2,1,0:T(8,128)(2,1...) custom-call(f32[49]{0:T(128)} %get-tuple-element.228.area_ref, ...), custom_call_target="tpu_custom_call" | custom-call | bytes 116271888 | tf_op jit(solution)/shard_map/score/pallas_call | solution.py:92
  467.6 2.5 collective-permute-start.37
  472.1 3.8 collective-permute-done.35.refs_9_
  476.0 6.3 collective-permute-done.36.refs_10_
  482.3 7.4 collective-permute-done.37.refs_11_
  489.6 39.1 %collective-permute-done.38.refs_12_ = bf16[21,64,128]{2,1,0:T(8,128)(2,1)S(1)} collective-permute-done((bf16[21,64,128]{2,1,0:T(8,128)(2,1)}, bf16[21,64,128]{2,1,0:T(8,128)(2,1)S(1)}, u32[]{:S(2)}, u32[]{:S(2)}) %collective-permute-start.38) | collective-permute-done | bytes 344096 | tf_op jit(solution)/shard_map/ppermute | solution.py:930
  529.9 19.3 %score.5 = (bf16[21,80,720]{2,1,0:T(8,128)(2,1)}, bf16[21,64,128]{2,1,0:T(8,128)(2,1)}, bf16[21,64,128]{2,1,0:T(8,128)(2,1)}, bf16[21,64,128]{2,1,0:T(8,128)(2,1...) custom-call(f32[49]{0:T(128)} %get-tuple-element.228.area_ref, ...), custom_call_target="tpu_custom_call" | custom-call | bytes 116271888 | tf_op jit(solution)/shard_map/score/pallas_call | solution.py:92
  549.3 14.4 %high_adjoint.1 = bf16[14,5,112,128]{3,2,1,0:T(8,128)(2,1)} custom-call(bf16[7,224,128]{2,1,0:T(8,128)(2,1)} %get-tuple-element.203.refs_0_, bf16[21,224,128]{2,1,0:T(8,128)(2,1)} %get-tuple-element.204.refs_1_, bf16[21,224,128]{2,1,0:T(8,128)(2,1)} %get-tuple-element.205.refs_2_, bf16[56,112,128]{2,1,0:T(8,128)(2,1)} %get-tuple-element.133.inv.refs_3_, ...), custom_call_target="tpu_custom_call" | custom-call | bytes 34734080 | tf_op jit(solution)/shard_map/high_adjoint/pallas_call | solution.py:92
  564.9 3.3 collective-permute-start.45
  568.2 11.1 %collective-permute-done.42.refs_17_ = bf16[21,64,128]{2,1,0:T(8,128)(2,1)S(1)} collective-permute-done((bf16[21,64,128]{2,1,0:T(8,128)(2,1)S(1)}, bf16[21,64,128]{2,1,0:T(8,128)(2,1)S(1)}, u32[]{:S(2)}, u32[]{:S(2)}) %collective-permute-start.42) | collective-permute-done | bytes 344096 | tf_op jit(solution)/shard_map/ppermute | solution.py:930
  579.3 13.4 %collective-permute-done.43.refs_18_ = bf16[21,64,128]{2,1,0:T(8,128)(2,1)S(1)} collective-permute-done((bf16[21,64,128]{2,1,0:T(8,128)(2,1)S(1)}, bf16[21,64,128]{2,1,0:T(8,128)(2,1)S(1)}, u32[]{:S(2)}, u32[]{:S(2)}) %collective-permute-start.43) | collective-permute-done | bytes 344096 | tf_op jit(solution)/shard_map/ppermute | solution.py:930
  593.8 13.8 %collective-permute-done.44.refs_19_ = bf16[21,64,128]{2,1,0:T(8,128)(2,1)S(1)} collective-permute-done((bf16[21,64,128]{2,1,0:T(8,128)(2,1)}, bf16[21,64,128]{2,1,0:T(8,128)(2,1)S(1)}, u32[]{:S(2)}, u32[]{:S(2)}) %collective-permute-start.44) | collective-permute-done | bytes 344096 | tf_op jit(solution)/shard_map/ppermute | solution.py:930
  607.6 39.0 %collective-permute-done.45.refs_20_ = bf16[21,64,128]{2,1,0:T(8,128)(2,1)S(1)} collective-permute-done((bf16[21,64,128]{2,1,0:T(8,128)(2,1)}, bf16[21,64,128]{2,1,0:T(8,128)(2,1)S(1)}, u32[]{:S(2)}, u32[]{:S(2)}) %collective-permute-start.45) | collective-permute-done | bytes 344096 | tf_op jit(solution)/shard_map/ppermute | solution.py:930
  646.5 3.6 collective-permute-done.46.refs_21_
  651.7 38.1 %spectrum_backward.1 = (bf16[49,40,128]{2,1,0:T(8,128)(2,1)}, bf16[49,40,128]{2,1,0:T(8,128)(2,1)}, bf16[49,40,128]{2,1,0:T(8,128)(2,1)}, bf16[49,40,128]{2,1,0:...) custom-call(bf16[7,64,128]{2,1,0:T(8,128)(2,1)} %get-tuple-element.1, ...), custom_call_target="tpu_custom_call" | custom-call | bytes 119209984 | tf_op jit(solution)/shard_map/spectrum_backward/pallas_call | solution.py:92
  689.9 2.5 collective-permute-start.51
  693.1 2.4 pad_maximum_fusion.5.main_ref
  697.3 2.9 collective-permute-start.53
  700.2 2.9 collective-permute-start.54
  703.0 10.1 %all-reduce.20.cloned.1.call-done.grads = bf16[14,5,112,128]{3,2,1,0:T(8,128)(2,1)} async-done(((bf16[14,5,112,128]{3,2,1,0:T(8,128)(2,1)}), bf16[14,5,112,128]{3,2,1,0:T(8,128)(2,1)}) %all-reduce.20.cloned.1.call-update) | async-done | bytes 2007056 | tf_op jit(solution)/shard_map/psum | solution.py:995
  713.9 38.3 %collective-permute-start.49 = (bf16[49,40,128]{2,1,0:T(8,128)(2,1)}, bf16[49,40,128]{2,1,0:T(8,128)(2,1)S(1)}, u32[]{:S(2)}, u32[]{:S(2)}) collective-permute-start(bf16[49,40,128]{2,1,0:T(8,128)(2,1)} %get-tuple-element.218), channel_id=1, source_target_pairs={{0,7},{1,0},{2,1},{3,2},{4,3},{5,4},{6,5},{7,6},{8,15},{9,8},{10,9... | collective-permute-start | bytes 1505288 | tf_op jit(solution)/shard_map/ppermute | solution.py:930
  752.2 18.2 %collective-permute-start.55 = (bf16[49,40,128]{2,1,0:T(8,128)(2,1)}, bf16[49,40,128]{2,1,0:T(8,128)(2,1)}, u32[]{:S(2)}, u32[]{:S(2)}) collective-permute-start(bf16[49,40,128]{2,1,0:T(8,128)(2,1)} %get-tuple-element.224), channel_id=1, source_target_pairs={{0,1},{1,2},{2,3},{3,4},{4,5},{5,6},{6,7},{7,0},{8,9},{9,10},{10,1... | collective-permute-start | bytes 1505288 | tf_op jit(solution)/shard_map/ppermute | solution.py:930
  770.4 5.0 fusion
  775.4 3.5 pad_maximum_fusion.2.grad_ref
  778.9 11.4 %high_zonal.1.refs_8_ = bf16[49,144,128]{2,1,0:T(8,128)(2,1)} custom-call(bf16[14,5,112,128]{3,2,1,0:T(8,128)(2,1)} %all-reduce.20.cloned.1.call-done.grads, bf16[56,112,128]{2,1,0:T(8,128)(2,1)} %get-tuple-element.132.fwd), custom_call_target="tpu_custom_call" | custom-call | bytes 21676032 | tf_op jit(solution)/shard_map/high_zonal/pallas_call | solution.py:92
  792.5 21.2 %finish.1 = bf16[49,80,720]{2,1,0:T(8,128)(2,1)} custom-call(f32[49]{0:T(128)} %copy-done.62, bf16[49,80,720]{2,1,0:T(8,128)(2,1)} %pad_maximum_fusion.2.grad_ref, bf16[736,720]{1,0:T(8,128)(2,1)} %pad_maximum_fusion.5.main_ref, bf16[768,720]{1,0:T(8,128)(2,1)} %pad_maximum_fusion.3.rest_ref, bf16[80,80]{1,0:T(8,128)(2,1)} %pad.68.through_ref, ...), custom_call_target="tpu_custom_call" | custom-call | bytes 77155088 | tf_op jit(solution)/shard_map/finish/pallas_call | solution.py:92
  813.7 5.7 slice_bitcast_fusion
  (295 shorter events, 51.4 us)
Async XLA Ops:
  7.2 221.0 %all-reduce.18.cloned.1.call-start = ((), (), s32[]{:S(2)}) async-start(), calls=%async_computation | async-start | bytes 4014080 | tf_op jit(solution)/shard_map/psum | solution.py:953
  29.1 79.5 %collective-permute-start = (bf16[49,40,128]{2,1,0:T(8,128)(2,1)}, bf16[49,40,128]{2,1,0:T(8,128)(2,1)}, u32[]{:S(2)}, u32[]{:S(2)}) collective-permute-start(bf16[49,40,128]{2,1,0:T(8,128)(2,1)} %get-tuple-element.115), channel_id=1, source_target_pairs={{0,7},{1,0},{2,1},{3,2},{4,3},{5,4},{6,5},{7,6},{8,15},{9,8},{10,9... | collective-permute-start | bytes 1505288 | tf_op jit(solution)/shard_map/ppermute | solution.py:930
  35.1 75.4 %collective-permute-start.1 = (bf16[49,40,128]{2,1,0:T(8,128)(2,1)}, bf16[49,40,128]{2,1,0:T(8,128)(2,1)}, u32[]{:S(2)}, u32[]{:S(2)}) collective-permute-start(bf16[49,40,128]{2,1,0:T(8,128)(2,1)} %get-tuple-element.116), channel_id=1, source_target_pairs={{0,6},{1,7},{2,0},{3,1},{4,2},{5,3},{6,4},{7,5},{8,14},{9,15},{10,... | collective-permute-start | bytes 1505288 | tf_op jit(solution)/shard_map/ppermute | solution.py:930
  35.5 77.3 %collective-permute-start.2 = (bf16[49,40,128]{2,1,0:T(8,128)(2,1)}, bf16[49,40,128]{2,1,0:T(8,128)(2,1)}, u32[]{:S(2)}, u32[]{:S(2)}) collective-permute-start(bf16[49,40,128]{2,1,0:T(8,128)(2,1)} %get-tuple-element.117), channel_id=1, source_target_pairs={{0,5},{1,6},{2,7},{3,0},{4,1},{5,2},{6,3},{7,4},{8,13},{9,14},{10,... | collective-permute-start | bytes 1505288 | tf_op jit(solution)/shard_map/ppermute | solution.py:930
  35.5 107.4 %collective-permute-start.3 = (bf16[49,40,128]{2,1,0:T(8,128)(2,1)}, bf16[49,40,128]{2,1,0:T(8,128)(2,1)}, u32[]{:S(2)}, u32[]{:S(2)}) collective-permute-start(bf16[49,40,128]{2,1,0:T(8,128)(2,1)} %get-tuple-element.118), channel_id=1, source_target_pairs={{0,4},{1,5},{2,6},{3,7},{4,0},{5,1},{6,2},{7,3},{8,12},{9,13},{10,... | collective-permute-start | bytes 1505288 | tf_op jit(solution)/shard_map/ppermute | solution.py:930
  38.5 104.6 %collective-permute-start.4 = (bf16[49,40,128]{2,1,0:T(8,128)(2,1)}, bf16[49,40,128]{2,1,0:T(8,128)(2,1)}, u32[]{:S(2)}, u32[]{:S(2)}) collective-permute-start(bf16[49,40,128]{2,1,0:T(8,128)(2,1)} %get-tuple-element.119), channel_id=1, source_target_pairs={{0,3},{1,4},{2,5},{3,6},{4,7},{5,0},{6,1},{7,2},{8,11},{9,12},{10,... | collective-permute-start | bytes 1505288 | tf_op jit(solution)/shard_map/ppermute | solution.py:930
  75.3 341.1 %all-gather.7.cloned.1.call-start = ((), (), s32[]{:S(2)}) async-start(), calls=%async_computation.2 | async-start | bytes 4300800 | tf_op jit(solution)/shard_map/all_gather | solution.py:984
  108.6 34.5 %collective-permute-start.5 = (bf16[49,40,128]{2,1,0:T(8,128)(2,1)}, bf16[49,40,128]{2,1,0:T(8,128)(2,1)S(1)}, u32[]{:S(2)}, u32[]{:S(2)}) collective-permute-start(bf16[49,40,128]{2,1,0:T(8,128)(2,1)} %get-tuple-element.120), channel_id=1, source_target_pairs={{0,2},{1,3},{2,4},{3,5},{4,6},{5,7},{6,0},{7,1},{8,10},{9,11},{10,... | collective-permute-start | bytes 1505288 | tf_op jit(solution)/shard_map/ppermute | solution.py:930
  110.4 32.7 %collective-permute-start.6 = (bf16[49,40,128]{2,1,0:T(8,128)(2,1)}, bf16[49,40,128]{2,1,0:T(8,128)(2,1)}, u32[]{:S(2)}, u32[]{:S(2)}) collective-permute-start(bf16[49,40,128]{2,1,0:T(8,128)(2,1)} %get-tuple-element.121), channel_id=1, source_target_pairs={{0,1},{1,2},{2,3},{3,4},{4,5},{5,6},{6,7},{7,0},{8,9},{9,10},{10,1... | collective-permute-start | bytes 1505288 | tf_op jit(solution)/shard_map/ppermute | solution.py:930
  182.1 21.0 %collective-permute-start.10 = (bf16[7,64,128]{2,1,0:T(8,128)(2,1)}, bf16[7,64,128]{2,1,0:T(8,128)(2,1)S(1)}, u32[]{:S(2)}, u32[]{:S(2)}) collective-permute-start(bf16[7,64,128]{2,1,0:T(8,128)(2,1)} %get-tuple-element.128), channel_id=1, source_target_pairs={{0,4},{1,5},{2,6},{3,7},{4,0},{5,1},{6,2},{7,3},{8,12},{9,13},{10,... | collective-permute-start | bytes 344072 | tf_op jit(solution)/shard_map/ppermute | solution.py:930
  185.3 25.8 %collective-permute-start.11 = (bf16[7,64,128]{2,1,0:T(8,128)(2,1)}, bf16[7,64,128]{2,1,0:T(8,128)(2,1)S(1)}, u32[]{:S(2)}, u32[]{:S(2)}) collective-permute-start(bf16[7,64,128]{2,1,0:T(8,128)(2,1)} %get-tuple-element.129), channel_id=1, source_target_pairs={{0,3},{1,4},{2,5},{3,6},{4,7},{5,0},{6,1},{7,2},{8,11},{9,12},{10,... | collective-permute-start | bytes 344072 | tf_op jit(solution)/shard_map/ppermute | solution.py:930
  185.3 58.8 %collective-permute-start.12 = (bf16[7,64,128]{2,1,0:T(8,128)(2,1)}, bf16[7,64,128]{2,1,0:T(8,128)(2,1)S(1)}, u32[]{:S(2)}, u32[]{:S(2)}) collective-permute-start(bf16[7,64,128]{2,1,0:T(8,128)(2,1)} %get-tuple-element.130), channel_id=1, source_target_pairs={{0,2},{1,3},{2,4},{3,5},{4,6},{5,7},{6,0},{7,1},{8,10},{9,11},{10,... | collective-permute-start | bytes 344072 | tf_op jit(solution)/shard_map/ppermute | solution.py:930
  186.4 57.8 %collective-permute-start.13 = (bf16[7,64,128]{2,1,0:T(8,128)(2,1)}, bf16[7,64,128]{2,1,0:T(8,128)(2,1)S(1)}, u32[]{:S(2)}, u32[]{:S(2)}) collective-permute-start(bf16[7,64,128]{2,1,0:T(8,128)(2,1)} %get-tuple-element.131), channel_id=1, source_target_pairs={{0,1},{1,2},{2,3},{3,4},{4,5},{5,6},{6,7},{7,0},{8,9},{9,10},{10,1... | collective-permute-start | bytes 344072 | tf_op jit(solution)/shard_map/ppermute | solution.py:930
  188.0 56.2 %collective-permute-start.7 = (bf16[7,64,128]{2,1,0:T(8,128)(2,1)}, bf16[7,64,128]{2,1,0:T(8,128)(2,1)S(1)}, u32[]{:S(2)}, u32[]{:S(2)}) collective-permute-start(bf16[7,64,128]{2,1,0:T(8,128)(2,1)} %get-tuple-element.125), channel_id=1, source_target_pairs={{0,7},{1,0},{2,1},{3,2},{4,3},{5,4},{6,5},{7,6},{8,15},{9,8},{10,9... | collective-permute-start | bytes 344072 | tf_op jit(solution)/shard_map/ppermute | solution.py:930
  203.1 41.1 %collective-permute-start.8 = (bf16[7,64,128]{2,1,0:T(8,128)(2,1)}, bf16[7,64,128]{2,1,0:T(8,128)(2,1)S(1)}, u32[]{:S(2)}, u32[]{:S(2)}) collective-permute-start(bf16[7,64,128]{2,1,0:T(8,128)(2,1)} %get-tuple-element.126), channel_id=1, source_target_pairs={{0,6},{1,7},{2,0},{3,1},{4,2},{5,3},{6,4},{7,5},{8,14},{9,15},{10,... | collective-permute-start | bytes 344072 | tf_op jit(solution)/shard_map/ppermute | solution.py:930
  211.1 33.1 %collective-permute-start.9 = (bf16[7,64,128]{2,1,0:T(8,128)(2,1)}, bf16[7,64,128]{2,1,0:T(8,128)(2,1)}, u32[]{:S(2)}, u32[]{:S(2)}) collective-permute-start(bf16[7,64,128]{2,1,0:T(8,128)(2,1)} %get-tuple-element.127), channel_id=1, source_target_pairs={{0,5},{1,6},{2,7},{3,0},{4,1},{5,2},{6,3},{7,4},{8,13},{9,14},{10,... | collective-permute-start | bytes 344072 | tf_op jit(solution)/shard_map/ppermute | solution.py:930
  252.6 194.1 %all-gather.9.cloned.1.call-start = ((), (), s32[]{:S(2)}) async-start(), calls=%async_computation.3 | async-start | bytes 12902400 | tf_op jit(solution)/shard_map/all_gather | solution.py:984
  252.7 10.3 %collective-permute-start.14 = (bf16[21,64,128]{2,1,0:T(8,128)(2,1)S(1)}, bf16[21,64,128]{2,1,0:T(8,128)(2,1)S(1)}, u32[]{:S(2)}, u32[]{:S(2)}) collective-permute-start(bf16[21,64,128]{2,1,0:T(8,128)(2,1)S(1)} %copy-done.69), channel_id=1, source_target_pairs={{0,7},{1,0},{2,1},{3,2},{4,3},{5,4},{6,5},{7,6},{8,15},{9,8},{10,9... | collective-permute-start | bytes 1032200 | tf_op jit(solution)/shard_map/ppermute | solution.py:930
  252.9 18.1 %collective-permute-start.15 = (bf16[21,64,128]{2,1,0:T(8,128)(2,1)S(1)}, bf16[21,64,128]{2,1,0:T(8,128)(2,1)S(1)}, u32[]{:S(2)}, u32[]{:S(2)}) collective-permute-start(bf16[21,64,128]{2,1,0:T(8,128)(2,1)S(1)} %copy-done.68), channel_id=1, source_target_pairs={{0,6},{1,7},{2,0},{3,1},{4,2},{5,3},{6,4},{7,5},{8,14},{9,15},{10,... | collective-permute-start | bytes 1032200 | tf_op jit(solution)/shard_map/ppermute | solution.py:930
  254.2 22.9 %collective-permute-start.16 = (bf16[21,64,128]{2,1,0:T(8,128)(2,1)}, bf16[21,64,128]{2,1,0:T(8,128)(2,1)S(1)}, u32[]{:S(2)}, u32[]{:S(2)}) collective-permute-start(bf16[21,64,128]{2,1,0:T(8,128)(2,1)} %get-tuple-element.139), channel_id=1, source_target_pairs={{0,5},{1,6},{2,7},{3,0},{4,1},{5,2},{6,3},{7,4},{8,13},{9,14},{10,... | collective-permute-start | bytes 1032200 | tf_op jit(solution)/shard_map/ppermute | solution.py:930
  254.2 57.8 %collective-permute-start.17 = (bf16[21,64,128]{2,1,0:T(8,128)(2,1)}, bf16[21,64,128]{2,1,0:T(8,128)(2,1)S(1)}, u32[]{:S(2)}, u32[]{:S(2)}) collective-permute-start(bf16[21,64,128]{2,1,0:T(8,128)(2,1)} %get-tuple-element.140), channel_id=1, source_target_pairs={{0,4},{1,5},{2,6},{3,7},{4,0},{5,1},{6,2},{7,3},{8,12},{9,13},{10,... | collective-permute-start | bytes 1032200 | tf_op jit(solution)/shard_map/ppermute | solution.py:930
  258.5 54.7 %collective-permute-start.18 = (bf16[21,64,128]{2,1,0:T(8,128)(2,1)}, bf16[21,64,128]{2,1,0:T(8,128)(2,1)S(1)}, u32[]{:S(2)}, u32[]{:S(2)}) collective-permute-start(bf16[21,64,128]{2,1,0:T(8,128)(2,1)} %get-tuple-element.141), channel_id=1, source_target_pairs={{0,3},{1,4},{2,5},{3,6},{4,7},{5,0},{6,1},{7,2},{8,11},{9,12},{10,... | collective-permute-start | bytes 1032200 | tf_op jit(solution)/shard_map/ppermute | solution.py:930
  263.0 50.2 %collective-permute-start.19 = (bf16[21,64,128]{2,1,0:T(8,128)(2,1)}, bf16[21,64,128]{2,1,0:T(8,128)(2,1)S(1)}, u32[]{:S(2)}, u32[]{:S(2)}) collective-permute-start(bf16[21,64,128]{2,1,0:T(8,128)(2,1)} %get-tuple-element.142), channel_id=1, source_target_pairs={{0,2},{1,3},{2,4},{3,5},{4,6},{5,7},{6,0},{7,1},{8,10},{9,11},{10,... | collective-permute-start | bytes 1032200 | tf_op jit(solution)/shard_map/ppermute | solution.py:930
  271.0 42.2 %collective-permute-start.20 = (bf16[21,64,128]{2,1,0:T(8,128)(2,1)}, bf16[21,64,128]{2,1,0:T(8,128)(2,1)S(1)}, u32[]{:S(2)}, u32[]{:S(2)}) collective-permute-start(bf16[21,64,128]{2,1,0:T(8,128)(2,1)} %get-tuple-element.143), channel_id=1, source_target_pairs={{0,1},{1,2},{2,3},{3,4},{4,5},{5,6},{6,7},{7,0},{8,9},{9,10},{10,1... | collective-permute-start | bytes 1032200 | tf_op jit(solution)/shard_map/ppermute | solution.py:930
  331.3 198.7 %all-gather.11.cloned.1.call-start = ((), (), s32[]{:S(2)}) async-start(), calls=%async_computation.4 | async-start | bytes 12902400 | tf_op jit(solution)/shard_map/all_gather | solution.py:984
  332.2 8.9 %collective-permute-start.21 = (bf16[21,64,128]{2,1,0:T(8,128)(2,1)S(1)}, bf16[21,64,128]{2,1,0:T(8,128)(2,1)S(1)}, u32[]{:S(2)}, u32[]{:S(2)}) collective-permute-start(bf16[21,64,128]{2,1,0:T(8,128)(2,1)S(1)} %copy-done.67), channel_id=1, source_target_pairs={{0,7},{1,0},{2,1},{3,2},{4,3},{5,4},{6,5},{7,6},{8,15},{9,8},{10,9... | collective-permute-start | bytes 1032200 | tf_op jit(solution)/shard_map/ppermute | solution.py:930
  332.3 16.2 %collective-permute-start.22 = (bf16[21,64,128]{2,1,0:T(8,128)(2,1)S(1)}, bf16[21,64,128]{2,1,0:T(8,128)(2,1)S(1)}, u32[]{:S(2)}, u32[]{:S(2)}) collective-permute-start(bf16[21,64,128]{2,1,0:T(8,128)(2,1)S(1)} %copy-done.66), channel_id=1, source_target_pairs={{0,6},{1,7},{2,0},{3,1},{4,2},{5,3},{6,4},{7,5},{8,14},{9,15},{10,... | collective-permute-start | bytes 1032200 | tf_op jit(solution)/shard_map/ppermute | solution.py:930
  333.3 22.3 %collective-permute-start.23 = (bf16[21,64,128]{2,1,0:T(8,128)(2,1)}, bf16[21,64,128]{2,1,0:T(8,128)(2,1)S(1)}, u32[]{:S(2)}, u32[]{:S(2)}) collective-permute-start(bf16[21,64,128]{2,1,0:T(8,128)(2,1)} %get-tuple-element.148), channel_id=1, source_target_pairs={{0,5},{1,6},{2,7},{3,0},{4,1},{5,2},{6,3},{7,4},{8,13},{9,14},{10,... | collective-permute-start | bytes 1032200 | tf_op jit(solution)/shard_map/ppermute | solution.py:930
  338.1 58.4 %collective-permute-start.24 = (bf16[21,64,128]{2,1,0:T(8,128)(2,1)}, bf16[21,64,128]{2,1,0:T(8,128)(2,1)S(1)}, u32[]{:S(2)}, u32[]{:S(2)}) collective-permute-start(bf16[21,64,128]{2,1,0:T(8,128)(2,1)} %get-tuple-element.149), channel_id=1, source_target_pairs={{0,4},{1,5},{2,6},{3,7},{4,0},{5,1},{6,2},{7,3},{8,12},{9,13},{10,... | collective-permute-start | bytes 1032200 | tf_op jit(solution)/shard_map/ppermute | solution.py:930
  338.1 59.6 %collective-permute-start.25 = (bf16[21,64,128]{2,1,0:T(8,128)(2,1)}, bf16[21,64,128]{2,1,0:T(8,128)(2,1)S(1)}, u32[]{:S(2)}, u32[]{:S(2)}) collective-permute-start(bf16[21,64,128]{2,1,0:T(8,128)(2,1)} %get-tuple-element.150), channel_id=1, source_target_pairs={{0,3},{1,4},{2,5},{3,6},{4,7},{5,0},{6,1},{7,2},{8,11},{9,12},{10,... | collective-permute-start | bytes 1032200 | tf_op jit(solution)/shard_map/ppermute | solution.py:930
  341.1 56.5 %collective-permute-start.26 = (bf16[21,64,128]{2,1,0:T(8,128)(2,1)S(1)}, bf16[21,64,128]{2,1,0:T(8,128)(2,1)S(1)}, u32[]{:S(2)}, u32[]{:S(2)}) collective-permute-start(bf16[21,64,128]{2,1,0:T(8,128)(2,1)S(1)} %copy-done.65), channel_id=1, source_target_pairs={{0,2},{1,3},{2,4},{3,5},{4,6},{5,7},{6,0},{7,1},{8,10},{9,11},{10,... | collective-permute-start | bytes 1032200 | tf_op jit(solution)/shard_map/ppermute | solution.py:930
  348.4 49.2 %collective-permute-start.27 = (bf16[21,64,128]{2,1,0:T(8,128)(2,1)S(1)}, bf16[21,64,128]{2,1,0:T(8,128)(2,1)S(1)}, u32[]{:S(2)}, u32[]{:S(2)}) collective-permute-start(bf16[21,64,128]{2,1,0:T(8,128)(2,1)S(1)} %copy-done.64), channel_id=1, source_target_pairs={{0,1},{1,2},{2,3},{3,4},{4,5},{5,6},{6,7},{7,0},{8,9},{9,10},{10,1... | collective-permute-start | bytes 1032200 | tf_op jit(solution)/shard_map/ppermute | solution.py:930
  415.6 297.5 %all-reduce.20.cloned.1.call-start = ((), (), s32[]{:S(2)}) async-start(), calls=%async_computation.1 | async-start | bytes 4014080 | tf_op jit(solution)/shard_map/psum | solution.py:995
  425.6 6.2 collective-permute-start.28
  425.6 7.1 collective-permute-start.29
  426.4 8.1 collective-permute-start.30
  426.4 17.7 %collective-permute-start.31 = (bf16[7,64,128]{2,1,0:T(8,128)(2,1)}, bf16[7,64,128]{2,1,0:T(8,128)(2,1)S(1)}, u32[]{:S(2)}, u32[]{:S(2)}) collective-permute-start(bf16[7,64,128]{2,1,0:T(8,128)(2,1)} %get-tuple-element.161), channel_id=1, source_target_pairs={{0,4},{1,5},{2,6},{3,7},{4,0},{5,1},{6,2},{7,3},{8,12},{9,13},{10,... | collective-permute-start | bytes 344072 | tf_op jit(solution)/shard_map/ppermute | solution.py:930
  430.0 16.7 %collective-permute-start.32 = (bf16[7,64,128]{2,1,0:T(8,128)(2,1)}, bf16[7,64,128]{2,1,0:T(8,128)(2,1)S(1)}, u32[]{:S(2)}, u32[]{:S(2)}) collective-permute-start(bf16[7,64,128]{2,1,0:T(8,128)(2,1)} %get-tuple-element.162), channel_id=1, source_target_pairs={{0,3},{1,4},{2,5},{3,6},{4,7},{5,0},{6,1},{7,2},{8,11},{9,12},{10,... | collective-permute-start | bytes 344072 | tf_op jit(solution)/shard_map/ppermute | solution.py:930
  431.8 14.8 %collective-permute-start.33 = (bf16[7,64,128]{2,1,0:T(8,128)(2,1)}, bf16[7,64,128]{2,1,0:T(8,128)(2,1)S(1)}, u32[]{:S(2)}, u32[]{:S(2)}) collective-permute-start(bf16[7,64,128]{2,1,0:T(8,128)(2,1)} %get-tuple-element.163), channel_id=1, source_target_pairs={{0,2},{1,3},{2,4},{3,5},{4,6},{5,7},{6,0},{7,1},{8,10},{9,11},{10,... | collective-permute-start | bytes 344072 | tf_op jit(solution)/shard_map/ppermute | solution.py:930
  432.6 14.0 %collective-permute-start.34 = (bf16[7,64,128]{2,1,0:T(8,128)(2,1)}, bf16[7,64,128]{2,1,0:T(8,128)(2,1)}, u32[]{:S(2)}, u32[]{:S(2)}) collective-permute-start(bf16[7,64,128]{2,1,0:T(8,128)(2,1)} %get-tuple-element.164), channel_id=1, source_target_pairs={{0,1},{1,2},{2,3},{3,4},{4,5},{5,6},{6,7},{7,0},{8,9},{9,10},{10,1... | collective-permute-start | bytes 344072 | tf_op jit(solution)/shard_map/ppermute | solution.py:930
  465.9 10.1 %collective-permute-start.35 = (bf16[21,64,128]{2,1,0:T(8,128)(2,1)}, bf16[21,64,128]{2,1,0:T(8,128)(2,1)S(1)}, u32[]{:S(2)}, u32[]{:S(2)}) collective-permute-start(bf16[21,64,128]{2,1,0:T(8,128)(2,1)} %get-tuple-element.169), channel_id=1, source_target_pairs={{0,7},{1,0},{2,1},{3,2},{4,3},{5,4},{6,5},{7,6},{8,15},{9,8},{10,9... | collective-permute-start | bytes 1032200 | tf_op jit(solution)/shard_map/ppermute | solution.py:930
  466.0 16.3 %collective-permute-start.36 = (bf16[21,64,128]{2,1,0:T(8,128)(2,1)}, bf16[21,64,128]{2,1,0:T(8,128)(2,1)S(1)}, u32[]{:S(2)}, u32[]{:S(2)}) collective-permute-start(bf16[21,64,128]{2,1,0:T(8,128)(2,1)} %get-tuple-element.170), channel_id=1, source_target_pairs={{0,6},{1,7},{2,0},{3,1},{4,2},{5,3},{6,4},{7,5},{8,14},{9,15},{10,... | collective-permute-start | bytes 1032200 | tf_op jit(solution)/shard_map/ppermute | solution.py:930
  467.6 22.0 %collective-permute-start.37 = (bf16[21,64,128]{2,1,0:T(8,128)(2,1)}, bf16[21,64,128]{2,1,0:T(8,128)(2,1)S(1)}, u32[]{:S(2)}, u32[]{:S(2)}) collective-permute-start(bf16[21,64,128]{2,1,0:T(8,128)(2,1)} %get-tuple-element.171), channel_id=1, source_target_pairs={{0,5},{1,6},{2,7},{3,0},{4,1},{5,2},{6,3},{7,4},{8,13},{9,14},{10,... | collective-permute-start | bytes 1032200 | tf_op jit(solution)/shard_map/ppermute | solution.py:930
  470.1 58.6 %collective-permute-start.38 = (bf16[21,64,128]{2,1,0:T(8,128)(2,1)}, bf16[21,64,128]{2,1,0:T(8,128)(2,1)S(1)}, u32[]{:S(2)}, u32[]{:S(2)}) collective-permute-start(bf16[21,64,128]{2,1,0:T(8,128)(2,1)} %get-tuple-element.172), channel_id=1, source_target_pairs={{0,4},{1,5},{2,6},{3,7},{4,0},{5,1},{6,2},{7,3},{8,12},{9,13},{10,... | collective-permute-start | bytes 1032200 | tf_op jit(solution)/shard_map/ppermute | solution.py:930
  470.3 59.5 %collective-permute-start.39 = (bf16[21,64,128]{2,1,0:T(8,128)(2,1)}, bf16[21,64,128]{2,1,0:T(8,128)(2,1)S(1)}, u32[]{:S(2)}, u32[]{:S(2)}) collective-permute-start(bf16[21,64,128]{2,1,0:T(8,128)(2,1)} %get-tuple-element.173), channel_id=1, source_target_pairs={{0,3},{1,4},{2,5},{3,6},{4,7},{5,0},{6,1},{7,2},{8,11},{9,12},{10,... | collective-permute-start | bytes 1032200 | tf_op jit(solution)/shard_map/ppermute | solution.py:930
  476.0 53.9 %collective-permute-start.40 = (bf16[21,64,128]{2,1,0:T(8,128)(2,1)}, bf16[21,64,128]{2,1,0:T(8,128)(2,1)S(1)}, u32[]{:S(2)}, u32[]{:S(2)}) collective-permute-start(bf16[21,64,128]{2,1,0:T(8,128)(2,1)} %get-tuple-element.174), channel_id=1, source_target_pairs={{0,2},{1,3},{2,4},{3,5},{4,6},{5,7},{6,0},{7,1},{8,10},{9,11},{10,... | collective-permute-start | bytes 1032200 | tf_op jit(solution)/shard_map/ppermute | solution.py:930
  482.3 47.6 %collective-permute-start.41 = (bf16[21,64,128]{2,1,0:T(8,128)(2,1)}, bf16[21,64,128]{2,1,0:T(8,128)(2,1)S(1)}, u32[]{:S(2)}, u32[]{:S(2)}) collective-permute-start(bf16[21,64,128]{2,1,0:T(8,128)(2,1)} %get-tuple-element.175), channel_id=1, source_target_pairs={{0,1},{1,2},{2,3},{3,4},{4,5},{5,6},{6,7},{7,0},{8,9},{9,10},{10,1... | collective-permute-start | bytes 1032200 | tf_op jit(solution)/shard_map/ppermute | solution.py:930
  563.7 15.5 %collective-permute-start.42 = (bf16[21,64,128]{2,1,0:T(8,128)(2,1)S(1)}, bf16[21,64,128]{2,1,0:T(8,128)(2,1)S(1)}, u32[]{:S(2)}, u32[]{:S(2)}) collective-permute-start(bf16[21,64,128]{2,1,0:T(8,128)(2,1)S(1)} %copy-done.72), channel_id=1, source_target_pairs={{0,7},{1,0},{2,1},{3,2},{4,3},{5,4},{6,5},{7,6},{8,15},{9,8},{10,9... | collective-permute-start | bytes 1032200 | tf_op jit(solution)/shard_map/ppermute | solution.py:930
  563.8 28.9 %collective-permute-start.43 = (bf16[21,64,128]{2,1,0:T(8,128)(2,1)S(1)}, bf16[21,64,128]{2,1,0:T(8,128)(2,1)S(1)}, u32[]{:S(2)}, u32[]{:S(2)}) collective-permute-start(bf16[21,64,128]{2,1,0:T(8,128)(2,1)S(1)} %copy-done.71), channel_id=1, source_target_pairs={{0,6},{1,7},{2,0},{3,1},{4,2},{5,3},{6,4},{7,5},{8,14},{9,15},{10,... | collective-permute-start | bytes 1032200 | tf_op jit(solution)/shard_map/ppermute | solution.py:930
  564.9 42.7 %collective-permute-start.44 = (bf16[21,64,128]{2,1,0:T(8,128)(2,1)}, bf16[21,64,128]{2,1,0:T(8,128)(2,1)S(1)}, u32[]{:S(2)}, u32[]{:S(2)}) collective-permute-start(bf16[21,64,128]{2,1,0:T(8,128)(2,1)} %get-tuple-element.209), channel_id=1, source_target_pairs={{0,5},{1,6},{2,7},{3,0},{4,1},{5,2},{6,3},{7,4},{8,13},{9,14},{10,... | collective-permute-start | bytes 1032200 | tf_op jit(solution)/shard_map/ppermute | solution.py:930
  564.9 81.6 %collective-permute-start.45 = (bf16[21,64,128]{2,1,0:T(8,128)(2,1)}, bf16[21,64,128]{2,1,0:T(8,128)(2,1)S(1)}, u32[]{:S(2)}, u32[]{:S(2)}) collective-permute-start(bf16[21,64,128]{2,1,0:T(8,128)(2,1)} %get-tuple-element.210), channel_id=1, source_target_pairs={{0,4},{1,5},{2,6},{3,7},{4,0},{5,1},{6,2},{7,3},{8,12},{9,13},{10,... | collective-permute-start | bytes 1032200 | tf_op jit(solution)/shard_map/ppermute | solution.py:930
  568.2 81.9 %collective-permute-start.46 = (bf16[21,64,128]{2,1,0:T(8,128)(2,1)}, bf16[21,64,128]{2,1,0:T(8,128)(2,1)S(1)}, u32[]{:S(2)}, u32[]{:S(2)}) collective-permute-start(bf16[21,64,128]{2,1,0:T(8,128)(2,1)} %get-tuple-element.211), channel_id=1, source_target_pairs={{0,3},{1,4},{2,5},{3,6},{4,7},{5,0},{6,1},{7,2},{8,11},{9,12},{10,... | collective-permute-start | bytes 1032200 | tf_op jit(solution)/shard_map/ppermute | solution.py:930
  579.3 70.9 %collective-permute-start.47 = (bf16[21,64,128]{2,1,0:T(8,128)(2,1)}, bf16[21,64,128]{2,1,0:T(8,128)(2,1)S(1)}, u32[]{:S(2)}, u32[]{:S(2)}) collective-permute-start(bf16[21,64,128]{2,1,0:T(8,128)(2,1)} %get-tuple-element.212), channel_id=1, source_target_pairs={{0,2},{1,3},{2,4},{3,5},{4,6},{5,7},{6,0},{7,1},{8,10},{9,11},{10,... | collective-permute-start | bytes 1032200 | tf_op jit(solution)/shard_map/ppermute | solution.py:930
  592.7 57.4 %collective-permute-start.48 = (bf16[21,64,128]{2,1,0:T(8,128)(2,1)S(1)}, bf16[21,64,128]{2,1,0:T(8,128)(2,1)S(1)}, u32[]{:S(2)}, u32[]{:S(2)}) collective-permute-start(bf16[21,64,128]{2,1,0:T(8,128)(2,1)S(1)} %copy-done.70), channel_id=1, source_target_pairs={{0,1},{1,2},{2,3},{3,4},{4,5},{5,6},{6,7},{7,0},{8,9},{9,10},{10,1... | collective-permute-start | bytes 1032200 | tf_op jit(solution)/shard_map/ppermute | solution.py:930
  593.8 99.4 %copy-start.29 = (bf16[224,720]{1,0:T(8,128)(2,1)S(1)}, bf16[224,720]{1,0:T(8,128)(2,1)}, u32[]{:S(2)}) copy-start(bf16[224,720]{1,0:T(8,128)(2,1)} %constant.100.clone) | copy-start | bytes 967684
  689.8 24.2 %collective-permute-start.50 = (bf16[49,40,128]{2,1,0:T(8,128)(2,1)}, bf16[49,40,128]{2,1,0:T(8,128)(2,1)}, u32[]{:S(2)}, u32[]{:S(2)}) collective-permute-start(bf16[49,40,128]{2,1,0:T(8,128)(2,1)} %get-tuple-element.219), channel_id=1, source_target_pairs={{0,6},{1,7},{2,0},{3,1},{4,2},{5,3},{6,4},{7,5},{8,14},{9,15},{10,... | collective-permute-start | bytes 1505288 | tf_op jit(solution)/shard_map/ppermute | solution.py:930
  689.9 62.4 %collective-permute-start.51 = (bf16[49,40,128]{2,1,0:T(8,128)(2,1)}, bf16[49,40,128]{2,1,0:T(8,128)(2,1)}, u32[]{:S(2)}, u32[]{:S(2)}) collective-permute-start(bf16[49,40,128]{2,1,0:T(8,128)(2,1)} %get-tuple-element.220), channel_id=1, source_target_pairs={{0,5},{1,6},{2,7},{3,0},{4,1},{5,2},{6,3},{7,4},{8,13},{9,14},{10,... | collective-permute-start | bytes 1505288 | tf_op jit(solution)/shard_map/ppermute | solution.py:930
  693.1 77.3 %copy-start.2 = (bf16[21,80,720]{2,1,0:T(8,128)(2,1)S(1)}, bf16[21,80,720]{2,1,0:T(8,128)(2,1)}, u32[]{:S(2)}) copy-start(bf16[21,80,720]{2,1,0:T(8,128)(2,1)} %get-tuple-element.165.own_ref) | copy-start | bytes 7257604
  693.1 77.3 %copy-start.5 = (bf16[7,80,720]{2,1,0:T(8,128)(2,1)S(1)}, bf16[7,80,720]{2,1,0:T(8,128)(2,1)}, u32[]{:S(2)}) copy-start(bf16[7,80,720]{2,1,0:T(8,128)(2,1)} %get-tuple-element.134.own_ref) | copy-start | bytes 2419204
  696.7 93.6 %collective-permute-start.52 = (bf16[49,40,128]{2,1,0:T(8,128)(2,1)}, bf16[49,40,128]{2,1,0:T(8,128)(2,1)}, u32[]{:S(2)}, u32[]{:S(2)}) collective-permute-start(bf16[49,40,128]{2,1,0:T(8,128)(2,1)} %get-tuple-element.221), channel_id=1, source_target_pairs={{0,4},{1,5},{2,6},{3,7},{4,0},{5,1},{6,2},{7,3},{8,12},{9,13},{10,... | collective-permute-start | bytes 1505288 | tf_op jit(solution)/shard_map/ppermute | solution.py:930
  697.3 94.5 %collective-permute-start.53 = (bf16[49,40,128]{2,1,0:T(8,128)(2,1)}, bf16[49,40,128]{2,1,0:T(8,128)(2,1)}, u32[]{:S(2)}, u32[]{:S(2)}) collective-permute-start(bf16[49,40,128]{2,1,0:T(8,128)(2,1)} %get-tuple-element.222), channel_id=1, source_target_pairs={{0,3},{1,4},{2,5},{3,6},{4,7},{5,0},{6,1},{7,2},{8,11},{9,12},{10,... | collective-permute-start | bytes 1505288 | tf_op jit(solution)/shard_map/ppermute | solution.py:930
  700.2 91.6 %collective-permute-start.54 = (bf16[49,40,128]{2,1,0:T(8,128)(2,1)}, bf16[49,40,128]{2,1,0:T(8,128)(2,1)}, u32[]{:S(2)}, u32[]{:S(2)}) collective-permute-start(bf16[49,40,128]{2,1,0:T(8,128)(2,1)} %get-tuple-element.223), channel_id=1, source_target_pairs={{0,2},{1,3},{2,4},{3,5},{4,6},{5,7},{6,0},{7,1},{8,10},{9,11},{10,... | collective-permute-start | bytes 1505288 | tf_op jit(solution)/shard_map/ppermute | solution.py:930
  713.9 77.8 %collective-permute-start.49 = (bf16[49,40,128]{2,1,0:T(8,128)(2,1)}, bf16[49,40,128]{2,1,0:T(8,128)(2,1)S(1)}, u32[]{:S(2)}, u32[]{:S(2)}) collective-permute-start(bf16[49,40,128]{2,1,0:T(8,128)(2,1)} %get-tuple-element.218), channel_id=1, source_target_pairs={{0,7},{1,0},{2,1},{3,2},{4,3},{5,4},{6,5},{7,6},{8,15},{9,8},{10,9... | collective-permute-start | bytes 1505288 | tf_op jit(solution)/shard_map/ppermute | solution.py:930
  752.2 39.8 %collective-permute-start.55 = (bf16[49,40,128]{2,1,0:T(8,128)(2,1)}, bf16[49,40,128]{2,1,0:T(8,128)(2,1)}, u32[]{:S(2)}, u32[]{:S(2)}) collective-permute-start(bf16[49,40,128]{2,1,0:T(8,128)(2,1)} %get-tuple-element.224), channel_id=1, source_target_pairs={{0,1},{1,2},{2,3},{3,4},{4,5},{5,6},{6,7},{7,0},{8,9},{9,10},{10,1... | collective-permute-start | bytes 1505288 | tf_op jit(solution)/shard_map/ppermute | solution.py:930
  (70 other events, 1470.9 us)
Sparse Core Ops, SparseCore 0:
  75.4 152.6 all-reduce.17
  252.7 28.2 all-gather.6
  331.4 70.5 all-gather.8
  415.7 66.8 all-gather.10
  563.8 149.2 all-reduce.19

commit v6 on v5

--- a/solution.py
+++ b/solution.py
@@ -249,7 +249,7 @@
 
 
 def analyse_low(plan, x, dft):
-    return analyse(plan, analyse_low_kernel, "analyse_low", x, dft, plan.rows1, LANES, plan.n)
+    return list(analyse(plan, analyse_low_kernel, "analyse_low", x, dft, plan.rows1, LANES, plan.n))
 
 
 def analyse_high(plan, x, dft):
@@ -670,7 +670,8 @@
     )
 
 
-def score_kernel(plan, first, members, area_ref, own_ref, all_ref, obs_ref, slope_ref, idft_ref, dec_ref, *refs):
+def score_kernel(plan, first, others, area_ref, own_ref, obs_ref, slope_ref, idft_ref, dec_ref, *refs):
+    other_refs, refs = refs[:others], refs[others:]
     grad_ref, outs, (out_high, right) = refs[0], refs[1 : 1 + plan.n], refs[1 + plan.n :]
     c = plan.channels
     base = first + pl.program_id(0) * plan.rb
@@ -680,10 +681,10 @@
         own = own_ref[r].astype(F32)
         gap = own - obs_ref[r].astype(F32)
         total = gap * lax.rsqrt(jnp.sum(gap * gap, axis=0, keepdims=True) + EPSILON)
-        for e in range(members):
-            gap = own - all_ref[e, r].astype(F32)
+        for ref in other_refs:
+            gap = own - ref[r].astype(F32)
             near = lax.rsqrt(jnp.sum(gap * gap, axis=0, keepdims=True) + EPSILON)
-            total = total - gap * (near * (1.0 / members))
+            total = total - gap * (near * (1.0 / (others + 1)))
         grad = (total * area).astype(BF)
         grad_ref[r] = grad
         block = jnp.dot(dec_ref[...], grad, preferred_element_type=F32)
@@ -710,27 +711,26 @@
         out_high[r] = high[:, r * c : (r + 1) * c]
 
 
-def score(plan, chunk, area, own, everyone, observed, slope, idft, dec):
+def score(plan, chunk, area, own, others, observed, slope, idft, dec):
     first, count = chunk
     skip = first // plan.rb
-    members = everyone.shape[0]
     cell = (plan.rb, plan.fpad, plan.lon)
     out_shape = (count, plan.rows2, LANES)
     high = 4 * plan.pairs
     here = pl.BlockSpec(cell, lambda i: (i, 0, 0))
     grad, *outs = call(
-        functools.partial(score_kernel, plan, first, members),
+        functools.partial(score_kernel, plan, first, len(others)),
         "score",
-        [area, own, everyone, observed, slope, idft, dec],
+        [area, own, observed, slope, idft, dec, *others],
         [
             pl.BlockSpec(memory_space=pltpu.SMEM),
             here,
-            pl.BlockSpec((members,) + cell, lambda i: (0, i, 0, 0)),
             pl.BlockSpec(cell, lambda i: (i + skip, 0, 0)),
             pl.BlockSpec((plan.rb, plan.channels, plan.lon), lambda i: (i, 0, 0)),
             whole(idft.shape),
             whole(dec.shape),
-        ],
+        ]
+        + [here] * len(others),
         [here]
         + [pl.BlockSpec((plan.rb, plan.rows2, LANES), lambda i: (i, 0, 0))] * plan.n
         + [pl.BlockSpec((plan.rb, high, LANES), lambda i: (i, 0, 0))],
@@ -924,14 +924,32 @@
         [low_rest.reshape(-1, lon), jnp.asarray(quads.transpose(3, 0, 1, 2, 4).reshape(-1, lon))]
     )
 
+    def other_members(block):
+        size = lax.axis_size("member")
+        chips = size // 2
+        if size % 2:
+            ring = range(1, size)
+            return [lax.ppermute(block, "member", [(i, (i + d) % size) for i in range(size)]) for d in ring]
+        blocks = [block]
+        for d in range(1, chips):
+            to = [(i, (i // 2 + d) % chips * 2 + i % 2) for i in range(size)]
+            blocks.append(lax.ppermute(block, "member", to))
+        swap = [(i, i + 1 - 2 * (i % 2)) for i in range(size)]
+        return blocks[1:] + [lax.ppermute(b, "member", swap) for b in blocks]
+
+    def outward(block):
+        return jnp.transpose(block[:, :fields], (1, 0, 2))[None]
+
     def exchange(parts):
         got = [parts[0]] + [None] * (n - 1)
         for s in sorted(range(1, n), key=lambda s: abs(2 * s - n)):
             got[n - s] = lax.ppermute(parts[s], "space", [(i, (i + s) % n) for i in range(n)])
         return got
 
-    recv = exchange(analyse_low(plan, rows, dft_low))
-    zonal_high = analyse_high(plan, rows, dft_high)
+    sent = analyse_low(plan, rows, dft_low)
+    rows_next, sent[0] = lax.optimization_barrier((rows, sent[0]))
+    recv = exchange(sent)
+    zonal_high = analyse_high(plan, rows_next, dft_high)
 
     half = plan.half_lanes
 
@@ -966,10 +984,11 @@
     reach = ceil_to(plan.low + plan.pairs + plan.span, 8)
     longer = jnp.pad(degree_gain, ((0, reach + 8 - degree_gain.shape[0]), (0, 0)))
     gain_long = jnp.stack([longer[s : s + reach] for s in range(8)])
-    synth_high = high_synthesis(plan, high_coeffs, high_inv, mix, gain_long)
 
     def after(value, other):
         return lax.optimization_barrier((value, other))
+
+    synth_high = high_synthesis(plan, high_coeffs, high_inv, mix, gain_long)
 
     predictions, grads, returned, returned_high = [], [], [], []
     gathered = []
@@ -981,12 +1000,12 @@
             plan, chunk, live_now, rows, idft, enc_t, dec_t, synth[i], synth_high
         )
         predictions.append(pred)
-        gathered.append((lax.all_gather(pred[None], "member", axis=0, tiled=True), slope))
+        gathered.append((other_members(pred), slope))
     for i, chunk in enumerate(plan.chunks):
-        pred, (everyone, slope) = predictions[i], gathered[i]
+        pred, (others, slope) = predictions[i], gathered[i]
         if i:
             pred, returned[i - 1] = after(pred, returned[i - 1])
-        grad, out, out_high = score(plan, chunk, area, pred, everyone, truth, slope, idft, dec)
+        grad, out, out_high = score(plan, chunk, area, pred, others, truth, slope, idft, dec)
         grads.append(grad)
         returned_high.append(out_high)
         if i == len(plan.chunks) - 1:
@@ -996,18 +1015,19 @@
         returned.append(exchange(out))
 
     parts = spectrum_backward(plan, returned, low_fwd, low_inv, mix_back, gain)
-    ends, high_grads = after([parts[1], parts[n - 1]], high_grads)
+    zonal_grad = high_zonal(plan, high_grads, high_fwd)
+    grads = jnp.concatenate(grads)
+    predictions = outward(jnp.concatenate(predictions))
+    ends, (zonal_grad, grads, predictions) = after(
+        [parts[1], parts[n - 1]], (zonal_grad, grads, predictions)
+    )
     parts = [parts[0], ends[0], *parts[2 : n - 1], ends[1]]
-    zonal_grad = high_zonal(plan, high_grads, high_fwd)
     last = exchange(parts)
     state_grad = finish(
-        plan, live_own, jnp.concatenate(grads), dft_main, dft_rest, through, last, zonal_grad
-    )
-
-    def outward(block):
-        return jnp.transpose(block[:, :fields], (1, 0, 2))[None]
-
-    return (outward(jnp.concatenate(predictions)), outward(state_grad))
+        plan, live_own, grads, dft_main, dft_rest, through, last, zonal_grad
+    )
+
+    return (predictions, outward(state_grad))
 
 
 def solution(mesh):

time: 828 us -> 874 us (1.056)
  starting transfers between devices: 119 us -> 189 us
  waiting for transfers between devices: 338 us -> 322 us
    ppermute x56, waiting for transfers between devices: 311 us -> 245 us  [exchange(): lax.ppermute(parts[s], 'space', [(i, (i + s) % n) for i in range(n)])]
    ppermute x56, starting transfers between devices: 119 us -> 185 us  [exchange(): lax.ppermute(parts[s], 'space', [(i, (i + s) % n) for i in range(n)])]
    ppermute x0 -> x9, waiting for transfers between devices: none -> 37.9 us  [the longest x3 36.5 us: other_members(): blocks.append(lax.ppermute(block, 'member', to))]
    psum x1, waiting for transfers between devices: 10.1 us -> 34.4 us  [on_device(): high_grads = lax.psum(high_grads, 'space')]
    psum x1, waiting for transfers between devices: 17 us -> 4.74 us  [on_device(): high_coeffs = lax.psum(high_partial(plan, zonal_high, high_fwd), 'space')]
  transfers between devices with their start and end apart: 61 -> 67, of which waited for: 33 -> 38; matrix products, arithmetic and copies ran while one was open for 5% -> 4% of each run, Pallas kernels for 26% -> 24%
where the time goes in v6:
time: 874 us; the launch traced here: 872 us
  waiting for transfers between devices  322 us (37%)
  Pallas kernels  291 us (33%)
  starting transfers between devices  189 us (22%)
  local copies, waits for them, and re-layouts  34.4 us (4%)
  other arithmetic  19 us (2%)
  between operations  14.7 us (2%)
    pallas_call x17, Pallas kernels, call(): pl.pallas_call(kernel, grid=grid, in_specs=in_specs, out_specs=out_specs,...  291 us
    ppermute x56, waiting for transfers between devices, exchange(): lax.ppermute(parts[s], 'space', [(i, (i + s) % n) for i in range(n)])  245 us
    ppermute x56, starting transfers between devices, exchange(): lax.ppermute(parts[s], 'space', [(i, (i + s) % n) for i in range(n)])  185 us
    ppermute x3, waiting for transfers between devices, other_members(): blocks.append(lax.ppermute(block, 'member', to))  36.5 us
    psum x1, waiting for transfers between devices, on_device(): high_grads = lax.psum(high_grads, 'space')  34.4 us
  transfers between devices with their start and end apart: 67, of which 38 were waited for; matrix products, arithmetic and copies ran while one was open for 4% of the time, Pallas kernels for 24%

profile of v6, /device:TPU:0, one launch (start us, length us, event | category | flops | bytes accessed | tf_op | source)
XLA Modules:
  0.0 871.9 jit_solution(5127861100115131689)
XLA Ops:
  7.2 6.1 pad.55.x_ref
  14.3 13.8 %analyse_low.1 = (bf16[49,40,128]{2,1,0:T(8,128)(2,1)}, bf16[49,40,128]{2,1,0:T(8,128)(2,1)}, bf16[49,40,128]{2,1,0:T(8,128)(2,1)}, bf16[49,40,128]{2,1,0:T(8,12...) custom-call(bf16[49,80,720]{2,1,0:T(8,128)(2,1)} %pad.55.x_ref, ...), custom_call_target="tpu_custom_call" | custom-call | bytes 41584640 | tf_op jit(solution)/shard_map/analyse_low/pallas_call | solution.py:92
  28.1 6.0 collective-permute-start
  39.6 15.0 %analyse_high.1.zonal = bf16[49,112,256]{2,1,0:T(8,128)(2,1)} custom-call(bf16[49,80,720]{2,1,0:T(8,128)(2,1)} %pad.55.x_ref, bf16[2,112,720]{2,1,0:T(8,128)(2,1)} %constant.97.clone.dft_ref), custom_call_target="tpu_custom_call" | custom-call | bytes 35108864 | tf_op jit(solution)/shard_map/analyse_high/pallas_call | solution.py:92
  55.8 6.6 legendre_tables.3
  62.4 11.9 %high_partial.1 = bf16[14,5,112,128]{3,2,1,0:T(8,128)(2,1)} custom-call(bf16[49,112,256]{2,1,0:T(8,128)(2,1)} %analyse_high.1.zonal, bf16[56,112,128]{2,1,0:T(8,128)(2,1)} %get-tuple-element.139.fwd), custom_call_target="tpu_custom_call" | custom-call | bytes 25690112 | tf_op jit(solution)/shard_map/high_partial/pallas_call | solution.py:92
  82.3 6.0 pad.54.obs_ref
  94.4 19.3 %legendre_tables.2 = (bf16[32,368,392]{2,1,0:T(8,128)(2,1)}, bf16[32,368,392]{2,1,0:T(8,128)(2,1)}) custom-call(f32[32,128]{1,0:T(8,128)} %broadcast_in_dim.18.m_ref, f32[32,128]{1,0:T(8,128)} %convert_element_type.65.shift_ref, f32[32,512]{1,0:T(8,128)} %pad.58.start_ref, f32[1,512]{1,0:T(1,128)} %bitcast.92, f32[1,512]{1,0:T(1,128)} %bitcast.93, ...), custom_call_target="tpu_custom_call" | custom-call | bytes 74276864 | tf_op jit(solution)/shard_map/legendre_tables/pallas_call | solution.py:92
  113.8 28.1 %collective-permute-done.3.refs_4_ = bf16[49,40,128]{2,1,0:T(8,128)(2,1)} collective-permute-done((bf16[49,40,128]{2,1,0:T(8,128)(2,1)}, bf16[49,40,128]{2,1,0:T(8,128)(2,1)}, u32[]{:S(2)}, u32[]{:S(2)}) %collective-permute-start.3) | collective-permute-done | bytes 501792 | tf_op jit(solution)/shard_map/ppermute | solution.py:946
  142.2 38.1 %spectrum_forward.1 = (bf16[7,64,128]{2,1,0:T(8,128)(2,1)}, bf16[7,64,128]{2,1,0:T(8,128)(2,1)}, bf16[7,64,128]{2,1,0:T(8,128)(2,1)}, bf16[7,64,128]{2,1,0:T(8,1...) custom-call(bf16[49,40,128]{2,1,0:T(8,128)(2,1)} %get-tuple-element., ...), custom_call_target="tpu_custom_call" | custom-call | bytes 119209984 | tf_op jit(solution)/shard_map/spectrum_forward/pallas_call | solution.py:92
  180.4 4.4 collective-permute-start.8
  189.2 7.4 collective-permute-done.7.refs_1_
  196.5 9.0 %collective-permute-start.12 = (bf16[21,64,128]{2,1,0:T(8,128)(2,1)}, bf16[21,64,128]{2,1,0:T(8,128)(2,1)}, u32[]{:S(2)}, u32[]{:S(2)}) collective-permute-start(bf16[21,64,128]{2,1,0:T(8,128)(2,1)} %get-tuple-element.136), channel_id=1, source_target_pairs={{0,2},{1,3},{2,4},{3,5},{4,6},{5,7},{6,0},{7,1},{8,10},{9,11},{10,... | collective-permute-start | bytes 1032200 | tf_op jit(solution)/shard_map/ppermute | solution.py:946
  205.5 12.9 %collective-permute-done.8.refs_2_ = bf16[21,64,128]{2,1,0:T(8,128)(2,1)S(1)} collective-permute-done((bf16[21,64,128]{2,1,0:T(8,128)(2,1)}, bf16[21,64,128]{2,1,0:T(8,128)(2,1)S(1)}, u32[]{:S(2)}, u32[]{:S(2)}) %collective-permute-start.8) | collective-permute-done | bytes 344096 | tf_op jit(solution)/shard_map/ppermute | solution.py:946
  222.1 4.7 all-reduce.18.cloned.1.call-done.coeffs
  226.8 16.0 %high_synthesis.1.refs_8_ = bf16[49,224,128]{2,1,0:T(8,128)(2,1)} custom-call(bf16[14,5,112,128]{3,2,1,0:T(8,128)(2,1)} %all-reduce.18.cloned.1.call-done.coeffs, bf16[56,112,128]{2,1,0:T(8,128)(2,1)} %get-tuple-element.140.inv.refs_3_, bf16[4,256,256]{2,1,0:T(8,128)(2,1)} %copy.33.refs_10_.mix, f32[8,424,128]{2,1,0:T(8,128)} %copy-done.5), custom_call_target="tpu_custom_call" | custom-call | bytes 34734080 | tf_op jit(solution)/shard_map/high_synthesis/pallas_call | solution.py:92
  242.9 21.9 %collective-permute-done.10.refs_4_ = bf16[21,64,128]{2,1,0:T(8,128)(2,1)} collective-permute-done((bf16[21,64,128]{2,1,0:T(8,128)(2,1)}, bf16[21,64,128]{2,1,0:T(8,128)(2,1)}, u32[]{:S(2)}, u32[]{:S(2)}) %collective-permute-start.10) | collective-permute-done | bytes 344096 | tf_op jit(solution)/shard_map/ppermute | solution.py:946
  265.7 17.1 %predict.3 = (bf16[21,80,720]{2,1,0:T(8,128)(2,1)}, bf16[21,128,720]{2,1,0:T(8,128)(2,1)}) custom-call(f32[49]{0:T(128)} %copy-done.50, bf16[49,80,720]{2,1,0:T(8,128)(2,1)} %pad.55.x_ref, bf16[736,720]{1,0:T(8,128)(2,1)} %pad_maximum_fusion.4.idft_ref, bf16[128,80]{1,0:T(8,128)(2,1)} %pad.56.enc_ref, bf16[80,128]{1,0:T(8,128)(2,1)} %pad.57.dec_ref, ...), custom_call_target="tpu_custom_call" | custom-call | bytes 74392336 | tf_op jit(solution)/shard_map/predict/pallas_call | solution.py:92
  288.8 5.6 collective-permute-done.31.refs_1_
  295.1 5.2 collective-permute-done.32.refs_2_
  300.3 30.8 %collective-permute-start.36 = (bf16[21,64,128]{2,1,0:T(8,128)(2,1)S(1)}, bf16[21,64,128]{2,1,0:T(8,128)(2,1)S(1)}, u32[]{:S(2)}, u32[]{:S(2)}) collective-permute-start(bf16[21,64,128]{2,1,0:T(8,128)(2,1)S(1)} %copy-done.53), channel_id=1, source_target_pairs={{0,2},{1,3},{2,4},{3,5},{4,6},{5,7},{6,0},{7,1},{8,10},{9,11},{10,... | collective-permute-start | bytes 1032200 | tf_op jit(solution)/shard_map/ppermute | solution.py:946
  331.1 8.3 collective-permute-start.37
  339.4 4.8 collective-permute-done.34.refs_4_
  347.0 17.1 %predict.5 = (bf16[21,80,720]{2,1,0:T(8,128)(2,1)}, bf16[21,128,720]{2,1,0:T(8,128)(2,1)}) custom-call(f32[49]{0:T(128)} %copy-done.50, bf16[49,80,720]{2,1,0:T(8,128)(2,1)} %pad.55.x_ref, bf16[736,720]{1,0:T(8,128)(2,1)} %pad_maximum_fusion.4.idft_ref, bf16[128,80]{1,0:T(8,128)(2,1)} %pad.56.enc_ref, bf16[80,128]{1,0:T(8,128)(2,1)} %pad.57.dec_ref, ...), custom_call_target="tpu_custom_call" | custom-call | bytes 74392336 | tf_op jit(solution)/shard_map/predict/pallas_call | solution.py:92
  374.6 8.7 collective-permute-start.19
  387.1 6.9 collective-permute-done.20.refs_7_
  394.0 7.6 predict.4
  403.1 36.5 %collective-permute-done.21.refs_0_ = bf16[7,80,720]{2,1,0:T(8,128)(2,1)} collective-permute-done((bf16[7,80,720]{2,1,0:T(8,128)(2,1)}, bf16[7,80,720]{2,1,0:T(8,128)(2,1)}, u32[]{:S(2)}, u32[]{:S(2)}) %collective-permute-start.21) | collective-permute-done | bytes 806432 | tf_op jit(solution)/shard_map/ppermute | solution.py:936
  442.3 8.2 score.3
  450.5 5.4 collective-permute-done.24.refs_1_
  457.4 3.6 collective-permute-done.25.refs_2_
  460.9 3.3 collective-permute-start.26
  469.3 3.5 collective-permute-done.27.refs_4_
  472.8 6.6 collective-permute-start.28
  482.4 3.6 collective-permute-start.29
  486.0 4.6 collective-permute-done.29.refs_6_
  490.6 4.8 collective-permute-start.30
  498.9 17.9 %score.4 = (bf16[21,80,720]{2,1,0:T(8,128)(2,1)}, bf16[21,64,128]{2,1,0:T(8,128)(2,1)}, bf16[21,64,128]{2,1,0:T(8,128)(2,1)}, bf16[21,64,128]{2,1,0:T(8,128)(2,1...) custom-call(f32[49]{0:T(128)} %get-tuple-element.236.area_ref, ...), custom_call_target="tpu_custom_call" | custom-call | bytes 106595088 | tf_op jit(solution)/shard_map/score/pallas_call | solution.py:92
  518.1 3.3 collective-permute-start.43
  521.3 6.5 collective-permute-done.41.refs_9_
  527.8 4.8 collective-permute-start.44
  534.3 4.2 collective-permute-start.45
  538.5 3.2 collective-permute-done.43.refs_11_
  541.6 21.2 %collective-permute-start.46 = (bf16[21,64,128]{2,1,0:T(8,128)(2,1)}, bf16[21,64,128]{2,1,0:T(8,128)(2,1)}, u32[]{:S(2)}, u32[]{:S(2)}) collective-permute-start(bf16[21,64,128]{2,1,0:T(8,128)(2,1)} %get-tuple-element.186), channel_id=1, source_target_pairs={{0,2},{1,3},{2,4},{3,5},{4,6},{5,7},{6,0},{7,1},{8,10},{9,11},{10,... | collective-permute-start | bytes 1032200 | tf_op jit(solution)/shard_map/ppermute | solution.py:946
  562.8 6.8 collective-permute-done.44.refs_12_
  569.7 11.8 %collective-permute-done.47.refs_15_ = bf16[21,64,128]{2,1,0:T(8,128)(2,1)} collective-permute-done((bf16[21,64,128]{2,1,0:T(8,128)(2,1)}, bf16[21,64,128]{2,1,0:T(8,128)(2,1)}, u32[]{:S(2)}, u32[]{:S(2)}) %collective-permute-start.47) | collective-permute-done | bytes 344096 | tf_op jit(solution)/shard_map/ppermute | solution.py:946
  581.5 17.9 %score.5 = (bf16[21,80,720]{2,1,0:T(8,128)(2,1)}, bf16[21,64,128]{2,1,0:T(8,128)(2,1)}, bf16[21,64,128]{2,1,0:T(8,128)(2,1)}, bf16[21,64,128]{2,1,0:T(8,128)(2,1...) custom-call(f32[49]{0:T(128)} %get-tuple-element.236.area_ref, ...), custom_call_target="tpu_custom_call" | custom-call | bytes 106595088 | tf_op jit(solution)/shard_map/score/pallas_call | solution.py:92
  599.4 14.3 %high_adjoint.1 = bf16[14,5,112,128]{3,2,1,0:T(8,128)(2,1)} custom-call(bf16[7,224,128]{2,1,0:T(8,128)(2,1)} %get-tuple-element.206.refs_0_, bf16[21,224,128]{2,1,0:T(8,128)(2,1)} %get-tuple-element.207.refs_1_, bf16[21,224,128]{2,1,0:T(8,128)(2,1)} %get-tuple-element.208.refs_2_, bf16[56,112,128]{2,1,0:T(8,128)(2,1)} %get-tuple-element.140.inv.refs_3_, ...), custom_call_target="tpu_custom_call" | custom-call | bytes 34734080 | tf_op jit(solution)/shard_map/high_adjoint/pallas_call | solution.py:92
  614.0 4.2 collective-permute-start.54
  618.2 11.6 %collective-permute-done.51.refs_17_ = bf16[21,64,128]{2,1,0:T(8,128)(2,1)} collective-permute-done((bf16[21,64,128]{2,1,0:T(8,128)(2,1)S(1)}, bf16[21,64,128]{2,1,0:T(8,128)(2,1)}, u32[]{:S(2)}, u32[]{:S(2)}) %collective-permute-start.51) | collective-permute-done | bytes 344096 | tf_op jit(solution)/shard_map/ppermute | solution.py:946
  629.8 14.7 %collective-permute-done.52.refs_18_ = bf16[21,64,128]{2,1,0:T(8,128)(2,1)} collective-permute-done((bf16[21,64,128]{2,1,0:T(8,128)(2,1)S(1)}, bf16[21,64,128]{2,1,0:T(8,128)(2,1)}, u32[]{:S(2)}, u32[]{:S(2)}) %collective-permute-start.52) | collective-permute-done | bytes 344096 | tf_op jit(solution)/shard_map/ppermute | solution.py:946
  645.6 10.0 %collective-permute-done.53.refs_19_ = bf16[21,64,128]{2,1,0:T(8,128)(2,1)} collective-permute-done((bf16[21,64,128]{2,1,0:T(8,128)(2,1)}, bf16[21,64,128]{2,1,0:T(8,128)(2,1)}, u32[]{:S(2)}, u32[]{:S(2)}) %collective-permute-start.53) | collective-permute-done | bytes 344096 | tf_op jit(solution)/shard_map/ppermute | solution.py:946
  655.6 33.1 %collective-permute-done.54.refs_20_ = bf16[21,64,128]{2,1,0:T(8,128)(2,1)} collective-permute-done((bf16[21,64,128]{2,1,0:T(8,128)(2,1)}, bf16[21,64,128]{2,1,0:T(8,128)(2,1)}, u32[]{:S(2)}, u32[]{:S(2)}) %collective-permute-start.54) | collective-permute-done | bytes 344096 | tf_op jit(solution)/shard_map/ppermute | solution.py:946
  690.4 38.2 %spectrum_backward.1 = (bf16[49,40,128]{2,1,0:T(8,128)(2,1)}, bf16[49,40,128]{2,1,0:T(8,128)(2,1)}, bf16[49,40,128]{2,1,0:T(8,128)(2,1)}, bf16[49,40,128]{2,1,0:...) custom-call(bf16[7,64,128]{2,1,0:T(8,128)(2,1)} %get-tuple-element.1, ...), custom_call_target="tpu_custom_call" | custom-call | bytes 119209984 | tf_op jit(solution)/shard_map/spectrum_backward/pallas_call | solution.py:92
  730.4 5.1 fusion
  735.5 3.5 pad_maximum_fusion.2.grad_ref
  745.1 34.4 %all-reduce.20.cloned.1.call-done.grads = bf16[14,5,112,128]{3,2,1,0:T(8,128)(2,1)} async-done(((bf16[14,5,112,128]{3,2,1,0:T(8,128)(2,1)}), bf16[14,5,112,128]{3,2,1,0:T(8,128)(2,1)}) %all-reduce.20.cloned.1.call-update) | async-done | bytes 2007056 | tf_op jit(solution)/shard_map/psum | solution.py:1014
  779.5 11.3 %high_zonal.1.refs_8_ = bf16[49,144,128]{2,1,0:T(8,128)(2,1)} custom-call(bf16[14,5,112,128]{3,2,1,0:T(8,128)(2,1)} %all-reduce.20.cloned.1.call-done.grads, bf16[56,112,128]{2,1,0:T(8,128)(2,1)} %get-tuple-element.139.fwd), custom_call_target="tpu_custom_call" | custom-call | bytes 21676032 | tf_op jit(solution)/shard_map/high_zonal/pallas_call | solution.py:92
  790.8 15.4 %collective-permute-start.58 = (bf16[49,40,128]{2,1,0:T(8,128)(2,1)}, bf16[49,40,128]{2,1,0:T(8,128)(2,1)S(1)}, u32[]{:S(2)}, u32[]{:S(2)}) collective-permute-start(bf16[49,40,128]{2,1,0:T(8,128)(2,1)} %get-tuple-element.226), channel_id=1, source_target_pairs={{0,7},{1,0},{2,1},{3,2},{4,3},{5,4},{6,5},{7,6},{8,15},{9,8},{10,9... | collective-permute-start | bytes 1505288 | tf_op jit(solution)/shard_map/ppermute | solution.py:946
  806.2 9.7 %collective-permute-start.64 = (bf16[49,40,128]{2,1,0:T(8,128)(2,1)}, bf16[49,40,128]{2,1,0:T(8,128)(2,1)S(1)}, u32[]{:S(2)}, u32[]{:S(2)}) collective-permute-start(bf16[49,40,128]{2,1,0:T(8,128)(2,1)} %get-tuple-element.232), channel_id=1, source_target_pairs={{0,1},{1,2},{2,3},{3,4},{4,5},{5,6},{6,7},{7,0},{8,9},{9,10},{10,1... | collective-permute-start | bytes 1505288 | tf_op jit(solution)/shard_map/ppermute | solution.py:946
  819.9 5.1 collective-permute-done.61.refs_4_
  825.0 11.4 %collective-permute-done.62.refs_5_ = bf16[49,40,128]{2,1,0:T(8,128)(2,1)S(1)} collective-permute-done((bf16[49,40,128]{2,1,0:T(8,128)(2,1)}, bf16[49,40,128]{2,1,0:T(8,128)(2,1)S(1)}, u32[]{:S(2)}, u32[]{:S(2)}) %collective-permute-start.62) | collective-permute-done | bytes 501792 | tf_op jit(solution)/shard_map/ppermute | solution.py:946
  838.2 21.1 %finish.1 = bf16[49,80,720]{2,1,0:T(8,128)(2,1)} custom-call(f32[49]{0:T(128)} %copy-done.50, bf16[49,80,720]{2,1,0:T(8,128)(2,1)} %pad_maximum_fusion.2.grad_ref, bf16[736,720]{1,0:T(8,128)(2,1)} %pad_maximum_fusion.5.main_ref, bf16[768,720]{1,0:T(8,128)(2,1)} %pad_maximum_fusion.3.rest_ref, bf16[80,80]{1,0:T(8,128)(2,1)} %pad.68.through_ref, ...), custom_call_target="tpu_custom_call" | custom-call | bytes 77155088 | tf_op jit(solution)/shard_map/finish/pallas_call | solution.py:92
  859.4 5.7 slice_bitcast_fusion
  (282 shorter events, 91.7 us)
Async XLA Ops:
  7.2 219.7 %all-reduce.18.cloned.1.call-start = ((), (), s32[]{:S(2)}) async-start(), calls=%async_computation | async-start | bytes 4014080 | tf_op jit(solution)/shard_map/psum | solution.py:971
  28.1 51.2 %collective-permute-start = (bf16[49,40,128]{2,1,0:T(8,128)(2,1)}, bf16[49,40,128]{2,1,0:T(8,128)(2,1)S(1)}, u32[]{:S(2)}, u32[]{:S(2)}) collective-permute-start(bf16[49,40,128]{2,1,0:T(8,128)(2,1)} %get-tuple-element.121), channel_id=1, source_target_pairs={{0,7},{1,0},{2,1},{3,2},{4,3},{5,4},{6,5},{7,6},{8,15},{9,8},{10,9... | collective-permute-start | bytes 1505288 | tf_op jit(solution)/shard_map/ppermute | solution.py:946
  34.1 47.0 %collective-permute-start.1 = (bf16[49,40,128]{2,1,0:T(8,128)(2,1)}, bf16[49,40,128]{2,1,0:T(8,128)(2,1)}, u32[]{:S(2)}, u32[]{:S(2)}) collective-permute-start(bf16[49,40,128]{2,1,0:T(8,128)(2,1)} %get-tuple-element.122), channel_id=1, source_target_pairs={{0,6},{1,7},{2,0},{3,1},{4,2},{5,3},{6,4},{7,5},{8,14},{9,15},{10,... | collective-permute-start | bytes 1505288 | tf_op jit(solution)/shard_map/ppermute | solution.py:946
  34.5 79.2 %collective-permute-start.2 = (bf16[49,40,128]{2,1,0:T(8,128)(2,1)}, bf16[49,40,128]{2,1,0:T(8,128)(2,1)}, u32[]{:S(2)}, u32[]{:S(2)}) collective-permute-start(bf16[49,40,128]{2,1,0:T(8,128)(2,1)} %get-tuple-element.123), channel_id=1, source_target_pairs={{0,5},{1,6},{2,7},{3,0},{4,1},{5,2},{6,3},{7,4},{8,13},{9,14},{10,... | collective-permute-start | bytes 1505288 | tf_op jit(solution)/shard_map/ppermute | solution.py:946
  34.5 107.4 %collective-permute-start.3 = (bf16[49,40,128]{2,1,0:T(8,128)(2,1)}, bf16[49,40,128]{2,1,0:T(8,128)(2,1)}, u32[]{:S(2)}, u32[]{:S(2)}) collective-permute-start(bf16[49,40,128]{2,1,0:T(8,128)(2,1)} %get-tuple-element.124), channel_id=1, source_target_pairs={{0,4},{1,5},{2,6},{3,7},{4,0},{5,1},{6,2},{7,3},{8,12},{9,13},{10,... | collective-permute-start | bytes 1505288 | tf_op jit(solution)/shard_map/ppermute | solution.py:946
  37.5 104.6 %collective-permute-start.4 = (bf16[49,40,128]{2,1,0:T(8,128)(2,1)}, bf16[49,40,128]{2,1,0:T(8,128)(2,1)}, u32[]{:S(2)}, u32[]{:S(2)}) collective-permute-start(bf16[49,40,128]{2,1,0:T(8,128)(2,1)} %get-tuple-element.125), channel_id=1, source_target_pairs={{0,3},{1,4},{2,5},{3,6},{4,7},{5,0},{6,1},{7,2},{8,11},{9,12},{10,... | collective-permute-start | bytes 1505288 | tf_op jit(solution)/shard_map/ppermute | solution.py:946
  74.3 705.2 %all-reduce.20.cloned.1.call-start = ((), (), s32[]{:S(2)}) async-start(), calls=%async_computation.1 | async-start | bytes 4014080 | tf_op jit(solution)/shard_map/psum | solution.py:1014
  79.2 62.9 %collective-permute-start.5 = (bf16[49,40,128]{2,1,0:T(8,128)(2,1)}, bf16[49,40,128]{2,1,0:T(8,128)(2,1)}, u32[]{:S(2)}, u32[]{:S(2)}) collective-permute-start(bf16[49,40,128]{2,1,0:T(8,128)(2,1)} %get-tuple-element.126), channel_id=1, source_target_pairs={{0,2},{1,3},{2,4},{3,5},{4,6},{5,7},{6,0},{7,1},{8,10},{9,11},{10,... | collective-permute-start | bytes 1505288 | tf_op jit(solution)/shard_map/ppermute | solution.py:946
  81.0 61.1 %collective-permute-start.6 = (bf16[49,40,128]{2,1,0:T(8,128)(2,1)}, bf16[49,40,128]{2,1,0:T(8,128)(2,1)}, u32[]{:S(2)}, u32[]{:S(2)}) collective-permute-start(bf16[49,40,128]{2,1,0:T(8,128)(2,1)} %get-tuple-element.127), channel_id=1, source_target_pairs={{0,1},{1,2},{2,3},{3,4},{4,5},{5,6},{6,7},{7,0},{8,9},{9,10},{10,1... | collective-permute-start | bytes 1505288 | tf_op jit(solution)/shard_map/ppermute | solution.py:946
  180.3 16.2 %collective-permute-start.7 = (bf16[21,64,128]{2,1,0:T(8,128)(2,1)}, bf16[21,64,128]{2,1,0:T(8,128)(2,1)S(1)}, u32[]{:S(2)}, u32[]{:S(2)}) collective-permute-start(bf16[21,64,128]{2,1,0:T(8,128)(2,1)} %get-tuple-element.131), channel_id=1, source_target_pairs={{0,7},{1,0},{2,1},{3,2},{4,3},{5,4},{6,5},{7,6},{8,15},{9,8},{10,9... | collective-permute-start | bytes 1032200 | tf_op jit(solution)/shard_map/ppermute | solution.py:946
  180.4 38.1 %collective-permute-start.8 = (bf16[21,64,128]{2,1,0:T(8,128)(2,1)}, bf16[21,64,128]{2,1,0:T(8,128)(2,1)S(1)}, u32[]{:S(2)}, u32[]{:S(2)}) collective-permute-start(bf16[21,64,128]{2,1,0:T(8,128)(2,1)} %get-tuple-element.132), channel_id=1, source_target_pairs={{0,6},{1,7},{2,0},{3,1},{4,2},{5,3},{6,4},{7,5},{8,14},{9,15},{10,... | collective-permute-start | bytes 1032200 | tf_op jit(solution)/shard_map/ppermute | solution.py:946
  184.8 58.1 %collective-permute-start.9 = (bf16[21,64,128]{2,1,0:T(8,128)(2,1)}, bf16[21,64,128]{2,1,0:T(8,128)(2,1)}, u32[]{:S(2)}, u32[]{:S(2)}) collective-permute-start(bf16[21,64,128]{2,1,0:T(8,128)(2,1)} %get-tuple-element.133), channel_id=1, source_target_pairs={{0,5},{1,6},{2,7},{3,0},{4,1},{5,2},{6,3},{7,4},{8,13},{9,14},{10,... | collective-permute-start | bytes 1032200 | tf_op jit(solution)/shard_map/ppermute | solution.py:946
  186.4 78.4 %collective-permute-start.10 = (bf16[21,64,128]{2,1,0:T(8,128)(2,1)}, bf16[21,64,128]{2,1,0:T(8,128)(2,1)}, u32[]{:S(2)}, u32[]{:S(2)}) collective-permute-start(bf16[21,64,128]{2,1,0:T(8,128)(2,1)} %get-tuple-element.134), channel_id=1, source_target_pairs={{0,4},{1,5},{2,6},{3,7},{4,0},{5,1},{6,2},{7,3},{8,12},{9,13},{10,... | collective-permute-start | bytes 1032200 | tf_op jit(solution)/shard_map/ppermute | solution.py:946
  189.2 76.4 %collective-permute-start.11 = (bf16[21,64,128]{2,1,0:T(8,128)(2,1)}, bf16[21,64,128]{2,1,0:T(8,128)(2,1)}, u32[]{:S(2)}, u32[]{:S(2)}) collective-permute-start(bf16[21,64,128]{2,1,0:T(8,128)(2,1)} %get-tuple-element.135), channel_id=1, source_target_pairs={{0,3},{1,4},{2,5},{3,6},{4,7},{5,0},{6,1},{7,2},{8,11},{9,12},{10,... | collective-permute-start | bytes 1032200 | tf_op jit(solution)/shard_map/ppermute | solution.py:946
  196.5 69.1 %collective-permute-start.12 = (bf16[21,64,128]{2,1,0:T(8,128)(2,1)}, bf16[21,64,128]{2,1,0:T(8,128)(2,1)}, u32[]{:S(2)}, u32[]{:S(2)}) collective-permute-start(bf16[21,64,128]{2,1,0:T(8,128)(2,1)} %get-tuple-element.136), channel_id=1, source_target_pairs={{0,2},{1,3},{2,4},{3,5},{4,6},{5,7},{6,0},{7,1},{8,10},{9,11},{10,... | collective-permute-start | bytes 1032200 | tf_op jit(solution)/shard_map/ppermute | solution.py:946
  218.4 47.2 %collective-permute-start.13 = (bf16[21,64,128]{2,1,0:T(8,128)(2,1)}, bf16[21,64,128]{2,1,0:T(8,128)(2,1)}, u32[]{:S(2)}, u32[]{:S(2)}) collective-permute-start(bf16[21,64,128]{2,1,0:T(8,128)(2,1)} %get-tuple-element.137), channel_id=1, source_target_pairs={{0,1},{1,2},{2,3},{3,4},{4,5},{5,6},{6,7},{7,0},{8,9},{9,10},{10,1... | collective-permute-start | bytes 1032200 | tf_op jit(solution)/shard_map/ppermute | solution.py:946
  282.8 103.8 %collective-permute-start.38 = (bf16[21,80,720]{2,1,0:T(8,128)(2,1)}, bf16[21,80,720]{2,1,0:T(8,128)(2,1)}, u32[]{:S(2)}, u32[]{:S(2)}) collective-permute-start(bf16[21,80,720]{2,1,0:T(8,128)(2,1)} %get-tuple-element.178.own_ref), channel_id=1, source_target_pairs={{0,16},{8,24},{16,0},{24,8},{1,17},{9,25},{17,1},{25,9},{2,18},{10... | collective-permute-start | bytes 7257608 | tf_op jit(solution)/shard_map/ppermute | solution.py:936
  284.3 10.1 %collective-permute-start.31 = (bf16[21,64,128]{2,1,0:T(8,128)(2,1)S(1)}, bf16[21,64,128]{2,1,0:T(8,128)(2,1)S(1)}, u32[]{:S(2)}, u32[]{:S(2)}) collective-permute-start(bf16[21,64,128]{2,1,0:T(8,128)(2,1)S(1)} %copy-done.56), channel_id=1, source_target_pairs={{0,7},{1,0},{2,1},{3,2},{4,3},{5,4},{6,5},{7,6},{8,15},{9,8},{10,9... | collective-permute-start | bytes 1032200 | tf_op jit(solution)/shard_map/ppermute | solution.py:946
  284.3 15.9 %collective-permute-start.32 = (bf16[21,64,128]{2,1,0:T(8,128)(2,1)S(1)}, bf16[21,64,128]{2,1,0:T(8,128)(2,1)S(1)}, u32[]{:S(2)}, u32[]{:S(2)}) collective-permute-start(bf16[21,64,128]{2,1,0:T(8,128)(2,1)S(1)} %copy-done.55), channel_id=1, source_target_pairs={{0,6},{1,7},{2,0},{3,1},{4,2},{5,3},{6,4},{7,5},{8,14},{9,15},{10,... | collective-permute-start | bytes 1032200 | tf_op jit(solution)/shard_map/ppermute | solution.py:946
  285.3 45.7 %collective-permute-start.33 = (bf16[21,64,128]{2,1,0:T(8,128)(2,1)S(1)}, bf16[21,64,128]{2,1,0:T(8,128)(2,1)S(1)}, u32[]{:S(2)}, u32[]{:S(2)}) collective-permute-start(bf16[21,64,128]{2,1,0:T(8,128)(2,1)S(1)} %copy-done.54), channel_id=1, source_target_pairs={{0,5},{1,6},{2,7},{3,0},{4,1},{5,2},{6,3},{7,4},{8,13},{9,14},{10,... | collective-permute-start | bytes 1032200 | tf_op jit(solution)/shard_map/ppermute | solution.py:946
  286.2 57.9 %collective-permute-start.34 = (bf16[21,64,128]{2,1,0:T(8,128)(2,1)}, bf16[21,64,128]{2,1,0:T(8,128)(2,1)S(1)}, u32[]{:S(2)}, u32[]{:S(2)}) collective-permute-start(bf16[21,64,128]{2,1,0:T(8,128)(2,1)} %get-tuple-element.173), channel_id=1, source_target_pairs={{0,4},{1,5},{2,6},{3,7},{4,0},{5,1},{6,2},{7,3},{8,12},{9,13},{10,... | collective-permute-start | bytes 1032200 | tf_op jit(solution)/shard_map/ppermute | solution.py:946
  294.4 50.9 %collective-permute-start.35 = (bf16[21,64,128]{2,1,0:T(8,128)(2,1)}, bf16[21,64,128]{2,1,0:T(8,128)(2,1)S(1)}, u32[]{:S(2)}, u32[]{:S(2)}) collective-permute-start(bf16[21,64,128]{2,1,0:T(8,128)(2,1)} %get-tuple-element.174), channel_id=1, source_target_pairs={{0,3},{1,4},{2,5},{3,6},{4,7},{5,0},{6,1},{7,2},{8,11},{9,12},{10,... | collective-permute-start | bytes 1032200 | tf_op jit(solution)/shard_map/ppermute | solution.py:946
  300.3 45.1 %collective-permute-start.36 = (bf16[21,64,128]{2,1,0:T(8,128)(2,1)S(1)}, bf16[21,64,128]{2,1,0:T(8,128)(2,1)S(1)}, u32[]{:S(2)}, u32[]{:S(2)}) collective-permute-start(bf16[21,64,128]{2,1,0:T(8,128)(2,1)S(1)} %copy-done.53), channel_id=1, source_target_pairs={{0,2},{1,3},{2,4},{3,5},{4,6},{5,7},{6,0},{7,1},{8,10},{9,11},{10,... | collective-permute-start | bytes 1032200 | tf_op jit(solution)/shard_map/ppermute | solution.py:946
  331.1 14.3 %collective-permute-start.37 = (bf16[21,64,128]{2,1,0:T(8,128)(2,1)S(1)}, bf16[21,64,128]{2,1,0:T(8,128)(2,1)S(1)}, u32[]{:S(2)}, u32[]{:S(2)}) collective-permute-start(bf16[21,64,128]{2,1,0:T(8,128)(2,1)S(1)} %copy-done.52), channel_id=1, source_target_pairs={{0,1},{1,2},{2,3},{3,4},{4,5},{5,6},{6,7},{7,0},{8,9},{9,10},{10,1... | collective-permute-start | bytes 1032200 | tf_op jit(solution)/shard_map/ppermute | solution.py:946
  364.2 75.9 %collective-permute-start.48 = (bf16[21,80,720]{2,1,0:T(8,128)(2,1)}, bf16[21,80,720]{2,1,0:T(8,128)(2,1)}, u32[]{:S(2)}, u32[]{:S(2)}) collective-permute-start(bf16[21,80,720]{2,1,0:T(8,128)(2,1)} %get-tuple-element.196.own_ref), channel_id=1, source_target_pairs={{0,16},{8,24},{16,0},{24,8},{1,17},{9,25},{17,1},{25,9},{2,18},{10... | collective-permute-start | bytes 7257608 | tf_op jit(solution)/shard_map/ppermute | solution.py:936
  364.8 7.6 collective-permute-start.15
  367.5 7.1 collective-permute-start.16
  369.6 16.6 %collective-permute-start.17 = (bf16[7,64,128]{2,1,0:T(8,128)(2,1)}, bf16[7,64,128]{2,1,0:T(8,128)(2,1)S(1)}, u32[]{:S(2)}, u32[]{:S(2)}) collective-permute-start(bf16[7,64,128]{2,1,0:T(8,128)(2,1)} %get-tuple-element.146), channel_id=1, source_target_pairs={{0,4},{1,5},{2,6},{3,7},{4,0},{5,1},{6,2},{7,3},{8,12},{9,13},{10,... | collective-permute-start | bytes 344072 | tf_op jit(solution)/shard_map/ppermute | solution.py:946
  372.4 14.1 %collective-permute-start.18 = (bf16[7,64,128]{2,1,0:T(8,128)(2,1)}, bf16[7,64,128]{2,1,0:T(8,128)(2,1)S(1)}, u32[]{:S(2)}, u32[]{:S(2)}) collective-permute-start(bf16[7,64,128]{2,1,0:T(8,128)(2,1)} %get-tuple-element.147), channel_id=1, source_target_pairs={{0,3},{1,4},{2,5},{3,6},{4,7},{5,0},{6,1},{7,2},{8,11},{9,12},{10,... | collective-permute-start | bytes 344072 | tf_op jit(solution)/shard_map/ppermute | solution.py:946
  374.6 12.4 %collective-permute-start.19 = (bf16[7,64,128]{2,1,0:T(8,128)(2,1)}, bf16[7,64,128]{2,1,0:T(8,128)(2,1)S(1)}, u32[]{:S(2)}, u32[]{:S(2)}) collective-permute-start(bf16[7,64,128]{2,1,0:T(8,128)(2,1)} %get-tuple-element.148), channel_id=1, source_target_pairs={{0,2},{1,3},{2,4},{3,5},{4,6},{5,7},{6,0},{7,1},{8,10},{9,11},{10,... | collective-permute-start | bytes 344072 | tf_op jit(solution)/shard_map/ppermute | solution.py:946
  386.2 7.8 collective-permute-start.20
  386.5 111.8 %collective-permute-start.39 = (bf16[21,80,720]{2,1,0:T(8,128)(2,1)S(1)}, bf16[21,80,720]{2,1,0:T(8,128)(2,1)}, u32[]{:S(2)}, u32[]{:S(2)}) collective-permute-start(bf16[21,80,720]{2,1,0:T(8,128)(2,1)S(1)} %copy-done.3), channel_id=1, source_target_pairs={{0,8},{8,0},{16,24},{24,16},{1,9},{9,1},{17,25},{25,17},{2,10},{10... | collective-permute-start | bytes 7257608 | tf_op jit(solution)/shard_map/ppermute | solution.py:938
  386.6 111.7 %collective-permute-start.40 = (bf16[21,80,720]{2,1,0:T(8,128)(2,1)}, bf16[21,80,720]{2,1,0:T(8,128)(2,1)}, u32[]{:S(2)}, u32[]{:S(2)}) collective-permute-start(bf16[21,80,720]{2,1,0:T(8,128)(2,1)} %collective-permute-done.38.refs_0_), channel_id=1, source_target_pairs={{0,8},{8,0},{16,24},{24,16},{1,9},{9,1},{17,25},{25,17},{2,10},{10... | collective-permute-start | bytes 7257608 | tf_op jit(solution)/shard_map/ppermute | solution.py:938
  401.6 37.9 %collective-permute-start.21 = (bf16[7,80,720]{2,1,0:T(8,128)(2,1)}, bf16[7,80,720]{2,1,0:T(8,128)(2,1)}, u32[]{:S(2)}, u32[]{:S(2)}) collective-permute-start(bf16[7,80,720]{2,1,0:T(8,128)(2,1)} %get-tuple-element.150.own_ref), channel_id=1, source_target_pairs={{0,16},{8,24},{16,0},{24,8},{1,17},{9,25},{17,1},{25,9},{2,18},{10... | collective-permute-start | bytes 2419208 | tf_op jit(solution)/shard_map/ppermute | solution.py:936
  403.1 36.5 %collective-permute-start.22 = (bf16[7,80,720]{2,1,0:T(8,128)(2,1)}, bf16[7,80,720]{2,1,0:T(8,128)(2,1)}, u32[]{:S(2)}, u32[]{:S(2)}) collective-permute-start(bf16[7,80,720]{2,1,0:T(8,128)(2,1)} %get-tuple-element.150.own_ref), channel_id=1, source_target_pairs={{0,8},{8,0},{16,24},{24,16},{1,9},{9,1},{17,25},{25,17},{2,10},{10... | collective-permute-start | bytes 2419208 | tf_op jit(solution)/shard_map/ppermute | solution.py:938
  439.6 141.9 %collective-permute-start.49 = (bf16[21,80,720]{2,1,0:T(8,128)(2,1)}, bf16[21,80,720]{2,1,0:T(8,128)(2,1)}, u32[]{:S(2)}, u32[]{:S(2)}) collective-permute-start(bf16[21,80,720]{2,1,0:T(8,128)(2,1)} %get-tuple-element.196.own_ref), channel_id=1, source_target_pairs={{0,8},{8,0},{16,24},{24,16},{1,9},{9,1},{17,25},{25,17},{2,10},{10... | collective-permute-start | bytes 7257608 | tf_op jit(solution)/shard_map/ppermute | solution.py:938
  440.1 141.4 %collective-permute-start.50 = (bf16[21,80,720]{2,1,0:T(8,128)(2,1)}, bf16[21,80,720]{2,1,0:T(8,128)(2,1)}, u32[]{:S(2)}, u32[]{:S(2)}) collective-permute-start(bf16[21,80,720]{2,1,0:T(8,128)(2,1)} %collective-permute-done.48.refs_0_), channel_id=1, source_target_pairs={{0,8},{8,0},{16,24},{24,16},{1,9},{9,1},{17,25},{25,17},{2,10},{10... | collective-permute-start | bytes 7257608 | tf_op jit(solution)/shard_map/ppermute | solution.py:938
  450.5 5.4 collective-permute-start.24
  460.9 5.9 collective-permute-start.26
  466.9 5.9 collective-permute-start.27
  472.8 9.6 %collective-permute-start.28 = (bf16[7,64,128]{2,1,0:T(8,128)(2,1)}, bf16[7,64,128]{2,1,0:T(8,128)(2,1)S(1)}, u32[]{:S(2)}, u32[]{:S(2)}) collective-permute-start(bf16[7,64,128]{2,1,0:T(8,128)(2,1)} %get-tuple-element.158), channel_id=1, source_target_pairs={{0,3},{1,4},{2,5},{3,6},{4,7},{5,0},{6,1},{7,2},{8,11},{9,12},{10,... | collective-permute-start | bytes 344072 | tf_op jit(solution)/shard_map/ppermute | solution.py:946
  482.4 8.2 collective-permute-start.29
  490.6 7.7 collective-permute-start.30
  516.8 11.0 %collective-permute-start.41 = (bf16[21,64,128]{2,1,0:T(8,128)(2,1)}, bf16[21,64,128]{2,1,0:T(8,128)(2,1)}, u32[]{:S(2)}, u32[]{:S(2)}) collective-permute-start(bf16[21,64,128]{2,1,0:T(8,128)(2,1)} %get-tuple-element.181), channel_id=1, source_target_pairs={{0,7},{1,0},{2,1},{3,2},{4,3},{5,4},{6,5},{7,6},{8,15},{9,8},{10,9... | collective-permute-start | bytes 1032200 | tf_op jit(solution)/shard_map/ppermute | solution.py:946
  518.1 16.2 %collective-permute-start.42 = (bf16[21,64,128]{2,1,0:T(8,128)(2,1)}, bf16[21,64,128]{2,1,0:T(8,128)(2,1)}, u32[]{:S(2)}, u32[]{:S(2)}) collective-permute-start(bf16[21,64,128]{2,1,0:T(8,128)(2,1)} %get-tuple-element.182), channel_id=1, source_target_pairs={{0,6},{1,7},{2,0},{3,1},{4,2},{5,3},{6,4},{7,5},{8,14},{9,15},{10,... | collective-permute-start | bytes 1032200 | tf_op jit(solution)/shard_map/ppermute | solution.py:946
  518.1 23.6 %collective-permute-start.43 = (bf16[21,64,128]{2,1,0:T(8,128)(2,1)}, bf16[21,64,128]{2,1,0:T(8,128)(2,1)}, u32[]{:S(2)}, u32[]{:S(2)}) collective-permute-start(bf16[21,64,128]{2,1,0:T(8,128)(2,1)} %get-tuple-element.183), channel_id=1, source_target_pairs={{0,5},{1,6},{2,7},{3,0},{4,1},{5,2},{6,3},{7,4},{8,13},{9,14},{10,... | collective-permute-start | bytes 1032200 | tf_op jit(solution)/shard_map/ppermute | solution.py:946
  527.8 41.9 %collective-permute-start.44 = (bf16[21,64,128]{2,1,0:T(8,128)(2,1)}, bf16[21,64,128]{2,1,0:T(8,128)(2,1)}, u32[]{:S(2)}, u32[]{:S(2)}) collective-permute-start(bf16[21,64,128]{2,1,0:T(8,128)(2,1)} %get-tuple-element.184), channel_id=1, source_target_pairs={{0,4},{1,5},{2,6},{3,7},{4,0},{5,1},{6,2},{7,3},{8,12},{9,13},{10,... | collective-permute-start | bytes 1032200 | tf_op jit(solution)/shard_map/ppermute | solution.py:946
  534.3 35.4 %collective-permute-start.45 = (bf16[21,64,128]{2,1,0:T(8,128)(2,1)}, bf16[21,64,128]{2,1,0:T(8,128)(2,1)}, u32[]{:S(2)}, u32[]{:S(2)}) collective-permute-start(bf16[21,64,128]{2,1,0:T(8,128)(2,1)} %get-tuple-element.185), channel_id=1, source_target_pairs={{0,3},{1,4},{2,5},{3,6},{4,7},{5,0},{6,1},{7,2},{8,11},{9,12},{10,... | collective-permute-start | bytes 1032200 | tf_op jit(solution)/shard_map/ppermute | solution.py:946
  541.6 28.0 %collective-permute-start.46 = (bf16[21,64,128]{2,1,0:T(8,128)(2,1)}, bf16[21,64,128]{2,1,0:T(8,128)(2,1)}, u32[]{:S(2)}, u32[]{:S(2)}) collective-permute-start(bf16[21,64,128]{2,1,0:T(8,128)(2,1)} %get-tuple-element.186), channel_id=1, source_target_pairs={{0,2},{1,3},{2,4},{3,5},{4,6},{5,7},{6,0},{7,1},{8,10},{9,11},{10,... | collective-permute-start | bytes 1032200 | tf_op jit(solution)/shard_map/ppermute | solution.py:946
  569.7 11.8 %collective-permute-start.47 = (bf16[21,64,128]{2,1,0:T(8,128)(2,1)}, bf16[21,64,128]{2,1,0:T(8,128)(2,1)}, u32[]{:S(2)}, u32[]{:S(2)}) collective-permute-start(bf16[21,64,128]{2,1,0:T(8,128)(2,1)} %get-tuple-element.187), channel_id=1, source_target_pairs={{0,1},{1,2},{2,3},{3,4},{4,5},{5,6},{6,7},{7,0},{8,9},{9,10},{10,1... | collective-permute-start | bytes 1032200 | tf_op jit(solution)/shard_map/ppermute | solution.py:946
  613.8 16.1 %collective-permute-start.51 = (bf16[21,64,128]{2,1,0:T(8,128)(2,1)S(1)}, bf16[21,64,128]{2,1,0:T(8,128)(2,1)}, u32[]{:S(2)}, u32[]{:S(2)}) collective-permute-start(bf16[21,64,128]{2,1,0:T(8,128)(2,1)S(1)} %copy-done.58), channel_id=1, source_target_pairs={{0,7},{1,0},{2,1},{3,2},{4,3},{5,4},{6,5},{7,6},{8,15},{9,8},{10,9... | collective-permute-start | bytes 1032200 | tf_op jit(solution)/shard_map/ppermute | solution.py:946
  613.8 30.7 %collective-permute-start.52 = (bf16[21,64,128]{2,1,0:T(8,128)(2,1)S(1)}, bf16[21,64,128]{2,1,0:T(8,128)(2,1)}, u32[]{:S(2)}, u32[]{:S(2)}) collective-permute-start(bf16[21,64,128]{2,1,0:T(8,128)(2,1)S(1)} %copy-done.57), channel_id=1, source_target_pairs={{0,6},{1,7},{2,0},{3,1},{4,2},{5,3},{6,4},{7,5},{8,14},{9,15},{10,... | collective-permute-start | bytes 1032200 | tf_op jit(solution)/shard_map/ppermute | solution.py:946
  613.9 41.7 %collective-permute-start.53 = (bf16[21,64,128]{2,1,0:T(8,128)(2,1)}, bf16[21,64,128]{2,1,0:T(8,128)(2,1)}, u32[]{:S(2)}, u32[]{:S(2)}) collective-permute-start(bf16[21,64,128]{2,1,0:T(8,128)(2,1)} %get-tuple-element.212), channel_id=1, source_target_pairs={{0,5},{1,6},{2,7},{3,0},{4,1},{5,2},{6,3},{7,4},{8,13},{9,14},{10,... | collective-permute-start | bytes 1032200 | tf_op jit(solution)/shard_map/ppermute | solution.py:946
  614.0 74.8 %collective-permute-start.54 = (bf16[21,64,128]{2,1,0:T(8,128)(2,1)}, bf16[21,64,128]{2,1,0:T(8,128)(2,1)}, u32[]{:S(2)}, u32[]{:S(2)}) collective-permute-start(bf16[21,64,128]{2,1,0:T(8,128)(2,1)} %get-tuple-element.213), channel_id=1, source_target_pairs={{0,4},{1,5},{2,6},{3,7},{4,0},{5,1},{6,2},{7,3},{8,12},{9,13},{10,... | collective-permute-start | bytes 1032200 | tf_op jit(solution)/shard_map/ppermute | solution.py:946
  618.2 72.2 %collective-permute-start.55 = (bf16[21,64,128]{2,1,0:T(8,128)(2,1)}, bf16[21,64,128]{2,1,0:T(8,128)(2,1)}, u32[]{:S(2)}, u32[]{:S(2)}) collective-permute-start(bf16[21,64,128]{2,1,0:T(8,128)(2,1)} %get-tuple-element.214), channel_id=1, source_target_pairs={{0,3},{1,4},{2,5},{3,6},{4,7},{5,0},{6,1},{7,2},{8,11},{9,12},{10,... | collective-permute-start | bytes 1032200 | tf_op jit(solution)/shard_map/ppermute | solution.py:946
  629.8 60.6 %collective-permute-start.56 = (bf16[21,64,128]{2,1,0:T(8,128)(2,1)}, bf16[21,64,128]{2,1,0:T(8,128)(2,1)}, u32[]{:S(2)}, u32[]{:S(2)}) collective-permute-start(bf16[21,64,128]{2,1,0:T(8,128)(2,1)} %get-tuple-element.215), channel_id=1, source_target_pairs={{0,2},{1,3},{2,4},{3,5},{4,6},{5,7},{6,0},{7,1},{8,10},{9,11},{10,... | collective-permute-start | bytes 1032200 | tf_op jit(solution)/shard_map/ppermute | solution.py:946
  644.6 45.8 %collective-permute-start.57 = (bf16[21,64,128]{2,1,0:T(8,128)(2,1)}, bf16[21,64,128]{2,1,0:T(8,128)(2,1)}, u32[]{:S(2)}, u32[]{:S(2)}) collective-permute-start(bf16[21,64,128]{2,1,0:T(8,128)(2,1)} %get-tuple-element.216), channel_id=1, source_target_pairs={{0,1},{1,2},{2,3},{3,4},{4,5},{5,6},{6,7},{7,0},{8,9},{9,10},{10,1... | collective-permute-start | bytes 1032200 | tf_op jit(solution)/shard_map/ppermute | solution.py:946
  728.6 62.2 %collective-permute-start.59 = (bf16[49,40,128]{2,1,0:T(8,128)(2,1)}, bf16[49,40,128]{2,1,0:T(8,128)(2,1)S(1)}, u32[]{:S(2)}, u32[]{:S(2)}) collective-permute-start(bf16[49,40,128]{2,1,0:T(8,128)(2,1)} %get-tuple-element.227), channel_id=1, source_target_pairs={{0,6},{1,7},{2,0},{3,1},{4,2},{5,3},{6,4},{7,5},{8,14},{9,15},{10,... | collective-permute-start | bytes 1505288 | tf_op jit(solution)/shard_map/ppermute | solution.py:946
  728.7 77.5 %collective-permute-start.60 = (bf16[49,40,128]{2,1,0:T(8,128)(2,1)}, bf16[49,40,128]{2,1,0:T(8,128)(2,1)}, u32[]{:S(2)}, u32[]{:S(2)}) collective-permute-start(bf16[49,40,128]{2,1,0:T(8,128)(2,1)} %get-tuple-element.228), channel_id=1, source_target_pairs={{0,5},{1,6},{2,7},{3,0},{4,1},{5,2},{6,3},{7,4},{8,13},{9,14},{10,... | collective-permute-start | bytes 1505288 | tf_op jit(solution)/shard_map/ppermute | solution.py:946
  738.9 86.1 %collective-permute-start.61 = (bf16[49,40,128]{2,1,0:T(8,128)(2,1)}, bf16[49,40,128]{2,1,0:T(8,128)(2,1)S(1)}, u32[]{:S(2)}, u32[]{:S(2)}) collective-permute-start(bf16[49,40,128]{2,1,0:T(8,128)(2,1)} %get-tuple-element.229), channel_id=1, source_target_pairs={{0,4},{1,5},{2,6},{3,7},{4,0},{5,1},{6,2},{7,3},{8,12},{9,13},{10,... | collective-permute-start | bytes 1505288 | tf_op jit(solution)/shard_map/ppermute | solution.py:946
  740.9 95.6 %collective-permute-start.62 = (bf16[49,40,128]{2,1,0:T(8,128)(2,1)}, bf16[49,40,128]{2,1,0:T(8,128)(2,1)S(1)}, u32[]{:S(2)}, u32[]{:S(2)}) collective-permute-start(bf16[49,40,128]{2,1,0:T(8,128)(2,1)} %get-tuple-element.230), channel_id=1, source_target_pairs={{0,3},{1,4},{2,5},{3,6},{4,7},{5,0},{6,1},{7,2},{8,11},{9,12},{10,... | collective-permute-start | bytes 1505288 | tf_op jit(solution)/shard_map/ppermute | solution.py:946
  742.3 94.2 %collective-permute-start.63 = (bf16[49,40,128]{2,1,0:T(8,128)(2,1)}, bf16[49,40,128]{2,1,0:T(8,128)(2,1)S(1)}, u32[]{:S(2)}, u32[]{:S(2)}) collective-permute-start(bf16[49,40,128]{2,1,0:T(8,128)(2,1)} %get-tuple-element.231), channel_id=1, source_target_pairs={{0,2},{1,3},{2,4},{3,5},{4,6},{5,7},{6,0},{7,1},{8,10},{9,11},{10,... | collective-permute-start | bytes 1505288 | tf_op jit(solution)/shard_map/ppermute | solution.py:946
  790.8 45.7 %collective-permute-start.58 = (bf16[49,40,128]{2,1,0:T(8,128)(2,1)}, bf16[49,40,128]{2,1,0:T(8,128)(2,1)S(1)}, u32[]{:S(2)}, u32[]{:S(2)}) collective-permute-start(bf16[49,40,128]{2,1,0:T(8,128)(2,1)} %get-tuple-element.226), channel_id=1, source_target_pairs={{0,7},{1,0},{2,1},{3,2},{4,3},{5,4},{6,5},{7,6},{8,15},{9,8},{10,9... | collective-permute-start | bytes 1505288 | tf_op jit(solution)/shard_map/ppermute | solution.py:946
  806.2 31.2 %collective-permute-start.64 = (bf16[49,40,128]{2,1,0:T(8,128)(2,1)}, bf16[49,40,128]{2,1,0:T(8,128)(2,1)S(1)}, u32[]{:S(2)}, u32[]{:S(2)}) collective-permute-start(bf16[49,40,128]{2,1,0:T(8,128)(2,1)} %get-tuple-element.232), channel_id=1, source_target_pairs={{0,1},{1,2},{2,3},{3,4},{4,5},{5,6},{6,7},{7,0},{8,9},{9,10},{10,1... | collective-permute-start | bytes 1505288 | tf_op jit(solution)/shard_map/ppermute | solution.py:946
  (65 other events, 1329.9 us)
Sparse Core Ops, SparseCore 0:
  74.4 152.4 all-reduce.17
  613.9 165.5 all-reduce.19

commit v7 on v5

--- a/solution.py
+++ b/solution.py
@@ -51,7 +51,8 @@
         self.rb = max(k for k in range(1, 9) if band % k == 0)
         blocks = band // self.rb
         half = blocks // 2
-        counts = [count for count in (1, blocks - 1 - half, half) if count > 0]
+        rest = (blocks - half) // 2
+        counts = [count for count in (rest, blocks - half - rest, half) if count > 0]
         self.chunks = []
         start = 0
         for count in counts:
@@ -249,7 +250,7 @@
 
 
 def analyse_low(plan, x, dft):
-    return analyse(plan, analyse_low_kernel, "analyse_low", x, dft, plan.rows1, LANES, plan.n)
+    return list(analyse(plan, analyse_low_kernel, "analyse_low", x, dft, plan.rows1, LANES, plan.n))
 
 
 def analyse_high(plan, x, dft):
@@ -924,14 +925,19 @@
         [low_rest.reshape(-1, lon), jnp.asarray(quads.transpose(3, 0, 1, 2, 4).reshape(-1, lon))]
     )
 
+    def outward(block):
+        return jnp.transpose(block[:, :fields], (1, 0, 2))[None]
+
     def exchange(parts):
         got = [parts[0]] + [None] * (n - 1)
         for s in sorted(range(1, n), key=lambda s: abs(2 * s - n)):
             got[n - s] = lax.ppermute(parts[s], "space", [(i, (i + s) % n) for i in range(n)])
         return got
 
-    recv = exchange(analyse_low(plan, rows, dft_low))
-    zonal_high = analyse_high(plan, rows, dft_high)
+    sent = analyse_low(plan, rows, dft_low)
+    rows_next, sent[0] = lax.optimization_barrier((rows, sent[0]))
+    recv = exchange(sent)
+    zonal_high = analyse_high(plan, rows_next, dft_high)
 
     half = plan.half_lanes
 
@@ -966,10 +972,11 @@
     reach = ceil_to(plan.low + plan.pairs + plan.span, 8)
     longer = jnp.pad(degree_gain, ((0, reach + 8 - degree_gain.shape[0]), (0, 0)))
     gain_long = jnp.stack([longer[s : s + reach] for s in range(8)])
-    synth_high = high_synthesis(plan, high_coeffs, high_inv, mix, gain_long)
 
     def after(value, other):
         return lax.optimization_barrier((value, other))
+
+    synth_high = high_synthesis(plan, high_coeffs, high_inv, mix, gain_long)
 
     predictions, grads, returned, returned_high = [], [], [], []
     gathered = []
@@ -996,18 +1003,19 @@
         returned.append(exchange(out))
 
     parts = spectrum_backward(plan, returned, low_fwd, low_inv, mix_back, gain)
-    ends, high_grads = after([parts[1], parts[n - 1]], high_grads)
+    zonal_grad = high_zonal(plan, high_grads, high_fwd)
+    grads = jnp.concatenate(grads)
+    predictions = outward(jnp.concatenate(predictions))
+    ends, (zonal_grad, grads, predictions) = after(
+        [parts[1], parts[n - 1]], (zonal_grad, grads, predictions)
+    )
     parts = [parts[0], ends[0], *parts[2 : n - 1], ends[1]]
-    zonal_grad = high_zonal(plan, high_grads, high_fwd)
     last = exchange(parts)
     state_grad = finish(
-        plan, live_own, jnp.concatenate(grads), dft_main, dft_rest, through, last, zonal_grad
-    )
-
-    def outward(block):
-        return jnp.transpose(block[:, :fields], (1, 0, 2))[None]
-
-    return (outward(jnp.concatenate(predictions)), outward(state_grad))
+        plan, live_own, grads, dft_main, dft_rest, through, last, zonal_grad
+    )
+
+    return (predictions, outward(state_grad))
 
 
 def solution(mesh):

time: 828 us -> 814 us (0.983)
    ppermute x56, waiting for transfers between devices: 311 us -> 300 us  [exchange(): lax.ppermute(parts[s], 'space', [(i, (i + s) % n) for i in range(n)])]
    psum x1, waiting for transfers between devices: 17 us -> 25.4 us  [on_device(): high_coeffs = lax.psum(high_partial(plan, zonal_high, high_fwd), 'space')]
  transfers between devices with their start and end apart: 61 -> 61, of which waited for: 33 -> 31; matrix products, arithmetic and copies ran while one was open for 5% -> 4% of each run, Pallas kernels for 26% -> 26%
where the time goes in v7:
time: 814 us; the launch traced here: 812 us
  waiting for transfers between devices  331 us (41%)
  Pallas kernels  295 us (36%)
  starting transfers between devices  114 us (14%)
  local copies, waits for them, and re-layouts  37.3 us (5%)
  other arithmetic  18.3 us (2%)
  between operations  14.5 us (2%)
    ppermute x56, waiting for transfers between devices, exchange(): lax.ppermute(parts[s], 'space', [(i, (i + s) % n) for i in range(n)])  300 us
    pallas_call x17, Pallas kernels, call(): pl.pallas_call(kernel, grid=grid, in_specs=in_specs, out_specs=out_specs,...  295 us
    ppermute x56, starting transfers between devices, exchange(): lax.ppermute(parts[s], 'space', [(i, (i + s) % n) for i in range(n)])  114 us
    psum x1, waiting for transfers between devices, on_device(): high_coeffs = lax.psum(high_partial(plan, zonal_high, high_fwd), 'space')  25.4 us
  transfers between devices with their start and end apart: 61, of which 31 were waited for; matrix products, arithmetic and copies ran while one was open for 4% of the time, Pallas kernels for 26%

profile of v7, /device:TPU:0, one launch (start us, length us, event | category | flops | bytes accessed | tf_op | source)
XLA Modules:
  0.0 811.7 jit_solution(8596499345704681069)
XLA Ops:
  7.2 6.1 pad.55.x_ref
  14.3 13.8 %analyse_low.1 = (bf16[49,40,128]{2,1,0:T(8,128)(2,1)}, bf16[49,40,128]{2,1,0:T(8,128)(2,1)}, bf16[49,40,128]{2,1,0:T(8,128)(2,1)}, bf16[49,40,128]{2,1,0:T(8,12...) custom-call(bf16[49,80,720]{2,1,0:T(8,128)(2,1)} %pad.55.x_ref, ...), custom_call_target="tpu_custom_call" | custom-call | bytes 41584640 | tf_op jit(solution)/shard_map/analyse_low/pallas_call | solution.py:93
  28.1 6.0 collective-permute-start
  34.6 3.0 collective-permute-start.3
  39.5 15.0 %analyse_high.1.zonal = bf16[49,112,256]{2,1,0:T(8,128)(2,1)} custom-call(bf16[49,80,720]{2,1,0:T(8,128)(2,1)} %pad.55.x_ref, bf16[2,112,720]{2,1,0:T(8,128)(2,1)} %constant.97.clone.dft_ref), custom_call_target="tpu_custom_call" | custom-call | bytes 35108864 | tf_op jit(solution)/shard_map/analyse_high/pallas_call | solution.py:93
  55.8 6.6 legendre_tables.3
  62.4 11.8 %high_partial.1 = bf16[14,5,112,128]{3,2,1,0:T(8,128)(2,1)} custom-call(bf16[49,112,256]{2,1,0:T(8,128)(2,1)} %analyse_high.1.zonal, bf16[56,112,128]{2,1,0:T(8,128)(2,1)} %get-tuple-element.139.fwd), custom_call_target="tpu_custom_call" | custom-call | bytes 25690112 | tf_op jit(solution)/shard_map/high_partial/pallas_call | solution.py:93
  89.7 19.3 %legendre_tables.2 = (bf16[32,368,392]{2,1,0:T(8,128)(2,1)}, bf16[32,368,392]{2,1,0:T(8,128)(2,1)}) custom-call(f32[32,128]{1,0:T(8,128)} %broadcast_in_dim.46.m_ref, f32[32,128]{1,0:T(8,128)} %convert_element_type.65.shift_ref, f32[32,512]{1,0:T(8,128)} %pad.58.start_ref, f32[1,512]{1,0:T(1,128)} %bitcast.98, f32[1,512]{1,0:T(1,128)} %bitcast.99, ...), custom_call_target="tpu_custom_call" | custom-call | bytes 74276864 | tf_op jit(solution)/shard_map/legendre_tables/pallas_call | solution.py:93
  109.1 32.8 %collective-permute-done.3.refs_4_ = bf16[49,40,128]{2,1,0:T(8,128)(2,1)} collective-permute-done((bf16[49,40,128]{2,1,0:T(8,128)(2,1)}, bf16[49,40,128]{2,1,0:T(8,128)(2,1)}, u32[]{:S(2)}, u32[]{:S(2)}) %collective-permute-start.3) | collective-permute-done | bytes 501792 | tf_op jit(solution)/shard_map/ppermute | solution.py:934
  143.0 38.1 %spectrum_forward.1 = (bf16[14,64,128]{2,1,0:T(8,128)(2,1)}, bf16[14,64,128]{2,1,0:T(8,128)(2,1)}, bf16[14,64,128]{2,1,0:T(8,128)(2,1)}, bf16[14,64,128]{2,1,0:T...) custom-call(bf16[49,40,128]{2,1,0:T(8,128)(2,1)} %get-tuple-element., ...), custom_call_target="tpu_custom_call" | custom-call | bytes 119209984 | tf_op jit(solution)/shard_map/spectrum_forward/pallas_call | solution.py:93
  181.2 3.6 collective-permute-start.15
  186.0 2.1 collective-permute-start.16
  188.1 2.3 collective-permute-start.17
  190.4 3.2 collective-permute-done.14.refs_1_
  193.6 5.8 collective-permute-start.19
  199.3 11.4 %collective-permute-done.15.refs_2_ = bf16[14,64,128]{2,1,0:T(8,128)(2,1)S(1)} collective-permute-done((bf16[14,64,128]{2,1,0:T(8,128)(2,1)}, bf16[14,64,128]{2,1,0:T(8,128)(2,1)S(1)}, u32[]{:S(2)}, u32[]{:S(2)}) %collective-permute-start.15) | collective-permute-done | bytes 229408 | tf_op jit(solution)/shard_map/ppermute | solution.py:934
  212.0 25.4 %all-reduce.18.cloned.1.call-done.coeffs = bf16[14,5,112,128]{3,2,1,0:T(8,128)(2,1)} async-done(((bf16[14,5,112,128]{3,2,1,0:T(8,128)(2,1)}), bf16[14,5,112,128]{3,2,1,0:T(8,128)(2,1)}) %all-reduce.18.cloned.1.call-update) | async-done | bytes 2007056 | tf_op jit(solution)/shard_map/psum | solution.py:959
  237.4 16.0 %high_synthesis.1.refs_8_ = bf16[49,224,128]{2,1,0:T(8,128)(2,1)} custom-call(bf16[14,5,112,128]{3,2,1,0:T(8,128)(2,1)} %all-reduce.18.cloned.1.call-done.coeffs, bf16[56,112,128]{2,1,0:T(8,128)(2,1)} %get-tuple-element.140.inv.refs_3_, bf16[4,256,256]{2,1,0:T(8,128)(2,1)} %copy.38.refs_10_.mix, f32[8,424,128]{2,1,0:T(8,128)} %copy-done.4), custom_call_target="tpu_custom_call" | custom-call | bytes 34734080 | tf_op jit(solution)/shard_map/high_synthesis/pallas_call | solution.py:93
  254.2 12.6 %predict.4 = (bf16[14,80,720]{2,1,0:T(8,128)(2,1)}, bf16[14,128,720]{2,1,0:T(8,128)(2,1)}) custom-call(f32[49]{0:T(128)} %copy-done.43, bf16[49,80,720]{2,1,0:T(8,128)(2,1)} %pad.55.x_ref, bf16[736,720]{1,0:T(8,128)(2,1)} %pad_maximum_fusion.4.idft_ref, bf16[128,80]{1,0:T(8,128)(2,1)} %pad.56.enc_ref, bf16[80,128]{1,0:T(8,128)(2,1)} %pad.57.dec_ref, ...), custom_call_target="tpu_custom_call" | custom-call | bytes 62335760 | tf_op jit(solution)/shard_map/predict/pallas_call | solution.py:93
  267.5 4.0 collective-permute-start.10
  271.5 2.6 collective-permute-done.7.refs_1_
  274.2 3.9 collective-permute-done.8.refs_2_
  278.1 6.0 pad.54.obs_ref
  284.2 20.0 %collective-permute-done.10.refs_4_ = bf16[14,64,128]{2,1,0:T(8,128)(2,1)S(1)} collective-permute-done((bf16[14,64,128]{2,1,0:T(8,128)(2,1)S(1)}, bf16[14,64,128]{2,1,0:T(8,128)(2,1)S(1)}, u32[]{:S(2)}, u32[]{:S(2)}) %collective-permute-start.10) | collective-permute-done | bytes 229408 | tf_op jit(solution)/shard_map/ppermute | solution.py:934
  306.7 12.6 %predict.3 = (bf16[14,80,720]{2,1,0:T(8,128)(2,1)}, bf16[14,128,720]{2,1,0:T(8,128)(2,1)}) custom-call(f32[49]{0:T(128)} %copy-done.43, bf16[49,80,720]{2,1,0:T(8,128)(2,1)} %pad.55.x_ref, bf16[736,720]{1,0:T(8,128)(2,1)} %pad_maximum_fusion.4.idft_ref, bf16[128,80]{1,0:T(8,128)(2,1)} %pad.56.enc_ref, bf16[80,128]{1,0:T(8,128)(2,1)} %pad.57.dec_ref, ...), custom_call_target="tpu_custom_call" | custom-call | bytes 62335760 | tf_op jit(solution)/shard_map/predict/pallas_call | solution.py:93
  319.4 2.4 collective-permute-start.29
  321.9 2.1 collective-permute-start.30
  328.0 2.4 collective-permute-start.33
  330.4 5.6 collective-permute-done.29.refs_2_
  336.1 6.8 collective-permute-done.30.refs_3_
  342.9 39.5 %collective-permute-done.31.refs_4_ = bf16[21,64,128]{2,1,0:T(8,128)(2,1)S(1)} collective-permute-done((bf16[21,64,128]{2,1,0:T(8,128)(2,1)}, bf16[21,64,128]{2,1,0:T(8,128)(2,1)S(1)}, u32[]{:S(2)}, u32[]{:S(2)}) %collective-permute-start.31) | collective-permute-done | bytes 344096 | tf_op jit(solution)/shard_map/ppermute | solution.py:934
  384.6 17.0 %predict.5 = (bf16[21,80,720]{2,1,0:T(8,128)(2,1)}, bf16[21,128,720]{2,1,0:T(8,128)(2,1)}) custom-call(f32[49]{0:T(128)} %copy-done.43, bf16[49,80,720]{2,1,0:T(8,128)(2,1)} %pad.55.x_ref, bf16[736,720]{1,0:T(8,128)(2,1)} %pad_maximum_fusion.4.idft_ref, bf16[128,80]{1,0:T(8,128)(2,1)} %pad.56.enc_ref, bf16[80,128]{1,0:T(8,128)(2,1)} %pad.57.dec_ref, ...), custom_call_target="tpu_custom_call" | custom-call | bytes 74392336 | tf_op jit(solution)/shard_map/predict/pallas_call | solution.py:93
  402.4 14.4 %score.3 = (bf16[14,80,720]{2,1,0:T(8,128)(2,1)}, bf16[14,64,128]{2,1,0:T(8,128)(2,1)}, bf16[14,64,128]{2,1,0:T(8,128)(2,1)}, bf16[14,64,128]{2,1,0:T(8,128)(2,1...) custom-call(f32[49]{0:T(128)} %get-tuple-element.236.area_ref, ...), custom_call_target="tpu_custom_call" | custom-call | bytes 86481680 | tf_op jit(solution)/shard_map/score/pallas_call | solution.py:93
  417.6 3.7 collective-permute-start.24
  421.3 3.6 collective-permute-done.21.refs_1_
  424.9 3.4 collective-permute-done.22.refs_2_
  428.5 4.7 collective-permute-done.23.refs_3_
  433.2 21.9 %collective-permute-done.24.refs_4_ = bf16[14,64,128]{2,1,0:T(8,128)(2,1)} collective-permute-done((bf16[14,64,128]{2,1,0:T(8,128)(2,1)}, bf16[14,64,128]{2,1,0:T(8,128)(2,1)}, u32[]{:S(2)}, u32[]{:S(2)}) %collective-permute-start.24) | collective-permute-done | bytes 229408 | tf_op jit(solution)/shard_map/ppermute | solution.py:934
  456.4 14.0 %score.4 = (bf16[14,80,720]{2,1,0:T(8,128)(2,1)}, bf16[14,64,128]{2,1,0:T(8,128)(2,1)}, bf16[14,64,128]{2,1,0:T(8,128)(2,1)}, bf16[14,64,128]{2,1,0:T(8,128)(2,1...) custom-call(f32[49]{0:T(128)} %get-tuple-element.236.area_ref, ...), custom_call_target="tpu_custom_call" | custom-call | bytes 86481680 | tf_op jit(solution)/shard_map/score/pallas_call | solution.py:93
  471.5 4.3 collective-permute-start.37
  477.9 2.4 collective-permute-start.40
  483.3 3.4 collective-permute-done.37.refs_11_
  486.7 28.3 %collective-permute-done.38.refs_12_ = bf16[14,64,128]{2,1,0:T(8,128)(2,1)} collective-permute-done((bf16[14,64,128]{2,1,0:T(8,128)(2,1)}, bf16[14,64,128]{2,1,0:T(8,128)(2,1)}, u32[]{:S(2)}, u32[]{:S(2)}) %collective-permute-start.38) | collective-permute-done | bytes 229408 | tf_op jit(solution)/shard_map/ppermute | solution.py:934
  516.2 19.1 %score.5 = (bf16[21,80,720]{2,1,0:T(8,128)(2,1)}, bf16[21,64,128]{2,1,0:T(8,128)(2,1)}, bf16[21,64,128]{2,1,0:T(8,128)(2,1)}, bf16[21,64,128]{2,1,0:T(8,128)(2,1...) custom-call(f32[49]{0:T(128)} %get-tuple-element.236.area_ref, ...), custom_call_target="tpu_custom_call" | custom-call | bytes 116271888 | tf_op jit(solution)/shard_map/score/pallas_call | solution.py:93
  535.3 14.3 %high_adjoint.1 = bf16[14,5,112,128]{3,2,1,0:T(8,128)(2,1)} custom-call(bf16[14,224,128]{2,1,0:T(8,128)(2,1)} %get-tuple-element.206.refs_0_, bf16[14,224,128]{2,1,0:T(8,128)(2,1)} %get-tuple-element.207.refs_1_, bf16[21,224,128]{2,1,0:T(8,128)(2,1)} %get-tuple-element.208.refs_2_, bf16[56,112,128]{2,1,0:T(8,128)(2,1)} %get-tuple-element.140.inv.refs_3_, ...), custom_call_target="tpu_custom_call" | custom-call | bytes 34734080 | tf_op jit(solution)/shard_map/high_adjoint/pallas_call | solution.py:93
  551.5 3.4 collective-permute-start.45
  554.9 12.0 %collective-permute-done.42.refs_17_ = bf16[21,64,128]{2,1,0:T(8,128)(2,1)S(1)} collective-permute-done((bf16[21,64,128]{2,1,0:T(8,128)(2,1)S(1)}, bf16[21,64,128]{2,1,0:T(8,128)(2,1)S(1)}, u32[]{:S(2)}, u32[]{:S(2)}) %collective-permute-start.42) | collective-permute-done | bytes 344096 | tf_op jit(solution)/shard_map/ppermute | solution.py:934
  567.0 13.7 %collective-permute-done.43.refs_18_ = bf16[21,64,128]{2,1,0:T(8,128)(2,1)S(1)} collective-permute-done((bf16[21,64,128]{2,1,0:T(8,128)(2,1)S(1)}, bf16[21,64,128]{2,1,0:T(8,128)(2,1)S(1)}, u32[]{:S(2)}, u32[]{:S(2)}) %collective-permute-start.43) | collective-permute-done | bytes 344096 | tf_op jit(solution)/shard_map/ppermute | solution.py:934
  581.4 14.1 %collective-permute-done.44.refs_19_ = bf16[21,64,128]{2,1,0:T(8,128)(2,1)} collective-permute-done((bf16[21,64,128]{2,1,0:T(8,128)(2,1)}, bf16[21,64,128]{2,1,0:T(8,128)(2,1)}, u32[]{:S(2)}, u32[]{:S(2)}) %collective-permute-start.44) | collective-permute-done | bytes 344096 | tf_op jit(solution)/shard_map/ppermute | solution.py:934
  595.5 38.0 %collective-permute-done.45.refs_20_ = bf16[21,64,128]{2,1,0:T(8,128)(2,1)} collective-permute-done((bf16[21,64,128]{2,1,0:T(8,128)(2,1)}, bf16[21,64,128]{2,1,0:T(8,128)(2,1)}, u32[]{:S(2)}, u32[]{:S(2)}) %collective-permute-start.45) | collective-permute-done | bytes 344096 | tf_op jit(solution)/shard_map/ppermute | solution.py:934
  633.5 3.4 collective-permute-done.46.refs_21_
  636.9 38.1 %spectrum_backward.1 = (bf16[49,40,128]{2,1,0:T(8,128)(2,1)}, bf16[49,40,128]{2,1,0:T(8,128)(2,1)}, bf16[49,40,128]{2,1,0:T(8,128)(2,1)}, bf16[49,40,128]{2,1,0:...) custom-call(bf16[14,64,128]{2,1,0:T(8,128)(2,1)} %get-tuple-element., ...), custom_call_target="tpu_custom_call" | custom-call | bytes 119209984 | tf_op jit(solution)/shard_map/spectrum_backward/pallas_call | solution.py:93
  675.1 3.5 collective-permute-start.51
  678.6 5.4 fusion
  684.0 3.5 pad_maximum_fusion.2.grad_ref
  690.9 2.9 collective-permute-start.54
  693.8 5.7 all-reduce.20.cloned.1.call-done.grads
  699.5 11.4 %high_zonal.1.refs_8_ = bf16[49,144,128]{2,1,0:T(8,128)(2,1)} custom-call(bf16[14,5,112,128]{3,2,1,0:T(8,128)(2,1)} %all-reduce.20.cloned.1.call-done.grads, bf16[56,112,128]{2,1,0:T(8,128)(2,1)} %get-tuple-element.139.fwd), custom_call_target="tpu_custom_call" | custom-call | bytes 21676032 | tf_op jit(solution)/shard_map/high_zonal/pallas_call | solution.py:93
  710.9 35.3 %collective-permute-start.49 = (bf16[49,40,128]{2,1,0:T(8,128)(2,1)}, bf16[49,40,128]{2,1,0:T(8,128)(2,1)S(1)}, u32[]{:S(2)}, u32[]{:S(2)}) collective-permute-start(bf16[49,40,128]{2,1,0:T(8,128)(2,1)} %get-tuple-element.226), channel_id=1, source_target_pairs={{0,7},{1,0},{2,1},{3,2},{4,3},{5,4},{6,5},{7,6},{8,15},{9,8},{10,9... | collective-permute-start | bytes 1505288 | tf_op jit(solution)/shard_map/ppermute | solution.py:934
  746.2 9.1 %collective-permute-start.55 = (bf16[49,40,128]{2,1,0:T(8,128)(2,1)}, bf16[49,40,128]{2,1,0:T(8,128)(2,1)}, u32[]{:S(2)}, u32[]{:S(2)}) collective-permute-start(bf16[49,40,128]{2,1,0:T(8,128)(2,1)} %get-tuple-element.232), channel_id=1, source_target_pairs={{0,1},{1,2},{2,3},{3,4},{4,5},{5,6},{6,7},{7,0},{8,9},{9,10},{10,1... | collective-permute-start | bytes 1505288 | tf_op jit(solution)/shard_map/ppermute | solution.py:934
  759.3 5.2 collective-permute-done.52.refs_4_
  764.5 12.9 %collective-permute-done.53.refs_5_ = bf16[49,40,128]{2,1,0:T(8,128)(2,1)S(1)} collective-permute-done((bf16[49,40,128]{2,1,0:T(8,128)(2,1)}, bf16[49,40,128]{2,1,0:T(8,128)(2,1)S(1)}, u32[]{:S(2)}, u32[]{:S(2)}) %collective-permute-start.53) | collective-permute-done | bytes 501792 | tf_op jit(solution)/shard_map/ppermute | solution.py:934
  778.3 21.1 %finish.1 = bf16[49,80,720]{2,1,0:T(8,128)(2,1)} custom-call(f32[49]{0:T(128)} %copy-done.43, bf16[49,80,720]{2,1,0:T(8,128)(2,1)} %pad_maximum_fusion.2.grad_ref, bf16[736,720]{1,0:T(8,128)(2,1)} %pad_maximum_fusion.5.main_ref, bf16[768,720]{1,0:T(8,128)(2,1)} %pad_maximum_fusion.3.rest_ref, bf16[80,80]{1,0:T(8,128)(2,1)} %pad.68.through_ref, ...), custom_call_target="tpu_custom_call" | custom-call | bytes 77155088 | tf_op jit(solution)/shard_map/finish/pallas_call | solution.py:93
  799.5 5.7 slice_bitcast_fusion
  (265 shorter events, 55.5 us)
Async XLA Ops:
  7.2 68.9 %copy-start = (bf16[128,128]{1,0:T(8,128)(2,1)S(1)}, bf16[128,128]{1,0:T(8,128)(2,1)}, u32[]{:S(2)}) copy-start(bf16[128,128]{1,0:T(8,128)(2,1)} %param.25) | copy-start | bytes 98308
  7.2 230.2 %all-reduce.18.cloned.1.call-start = ((), (), s32[]{:S(2)}) async-start(), calls=%async_computation | async-start | bytes 4014080 | tf_op jit(solution)/shard_map/psum | solution.py:959
  28.1 51.3 %collective-permute-start = (bf16[49,40,128]{2,1,0:T(8,128)(2,1)}, bf16[49,40,128]{2,1,0:T(8,128)(2,1)}, u32[]{:S(2)}, u32[]{:S(2)}) collective-permute-start(bf16[49,40,128]{2,1,0:T(8,128)(2,1)} %get-tuple-element.121), channel_id=1, source_target_pairs={{0,7},{1,0},{2,1},{3,2},{4,3},{5,4},{6,5},{7,6},{8,15},{9,8},{10,9... | collective-permute-start | bytes 1505288 | tf_op jit(solution)/shard_map/ppermute | solution.py:934
  34.1 47.1 %collective-permute-start.1 = (bf16[49,40,128]{2,1,0:T(8,128)(2,1)}, bf16[49,40,128]{2,1,0:T(8,128)(2,1)}, u32[]{:S(2)}, u32[]{:S(2)}) collective-permute-start(bf16[49,40,128]{2,1,0:T(8,128)(2,1)} %get-tuple-element.122), channel_id=1, source_target_pairs={{0,6},{1,7},{2,0},{3,1},{4,2},{5,3},{6,4},{7,5},{8,14},{9,15},{10,... | collective-permute-start | bytes 1505288 | tf_op jit(solution)/shard_map/ppermute | solution.py:934
  34.6 74.5 %collective-permute-start.2 = (bf16[49,40,128]{2,1,0:T(8,128)(2,1)}, bf16[49,40,128]{2,1,0:T(8,128)(2,1)}, u32[]{:S(2)}, u32[]{:S(2)}) collective-permute-start(bf16[49,40,128]{2,1,0:T(8,128)(2,1)} %get-tuple-element.123), channel_id=1, source_target_pairs={{0,5},{1,6},{2,7},{3,0},{4,1},{5,2},{6,3},{7,4},{8,13},{9,14},{10,... | collective-permute-start | bytes 1505288 | tf_op jit(solution)/shard_map/ppermute | solution.py:934
  34.6 107.3 %collective-permute-start.3 = (bf16[49,40,128]{2,1,0:T(8,128)(2,1)}, bf16[49,40,128]{2,1,0:T(8,128)(2,1)}, u32[]{:S(2)}, u32[]{:S(2)}) collective-permute-start(bf16[49,40,128]{2,1,0:T(8,128)(2,1)} %get-tuple-element.124), channel_id=1, source_target_pairs={{0,4},{1,5},{2,6},{3,7},{4,0},{5,1},{6,2},{7,3},{8,12},{9,13},{10,... | collective-permute-start | bytes 1505288 | tf_op jit(solution)/shard_map/ppermute | solution.py:934
  37.6 104.6 %collective-permute-start.4 = (bf16[49,40,128]{2,1,0:T(8,128)(2,1)}, bf16[49,40,128]{2,1,0:T(8,128)(2,1)}, u32[]{:S(2)}, u32[]{:S(2)}) collective-permute-start(bf16[49,40,128]{2,1,0:T(8,128)(2,1)} %get-tuple-element.125), channel_id=1, source_target_pairs={{0,3},{1,4},{2,5},{3,6},{4,7},{5,0},{6,1},{7,2},{8,11},{9,12},{10,... | collective-permute-start | bytes 1505288 | tf_op jit(solution)/shard_map/ppermute | solution.py:934
  74.2 328.2 %all-gather.7.cloned.1.call-start = ((), (), s32[]{:S(2)}) async-start(), calls=%async_computation.2 | async-start | bytes 8601600 | tf_op jit(solution)/shard_map/all_gather | solution.py:991
  79.4 62.8 %collective-permute-start.5 = (bf16[49,40,128]{2,1,0:T(8,128)(2,1)}, bf16[49,40,128]{2,1,0:T(8,128)(2,1)S(1)}, u32[]{:S(2)}, u32[]{:S(2)}) collective-permute-start(bf16[49,40,128]{2,1,0:T(8,128)(2,1)} %get-tuple-element.126), channel_id=1, source_target_pairs={{0,2},{1,3},{2,4},{3,5},{4,6},{5,7},{6,0},{7,1},{8,10},{9,11},{10,... | collective-permute-start | bytes 1505288 | tf_op jit(solution)/shard_map/ppermute | solution.py:934
  81.2 61.0 %collective-permute-start.6 = (bf16[49,40,128]{2,1,0:T(8,128)(2,1)}, bf16[49,40,128]{2,1,0:T(8,128)(2,1)}, u32[]{:S(2)}, u32[]{:S(2)}) collective-permute-start(bf16[49,40,128]{2,1,0:T(8,128)(2,1)} %get-tuple-element.127), channel_id=1, source_target_pairs={{0,1},{1,2},{2,3},{3,4},{4,5},{5,6},{6,7},{7,0},{8,9},{9,10},{10,1... | collective-permute-start | bytes 1505288 | tf_op jit(solution)/shard_map/ppermute | solution.py:934
  181.1 12.5 %collective-permute-start.14 = (bf16[14,64,128]{2,1,0:T(8,128)(2,1)}, bf16[14,64,128]{2,1,0:T(8,128)(2,1)S(1)}, u32[]{:S(2)}, u32[]{:S(2)}) collective-permute-start(bf16[14,64,128]{2,1,0:T(8,128)(2,1)} %get-tuple-element.143), channel_id=1, source_target_pairs={{0,7},{1,0},{2,1},{3,2},{4,3},{5,4},{6,5},{7,6},{8,15},{9,8},{10,9... | collective-permute-start | bytes 688136 | tf_op jit(solution)/shard_map/ppermute | solution.py:934
  181.2 29.5 %collective-permute-start.15 = (bf16[14,64,128]{2,1,0:T(8,128)(2,1)}, bf16[14,64,128]{2,1,0:T(8,128)(2,1)S(1)}, u32[]{:S(2)}, u32[]{:S(2)}) collective-permute-start(bf16[14,64,128]{2,1,0:T(8,128)(2,1)} %get-tuple-element.144), channel_id=1, source_target_pairs={{0,6},{1,7},{2,0},{3,1},{4,2},{5,3},{6,4},{7,5},{8,14},{9,15},{10,... | collective-permute-start | bytes 688136 | tf_op jit(solution)/shard_map/ppermute | solution.py:934
  186.0 67.4 %collective-permute-start.16 = (bf16[14,64,128]{2,1,0:T(8,128)(2,1)}, bf16[14,64,128]{2,1,0:T(8,128)(2,1)S(1)}, u32[]{:S(2)}, u32[]{:S(2)}) collective-permute-start(bf16[14,64,128]{2,1,0:T(8,128)(2,1)} %get-tuple-element.145), channel_id=1, source_target_pairs={{0,5},{1,6},{2,7},{3,0},{4,1},{5,2},{6,3},{7,4},{8,13},{9,14},{10,... | collective-permute-start | bytes 688136 | tf_op jit(solution)/shard_map/ppermute | solution.py:934
  188.1 65.3 %collective-permute-start.17 = (bf16[14,64,128]{2,1,0:T(8,128)(2,1)}, bf16[14,64,128]{2,1,0:T(8,128)(2,1)}, u32[]{:S(2)}, u32[]{:S(2)}) collective-permute-start(bf16[14,64,128]{2,1,0:T(8,128)(2,1)} %get-tuple-element.146), channel_id=1, source_target_pairs={{0,4},{1,5},{2,6},{3,7},{4,0},{5,1},{6,2},{7,3},{8,12},{9,13},{10,... | collective-permute-start | bytes 688136 | tf_op jit(solution)/shard_map/ppermute | solution.py:934
  190.4 63.1 %collective-permute-start.18 = (bf16[14,64,128]{2,1,0:T(8,128)(2,1)}, bf16[14,64,128]{2,1,0:T(8,128)(2,1)}, u32[]{:S(2)}, u32[]{:S(2)}) collective-permute-start(bf16[14,64,128]{2,1,0:T(8,128)(2,1)} %get-tuple-element.147), channel_id=1, source_target_pairs={{0,3},{1,4},{2,5},{3,6},{4,7},{5,0},{6,1},{7,2},{8,11},{9,12},{10,... | collective-permute-start | bytes 688136 | tf_op jit(solution)/shard_map/ppermute | solution.py:934
  193.6 59.9 %collective-permute-start.19 = (bf16[14,64,128]{2,1,0:T(8,128)(2,1)}, bf16[14,64,128]{2,1,0:T(8,128)(2,1)}, u32[]{:S(2)}, u32[]{:S(2)}) collective-permute-start(bf16[14,64,128]{2,1,0:T(8,128)(2,1)} %get-tuple-element.148), channel_id=1, source_target_pairs={{0,2},{1,3},{2,4},{3,5},{4,6},{5,7},{6,0},{7,1},{8,10},{9,11},{10,... | collective-permute-start | bytes 688136 | tf_op jit(solution)/shard_map/ppermute | solution.py:934
  210.7 42.8 %collective-permute-start.20 = (bf16[14,64,128]{2,1,0:T(8,128)(2,1)}, bf16[14,64,128]{2,1,0:T(8,128)(2,1)}, u32[]{:S(2)}, u32[]{:S(2)}) collective-permute-start(bf16[14,64,128]{2,1,0:T(8,128)(2,1)} %get-tuple-element.149), channel_id=1, source_target_pairs={{0,1},{1,2},{2,3},{3,4},{4,5},{5,6},{6,7},{7,0},{8,9},{9,10},{10,1... | collective-permute-start | bytes 688136 | tf_op jit(solution)/shard_map/ppermute | solution.py:934
  266.8 189.6 %all-gather.9.cloned.1.call-start = ((), (), s32[]{:S(2)}) async-start(), calls=%async_computation.3 | async-start | bytes 8601600 | tf_op jit(solution)/shard_map/all_gather | solution.py:991
  266.9 7.3 collective-permute-start.7
  267.1 11.0 %collective-permute-start.8 = (bf16[14,64,128]{2,1,0:T(8,128)(2,1)S(1)}, bf16[14,64,128]{2,1,0:T(8,128)(2,1)S(1)}, u32[]{:S(2)}, u32[]{:S(2)}) collective-permute-start(bf16[14,64,128]{2,1,0:T(8,128)(2,1)S(1)} %copy-done.56), channel_id=1, source_target_pairs={{0,6},{1,7},{2,0},{3,1},{4,2},{5,3},{6,4},{7,5},{8,14},{9,15},{10,... | collective-permute-start | bytes 688136 | tf_op jit(solution)/shard_map/ppermute | solution.py:934
  267.2 17.0 %collective-permute-start.9 = (bf16[14,64,128]{2,1,0:T(8,128)(2,1)S(1)}, bf16[14,64,128]{2,1,0:T(8,128)(2,1)S(1)}, u32[]{:S(2)}, u32[]{:S(2)}) collective-permute-start(bf16[14,64,128]{2,1,0:T(8,128)(2,1)S(1)} %copy-done.55), channel_id=1, source_target_pairs={{0,5},{1,6},{2,7},{3,0},{4,1},{5,2},{6,3},{7,4},{8,13},{9,14},{10,... | collective-permute-start | bytes 688136 | tf_op jit(solution)/shard_map/ppermute | solution.py:934
  267.5 36.7 %collective-permute-start.10 = (bf16[14,64,128]{2,1,0:T(8,128)(2,1)S(1)}, bf16[14,64,128]{2,1,0:T(8,128)(2,1)S(1)}, u32[]{:S(2)}, u32[]{:S(2)}) collective-permute-start(bf16[14,64,128]{2,1,0:T(8,128)(2,1)S(1)} %copy-done.54), channel_id=1, source_target_pairs={{0,4},{1,5},{2,6},{3,7},{4,0},{5,1},{6,2},{7,3},{8,12},{9,13},{10,... | collective-permute-start | bytes 688136 | tf_op jit(solution)/shard_map/ppermute | solution.py:934
  271.5 34.3 %collective-permute-start.11 = (bf16[14,64,128]{2,1,0:T(8,128)(2,1)S(1)}, bf16[14,64,128]{2,1,0:T(8,128)(2,1)S(1)}, u32[]{:S(2)}, u32[]{:S(2)}) collective-permute-start(bf16[14,64,128]{2,1,0:T(8,128)(2,1)S(1)} %copy-done.53), channel_id=1, source_target_pairs={{0,3},{1,4},{2,5},{3,6},{4,7},{5,0},{6,1},{7,2},{8,11},{9,12},{10,... | collective-permute-start | bytes 688136 | tf_op jit(solution)/shard_map/ppermute | solution.py:934
  274.2 31.7 %collective-permute-start.12 = (bf16[14,64,128]{2,1,0:T(8,128)(2,1)S(1)}, bf16[14,64,128]{2,1,0:T(8,128)(2,1)S(1)}, u32[]{:S(2)}, u32[]{:S(2)}) collective-permute-start(bf16[14,64,128]{2,1,0:T(8,128)(2,1)S(1)} %copy-done.52), channel_id=1, source_target_pairs={{0,2},{1,3},{2,4},{3,5},{4,6},{5,7},{6,0},{7,1},{8,10},{9,11},{10,... | collective-permute-start | bytes 688136 | tf_op jit(solution)/shard_map/ppermute | solution.py:934
  278.1 27.7 %collective-permute-start.13 = (bf16[14,64,128]{2,1,0:T(8,128)(2,1)S(1)}, bf16[14,64,128]{2,1,0:T(8,128)(2,1)S(1)}, u32[]{:S(2)}, u32[]{:S(2)}) collective-permute-start(bf16[14,64,128]{2,1,0:T(8,128)(2,1)S(1)} %copy-done.51), channel_id=1, source_target_pairs={{0,1},{1,2},{2,3},{3,4},{4,5},{5,6},{6,7},{7,0},{8,9},{9,10},{10,1... | collective-permute-start | bytes 688136 | tf_op jit(solution)/shard_map/ppermute | solution.py:934
  319.3 196.9 %all-gather.11.cloned.1.call-start = ((), (), s32[]{:S(2)}) async-start(), calls=%async_computation.4 | async-start | bytes 12902400 | tf_op jit(solution)/shard_map/all_gather | solution.py:991
  319.3 8.7 %collective-permute-start.28 = (bf16[21,64,128]{2,1,0:T(8,128)(2,1)S(1)}, bf16[21,64,128]{2,1,0:T(8,128)(2,1)S(1)}, u32[]{:S(2)}, u32[]{:S(2)}) collective-permute-start(bf16[21,64,128]{2,1,0:T(8,128)(2,1)S(1)} %copy-done.48), channel_id=1, source_target_pairs={{0,7},{1,0},{2,1},{3,2},{4,3},{5,4},{6,5},{7,6},{8,15},{9,8},{10,9... | collective-permute-start | bytes 1032200 | tf_op jit(solution)/shard_map/ppermute | solution.py:934
  319.4 16.6 %collective-permute-start.29 = (bf16[21,64,128]{2,1,0:T(8,128)(2,1)S(1)}, bf16[21,64,128]{2,1,0:T(8,128)(2,1)S(1)}, u32[]{:S(2)}, u32[]{:S(2)}) collective-permute-start(bf16[21,64,128]{2,1,0:T(8,128)(2,1)S(1)} %copy-done.47), channel_id=1, source_target_pairs={{0,6},{1,7},{2,0},{3,1},{4,2},{5,3},{6,4},{7,5},{8,14},{9,15},{10,... | collective-permute-start | bytes 1032200 | tf_op jit(solution)/shard_map/ppermute | solution.py:934
  321.9 21.0 %collective-permute-start.30 = (bf16[21,64,128]{2,1,0:T(8,128)(2,1)}, bf16[21,64,128]{2,1,0:T(8,128)(2,1)S(1)}, u32[]{:S(2)}, u32[]{:S(2)}) collective-permute-start(bf16[21,64,128]{2,1,0:T(8,128)(2,1)} %get-tuple-element.172), channel_id=1, source_target_pairs={{0,5},{1,6},{2,7},{3,0},{4,1},{5,2},{6,3},{7,4},{8,13},{9,14},{10,... | collective-permute-start | bytes 1032200 | tf_op jit(solution)/shard_map/ppermute | solution.py:934
  324.0 58.4 %collective-permute-start.31 = (bf16[21,64,128]{2,1,0:T(8,128)(2,1)}, bf16[21,64,128]{2,1,0:T(8,128)(2,1)S(1)}, u32[]{:S(2)}, u32[]{:S(2)}) collective-permute-start(bf16[21,64,128]{2,1,0:T(8,128)(2,1)} %get-tuple-element.173), channel_id=1, source_target_pairs={{0,4},{1,5},{2,6},{3,7},{4,0},{5,1},{6,2},{7,3},{8,12},{9,13},{10,... | collective-permute-start | bytes 1032200 | tf_op jit(solution)/shard_map/ppermute | solution.py:934
  324.0 59.6 %collective-permute-start.32 = (bf16[21,64,128]{2,1,0:T(8,128)(2,1)}, bf16[21,64,128]{2,1,0:T(8,128)(2,1)S(1)}, u32[]{:S(2)}, u32[]{:S(2)}) collective-permute-start(bf16[21,64,128]{2,1,0:T(8,128)(2,1)} %get-tuple-element.174), channel_id=1, source_target_pairs={{0,3},{1,4},{2,5},{3,6},{4,7},{5,0},{6,1},{7,2},{8,11},{9,12},{10,... | collective-permute-start | bytes 1032200 | tf_op jit(solution)/shard_map/ppermute | solution.py:934
  328.0 55.6 %collective-permute-start.33 = (bf16[21,64,128]{2,1,0:T(8,128)(2,1)S(1)}, bf16[21,64,128]{2,1,0:T(8,128)(2,1)S(1)}, u32[]{:S(2)}, u32[]{:S(2)}) collective-permute-start(bf16[21,64,128]{2,1,0:T(8,128)(2,1)S(1)} %copy-done.46), channel_id=1, source_target_pairs={{0,2},{1,3},{2,4},{3,5},{4,6},{5,7},{6,0},{7,1},{8,10},{9,11},{10,... | collective-permute-start | bytes 1032200 | tf_op jit(solution)/shard_map/ppermute | solution.py:934
  336.1 47.5 %collective-permute-start.34 = (bf16[21,64,128]{2,1,0:T(8,128)(2,1)S(1)}, bf16[21,64,128]{2,1,0:T(8,128)(2,1)S(1)}, u32[]{:S(2)}, u32[]{:S(2)}) collective-permute-start(bf16[21,64,128]{2,1,0:T(8,128)(2,1)S(1)} %copy-done.45), channel_id=1, source_target_pairs={{0,1},{1,2},{2,3},{3,4},{4,5},{5,6},{6,7},{7,0},{8,9},{9,10},{10,1... | collective-permute-start | bytes 1032200 | tf_op jit(solution)/shard_map/ppermute | solution.py:934
  401.6 297.8 %all-reduce.20.cloned.1.call-start = ((), (), s32[]{:S(2)}) async-start(), calls=%async_computation.1 | async-start | bytes 4014080 | tf_op jit(solution)/shard_map/psum | solution.py:1002
  416.8 8.0 collective-permute-start.21
  416.9 11.4 %collective-permute-start.22 = (bf16[14,64,128]{2,1,0:T(8,128)(2,1)}, bf16[14,64,128]{2,1,0:T(8,128)(2,1)}, u32[]{:S(2)}, u32[]{:S(2)}) collective-permute-start(bf16[14,64,128]{2,1,0:T(8,128)(2,1)} %get-tuple-element.155), channel_id=1, source_target_pairs={{0,6},{1,7},{2,0},{3,1},{4,2},{5,3},{6,4},{7,5},{8,14},{9,15},{10,... | collective-permute-start | bytes 688136 | tf_op jit(solution)/shard_map/ppermute | solution.py:934
  417.6 15.6 %collective-permute-start.23 = (bf16[14,64,128]{2,1,0:T(8,128)(2,1)}, bf16[14,64,128]{2,1,0:T(8,128)(2,1)}, u32[]{:S(2)}, u32[]{:S(2)}) collective-permute-start(bf16[14,64,128]{2,1,0:T(8,128)(2,1)} %get-tuple-element.156), channel_id=1, source_target_pairs={{0,5},{1,6},{2,7},{3,0},{4,1},{5,2},{6,3},{7,4},{8,13},{9,14},{10,... | collective-permute-start | bytes 688136 | tf_op jit(solution)/shard_map/ppermute | solution.py:934
  417.6 37.6 %collective-permute-start.24 = (bf16[14,64,128]{2,1,0:T(8,128)(2,1)}, bf16[14,64,128]{2,1,0:T(8,128)(2,1)}, u32[]{:S(2)}, u32[]{:S(2)}) collective-permute-start(bf16[14,64,128]{2,1,0:T(8,128)(2,1)} %get-tuple-element.157), channel_id=1, source_target_pairs={{0,4},{1,5},{2,6},{3,7},{4,0},{5,1},{6,2},{7,3},{8,12},{9,13},{10,... | collective-permute-start | bytes 688136 | tf_op jit(solution)/shard_map/ppermute | solution.py:934
  421.3 35.0 %collective-permute-start.25 = (bf16[14,64,128]{2,1,0:T(8,128)(2,1)}, bf16[14,64,128]{2,1,0:T(8,128)(2,1)}, u32[]{:S(2)}, u32[]{:S(2)}) collective-permute-start(bf16[14,64,128]{2,1,0:T(8,128)(2,1)} %get-tuple-element.158), channel_id=1, source_target_pairs={{0,3},{1,4},{2,5},{3,6},{4,7},{5,0},{6,1},{7,2},{8,11},{9,12},{10,... | collective-permute-start | bytes 688136 | tf_op jit(solution)/shard_map/ppermute | solution.py:934
  424.8 31.5 %collective-permute-start.26 = (bf16[14,64,128]{2,1,0:T(8,128)(2,1)}, bf16[14,64,128]{2,1,0:T(8,128)(2,1)}, u32[]{:S(2)}, u32[]{:S(2)}) collective-permute-start(bf16[14,64,128]{2,1,0:T(8,128)(2,1)} %get-tuple-element.159), channel_id=1, source_target_pairs={{0,2},{1,3},{2,4},{3,5},{4,6},{5,7},{6,0},{7,1},{8,10},{9,11},{10,... | collective-permute-start | bytes 688136 | tf_op jit(solution)/shard_map/ppermute | solution.py:934
  428.3 28.1 %collective-permute-start.27 = (bf16[14,64,128]{2,1,0:T(8,128)(2,1)}, bf16[14,64,128]{2,1,0:T(8,128)(2,1)}, u32[]{:S(2)}, u32[]{:S(2)}) collective-permute-start(bf16[14,64,128]{2,1,0:T(8,128)(2,1)} %get-tuple-element.160), channel_id=1, source_target_pairs={{0,1},{1,2},{2,3},{3,4},{4,5},{5,6},{6,7},{7,0},{8,9},{9,10},{10,1... | collective-permute-start | bytes 688136 | tf_op jit(solution)/shard_map/ppermute | solution.py:934
  470.4 7.5 collective-permute-start.35
  470.5 11.9 %collective-permute-start.36 = (bf16[14,64,128]{2,1,0:T(8,128)(2,1)}, bf16[14,64,128]{2,1,0:T(8,128)(2,1)}, u32[]{:S(2)}, u32[]{:S(2)}) collective-permute-start(bf16[14,64,128]{2,1,0:T(8,128)(2,1)} %get-tuple-element.182), channel_id=1, source_target_pairs={{0,6},{1,7},{2,0},{3,1},{4,2},{5,3},{6,4},{7,5},{8,14},{9,15},{10,... | collective-permute-start | bytes 688136 | tf_op jit(solution)/shard_map/ppermute | solution.py:934
  471.5 15.2 %collective-permute-start.37 = (bf16[14,64,128]{2,1,0:T(8,128)(2,1)}, bf16[14,64,128]{2,1,0:T(8,128)(2,1)}, u32[]{:S(2)}, u32[]{:S(2)}) collective-permute-start(bf16[14,64,128]{2,1,0:T(8,128)(2,1)} %get-tuple-element.183), channel_id=1, source_target_pairs={{0,5},{1,6},{2,7},{3,0},{4,1},{5,2},{6,3},{7,4},{8,13},{9,14},{10,... | collective-permute-start | bytes 688136 | tf_op jit(solution)/shard_map/ppermute | solution.py:934
  475.9 39.1 %collective-permute-start.38 = (bf16[14,64,128]{2,1,0:T(8,128)(2,1)}, bf16[14,64,128]{2,1,0:T(8,128)(2,1)}, u32[]{:S(2)}, u32[]{:S(2)}) collective-permute-start(bf16[14,64,128]{2,1,0:T(8,128)(2,1)} %get-tuple-element.184), channel_id=1, source_target_pairs={{0,4},{1,5},{2,6},{3,7},{4,0},{5,1},{6,2},{7,3},{8,12},{9,13},{10,... | collective-permute-start | bytes 688136 | tf_op jit(solution)/shard_map/ppermute | solution.py:934
  475.9 40.3 %collective-permute-start.39 = (bf16[14,64,128]{2,1,0:T(8,128)(2,1)}, bf16[14,64,128]{2,1,0:T(8,128)(2,1)}, u32[]{:S(2)}, u32[]{:S(2)}) collective-permute-start(bf16[14,64,128]{2,1,0:T(8,128)(2,1)} %get-tuple-element.185), channel_id=1, source_target_pairs={{0,3},{1,4},{2,5},{3,6},{4,7},{5,0},{6,1},{7,2},{8,11},{9,12},{10,... | collective-permute-start | bytes 688136 | tf_op jit(solution)/shard_map/ppermute | solution.py:934
  477.9 38.3 %collective-permute-start.40 = (bf16[14,64,128]{2,1,0:T(8,128)(2,1)}, bf16[14,64,128]{2,1,0:T(8,128)(2,1)}, u32[]{:S(2)}, u32[]{:S(2)}) collective-permute-start(bf16[14,64,128]{2,1,0:T(8,128)(2,1)} %get-tuple-element.186), channel_id=1, source_target_pairs={{0,2},{1,3},{2,4},{3,5},{4,6},{5,7},{6,0},{7,1},{8,10},{9,11},{10,... | collective-permute-start | bytes 688136 | tf_op jit(solution)/shard_map/ppermute | solution.py:934
  482.3 33.9 %collective-permute-start.41 = (bf16[14,64,128]{2,1,0:T(8,128)(2,1)}, bf16[14,64,128]{2,1,0:T(8,128)(2,1)}, u32[]{:S(2)}, u32[]{:S(2)}) collective-permute-start(bf16[14,64,128]{2,1,0:T(8,128)(2,1)} %get-tuple-element.187), channel_id=1, source_target_pairs={{0,1},{1,2},{2,3},{3,4},{4,5},{5,6},{6,7},{7,0},{8,9},{9,10},{10,1... | collective-permute-start | bytes 688136 | tf_op jit(solution)/shard_map/ppermute | solution.py:934
  550.5 16.4 %collective-permute-start.42 = (bf16[21,64,128]{2,1,0:T(8,128)(2,1)S(1)}, bf16[21,64,128]{2,1,0:T(8,128)(2,1)S(1)}, u32[]{:S(2)}, u32[]{:S(2)}) collective-permute-start(bf16[21,64,128]{2,1,0:T(8,128)(2,1)S(1)} %copy-done.50), channel_id=1, source_target_pairs={{0,7},{1,0},{2,1},{3,2},{4,3},{5,4},{6,5},{7,6},{8,15},{9,8},{10,9... | collective-permute-start | bytes 1032200 | tf_op jit(solution)/shard_map/ppermute | solution.py:934
  550.7 30.0 %collective-permute-start.43 = (bf16[21,64,128]{2,1,0:T(8,128)(2,1)S(1)}, bf16[21,64,128]{2,1,0:T(8,128)(2,1)S(1)}, u32[]{:S(2)}, u32[]{:S(2)}) collective-permute-start(bf16[21,64,128]{2,1,0:T(8,128)(2,1)S(1)} %copy-done.49), channel_id=1, source_target_pairs={{0,6},{1,7},{2,0},{3,1},{4,2},{5,3},{6,4},{7,5},{8,14},{9,15},{10,... | collective-permute-start | bytes 1032200 | tf_op jit(solution)/shard_map/ppermute | solution.py:934
  551.5 44.0 %collective-permute-start.44 = (bf16[21,64,128]{2,1,0:T(8,128)(2,1)}, bf16[21,64,128]{2,1,0:T(8,128)(2,1)}, u32[]{:S(2)}, u32[]{:S(2)}) collective-permute-start(bf16[21,64,128]{2,1,0:T(8,128)(2,1)} %get-tuple-element.212), channel_id=1, source_target_pairs={{0,5},{1,6},{2,7},{3,0},{4,1},{5,2},{6,3},{7,4},{8,13},{9,14},{10,... | collective-permute-start | bytes 1032200 | tf_op jit(solution)/shard_map/ppermute | solution.py:934
  551.5 82.0 %collective-permute-start.45 = (bf16[21,64,128]{2,1,0:T(8,128)(2,1)}, bf16[21,64,128]{2,1,0:T(8,128)(2,1)}, u32[]{:S(2)}, u32[]{:S(2)}) collective-permute-start(bf16[21,64,128]{2,1,0:T(8,128)(2,1)} %get-tuple-element.213), channel_id=1, source_target_pairs={{0,4},{1,5},{2,6},{3,7},{4,0},{5,1},{6,2},{7,3},{8,12},{9,13},{10,... | collective-permute-start | bytes 1032200 | tf_op jit(solution)/shard_map/ppermute | solution.py:934
  554.9 82.0 %collective-permute-start.46 = (bf16[21,64,128]{2,1,0:T(8,128)(2,1)}, bf16[21,64,128]{2,1,0:T(8,128)(2,1)}, u32[]{:S(2)}, u32[]{:S(2)}) collective-permute-start(bf16[21,64,128]{2,1,0:T(8,128)(2,1)} %get-tuple-element.214), channel_id=1, source_target_pairs={{0,3},{1,4},{2,5},{3,6},{4,7},{5,0},{6,1},{7,2},{8,11},{9,12},{10,... | collective-permute-start | bytes 1032200 | tf_op jit(solution)/shard_map/ppermute | solution.py:934
  566.9 69.9 %collective-permute-start.47 = (bf16[21,64,128]{2,1,0:T(8,128)(2,1)}, bf16[21,64,128]{2,1,0:T(8,128)(2,1)}, u32[]{:S(2)}, u32[]{:S(2)}) collective-permute-start(bf16[21,64,128]{2,1,0:T(8,128)(2,1)} %get-tuple-element.215), channel_id=1, source_target_pairs={{0,2},{1,3},{2,4},{3,5},{4,6},{5,7},{6,0},{7,1},{8,10},{9,11},{10,... | collective-permute-start | bytes 1032200 | tf_op jit(solution)/shard_map/ppermute | solution.py:934
  580.7 56.2 %collective-permute-start.48 = (bf16[21,64,128]{2,1,0:T(8,128)(2,1)}, bf16[21,64,128]{2,1,0:T(8,128)(2,1)}, u32[]{:S(2)}, u32[]{:S(2)}) collective-permute-start(bf16[21,64,128]{2,1,0:T(8,128)(2,1)} %get-tuple-element.216), channel_id=1, source_target_pairs={{0,1},{1,2},{2,3},{3,4},{4,5},{5,6},{6,7},{7,0},{8,9},{9,10},{10,1... | collective-permute-start | bytes 1032200 | tf_op jit(solution)/shard_map/ppermute | solution.py:934
  581.4 97.2 %copy-start.2 = (bf16[21,80,720]{2,1,0:T(8,128)(2,1)S(1)}, bf16[21,80,720]{2,1,0:T(8,128)(2,1)}, u32[]{:S(2)}) copy-start(bf16[21,80,720]{2,1,0:T(8,128)(2,1)} %get-tuple-element.196.own_ref) | copy-start | bytes 7257604
  675.0 35.9 %collective-permute-start.50 = (bf16[49,40,128]{2,1,0:T(8,128)(2,1)}, bf16[49,40,128]{2,1,0:T(8,128)(2,1)S(1)}, u32[]{:S(2)}, u32[]{:S(2)}) collective-permute-start(bf16[49,40,128]{2,1,0:T(8,128)(2,1)} %get-tuple-element.227), channel_id=1, source_target_pairs={{0,6},{1,7},{2,0},{3,1},{4,2},{5,3},{6,4},{7,5},{8,14},{9,15},{10,... | collective-permute-start | bytes 1505288 | tf_op jit(solution)/shard_map/ppermute | solution.py:934
  675.1 71.1 %collective-permute-start.51 = (bf16[49,40,128]{2,1,0:T(8,128)(2,1)}, bf16[49,40,128]{2,1,0:T(8,128)(2,1)}, u32[]{:S(2)}, u32[]{:S(2)}) collective-permute-start(bf16[49,40,128]{2,1,0:T(8,128)(2,1)} %get-tuple-element.228), channel_id=1, source_target_pairs={{0,5},{1,6},{2,7},{3,0},{4,1},{5,2},{6,3},{7,4},{8,13},{9,14},{10,... | collective-permute-start | bytes 1505288 | tf_op jit(solution)/shard_map/ppermute | solution.py:934
  687.4 77.0 %collective-permute-start.52 = (bf16[49,40,128]{2,1,0:T(8,128)(2,1)}, bf16[49,40,128]{2,1,0:T(8,128)(2,1)S(1)}, u32[]{:S(2)}, u32[]{:S(2)}) collective-permute-start(bf16[49,40,128]{2,1,0:T(8,128)(2,1)} %get-tuple-element.229), channel_id=1, source_target_pairs={{0,4},{1,5},{2,6},{3,7},{4,0},{5,1},{6,2},{7,3},{8,12},{9,13},{10,... | collective-permute-start | bytes 1505288 | tf_op jit(solution)/shard_map/ppermute | solution.py:934
  689.4 88.0 %collective-permute-start.53 = (bf16[49,40,128]{2,1,0:T(8,128)(2,1)}, bf16[49,40,128]{2,1,0:T(8,128)(2,1)S(1)}, u32[]{:S(2)}, u32[]{:S(2)}) collective-permute-start(bf16[49,40,128]{2,1,0:T(8,128)(2,1)} %get-tuple-element.230), channel_id=1, source_target_pairs={{0,3},{1,4},{2,5},{3,6},{4,7},{5,0},{6,1},{7,2},{8,11},{9,12},{10,... | collective-permute-start | bytes 1505288 | tf_op jit(solution)/shard_map/ppermute | solution.py:934
  690.9 65.2 %copy-start.5 = (bf16[8,32,2,720]{3,1,0,2:T(8,128)(2,1)S(1)}, bf16[8,32,2,720]{3,1,0,2:T(8,128)(2,1)}, u32[]{:S(2)}) copy-start(bf16[8,32,2,720]{3,1,0,2:T(8,128)(2,1)} %get-tuple-element.243) | copy-start | bytes 2211844
  690.9 86.4 %collective-permute-start.54 = (bf16[49,40,128]{2,1,0:T(8,128)(2,1)}, bf16[49,40,128]{2,1,0:T(8,128)(2,1)}, u32[]{:S(2)}, u32[]{:S(2)}) collective-permute-start(bf16[49,40,128]{2,1,0:T(8,128)(2,1)} %get-tuple-element.231), channel_id=1, source_target_pairs={{0,2},{1,3},{2,4},{3,5},{4,6},{5,7},{6,0},{7,1},{8,10},{9,11},{10,... | collective-permute-start | bytes 1505288 | tf_op jit(solution)/shard_map/ppermute | solution.py:934
  710.9 66.5 %collective-permute-start.49 = (bf16[49,40,128]{2,1,0:T(8,128)(2,1)}, bf16[49,40,128]{2,1,0:T(8,128)(2,1)S(1)}, u32[]{:S(2)}, u32[]{:S(2)}) collective-permute-start(bf16[49,40,128]{2,1,0:T(8,128)(2,1)} %get-tuple-element.226), channel_id=1, source_target_pairs={{0,7},{1,0},{2,1},{3,2},{4,3},{5,4},{6,5},{7,6},{8,15},{9,8},{10,9... | collective-permute-start | bytes 1505288 | tf_op jit(solution)/shard_map/ppermute | solution.py:934
  746.2 31.2 %collective-permute-start.55 = (bf16[49,40,128]{2,1,0:T(8,128)(2,1)}, bf16[49,40,128]{2,1,0:T(8,128)(2,1)}, u32[]{:S(2)}, u32[]{:S(2)}) collective-permute-start(bf16[49,40,128]{2,1,0:T(8,128)(2,1)} %get-tuple-element.232), channel_id=1, source_target_pairs={{0,1},{1,2},{2,3},{3,4},{4,5},{5,6},{6,7},{7,0},{8,9},{9,10},{10,1... | collective-permute-start | bytes 1505288 | tf_op jit(solution)/shard_map/ppermute | solution.py:934
  (55 other events, 792.2 us)
Sparse Core Ops, SparseCore 0:
  74.4 163.0 all-reduce.17
  266.9 46.9 all-gather.6
  319.4 49.5 all-gather.8
  401.7 66.5 all-gather.10
  549.7 149.7 all-reduce.19
